TPU v7x, 32 devices: a whole 2x2x4 slice. The times are simulated.
32 devices in a mesh: dp: 16 (over z, y, core), mp: 2 (over x).
Axes of the slice: x: 2, y: 2, z: 4, core: 2. Of those that a mesh axis runs over, the one named last changes fastest.
Arguments:
- image_tokens: bfloat16 [256, 64, 1536], P('dp'), may hold values from -6 to 6
- text_tokens: bfloat16 [256, 32, 1536], P('dp'), may hold values from -6 to 6
- image_weight: bfloat16 [1536, 1536], P(None, 'mp'), may hold values from -0.15625 to 0.15625
- text_weight: bfloat16 [1536, 1536], P(None, 'mp'), may hold values from -0.15625 to 0.15625
- logit_scale: float32 [1], replicated, may hold values from 6 to 14
- logit_bias: float32 [1], replicated, may hold values from -8 to -5
- loss_scale: float32 [1], replicated, may hold values from 256 to 4096
- valid_count: int32 [16], P('dp'), may hold values from 3 to 16, as said below
Outputs:
- loss: float32 [], replicated
- image_weight_grad: float32 [1536, 1536], P('dp', 'mp')
- text_weight_grad: float32 [1536, 1536], P('dp', 'mp')
Inputs may be any that keep to these rules, and one draw needn't show every extreme that they name: `valid_count`: at least one index of dp has all 16 pairs valid.
All inputs are finite; a program needn't handle non-finite values.
Results may differ from a plain program's by a relative error of at most 0.0014.
Values may be sent and summed in bfloat16 or wider, within the bound.
No kernel may reach another device: no remote copies, remote signals or barrier semaphores. Data moves between devices by JAX's collectives and lax.ppermute only.
A program may use at most 128 MiB of HBM per device.

v0:
```python
import jax
import jax.numpy as jnp
from jax import lax
from jax.sharding import PartitionSpec as P


def gelu_slope(values):
    return jax.jvp(
        lambda inner: jax.nn.gelu(inner, approximate=True), (values,), (jnp.ones_like(values),)
    )[1]


def tower_block(tokens, weight, offset):
    flat_tokens = tokens.reshape(-1, tokens.shape[2])
    preact = jnp.dot(flat_tokens, weight, preferred_element_type=jnp.float32)
    residual = lax.dynamic_slice_in_dim(flat_tokens, offset, weight.shape[1], 1).astype(jnp.float32)
    hidden = residual + jax.nn.gelu(preact, approximate=True)
    pooled = jnp.mean(hidden.reshape(tokens.shape[0], tokens.shape[1], -1), axis=1)
    return (flat_tokens, preact, pooled)


def contract_rows(left_rows, right_rows):
    return lax.dot_general(
        left_rows, right_rows, (((0,), (0,)), ((), ())), preferred_element_type=jnp.float32
    )


def row_products(left_rows, right_rows):
    return lax.dot_general(
        left_rows, right_rows, (((1,), (1,)), ((), ())), preferred_element_type=jnp.float32
    )


def weight_terms(flat_tokens, grad_preact):
    return contract_rows(flat_tokens, grad_preact)


def text_terms_of(dlogit, image_bf):
    return contract_rows(dlogit, image_bf)


def body(
    image_tokens,
    text_tokens,
    image_weight,
    text_weight,
    logit_scale,
    logit_bias,
    loss_scale,
    valid_count,
):
    samples_here = image_tokens.shape[0]
    half_width = image_weight.shape[1]
    cycle_size = lax.axis_size("dp")
    cycle_place = lax.axis_index("dp")
    model_place = lax.axis_index("mp")
    half_start = model_place * half_width
    image_flat, image_preact, image_pooled = tower_block(image_tokens, image_weight, half_start)
    text_flat, text_preact, text_pooled = tower_block(text_tokens, text_weight, half_start)
    image_sq, text_sq = lax.psum(
        (jnp.sum(image_pooled * image_pooled, axis=1), jnp.sum(text_pooled * text_pooled, axis=1)),
        "mp",
    )
    image_norm = jnp.sqrt(image_sq + 1e-06)
    text_norm = jnp.sqrt(text_sq + 1e-06)
    image_unit = image_pooled / image_norm[:, None]
    text_unit = text_pooled / text_norm[:, None]
    image_bf = image_unit.astype(jnp.bfloat16)
    text_bf = text_unit.astype(jnp.bfloat16)
    all_counts = lax.all_gather(valid_count, "dp", axis=0, tiled=True)
    total_count = jnp.sum(all_counts).astype(jnp.float32)
    logit_mult = logit_scale[0]
    offset_term = logit_bias[0]
    grad_coeff = loss_scale[0] / total_count
    positions = jnp.arange(samples_here, dtype=jnp.int32)
    own_usable = positions < lax.dynamic_index_in_dim(all_counts, cycle_place, 0, False)
    own_rows = cycle_place * samples_here + positions
    all_columns = samples_here * cycle_size
    image_full, text_full = (
        lax.all_gather(image_bf, "mp", axis=1, tiled=True),
        lax.all_gather(text_bf, "mp", axis=1, tiled=True),
    )
    all_text = lax.all_gather(text_full, "dp", axis=0, tiled=True)
    columns = jnp.arange(all_columns, dtype=jnp.int32)
    logits = logit_mult * row_products(image_full, all_text) + offset_term
    col_usable = columns % samples_here < jnp.take(all_counts, columns // samples_here)
    pair_sign = jnp.where(columns[None, :] == own_rows[:, None], 1.0, -1.0).astype(jnp.float32)
    weighting = own_usable[:, None] & col_usable[None, :]
    margin = -pair_sign * logits
    loss_part = jnp.sum(jnp.where(weighting, jax.nn.softplus(margin), 0.0))
    dlogit = (jnp.where(weighting, -pair_sign * jax.nn.sigmoid(margin), 0.0) * grad_coeff).astype(
        jnp.bfloat16
    )
    loss_local, dlogit = (loss_part, dlogit)
    own_text = lax.dynamic_slice_in_dim(all_text, half_start, half_width, 1)
    image_raw = jnp.dot(dlogit, own_text, preferred_element_type=jnp.float32)
    text_raw = lax.psum_scatter(
        text_terms_of(dlogit, image_bf), "dp", scatter_dimension=0, tiled=True
    )
    loss = lax.psum(loss_local / total_count, "dp")
    image_grad = logit_mult * image_raw
    text_grad = logit_mult * text_raw
    image_rad, text_rad = lax.psum(
        (jnp.sum(image_unit * image_grad, axis=1), jnp.sum(text_unit * text_grad, axis=1)), "mp"
    )
    image_gp = (image_grad - image_unit * image_rad[:, None]) / image_norm[:, None]
    text_gp = (text_grad - text_unit * text_rad[:, None]) / text_norm[:, None]
    image_count = image_tokens.shape[1]
    text_count = text_tokens.shape[1]
    image_slope = gelu_slope(image_preact.reshape(samples_here, image_count, half_width))
    text_slope = gelu_slope(text_preact.reshape(samples_here, text_count, half_width))
    image_gpre = (
        (image_gp[:, None, :] / image_count * image_slope)
        .astype(jnp.bfloat16)
        .reshape(-1, half_width)
    )
    text_gpre = (
        (text_gp[:, None, :] / text_count * text_slope).astype(jnp.bfloat16).reshape(-1, half_width)
    )
    image_weight_grad = lax.psum_scatter(
        weight_terms(image_flat, image_gpre), "dp", scatter_dimension=0, tiled=True
    )
    text_weight_grad = lax.psum_scatter(
        weight_terms(text_flat, text_gpre), "dp", scatter_dimension=0, tiled=True
    )
    return (loss, image_weight_grad, text_weight_grad)


def solution(mesh):
    placed = (
        P("dp", None, None),
        P("dp", None, None),
        P(None, "mp"),
        P(None, "mp"),
        P(),
        P(),
        P(),
        P("dp"),
    )
    return jax.shard_map(
        body,
        mesh=mesh,
        in_specs=placed,
        out_specs=(P(), P("dp", "mp"), P("dp", "mp")),
        check_vma=False,
    )
```

profile of v0, /device:TPU:0, one launch (start us, length us, event | category | flops | bytes accessed | tf_op | source)
XLA Modules:
  0.0 321.7 jit_solution(8115979757393268173)
XLA Ops:
  7.2 0.0 copy-start
  7.2 0.0 reduce-scatter.8.cloned.1.call-start
  9.5 1.2 dynamic-slice
  10.7 0.8 dynamic-update-slice
  12.1 13.7 %all-reduce = s32[16]{0:T(128)S(1)} all-reduce(s32[16]{0:T(128)S(1)} %dynamic-update-slice), channel_id=1, replica_groups=mesh['dp'=16,'mp'=2] {'dp'}, use_global_device_ids=true, to_apply=%add | all-reduce | flops 16 | bytes 128
  25.9 0.6 reduce_sum.77
  27.2 0.7 fusion.77
  27.9 0.7 iota_compare_fusion.1
  28.6 0.0 copy-start.2
  28.6 5.3 %bitcast_reduce_fusion.1 = (f32[16,768]{1,0:T(8,128)S(1)}, f32[512,768]{1,0:T(8,128)}) fusion(bf16[512,1536]{1,0:T(8,128)(2,1)} %bitcast.57, s32[]{:T(128)S(6)} %select_n.90, bf16[1536,768]{1,0:T(8,128)(2,1)} %param.11), kind=kOutput, calls=%fused_computation.49 | convolution fusion | flops 1212272640 | bytes 6340612 | tf_op jit(solution)/shard_map/dot_general | solution.py:15
  33.9 0.0 copy-done
  33.9 0.0 copy-done.2
  33.9 4.9 %bitcast_reduce_fusion = (f32[16,768]{1,0:T(8,128)S(1)}, f32[1024,768]{1,0:T(8,128)}) fusion(bf16[1024,1536]{1,0:T(8,128)(2,1)S(1)} %bitcast.56, s32[]{:T(128)S(6)} %select_n.90, bf16[1536,768]{1,0:T(8,128)(2,1)S(1)} %copy-done), kind=kOutput, calls=%fused_computation.25 | convolution fusion | flops 2424557568 | bytes 10272772 | tf_op jit(solution)/shard_map/dot_general | solution.py:15
  38.8 0.1 multiply_reduce_fusion.2
  38.9 5.0 %all-reduce.2 = (f32[16]{0:T(128)S(1)}, f32[16]{0:T(128)S(1)}) all-reduce(f32[16]{0:T(128)S(1)} %get-tuple-element.50, f32[16]{0:T(128)S(1)} %get-tuple-element.49), channel_id=1, replica_groups=mesh['dp'=16,'mp'=2] {'mp'}, use_global_device_ids=true, to_apply=%region_2.0 | all-reduce | flops 32 | bytes 256 | tf_op jit(solution)/shard_map/psum | solution.py:60
  43.9 0.1 fusion.75
  44.0 0.1 fusion.76
  44.1 4.5 %all_gather.14 = bf16[16,1536]{1,0:T(8,128)(2,1)S(1)} all-gather(bf16[16,768]{1,0:T(8,128)(2,1)S(1)} %fusion.76), channel_id=1, replica_groups=mesh['dp'=16,'mp'=2] {'mp'}, dimensions={1}, use_global_device_ids=true | all-gather | bytes 73728 | tf_op jit(solution)/shard_map/all_gather | solution.py:81
  48.6 4.5 %all_gather.13 = bf16[16,1536]{1,0:T(8,128)(2,1)S(1)} all-gather(bf16[16,768]{1,0:T(8,128)(2,1)S(1)} %fusion.75), channel_id=1, replica_groups=mesh['dp'=16,'mp'=2] {'mp'}, dimensions={1}, use_global_device_ids=true | all-gather | bytes 73728 | tf_op jit(solution)/shard_map/all_gather | solution.py:80
  53.0 20.1 %all_gather.15 = bf16[256,1536]{1,0:T(8,128)(2,1)S(1)} all-gather(bf16[16,1536]{1,0:T(8,128)(2,1)S(1)} %all_gather.14), channel_id=1, replica_groups=mesh['dp'=16,'mp'=2] {'dp'}, dimensions={0}, use_global_device_ids=true | all-gather | bytes 835584 | tf_op jit(solution)/shard_map/all_gather | solution.py:83
  73.2 4.3 %compare_select_fusion.2 = s32[256,1]{0,1:T(1,128)S(1)} fusion(s32[]{:T(128)} %bitcast.11, s32[]{:T(128)} %bitcast.12, s32[]{:T(128)} %bitcast.13, s32[]{:T(128)} %bitcast.14, s32[]{:T(128)} %bitcast.15, s32[]{:T(128)} %bitcast.17, s32[]{:T(128)} %bitcast.16), kind=kLoop, calls=%fused_computation.93 | loop fusion | flops 5888 | bytes 1052 | tf_op jit(solution)/shard_map/jit(_take)/gather | solution.py:86
  77.5 5.6 %fusion.60 = pred[256]{0:T(512)(128)(4,1)S(1)} fusion(pred[256]{0:T(512)(128)(4,1)S(1)} %get-tuple-element.41, pred[256]{0:T(512)(128)(4,1)S(1)} %get-tuple-element.42, pred[256]{0:T(512)(128)(4,1)S(1)} %get-tuple-element.43, pred[256]{0:T(512)(128)(4,1)S(1)} %get-tuple-element.44, pred[256]{0:T(512)(128)(4,1)S(1)} %get-tuple-element.45, ...), kind=kLoop, calls=%fused_computation.109 | loop fusion | flops 7424 | bytes 3620 | tf_op jit(solution)/shard_map/lt | solution.py:86
  83.1 0.9 fusion.57
  84.0 1.2 fusion.72
  85.3 0.0 reduce-scatter.8.cloned.1.call-update
  85.3 0.0 reduce-scatter.10.cloned.1.call-start
  85.3 0.3 multiply_reduce_fusion.1
  85.7 54.2 %reduce-scatter.8.cloned.1.call-done = f32[16,768]{1,0:T(8,128)} async-done(((f32[256,768]{1,0:T(8,128)}), f32[16,768]{1,0:T(8,128)}) %reduce-scatter.8.cloned.1.call-update) | async-done | bytes 49168 | tf_op jit(solution)/shard_map/reduce_scatter | solution.py:97
  139.9 1.0 multiply_reduce_fusion
  140.8 4.9 %all-reduce.1 = (f32[16]{0:T(128)S(1)}, f32[16]{0:T(128)S(1)}) all-reduce(f32[16]{0:T(128)S(1)} %get-tuple-element.39, f32[16]{0:T(128)S(1)} %multiply_reduce_fusion), channel_id=1, replica_groups=mesh['dp'=16,'mp'=2] {'mp'}, use_global_device_ids=true, to_apply=%region_10.11 | all-reduce | flops 32 | bytes 256 | tf_op jit(solution)/shard_map/psum | solution.py:103
  145.8 0.1 divide_multiply_fusion.1
  145.9 9.0 %convolution_bitcast_fusion.1 = f32[1536,768]{0,1:T(8,128)} fusion(bf16[16,64,1536]{2,1,0:T(8,128)(2,1)} %param.8, f32[16,64,768]{2,1,0:T(8,128)} %bitcast.58, f32[16,768]{1,0:T(8,128)S(1)} %divide_multiply_fusion.1), kind=kOutput, calls=%fused_computation.4 | convolution fusion | flops 2430074880 | bytes 11059200 | tf_op jit(solution)/shard_map/dot_general | solution.py:23
  154.9 6.0 %copy.17 = f32[1536,768]{1,0:T(8,128)} copy(f32[1536,768]{0,1:T(8,128)} %convolution_bitcast_fusion.1) | data formatting | bytes 9437184
  160.9 0.0 copy-start.1
  160.9 0.0 reduce-scatter.10.cloned.1.call-update
  161.0 0.0 reduce-scatter.12.cloned.1.call-start
  161.0 0.7 copy-done.1
  161.7 0.1 divide_multiply_fusion
  161.8 6.2 %convolution_bitcast_fusion = f32[1536,768]{0,1:T(8,128)} fusion(bf16[16,32,1536]{2,1,0:T(8,128)(2,1)} %param.9, f32[16,32,768]{2,1,0:T(8,128)} %bitcast.59, f32[16,768]{1,0:T(8,128)S(1)} %divide_multiply_fusion), kind=kOutput, calls=%fused_computation.3 | convolution fusion | flops 1215037440 | bytes 7913472 | tf_op jit(solution)/shard_map/dot_general | solution.py:23
  168.0 6.3 %copy.19 = f32[1536,768]{1,0:T(8,128)} copy(f32[1536,768]{0,1:T(8,128)} %convolution_bitcast_fusion) | data formatting | bytes 9437184
  174.3 0.0 reduce-scatter.12.cloned.1.call-update
  174.9 30.5 %psum.37 = f32[]{:T(128)} all-reduce(f32[]{:T(128)S(6)} %div.81), channel_id=1, replica_groups=mesh['dp'=16,'mp'=2] {'dp'}, use_global_device_ids=true, to_apply=%region_8.9 | all-reduce | flops 1 | bytes 8 | tf_op jit(solution)/shard_map/psum | solution.py:100
  205.4 30.6 %reduce-scatter.10.cloned.1.call-done = f32[96,768]{1,0:T(8,128)} async-done(((f32[1536,768]{1,0:T(8,128)}), f32[96,768]{1,0:T(8,128)}) %reduce-scatter.10.cloned.1.call-update) | async-done | bytes 294928
  236.0 79.1 %reduce-scatter.12.cloned.1.call-done = f32[96,768]{1,0:T(8,128)} async-done(((f32[1536,768]{1,0:T(8,128)}), f32[96,768]{1,0:T(8,128)}) %reduce-scatter.12.cloned.1.call-update) | async-done | bytes 294928
  (9 shorter events, 0.2 us)
Async XLA Ops:
  7.2 26.7 %copy-start = (bf16[1536,768]{1,0:T(8,128)(2,1)S(1)}, bf16[1536,768]{1,0:T(8,128)(2,1)}, u32[]{:S(2)}) copy-start(bf16[1536,768]{1,0:T(8,128)(2,1)} %param.10) | copy-start | bytes 7077892
  7.2 132.7 %reduce-scatter.8.cloned.1.call-start = ((), (), s32[]{:S(2)}) async-start(), calls=%async_computation.3 | async-start | bytes 835584 | tf_op jit(solution)/shard_map/reduce_scatter | solution.py:97
  28.6 5.3 %copy-start.2 = (bf16[16,64,1536]{2,1,0:T(8,128)(2,1)S(1)}, bf16[16,64,1536]{2,1,0:T(8,128)(2,1)}, u32[]{:S(2)}) copy-start(bf16[16,64,1536]{2,1,0:T(8,128)(2,1)} %param.8) | copy-start | bytes 9437188
  85.3 150.8 %reduce-scatter.10.cloned.1.call-start = ((), (), s32[]{:S(2)}) async-start(), calls=%async_computation.4 | async-start | bytes 5013504
  160.9 0.8 copy-start.1
  161.0 154.2 %reduce-scatter.12.cloned.1.call-start = ((), (), s32[]{:S(2)}) async-start(), calls=%async_computation.5 | async-start | bytes 5013504
Sparse Core Ops, SparseCore 0:
  85.4 54.4 reduce-scatter.7
  161.1 74.9 reduce-scatter.9
  240.5 74.6 reduce-scatter.11
where the time goes:
time: 322 us
  waiting for transfers between devices  164 us (51%)
  blocking collectives  83.2 us (26%)
  matrix products  27.9 us (9%)
  between operations  17.9 us (6%)
  local copies, waits for them, and re-layouts  15.8 us (5%)
  other arithmetic  12.8 us (4%)
    unnamed x5, waiting for transfers between devices  110 us
    reduce_scatter x1, waiting for transfers between devices, body(): lax.psum_scatter(text_terms_of(dlogit, image_bf), 'dp', scatter_dimension...  54.2 us
    psum x1, blocking collectives, body(): loss = lax.psum(loss_local / total_count, 'dp')  30.5 us
    all_gather x1, blocking collectives, body(): all_text = lax.all_gather(text_full, 'dp', axis=0, tiled=True)  20.1 us
    dot_general x3, matrix products, contract_rows(): lax.dot_general(left_rows, right_rows, (((0,), (0,)), ((), ())), preferre...  16.4 us
    unnamed x11, local copies, waits for them, and re-layouts  15.1 us
    unnamed x1, blocking collectives  13.7 us
    dot_general x2, matrix products, tower_block(): preact = jnp.dot(flat_tokens, weight, preferred_element_type=jnp.float32)  10.2 us
  transfers between devices with their start and end apart: 3, of which 3 were waited for; matrix products, arithmetic and copies ran while one was open for 4% of the time, Pallas kernels for 0%

commit v1 on v0

v1 whole, which is shorter than its diff:
```python
import functools

import jax
import jax.numpy as jnp
from jax import lax
from jax.experimental import pallas as pl
from jax.experimental.pallas import tpu as pltpu
from jax.sharding import PartitionSpec as P

F32 = jnp.float32
BF16 = jnp.bfloat16
ROWS = 256
VMEM_BYTES = 48 * 2**20
HALF_MAX = 16384.0


def vmem():
    return pl.BlockSpec(memory_space=pltpu.VMEM)


def smem():
    return pl.BlockSpec(memory_space=pltpu.SMEM)


def anyplace():
    return pl.BlockSpec(memory_space=pl.ANY)


def params():
    return pltpu.CompilerParams(vmem_limit_bytes=VMEM_BYTES)


def gelu_and_slope(x):
    c = 0.7978845608028654
    square = x * x
    t = jnp.tanh(c * (x + 0.044715 * (square * x)))
    cdf = 0.5 * (1.0 + t)
    slope = cdf + 0.5 * x * (1.0 - t * t) * (c * (1.0 + 3 * 0.044715 * square))
    return x * cdf, slope


def forward_kernel(
    tokens_of,
    place_ref,
    image_hbm,
    text_hbm,
    image_w_hbm,
    text_w_hbm,
    pooled_ref,
    square_ref,
    image_slope_hbm,
    text_slope_hbm,
    image_v,
    text_v,
    image_w,
    text_w,
    image_slope,
    text_slope,
    in_sem,
    w_sem,
    out_sem,
):
    width = image_w.shape[1]
    samples = pooled_ref.shape[0] // 2
    image_tok, text_tok = tokens_of
    jobs = []
    for hbm, buf, w, slope, slope_hbm, tok, base in (
        (text_hbm, text_v, text_w, text_slope, text_slope_hbm, text_tok, samples),
        (image_hbm, image_v, image_w, image_slope, image_slope_hbm, image_tok, 0),
    ):
        for start in range(0, buf.shape[0], ROWS):
            jobs.append((hbm, buf, w, slope, slope_hbm, tok, base, start))
    w_copies = {}
    in_copies = []
    for n, (hbm, buf, w, slope, slope_hbm, tok, base, start) in enumerate(jobs):
        if start == 0:
            first = hbm is text_hbm
            copy = pltpu.make_async_copy(
                text_w_hbm if first else image_w_hbm, w, w_sem.at[0 if first else 1]
            )
            copy.start()
            w_copies[n] = copy
        copy = pltpu.make_async_copy(
            hbm.at[pl.ds(start, ROWS), :], buf.at[pl.ds(start, ROWS), :], in_sem.at[n]
        )
        copy.start()
        in_copies.append(copy)
    column = pl.multiple_of(place_ref[0] * width, 128)
    out_copies = []
    for n, (hbm, buf, w, slope, slope_hbm, tok, base, start) in enumerate(jobs):
        if n in w_copies:
            w_copies[n].wait()
        in_copies[n].wait()
        preact = jnp.dot(buf[pl.ds(start, ROWS), :], w[...], preferred_element_type=F32)
        value, slant = gelu_and_slope(preact)
        slope[pl.ds(start, ROWS), :] = slant
        copy = pltpu.make_async_copy(
            slope.at[pl.ds(start, ROWS), :], slope_hbm.at[pl.ds(start, ROWS), :], out_sem.at[n]
        )
        copy.start()
        out_copies.append(copy)
        hidden = buf[pl.ds(start, ROWS), pl.ds(column, width)].astype(F32) + value
        group = ROWS // tok
        pooled = jnp.sum(hidden.reshape(group, tok, width), axis=1) / tok
        pooled_ref[pl.ds(base + start // tok, group), :] = pooled
    pooled = pooled_ref[...]
    total = jnp.sum(pooled * pooled, axis=1, keepdims=True)
    square_ref[...] = jnp.broadcast_to(total, square_ref.shape)
    for copy in out_copies:
        copy.wait()


def forward(place, image_flat, text_flat, image_w, text_w, samples):
    width = image_w.shape[1]
    depth = image_w.shape[0]
    rows_i, rows_t = image_flat.shape[0], text_flat.shape[0]
    jobs = (rows_i + rows_t) // ROWS
    return pl.pallas_call(
        functools.partial(forward_kernel, (rows_i // samples, rows_t // samples)),
        out_shape=(
            jax.ShapeDtypeStruct((2 * samples, width), F32),
            jax.ShapeDtypeStruct((2 * samples, 128), F32),
            jax.ShapeDtypeStruct((rows_i, width), F32),
            jax.ShapeDtypeStruct((rows_t, width), F32),
        ),
        in_specs=[smem()] + [anyplace()] * 4,
        out_specs=(vmem(), vmem(), anyplace(), anyplace()),
        scratch_shapes=[
            pltpu.VMEM((rows_i, depth), BF16),
            pltpu.VMEM((rows_t, depth), BF16),
            pltpu.VMEM((depth, width), BF16),
            pltpu.VMEM((depth, width), BF16),
            pltpu.VMEM((rows_i, width), F32),
            pltpu.VMEM((rows_t, width), F32),
            pltpu.SemaphoreType.DMA((jobs,)),
            pltpu.SemaphoreType.DMA((2,)),
            pltpu.SemaphoreType.DMA((jobs,)),
        ],
        compiler_params=params(),
        cost_estimate=pl.CostEstimate(
            flops=2 * (rows_i + rows_t) * depth * width,
            bytes_accessed=2 * (rows_i + rows_t) * (depth + 2 * width) + 4 * depth * width,
            transcendentals=(rows_i + rows_t) * width,
        ),
    )(place, image_flat, text_flat, image_w, text_w)


def turn_kernel(owner_ref, tokens_ref, out_ref, most_ref, turned):
    turned[...] = tokens_ref[...].T
    largest = jnp.max(jnp.abs(tokens_ref[...]).astype(F32), axis=0, keepdims=True)
    largest = jnp.broadcast_to(jnp.max(largest, axis=1, keepdims=True), most_ref.shape)

    @pl.when(pl.program_id(0) == 0)
    def _():
        most_ref[...] = jnp.zeros_like(most_ref)

    most_ref[...] = jnp.maximum(most_ref[...], largest)
    blocks = owner_ref.shape[0]
    height = out_ref.shape[0] // blocks
    for q in range(blocks):
        source = pl.multiple_of(owner_ref[q] * height, height)
        out_ref[q * height : (q + 1) * height, :] = turned[pl.ds(source, height), :]


def turn(owners, flat):
    rows, depth = flat.shape
    blocks = owners.shape[0]
    if (depth // blocks) % 16:
        turned = flat.T.reshape(blocks, depth // blocks, rows)[owners].reshape(depth, rows)
        return turned, jnp.max(jnp.abs(flat)).astype(F32)
    turned, most = pl.pallas_call(
        turn_kernel,
        out_shape=(
            jax.ShapeDtypeStruct((depth, rows), flat.dtype),
            jax.ShapeDtypeStruct((8, 128), F32),
        ),
        grid=(rows // ROWS,),
        in_specs=[smem(), pl.BlockSpec((ROWS, depth), lambda i: (i, 0))],
        out_specs=(
            pl.BlockSpec((depth, ROWS), lambda i: (0, i)),
            pl.BlockSpec((8, 128), lambda i: (0, 0)),
        ),
        scratch_shapes=[pltpu.VMEM((depth, ROWS), flat.dtype)],
        compiler_params=params(),
        cost_estimate=pl.CostEstimate(
            flops=0, bytes_accessed=4 * rows * depth, transcendentals=0
        ),
    )(owners, flat)
    return turned, most[0, 0]


def row_products(left, right):
    return lax.dot_general(left, right, (((1,), (1,)), ((), ())), preferred_element_type=F32)


def towers(blocks_ref, samples):
    blocks, _, width = blocks_ref.shape
    image = blocks_ref[:, :samples, :].reshape(blocks * samples, width)
    text = blocks_ref[:, samples:, :].reshape(blocks * samples, width)
    return image, text


def product_kernel(near_ref, far_ref, out_ref):
    samples = near_ref.shape[1] // 2
    own_image = near_ref[0, :samples, :]
    own_text = near_ref[0, samples:, :]
    start = 0
    for ref in (near_ref, far_ref):
        image, text = towers(ref, samples)
        stop = start + image.shape[0]
        out_ref[:samples, start:stop] = row_products(own_image, text)
        out_ref[samples:, start:stop] = row_products(own_text, image)
        start = stop


def products(near, far):
    blocks, both, _ = near.shape
    return pl.pallas_call(
        product_kernel,
        out_shape=jax.ShapeDtypeStruct((both, blocks * both), F32),
        in_specs=[vmem()] * 2,
        out_specs=vmem(),
        compiler_params=params(),
    )(near, far)


def middle_kernel(
    tokens_of,
    scalar_ref,
    own_ref,
    other_ref,
    column_ref,
    row_ref,
    near_ref,
    far_ref,
    unit_ref,
    norm_ref,
    grad_ref,
    loss_ref,
):
    samples = near_ref.shape[1] // 2
    split = near_ref.shape[0] * samples
    scale, bias, coeff = scalar_ref[0], scalar_ref[1], scalar_ref[2]
    dots = own_ref[...] + other_ref[...]
    logits = scale * dots + bias
    row = lax.broadcasted_iota(jnp.int32, dots.shape, 0) % samples
    column = lax.broadcasted_iota(jnp.int32, dots.shape, 1)
    sign = jnp.where(row == column, 1.0, -1.0).astype(F32)
    used = row_ref[...] * column_ref[...] > 0.5
    margin = -sign * logits
    small = jnp.exp(-jnp.abs(margin))
    soft = jnp.maximum(margin, 0.0) + jnp.log1p(small)
    sigmoid = jnp.where(margin >= 0, 1.0, small) / (1.0 + small)
    part = jnp.where(used, soft, 0.0)[:samples, :]
    loss_ref[...] = jnp.broadcast_to(
        jnp.sum(jnp.sum(part, axis=1, keepdims=True), axis=0, keepdims=True), loss_ref.shape
    )
    dlogit = (jnp.where(used, -sign * sigmoid, 0.0) * coeff).astype(BF16)
    radial = scale * jnp.sum(dlogit.astype(F32) * dots, axis=1, keepdims=True)
    near_image, near_text = towers(near_ref, samples)
    far_image, far_text = towers(far_ref, samples)
    for start, near, far, tokens in (
        (0, near_text, far_text, tokens_of[0]),
        (samples, near_image, far_image, tokens_of[1]),
    ):
        stop = start + samples
        weights = dlogit[start:stop, :]
        raw = jnp.dot(weights[:, :split], near, preferred_element_type=F32)
        raw += jnp.dot(weights[:, split:], far, preferred_element_type=F32)
        inward = unit_ref[start:stop, :] * radial[start:stop, :]
        grad_ref[start:stop, :] = (scale * raw - inward) / norm_ref[start:stop, :] / tokens


def middle(tokens_of, scalars, own, other, columns, rows, near, far, unit, norm):
    return pl.pallas_call(
        functools.partial(middle_kernel, tokens_of),
        out_shape=(
            jax.ShapeDtypeStruct(unit.shape, F32),
            jax.ShapeDtypeStruct((8, 128), F32),
        ),
        in_specs=[smem()] + [vmem()] * 8,
        out_specs=(vmem(), vmem()),
        compiler_params=params(),
    )(scalars, own, other, columns, rows, near, far, unit, norm)


def weight_kernel(grad_ref, slope_ref, turned_ref, send_ref, keep_ref, preact_grad):
    step = pl.program_id(0)
    half = pl.num_programs(0) // 2

    @pl.when(step == 0)
    def _():
        samples, width = grad_ref.shape
        rows = slope_ref.shape[0]
        slope = slope_ref[...].reshape(samples, rows // samples, width)
        grad = grad_ref[...].reshape(samples, 1, width)
        preact_grad[...] = (grad * slope).reshape(rows, width).astype(BF16)

    term = jnp.dot(turned_ref[...], preact_grad[...], preferred_element_type=F32)

    @pl.when(step < half)
    def _():
        send_ref[...] = term

    @pl.when(step >= half)
    def _():
        keep_ref[...] = term


def weight_terms(grad, slope, turned, start, width, base):
    depth, rows = turned.shape
    samples = grad.shape[0] // 2
    half = depth // 2 // ROWS
    chunk = start // width
    return pl.pallas_call(
        weight_kernel,
        grid=(2 * half,),
        out_shape=(jax.ShapeDtypeStruct((depth // 2, width), F32),) * 2,
        in_specs=[
            pl.BlockSpec((samples, width), lambda i: (base, chunk)),
            pl.BlockSpec((rows, width), lambda i: (0, chunk)),
            pl.BlockSpec((ROWS, rows), lambda i: ((i + half) % (2 * half), 0)),
        ],
        out_specs=(
            pl.BlockSpec((ROWS, width), lambda i: (jnp.minimum(i, half - 1), 0)),
            pl.BlockSpec((ROWS, width), lambda i: (jnp.maximum(i - half, 0), 0)),
        ),
        scratch_shapes=[pltpu.VMEM((rows, width), BF16)],
        compiler_params=params(),
        cost_estimate=pl.CostEstimate(
            flops=2 * depth * rows * width,
            bytes_accessed=2 * depth * rows + 4 * rows * width + 4 * depth * width,
            transcendentals=0,
        ),
    )(grad, slope, turned)


def body(
    image_tokens,
    text_tokens,
    image_weight,
    text_weight,
    logit_scale,
    logit_bias,
    loss_scale,
    valid_count,
):
    samples, image_tok, depth = image_tokens.shape
    text_tok = text_tokens.shape[1]
    width = image_weight.shape[1]
    cycle = lax.axis_size("dp")
    bits = cycle.bit_length() - 1
    place = lax.axis_index("dp")

    def swap(array, mask):
        return lax.ppermute(array, "dp", [(i, i ^ mask) for i in range(cycle)])

    def swap_halves(array):
        return lax.ppermute(array, "mp", [(0, 1), (1, 0)])

    def reverse(value):
        return sum(((value >> b) & 1) << (bits - 1 - b) for b in range(bits))

    image_flat = image_tokens.reshape(-1, depth)
    text_flat = text_tokens.reshape(-1, depth)
    owners = jnp.asarray([reverse(q) for q in range(cycle)], jnp.int32) ^ place

    counts = valid_count
    for b in reversed(range(bits)):
        counts = jnp.concatenate([counts, swap(counts, 1 << b)])
    positions = jnp.arange(samples, dtype=jnp.int32)
    columns = (positions[None, :] < counts[:, None]).astype(F32).reshape(1, -1)
    rows = (positions < valid_count[0]).astype(F32)
    rows = jnp.concatenate([rows, rows])[:, None]
    total = jnp.sum(counts).astype(F32)
    scalars = jnp.stack([logit_scale[0], logit_bias[0], loss_scale[0] / total])

    model_place = lax.axis_index("mp").astype(jnp.int32).reshape(1)
    pooled, square, image_slope, text_slope = forward(
        model_place, image_flat, text_flat, image_weight, text_weight, samples
    )
    norm = jnp.sqrt(square[:, :1] + swap_halves(square)[:, :1] + 1e-06)
    unit = pooled / norm
    unit_bf = unit.astype(BF16)

    gathered = unit_bf[None]
    low = 0
    if bits >= 2:
        low = bits - 2
        one, two = 1 << (bits - 1), 1 << (bits - 2)
        parts = [unit_bf] + [swap(unit_bf, mask) for mask in (one, two, one | two)]
        gathered = jnp.stack(parts)
    for b in reversed(range(1, low)):
        gathered = jnp.concatenate([gathered, swap(gathered, 1 << b)])
    near, far = gathered, swap(gathered, 1)

    image_turned, image_most = turn(owners, image_flat)
    text_turned, text_most = turn(owners, text_flat)

    own_dots = products(near, far)
    other_dots = swap_halves(own_dots)
    grad, loss_part = middle(
        (image_tok, text_tok), scalars, own_dots, other_dots, columns, rows, near, far, unit, norm
    )
    steepest = jnp.max(jnp.abs(grad).reshape(2, -1), axis=1)
    sizes = jnp.stack([image_most * image_tok, text_most * text_tok])
    loss_sum, limits = loss_part[0, :1], 1.2 * cycle * samples * sizes * steepest
    for b in range(bits):
        there = swap(jnp.concatenate([loss_sum, limits]), 1 << b)
        loss_sum, limits = loss_sum + there[:1], jnp.maximum(limits, there[1:])
    loss = loss_sum[0] / total

    def reduce(keep, send, factor):
        left = (keep + swap(send, 1)) * factor
        for b in range(1, low):
            half = left.shape[0] // 2
            there = swap(left[half:].astype(jnp.float16), 1 << b)
            left = left[:half] + there.astype(F32)
        if low:
            quarter = left.shape[0] // 4
            pieces = [
                swap(left[k * quarter : (k + 1) * quarter].astype(jnp.float16), mask)
                for k, mask in ((1, one), (2, two), (3, one | two))
            ]
            left = left[:quarter] + sum(piece.astype(F32) for piece in pieces)
        return left / factor

    outputs = []
    chunk = width // 2
    for slope, turned, base, limit in (
        (text_slope, text_turned, 1, limits[1]),
        (image_slope, image_turned, 0, limits[0]),
    ):
        factor = HALF_MAX / jnp.maximum(limit, 1e-30)
        done = []
        for start in range(0, width, chunk):
            send, keep = weight_terms(grad, slope, turned, start, chunk, base)
            done.append(reduce(keep, send, factor))
        outputs.append(jnp.concatenate(done, axis=1))
    return (loss, outputs[1], outputs[0])


def solution(mesh):
    placed = (
        P("dp", None, None),
        P("dp", None, None),
        P(None, "mp"),
        P(None, "mp"),
        P(),
        P(),
        P(),
        P("dp"),
    )
    return jax.shard_map(
        body,
        mesh=mesh,
        in_specs=placed,
        out_specs=(P(), P("dp", "mp"), P("dp", "mp")),
        check_vma=False,
    )
```

time: 322 us -> 164 us (0.51)
  waiting for transfers between devices: 164 us -> 33.4 us
  blocking collectives: 83.2 us -> 0 us
  starting transfers between devices: 0.12 us -> 37.7 us
  Pallas kernels: 0 us -> 36.5 us
  matrix products: 27.9 us -> 0 us
  other arithmetic: 12.8 us -> 22.7 us
  between operations: 17.9 us -> 10.9 us
  local copies, waits for them, and re-layouts: 15.8 us -> 21.8 us
    unnamed x5 -> x0, waiting for transfers between devices: 110 us -> none
    reduce_scatter x1 -> x0, waiting for transfers between devices: 54.2 us -> none  [body(): lax.psum_scatter(text_terms_of(dlogit, image_bf), 'dp', scatter_dimension...]
    psum x3 -> x0, blocking collectives: 40.4 us -> none  [the longest x1 30.5 us: body(): loss = lax.psum(loss_local / total_count, 'dp')]
    ppermute x0 -> x35, starting transfers between devices: none -> 37.7 us  [the longest x33 34.2 us: swap(): return lax.ppermute(array, 'dp', [(i, i ^ mask) for i in range(cycle)])]
    pallas_call x0 -> x9, Pallas kernels: none -> 36.5 us  [the longest x4 16.6 us: weight_terms(): pl.pallas_call(weight_kernel, grid=(2 * half,), out_shape=(jax.ShapeDtype...]
    ppermute x0 -> x35, waiting for transfers between devices: none -> 33.4 us  [the longest x33 31.6 us: swap(): return lax.ppermute(array, 'dp', [(i, i ^ mask) for i in range(cycle)])]
    all_gather x3 -> x0, blocking collectives: 29.1 us -> none  [the longest x1 20.1 us: body(): all_text = lax.all_gather(text_full, 'dp', axis=0, tiled=True)]
    dot_general x7 -> x0, matrix products: 27.9 us -> none  [the longest x3 16.4 us: contract_rows(): lax.dot_general(left_rows, right_rows, (((0,), (0,)), ((), ())), preferre...]
  transfers between devices with their start and end apart: 3 -> 35, of which waited for: 3 -> 17; matrix products, arithmetic and copies ran while one was open for 4% -> 19% of each run, Pallas kernels for 0% -> 4%
where the time goes in v1:
time: 164 us; the launch traced here: 163 us
  starting transfers between devices  37.7 us (23%)
  Pallas kernels  36.5 us (22%)
  waiting for transfers between devices  33.4 us (20%)
  other arithmetic  22.7 us (14%)
  local copies, waits for them, and re-layouts  21.8 us (13%)
  between operations  10.9 us (7%)
    ppermute x33, starting transfers between devices, swap(): return lax.ppermute(array, 'dp', [(i, i ^ mask) for i in range(cycle)])  34.2 us
    ppermute x33, waiting for transfers between devices, swap(): return lax.ppermute(array, 'dp', [(i, i ^ mask) for i in range(cycle)])  31.6 us
    pallas_call x4, Pallas kernels, weight_terms(): pl.pallas_call(weight_kernel, grid=(2 * half,), out_shape=(jax.ShapeDtype...  16.6 us
    unnamed x41, local copies, waits for them, and re-layouts  14.8 us
    pallas_call x1, Pallas kernels, forward(): pl.pallas_call(functools.partial(forward_kernel, (rows_i // samples, rows...  10.8 us
    pallas_call x2, Pallas kernels, turn(): pl.pallas_call(turn_kernel, out_shape=(jax.ShapeDtypeStruct((depth, rows)...  5.83 us
    mul x4, other arithmetic, reduce(): left = (keep + swap(send, 1)) * factor  5.66 us
    concatenate x3, other arithmetic, body(): counts = jnp.concatenate([counts, swap(counts, 1 << b)])  4.95 us
  transfers between devices with their start and end apart: 35, of which 17 were waited for; matrix products, arithmetic and copies ran while one was open for 19% of the time, Pallas kernels for 4%

profile of v1, /device:TPU:0, one launch (start us, length us, event | category | flops | bytes accessed | tf_op | source)
XLA Modules:
  0.0 162.9 jit_solution(9477590937421419405)
XLA Ops:
  0.6 1.4 copy-done.2
  2.0 1.7 %copy-done.13 = bf16[1536,768]{1,0:T(8,128)(2,1)S(1)} copy-done((bf16[1536,768]{1,0:T(8,128)(2,1)S(1)}, bf16[1536,768]{1,0:T(8,128)(2,1)}, u32[]{:S(2)}) %copy-start.13) | copy-done | bytes 2359320
  3.7 10.8 %shard_map.112 = (f32[32,768]{1,0:T(8,128)S(1)}, f32[32,128]{1,0:T(8,128)S(1)}, f32[1024,768]{1,0:T(8,128)}, f32[512,768]{1,0:T(8,128)S(1)}) custom-call(s32[1]{0:T(128)} %bitcast.4.place_ref, bf16[1024,1536]{1,0:T(8,128)(2,1)} %bitcast.32, bf16[512,1536]{1,0:T(8,128)(2,1)S(1)} %bitcast.30, bf16[1536,768]{1,0:T(8,128)(2,1)S(1)} %copy-done.13, ...), custom_call_target="tpu_custom_call" | custom-call | flops 3623878656 | bytes 14155776 | tf_op jit(solution)/shard_map/pallas_call | solution.py:118
  15.1 3.0 %collective-permute-start.4 = (f32[32,128]{1,0:T(8,128)S(1)}, f32[32,128]{1,0:T(8,128)S(1)}, u32[]{:S(2)}, u32[]{:S(2)}) collective-permute-start(f32[32,128]{1,0:T(8,128)S(1)} %get-tuple-element.22), channel_id=1, source_target_pairs={{0,1},{1,0},{2,3},{3,2},{4,5},{5,4},{6,7},{7,6},{8,9},{9,8},{10,11... | collective-permute-start | bytes 49160 | tf_op jit(solution)/shard_map/ppermute | solution.py:359
  18.1 2.6 %collective-permute-start = (s32[1]{0:T(128)}, s32[1]{0:T(128)}, u32[]{:S(2)}, u32[]{:S(2)}) collective-permute-start(s32[1]{0:T(128)} %param.16), channel_id=1, source_target_pairs={{0,16},{2,18},{4,20},{6,22},{8,24},{10,26},{12,28},{14,30},{16,0},... | collective-permute-start | bytes 20 | tf_op jit(solution)/shard_map/ppermute | solution.py:356
  21.5 1.4 copy-done.3
  22.9 1.7 %shard_map.116 = (bf16[1536,512]{1,0:T(8,128)(2,1)S(1)}, f32[8,128]{1,0:T(8,128)S(1)}) custom-call(s32[16]{0:T(128)S(1)} %broadcast_xor_fusion.owner_ref, bf16[512,1536]{1,0:T(8,128)(2,1)S(1)} %bitcast.31), custom_call_target="tpu_custom_call" | custom-call | bytes 3145728 | tf_op jit(solution)/shard_map/pallas_call | solution.py:171
  24.6 4.2 %shard_map.115 = (bf16[1536,1024]{1,0:T(8,128)(2,1)S(1)}, f32[8,128]{1,0:T(8,128)S(1)}) custom-call(s32[16]{0:T(128)S(1)} %broadcast_xor_fusion.owner_ref, bf16[1024,1536]{1,0:T(8,128)(2,1)} %bitcast.33), custom_call_target="tpu_custom_call" | custom-call | bytes 6291456 | tf_op jit(solution)/shard_map/pallas_call | solution.py:171
  28.8 1.7 %copy-done.1 = bf16[1536,1024]{1,0:T(8,128)(2,1)} copy-done((bf16[1536,1024]{1,0:T(8,128)(2,1)}, bf16[1536,1024]{1,0:T(8,128)(2,1)S(1)}, u32[]{:S(2)}) %copy-start.1) | copy-done | bytes 3145752
  35.4 1.6 %constant_dynamic-update-slice_fusion.4 = (bf16[8,32,768]{2,1,0:T(8,128)(2,1)S(1)}, bf16[32,768]{1,0:T(8,128)(2,1)}, f32[32,768]{1,0:T(8,128)}) fusion(f32[32,768]{1,0:T(8,128)} %copy-done.9, f32[32]{0:T(128)S(1)} %get-tuple-element.50), kind=kLoop, calls=%fused_computation.32 | loop fusion | flops 49151 | bytes 295040
  37.1 1.4 collective-permute-start.7
  38.4 1.7 %collective-permute-start.5 = (bf16[32,768]{1,0:T(8,128)(2,1)}, bf16[32,768]{1,0:T(8,128)(2,1)}, u32[]{:S(2)}, u32[]{:S(2)}) collective-permute-start(bf16[32,768]{1,0:T(8,128)(2,1)} %get-tuple-element.48), channel_id=1, source_target_pairs={{0,16},{2,18},{4,20},{6,22},{8,24},{10,26},{12,28},{14,30},{16,0},... | collective-permute-start | bytes 147464 | tf_op jit(solution)/shard_map/ppermute | solution.py:356
  40.1 1.4 collective-permute-start.6
  46.0 1.6 %collective-permute-start.8 = (bf16[4,32,768]{2,1,0:T(8,128)(2,1)S(1)}, bf16[4,32,768]{2,1,0:T(8,128)(2,1)S(1)}, u32[]{:S(2)}, u32[]{:S(2)}) collective-permute-start(bf16[4,32,768]{2,1,0:T(8,128)(2,1)S(1)} %pad_maximum_fusion.2), channel_id=1, source_target_pairs={{0,4},{2,6},{4,0},{6,2},{8,12},{10,14},{12,8},{14,10},{16,20},{18,... | collective-permute-start | bytes 589832 | tf_op jit(solution)/shard_map/ppermute | solution.py:356
  50.0 1.7 %collective-permute-done.8 = bf16[4,32,768]{2,1,0:T(8,128)(2,1)S(1)} collective-permute-done((bf16[4,32,768]{2,1,0:T(8,128)(2,1)S(1)}, bf16[4,32,768]{2,1,0:T(8,128)(2,1)S(1)}, u32[]{:S(2)}, u32[]{:S(2)}) %collective-permute-start.8) | collective-permute-done | bytes 196640 | tf_op jit(solution)/shard_map/ppermute | solution.py:356
  51.8 1.8 %pad_add_fusion.1 = s32[4]{0:T(128)} fusion(s32[2]{0:T(128)} %collective-permute-done.1, s32[1]{0:T(128)} %collective-permute-done, s32[1]{0:T(128)} %copy.21), kind=kLoop, calls=%fused_computation.38 | loop fusion | flops 8 | bytes 32 | tf_op jit(solution)/shard_map/concatenate | solution.py:370
  53.7 1.5 collective-permute-start.2
  57.4 1.9 %pad_add_fusion.2 = s32[8]{0:T(128)} fusion(s32[4]{0:T(128)} %collective-permute-done.2, s32[2]{0:T(128)} %collective-permute-done.1, s32[1]{0:T(128)} %collective-permute-done, s32[1]{0:T(128)} %copy.21), kind=kLoop, calls=%fused_computation.39 | loop fusion | flops 24 | bytes 64 | tf_op jit(solution)/shard_map/concatenate | solution.py:370
  63.2 1.9 %concatenate.45 = s32[16]{0:T(128)} concatenate(s32[1]{0:T(128)} %copy.21, s32[1]{0:T(128)} %collective-permute-done, s32[2]{0:T(128)} %collective-permute-done.1, s32[4]{0:T(128)} %collective-permute-done.2, s32[8]{0:T(128)} %collective-permute-done.3), dimensions={0} | concatenate | bytes 128 | tf_op jit(solution)/shard_map/concatenate | solution.py:370
  66.4 1.9 %shard_map.113.own_ref = f32[32,256]{1,0:T(8,128)} custom-call(bf16[8,32,768]{2,1,0:T(8,128)(2,1)S(1)} %constant_dynamic-update-slice_fusion.near_ref, bf16[8,32,768]{2,1,0:T(8,128)(2,1)} %collective-permute-done.9.far_ref), custom_call_target="tpu_custom_call" | custom-call | tf_op jit(solution)/shard_map/pallas_call | solution.py:218
  70.8 1.8 %collective-permute-done.10.other_ref = f32[32,256]{1,0:T(8,128)} collective-permute-done((f32[32,256]{1,0:T(8,128)}, f32[32,256]{1,0:T(8,128)}, u32[]{:S(2)}, u32[]{:S(2)}) %collective-permute-start.10) | collective-permute-done | bytes 32800 | tf_op jit(solution)/shard_map/ppermute | solution.py:359
  77.3 3.3 %shard_map.119 = (f32[768,384]{1,0:T(8,128)}, f32[768,384]{1,0:T(8,128)S(1)}) custom-call(f32[32,768]{1,0:T(8,128)S(1)} %get-tuple-element.26.grad_ref, f32[512,768]{1,0:T(8,128)S(1)} %get-tuple-element.33.slope_ref, bf16[1536,512]{1,0:T(8,128)(2,1)S(1)} %get-tuple-element.34.turned_ref), custom_call_target="tpu_custom_call" | custom-call | flops 603979776 | bytes 4718592 | tf_op jit(solution)/shard_map/pallas_call | solution.py:315
  80.7 2.2 %shard_map.120 = (f32[768,384]{1,0:T(8,128)S(1)}, f32[768,384]{1,0:T(8,128)S(1)}) custom-call(f32[32,768]{1,0:T(8,128)S(1)} %get-tuple-element.26.grad_ref, f32[512,768]{1,0:T(8,128)S(1)} %get-tuple-element.33.slope_ref, bf16[1536,512]{1,0:T(8,128)(2,1)S(1)} %get-tuple-element.34.turned_ref), custom_call_target="tpu_custom_call" | custom-call | flops 603979776 | bytes 4718592 | tf_op jit(solution)/shard_map/pallas_call | solution.py:315
  83.0 5.6 %shard_map.117 = (f32[768,384]{1,0:T(8,128)S(1)}, f32[768,384]{1,0:T(8,128)S(1)}) custom-call(f32[32,768]{1,0:T(8,128)S(1)} %get-tuple-element.26.grad_ref, f32[1024,768]{1,0:T(8,128)S(1)} %copy-done, bf16[1536,1024]{1,0:T(8,128)(2,1)} %copy-done.1), custom_call_target="tpu_custom_call" | custom-call | flops 1207959552 | bytes 7077888 | tf_op jit(solution)/shard_map/pallas_call | solution.py:315
  89.7 5.5 %shard_map.118 = (f32[768,384]{1,0:T(8,128)S(1)}, f32[768,384]{1,0:T(8,128)S(1)}) custom-call(f32[32,768]{1,0:T(8,128)S(1)} %get-tuple-element.26.grad_ref, f32[1024,768]{1,0:T(8,128)S(1)} %copy-done, bf16[1536,1024]{1,0:T(8,128)(2,1)} %copy-done.1), custom_call_target="tpu_custom_call" | custom-call | flops 1207959552 | bytes 7077888 | tf_op jit(solution)/shard_map/pallas_call | solution.py:315
  100.6 1.5 collective-permute-start.12
  102.2 2.0 %collective-permute-done.12 = f32[3]{0:T(128)S(1)} collective-permute-done((f32[3]{0:T(128)S(1)}, f32[3]{0:T(128)S(1)}, u32[]{:S(2)}, u32[]{:S(2)}) %collective-permute-start.12) | collective-permute-done | bytes 44 | tf_op jit(solution)/shard_map/ppermute | solution.py:356
  105.1 2.8 %collective-permute-done.13 = f32[3]{0:T(128)S(1)} collective-permute-done((f32[3]{0:T(128)S(1)}, f32[3]{0:T(128)S(1)}, u32[]{:S(2)}, u32[]{:S(2)}) %collective-permute-start.13) | collective-permute-done | bytes 44 | tf_op jit(solution)/shard_map/ppermute | solution.py:356
  108.7 3.8 %collective-permute-done.14 = f32[3]{0:T(128)S(1)} collective-permute-done((f32[3]{0:T(128)S(1)}, f32[3]{0:T(128)S(1)}, u32[]{:S(2)}, u32[]{:S(2)}) %collective-permute-start.14) | collective-permute-done | bytes 44 | tf_op jit(solution)/shard_map/ppermute | solution.py:356
  114.7 1.5 add_multiply_fusion.1
  116.2 1.6 collective-permute-start.26
  117.8 1.4 add_multiply_fusion
  119.8 1.4 add_multiply_fusion.3
  121.3 1.6 collective-permute-start.16
  122.9 1.4 add_multiply_fusion.2
  124.9 1.4 collective-permute-done.26
  127.1 1.5 collective-permute-start.28
  128.6 3.9 %collective-permute-done.31 = f16[384,384]{1,0:T(8,128)(2,1)S(1)} collective-permute-done((f16[384,384]{1,0:T(8,128)(2,1)S(1)}, f16[384,384]{1,0:T(8,128)(2,1)S(1)}, u32[]{:S(2)}, u32[]{:S(2)}) %collective-permute-start.31) | collective-permute-done | bytes 294944 | tf_op jit(solution)/shard_map/ppermute | solution.py:356
  132.6 1.6 collective-permute-start.29
  134.3 3.6 %collective-permute-done.16 = f16[384,384]{1,0:T(8,128)(2,1)S(1)} collective-permute-done((f16[384,384]{1,0:T(8,128)(2,1)S(1)}, f16[384,384]{1,0:T(8,128)(2,1)S(1)}, u32[]{:S(2)}, u32[]{:S(2)}) %collective-permute-start.16) | collective-permute-done | bytes 294944 | tf_op jit(solution)/shard_map/ppermute | solution.py:356
  138.6 2.4 %collective-permute-done.21 = f16[384,384]{1,0:T(8,128)(2,1)S(1)} collective-permute-done((f16[384,384]{1,0:T(8,128)(2,1)S(1)}, f16[384,384]{1,0:T(8,128)(2,1)S(1)}, u32[]{:S(2)}, u32[]{:S(2)}) %collective-permute-start.21) | collective-permute-done | bytes 294944 | tf_op jit(solution)/shard_map/ppermute | solution.py:356
  141.9 1.4 collective-permute-start.34
  143.4 1.4 collective-permute-start.17
  144.7 1.7 %collective-permute-start.18 = (f16[96,384]{1,0:T(8,128)(2,1)S(1)}, f16[96,384]{1,0:T(8,128)(2,1)S(1)}, u32[]{:S(2)}, u32[]{:S(2)}) collective-permute-start(f16[96,384]{1,0:T(8,128)(2,1)S(1)} %get-tuple-element.60), channel_id=1, source_target_pairs={{0,8},{2,10},{4,12},{6,14},{8,0},{10,2},{12,4},{14,6},{16,24},{18,... | collective-permute-start | bytes 221192 | tf_op jit(solution)/shard_map/ppermute | solution.py:356
  146.5 1.4 collective-permute-start.19
  149.1 2.4 %collective-permute-start.23 = (f16[96,384]{1,0:T(8,128)(2,1)S(1)}, f16[96,384]{1,0:T(8,128)(2,1)S(1)}, u32[]{:S(2)}, u32[]{:S(2)}) collective-permute-start(f16[96,384]{1,0:T(8,128)(2,1)S(1)} %get-tuple-element.63), channel_id=1, source_target_pairs={{0,8},{2,10},{4,12},{6,14},{8,0},{10,2},{12,4},{14,6},{16,24},{18,... | collective-permute-start | bytes 221192 | tf_op jit(solution)/shard_map/ppermute | solution.py:356
  151.5 3.3 %collective-permute-done.17 = f16[96,384]{1,0:T(8,128)(2,1)S(1)} collective-permute-done((f16[96,384]{1,0:T(8,128)(2,1)S(1)}, f16[96,384]{1,0:T(8,128)(2,1)S(1)}, u32[]{:S(2)}, u32[]{:S(2)}) %collective-permute-start.17) | collective-permute-done | bytes 73760 | tf_op jit(solution)/shard_map/ppermute | solution.py:356
  157.1 3.9 %collective-permute-done.24 = f16[96,384]{1,0:T(8,128)(2,1)S(1)} collective-permute-done((f16[96,384]{1,0:T(8,128)(2,1)S(1)}, f16[96,384]{1,0:T(8,128)(2,1)S(1)}, u32[]{:S(2)}, u32[]{:S(2)}) %collective-permute-start.24) | collective-permute-done | bytes 73760 | tf_op jit(solution)/shard_map/ppermute | solution.py:356
  (128 shorter events, 38.1 us)
Async XLA Ops:
  0.6 1.4 copy-start.2
  2.0 1.7 %copy-start.13 = (bf16[1536,768]{1,0:T(8,128)(2,1)S(1)}, bf16[1536,768]{1,0:T(8,128)(2,1)}, u32[]{:S(2)}) copy-start(bf16[1536,768]{1,0:T(8,128)(2,1)} %image_w_hbm.1) | copy-start | bytes 7077892
  3.7 17.7 %copy-start.18 = (s32[16]{0:T(128)S(1)}, s32[16]{0:T(128)}, u32[]{:S(2)}) copy-start(s32[16]{0:T(128)} %constant.32.clone) | copy-start | bytes 196
  15.1 20.2 %collective-permute-start.4 = (f32[32,128]{1,0:T(8,128)S(1)}, f32[32,128]{1,0:T(8,128)S(1)}, u32[]{:S(2)}, u32[]{:S(2)}) collective-permute-start(f32[32,128]{1,0:T(8,128)S(1)} %get-tuple-element.22), channel_id=1, source_target_pairs={{0,1},{1,0},{2,3},{3,2},{4,5},{5,4},{6,7},{7,6},{8,9},{9,8},{10,11... | collective-permute-start | bytes 49160 | tf_op jit(solution)/shard_map/ppermute | solution.py:359
  18.1 23.4 %collective-permute-start = (s32[1]{0:T(128)}, s32[1]{0:T(128)}, u32[]{:S(2)}, u32[]{:S(2)}) collective-permute-start(s32[1]{0:T(128)} %param.16), channel_id=1, source_target_pairs={{0,16},{2,18},{4,20},{6,22},{8,24},{10,26},{12,28},{14,30},{16,0},... | collective-permute-start | bytes 20 | tf_op jit(solution)/shard_map/ppermute | solution.py:356
  21.5 1.4 copy-start.3
  28.7 1.7 %copy-start.1 = (bf16[1536,1024]{1,0:T(8,128)(2,1)}, bf16[1536,1024]{1,0:T(8,128)(2,1)S(1)}, u32[]{:S(2)}) copy-start(bf16[1536,1024]{1,0:T(8,128)(2,1)S(1)} %get-tuple-element.28.turned_ref) | copy-start | bytes 9437188
  37.1 7.0 %collective-permute-start.7 = (bf16[32,768]{1,0:T(8,128)(2,1)}, bf16[32,768]{1,0:T(8,128)(2,1)}, u32[]{:S(2)}, u32[]{:S(2)}) collective-permute-start(bf16[32,768]{1,0:T(8,128)(2,1)} %get-tuple-element.48), channel_id=1, source_target_pairs={{0,24},{2,26},{4,28},{6,30},{8,16},{10,18},{12,20},{14,22},{16,8},... | collective-permute-start | bytes 147464 | tf_op jit(solution)/shard_map/ppermute | solution.py:356
  38.4 6.4 %collective-permute-start.5 = (bf16[32,768]{1,0:T(8,128)(2,1)}, bf16[32,768]{1,0:T(8,128)(2,1)}, u32[]{:S(2)}, u32[]{:S(2)}) collective-permute-start(bf16[32,768]{1,0:T(8,128)(2,1)} %get-tuple-element.48), channel_id=1, source_target_pairs={{0,16},{2,18},{4,20},{6,22},{8,24},{10,26},{12,28},{14,30},{16,0},... | collective-permute-start | bytes 147464 | tf_op jit(solution)/shard_map/ppermute | solution.py:356
  40.1 5.0 %collective-permute-start.6 = (bf16[32,768]{1,0:T(8,128)(2,1)}, bf16[32,768]{1,0:T(8,128)(2,1)}, u32[]{:S(2)}, u32[]{:S(2)}) collective-permute-start(bf16[32,768]{1,0:T(8,128)(2,1)} %get-tuple-element.48), channel_id=1, source_target_pairs={{0,8},{2,10},{4,12},{6,14},{8,0},{10,2},{12,4},{14,6},{16,24},{18,... | collective-permute-start | bytes 147464 | tf_op jit(solution)/shard_map/ppermute | solution.py:356
  42.7 9.1 %collective-permute-start.1 = (s32[2]{0:T(128)}, s32[2]{0:T(128)}, u32[]{:S(2)}, u32[]{:S(2)}) collective-permute-start(s32[2]{0:T(128)} %pad_add_fusion), channel_id=1, source_target_pairs={{0,8},{2,10},{4,12},{6,14},{8,0},{10,2},{12,4},{14,6},{16,24},{18,... | collective-permute-start | bytes 32 | tf_op jit(solution)/shard_map/ppermute | solution.py:356
  46.0 5.8 %collective-permute-start.8 = (bf16[4,32,768]{2,1,0:T(8,128)(2,1)S(1)}, bf16[4,32,768]{2,1,0:T(8,128)(2,1)S(1)}, u32[]{:S(2)}, u32[]{:S(2)}) collective-permute-start(bf16[4,32,768]{2,1,0:T(8,128)(2,1)S(1)} %pad_maximum_fusion.2), channel_id=1, source_target_pairs={{0,4},{2,6},{4,0},{6,2},{8,12},{10,14},{12,8},{14,10},{16,20},{18,... | collective-permute-start | bytes 589832 | tf_op jit(solution)/shard_map/ppermute | solution.py:356
  51.8 14.6 %collective-permute-start.9 = (bf16[8,32,768]{2,1,0:T(8,128)(2,1)S(1)}, bf16[8,32,768]{2,1,0:T(8,128)(2,1)}, u32[]{:S(2)}, u32[]{:S(2)}) collective-permute-start(bf16[8,32,768]{2,1,0:T(8,128)(2,1)S(1)} %constant_dynamic-update-slice_fusion.near_ref), channel_id=1, source_target_pairs={{0,2},{2,0},{4,6},{6,4},{8,10},{10,8},{12,14},{14,12},{16,18},{18,... | collective-permute-start | bytes 1179656 | tf_op jit(solution)/shard_map/ppermute | solution.py:356
  53.7 3.7 %collective-permute-start.2 = (s32[4]{0:T(128)}, s32[4]{0:T(128)}, u32[]{:S(2)}, u32[]{:S(2)}) collective-permute-start(s32[4]{0:T(128)} %pad_add_fusion.1), channel_id=1, source_target_pairs={{0,4},{2,6},{4,0},{6,2},{8,12},{10,14},{12,8},{14,10},{16,20},{18,... | collective-permute-start | bytes 56 | tf_op jit(solution)/shard_map/ppermute | solution.py:356
  59.2 2.0 %collective-permute-start.3 = (s32[8]{0:T(128)}, s32[8]{0:T(128)}, u32[]{:S(2)}, u32[]{:S(2)}) collective-permute-start(s32[8]{0:T(128)} %pad_add_fusion.2), channel_id=1, source_target_pairs={{0,2},{2,0},{4,6},{6,4},{8,10},{10,8},{12,14},{14,12},{16,18},{18,... | collective-permute-start | bytes 104 | tf_op jit(solution)/shard_map/ppermute | solution.py:356
  68.3 4.2 %collective-permute-start.10 = (f32[32,256]{1,0:T(8,128)}, f32[32,256]{1,0:T(8,128)}, u32[]{:S(2)}, u32[]{:S(2)}) collective-permute-start(f32[32,256]{1,0:T(8,128)} %shard_map.113.own_ref), channel_id=1, source_target_pairs={{0,1},{1,0},{2,3},{3,2},{4,5},{5,4},{6,7},{7,6},{8,9},{9,8},{10,11... | collective-permute-start | bytes 98312 | tf_op jit(solution)/shard_map/ppermute | solution.py:359
  80.7 2.2 %copy-start.6 = (f32[768,384]{1,0:T(8,128)}, f32[768,384]{1,0:T(8,128)S(1)}, u32[]{:S(2)}) copy-start(f32[768,384]{1,0:T(8,128)S(1)} %get-tuple-element.35) | copy-start | bytes 3538948
  80.7 2.3 %copy-start = (f32[1024,768]{1,0:T(8,128)S(1)}, f32[1024,768]{1,0:T(8,128)}, u32[]{:S(2)}) copy-start(f32[1024,768]{1,0:T(8,128)} %get-tuple-element.27.slope_ref) | copy-start | bytes 9437188
  82.8 5.8 %copy-start.4 = (f32[768,384]{1,0:T(8,128)}, f32[768,384]{1,0:T(8,128)S(1)}, u32[]{:S(2)}) copy-start(f32[768,384]{1,0:T(8,128)S(1)} %get-tuple-element.37) | copy-start | bytes 3538948
  82.8 5.8 %copy-start.16 = (f32[768,384]{1,0:T(8,128)}, f32[768,384]{1,0:T(8,128)S(1)}, u32[]{:S(2)}) copy-start(f32[768,384]{1,0:T(8,128)S(1)} %get-tuple-element.38) | copy-start | bytes 3538948
  88.6 1.0 copy-start.15
  89.7 25.0 %copy-start.7 = (f32[768,384]{1,0:T(8,128)S(1)}, f32[768,384]{1,0:T(8,128)}, u32[]{:S(2)}) copy-start(f32[768,384]{1,0:T(8,128)} %copy-done.6) | copy-start | bytes 3538948
  95.2 1.1 copy-start.14
  96.3 18.4 %collective-permute-start.25 = (f32[768,384]{1,0:T(8,128)}, f32[768,384]{1,0:T(8,128)}, u32[]{:S(2)}, u32[]{:S(2)}) collective-permute-start(f32[768,384]{1,0:T(8,128)} %get-tuple-element.36), channel_id=1, source_target_pairs={{0,2},{2,0},{4,6},{6,4},{8,10},{10,8},{12,14},{14,12},{16,18},{18,... | collective-permute-start | bytes 3538952 | tf_op jit(solution)/shard_map/ppermute | solution.py:356
  98.5 1.3 collective-permute-start.11
  99.0 18.8 %collective-permute-start.30 = (f32[768,384]{1,0:T(8,128)}, f32[768,384]{1,0:T(8,128)}, u32[]{:S(2)}, u32[]{:S(2)}) collective-permute-start(f32[768,384]{1,0:T(8,128)} %copy-done.16), channel_id=1, source_target_pairs={{0,2},{2,0},{4,6},{6,4},{8,10},{10,8},{12,14},{14,12},{16,18},{18,... | collective-permute-start | bytes 3538952 | tf_op jit(solution)/shard_map/ppermute | solution.py:356
  99.1 20.8 %collective-permute-start.15 = (f32[768,384]{1,0:T(8,128)}, f32[768,384]{1,0:T(8,128)}, u32[]{:S(2)}, u32[]{:S(2)}) collective-permute-start(f32[768,384]{1,0:T(8,128)} %copy-done.15), channel_id=1, source_target_pairs={{0,2},{2,0},{4,6},{6,4},{8,10},{10,8},{12,14},{14,12},{16,18},{18,... | collective-permute-start | bytes 3538952 | tf_op jit(solution)/shard_map/ppermute | solution.py:356
  99.5 23.4 %collective-permute-start.20 = (f32[768,384]{1,0:T(8,128)}, f32[768,384]{1,0:T(8,128)}, u32[]{:S(2)}, u32[]{:S(2)}) collective-permute-start(f32[768,384]{1,0:T(8,128)} %copy-done.14), channel_id=1, source_target_pairs={{0,2},{2,0},{4,6},{6,4},{8,10},{10,8},{12,14},{14,12},{16,18},{18,... | collective-permute-start | bytes 3538952 | tf_op jit(solution)/shard_map/ppermute | solution.py:356
  100.6 3.5 %collective-permute-start.12 = (f32[3]{0:T(128)S(1)}, f32[3]{0:T(128)S(1)}, u32[]{:S(2)}, u32[]{:S(2)}) collective-permute-start(f32[3]{0:T(128)S(1)} %pad_maximum_fusion.5), channel_id=1, source_target_pairs={{0,4},{2,6},{4,0},{6,2},{8,12},{10,14},{12,8},{14,10},{16,20},{18,... | collective-permute-start | bytes 44 | tf_op jit(solution)/shard_map/ppermute | solution.py:356
  104.4 3.5 %collective-permute-start.13 = (f32[3]{0:T(128)S(1)}, f32[3]{0:T(128)S(1)}, u32[]{:S(2)}, u32[]{:S(2)}) collective-permute-start(f32[3]{0:T(128)S(1)} %pad_maximum_fusion.6), channel_id=1, source_target_pairs={{0,8},{2,10},{4,12},{6,14},{8,0},{10,2},{12,4},{14,6},{16,24},{18,... | collective-permute-start | bytes 44 | tf_op jit(solution)/shard_map/ppermute | solution.py:356
  108.1 4.4 %collective-permute-start.14 = (f32[3]{0:T(128)S(1)}, f32[3]{0:T(128)S(1)}, u32[]{:S(2)}, u32[]{:S(2)}) collective-permute-start(f32[3]{0:T(128)S(1)} %pad_maximum_fusion.7), channel_id=1, source_target_pairs={{0,16},{2,18},{4,20},{6,22},{8,24},{10,26},{12,28},{14,30},{16,0},... | collective-permute-start | bytes 44 | tf_op jit(solution)/shard_map/ppermute | solution.py:356
  114.7 3.2 %copy-start.5 = (f32[768,384]{1,0:T(8,128)S(1)}, f32[768,384]{1,0:T(8,128)}, u32[]{:S(2)}) copy-start(f32[768,384]{1,0:T(8,128)} %copy-done.4) | copy-start | bytes 3538948
  116.2 10.0 %collective-permute-start.26 = (f16[384,384]{1,0:T(8,128)(2,1)S(1)}, f16[384,384]{1,0:T(8,128)(2,1)S(1)}, u32[]{:S(2)}, u32[]{:S(2)}) collective-permute-start(f16[384,384]{1,0:T(8,128)(2,1)S(1)} %slice_convert_fusion.1), channel_id=1, source_target_pairs={{0,4},{2,6},{4,0},{6,2},{8,12},{10,14},{12,8},{14,10},{16,20},{18,... | collective-permute-start | bytes 884744 | tf_op jit(solution)/shard_map/ppermute | solution.py:356
  119.3 13.3 %collective-permute-start.31 = (f16[384,384]{1,0:T(8,128)(2,1)S(1)}, f16[384,384]{1,0:T(8,128)(2,1)S(1)}, u32[]{:S(2)}, u32[]{:S(2)}) collective-permute-start(f16[384,384]{1,0:T(8,128)(2,1)S(1)} %slice_convert_fusion), channel_id=1, source_target_pairs={{0,4},{2,6},{4,0},{6,2},{8,12},{10,14},{12,8},{14,10},{16,20},{18,... | collective-permute-start | bytes 884744 | tf_op jit(solution)/shard_map/ppermute | solution.py:356
  121.3 16.6 %collective-permute-start.16 = (f16[384,384]{1,0:T(8,128)(2,1)S(1)}, f16[384,384]{1,0:T(8,128)(2,1)S(1)}, u32[]{:S(2)}, u32[]{:S(2)}) collective-permute-start(f16[384,384]{1,0:T(8,128)(2,1)S(1)} %slice_convert_fusion.3), channel_id=1, source_target_pairs={{0,4},{2,6},{4,0},{6,2},{8,12},{10,14},{12,8},{14,10},{16,20},{18,... | collective-permute-start | bytes 884744 | tf_op jit(solution)/shard_map/ppermute | solution.py:356
  124.3 16.7 %collective-permute-start.21 = (f16[384,384]{1,0:T(8,128)(2,1)S(1)}, f16[384,384]{1,0:T(8,128)(2,1)S(1)}, u32[]{:S(2)}, u32[]{:S(2)}) collective-permute-start(f16[384,384]{1,0:T(8,128)(2,1)S(1)} %slice_convert_fusion.2), channel_id=1, source_target_pairs={{0,4},{2,6},{4,0},{6,2},{8,12},{10,14},{12,8},{14,10},{16,20},{18,... | collective-permute-start | bytes 884744 | tf_op jit(solution)/shard_map/ppermute | solution.py:356
  126.4 15.6 %collective-permute-start.27 = (f16[96,384]{1,0:T(8,128)(2,1)S(1)}, f16[96,384]{1,0:T(8,128)(2,1)S(1)}, u32[]{:S(2)}, u32[]{:S(2)}) collective-permute-start(f16[96,384]{1,0:T(8,128)(2,1)S(1)} %get-tuple-element.52), channel_id=1, source_target_pairs={{0,16},{2,18},{4,20},{6,22},{8,24},{10,26},{12,28},{14,30},{16,0},... | collective-permute-start | bytes 221192 | tf_op jit(solution)/shard_map/ppermute | solution.py:356
  127.1 16.3 %collective-permute-start.28 = (f16[96,384]{1,0:T(8,128)(2,1)S(1)}, f16[96,384]{1,0:T(8,128)(2,1)S(1)}, u32[]{:S(2)}, u32[]{:S(2)}) collective-permute-start(f16[96,384]{1,0:T(8,128)(2,1)S(1)} %get-tuple-element.54), channel_id=1, source_target_pairs={{0,8},{2,10},{4,12},{6,14},{8,0},{10,2},{12,4},{14,6},{16,24},{18,... | collective-permute-start | bytes 221192 | tf_op jit(solution)/shard_map/ppermute | solution.py:356
  132.6 12.2 %collective-permute-start.29 = (f16[96,384]{1,0:T(8,128)(2,1)S(1)}, f16[96,384]{1,0:T(8,128)(2,1)S(1)}, u32[]{:S(2)}, u32[]{:S(2)}) collective-permute-start(f16[96,384]{1,0:T(8,128)(2,1)S(1)} %get-tuple-element.53), channel_id=1, source_target_pairs={{0,24},{2,26},{4,28},{6,30},{8,16},{10,18},{12,20},{14,22},{16,8},... | collective-permute-start | bytes 221192 | tf_op jit(solution)/shard_map/ppermute | solution.py:356
  137.9 8.6 %collective-permute-start.32 = (f16[96,384]{1,0:T(8,128)(2,1)S(1)}, f16[96,384]{1,0:T(8,128)(2,1)S(1)}, u32[]{:S(2)}, u32[]{:S(2)}) collective-permute-start(f16[96,384]{1,0:T(8,128)(2,1)S(1)} %get-tuple-element.55), channel_id=1, source_target_pairs={{0,16},{2,18},{4,20},{6,22},{8,24},{10,26},{12,28},{14,30},{16,0},... | collective-permute-start | bytes 221192 | tf_op jit(solution)/shard_map/ppermute | solution.py:356
  141.0 8.0 %collective-permute-start.33 = (f16[96,384]{1,0:T(8,128)(2,1)S(1)}, f16[96,384]{1,0:T(8,128)(2,1)S(1)}, u32[]{:S(2)}, u32[]{:S(2)}) collective-permute-start(f16[96,384]{1,0:T(8,128)(2,1)S(1)} %get-tuple-element.57), channel_id=1, source_target_pairs={{0,8},{2,10},{4,12},{6,14},{8,0},{10,2},{12,4},{14,6},{16,24},{18,... | collective-permute-start | bytes 221192 | tf_op jit(solution)/shard_map/ppermute | solution.py:356
  141.9 7.1 %collective-permute-start.34 = (f16[96,384]{1,0:T(8,128)(2,1)S(1)}, f16[96,384]{1,0:T(8,128)(2,1)S(1)}, u32[]{:S(2)}, u32[]{:S(2)}) collective-permute-start(f16[96,384]{1,0:T(8,128)(2,1)S(1)} %get-tuple-element.56), channel_id=1, source_target_pairs={{0,24},{2,26},{4,28},{6,30},{8,16},{10,18},{12,20},{14,22},{16,8},... | collective-permute-start | bytes 221192 | tf_op jit(solution)/shard_map/ppermute | solution.py:356
  143.4 11.5 %collective-permute-start.17 = (f16[96,384]{1,0:T(8,128)(2,1)S(1)}, f16[96,384]{1,0:T(8,128)(2,1)S(1)}, u32[]{:S(2)}, u32[]{:S(2)}) collective-permute-start(f16[96,384]{1,0:T(8,128)(2,1)S(1)} %get-tuple-element.58), channel_id=1, source_target_pairs={{0,16},{2,18},{4,20},{6,22},{8,24},{10,26},{12,28},{14,30},{16,0},... | collective-permute-start | bytes 221192 | tf_op jit(solution)/shard_map/ppermute | solution.py:356
  144.7 11.5 %collective-permute-start.18 = (f16[96,384]{1,0:T(8,128)(2,1)S(1)}, f16[96,384]{1,0:T(8,128)(2,1)S(1)}, u32[]{:S(2)}, u32[]{:S(2)}) collective-permute-start(f16[96,384]{1,0:T(8,128)(2,1)S(1)} %get-tuple-element.60), channel_id=1, source_target_pairs={{0,8},{2,10},{4,12},{6,14},{8,0},{10,2},{12,4},{14,6},{16,24},{18,... | collective-permute-start | bytes 221192 | tf_op jit(solution)/shard_map/ppermute | solution.py:356
  146.5 9.7 %collective-permute-start.19 = (f16[96,384]{1,0:T(8,128)(2,1)S(1)}, f16[96,384]{1,0:T(8,128)(2,1)S(1)}, u32[]{:S(2)}, u32[]{:S(2)}) collective-permute-start(f16[96,384]{1,0:T(8,128)(2,1)S(1)} %get-tuple-element.59), channel_id=1, source_target_pairs={{0,24},{2,26},{4,28},{6,30},{8,16},{10,18},{12,20},{14,22},{16,8},... | collective-permute-start | bytes 221192 | tf_op jit(solution)/shard_map/ppermute | solution.py:356
  149.1 8.1 %collective-permute-start.22 = (f16[96,384]{1,0:T(8,128)(2,1)S(1)}, f16[96,384]{1,0:T(8,128)(2,1)S(1)}, u32[]{:S(2)}, u32[]{:S(2)}) collective-permute-start(f16[96,384]{1,0:T(8,128)(2,1)S(1)} %get-tuple-element.61), channel_id=1, source_target_pairs={{0,16},{2,18},{4,20},{6,22},{8,24},{10,26},{12,28},{14,30},{16,0},... | collective-permute-start | bytes 221192 | tf_op jit(solution)/shard_map/ppermute | solution.py:356
  149.1 8.1 %collective-permute-start.23 = (f16[96,384]{1,0:T(8,128)(2,1)S(1)}, f16[96,384]{1,0:T(8,128)(2,1)S(1)}, u32[]{:S(2)}, u32[]{:S(2)}) collective-permute-start(f16[96,384]{1,0:T(8,128)(2,1)S(1)} %get-tuple-element.63), channel_id=1, source_target_pairs={{0,8},{2,10},{4,12},{6,14},{8,0},{10,2},{12,4},{14,6},{16,24},{18,... | collective-permute-start | bytes 221192 | tf_op jit(solution)/shard_map/ppermute | solution.py:356
  154.8 6.2 %collective-permute-start.24 = (f16[96,384]{1,0:T(8,128)(2,1)S(1)}, f16[96,384]{1,0:T(8,128)(2,1)S(1)}, u32[]{:S(2)}, u32[]{:S(2)}) collective-permute-start(f16[96,384]{1,0:T(8,128)(2,1)S(1)} %get-tuple-element.62), channel_id=1, source_target_pairs={{0,24},{2,26},{4,28},{6,30},{8,16},{10,18},{12,20},{14,22},{16,8},... | collective-permute-start | bytes 221192 | tf_op jit(solution)/shard_map/ppermute | solution.py:356
  (6 other events, 4.1 us)

commit v2 on v1

v2 whole, which is shorter than its diff:
```python
import functools

import jax
import jax.numpy as jnp
from jax import lax
from jax.experimental import pallas as pl
from jax.experimental.pallas import tpu as pltpu
from jax.sharding import PartitionSpec as P

F32 = jnp.float32
BF16 = jnp.bfloat16
ROWS = 256
JOB_ROWS = 512
ROOT = 0.7978845608028654
HALF_MAX = 16384.0
UNUSABLE = 2.0
CHUNKS = 2


def vmem():
    return pl.BlockSpec(memory_space=pltpu.VMEM)


def smem():
    return pl.BlockSpec(memory_space=pltpu.SMEM)


def anyplace():
    return pl.BlockSpec(memory_space=pl.ANY)


def hbm():
    return pl.BlockSpec(memory_space=pltpu.HBM)


def params(mib):
    return pltpu.CompilerParams(vmem_limit_bytes=mib * 2**20)


def gelu(x):
    return x * (0.5 * (1.0 + jnp.tanh(ROOT * (x + 0.044715 * (x * x * x)))))


def gelu_slope(x):
    square = x * x
    t = jnp.tanh(ROOT * (x + 0.044715 * (square * x)))
    rise = (0.5 * x) * (1.0 - t * t) * (ROOT + (3 * 0.044715 * ROOT) * square)
    return 0.5 * (1.0 + t) + rise


def in_strips(rows, width, height, work):
    def step(i, carry):
        here = pl.ds(pl.multiple_of(i * height, height), height)
        for column in range(0, width, 128):
            work(i, here, slice(column, column + 128))
        return carry

    lax.fori_loop(0, rows // height, step, 0)


def forward_kernel(
    tokens_of,
    place_ref,
    image_hbm,
    text_hbm,
    image_w_hbm,
    text_w_hbm,
    pooled_ref,
    square_ref,
    image_pre_hbm,
    text_pre_hbm,
    image_v,
    text_v,
    image_w,
    text_w,
    image_pre,
    text_pre,
    in_sem,
    w_sem,
    out_sem,
):
    width = image_w.shape[1]
    samples = pooled_ref.shape[0] // 2
    jobs = []
    for source, buf, w_source, w, pre, pre_out, tok, base in (
        (text_hbm, text_v, text_w_hbm, text_w, text_pre, text_pre_hbm, tokens_of[1], samples),
        (image_hbm, image_v, image_w_hbm, image_w, image_pre, image_pre_hbm, tokens_of[0], 0),
    ):
        for start in range(0, buf.shape[0], JOB_ROWS):
            jobs.append((source, buf, w_source, w, pre, pre_out, tok, base, start))
    waits = []
    weights = 0
    for n, (source, buf, w_source, w, _, _, _, _, start) in enumerate(jobs):
        here = []
        if start == 0:
            here.append(pltpu.make_async_copy(w_source, w, w_sem.at[weights]))
            weights += 1
        part = pl.ds(start, JOB_ROWS)
        here.append(pltpu.make_async_copy(source.at[part, :], buf.at[part, :], in_sem.at[n]))
        for copy in here:
            copy.start()
        waits.append(here)
    first = place_ref[0] * width

    def project(n):
        _, buf, _, w, pre, _, _, _, start = jobs[n]
        for copy in waits[n]:
            copy.wait()
        part = pl.ds(start, JOB_ROWS)
        pre[part, :] = jnp.dot(buf[part, :], w[...], preferred_element_type=F32)

    out_copies = []
    project(0)
    for n, (_, buf, _, _, pre, pre_out, tok, base, start) in enumerate(jobs):
        part = pl.ds(start, JOB_ROWS)
        copy = pltpu.make_async_copy(pre.at[part, :], pre_out.at[part, :], out_sem.at[n])
        copy.start()
        out_copies.append(copy)
        if n + 1 < len(jobs):
            project(n + 1)
        for row in range(start, start + JOB_ROWS, tok):
            sample = base + row // tok
            for column in range(0, width, 128):
                token_columns = pl.ds(pl.multiple_of(first + column, 128), 128)
                value = gelu(pre[row : row + tok, column : column + 128])
                hidden = buf[row : row + tok, token_columns].astype(F32) + value
                pooled_ref[sample : sample + 1, column : column + 128] = (
                    jnp.sum(hidden, axis=0, keepdims=True) / tok
                )
    pooled = pooled_ref[...]
    total = jnp.sum(pooled * pooled, axis=1, keepdims=True)
    square_ref[...] = jnp.broadcast_to(total, square_ref.shape)
    for copy in out_copies:
        copy.wait()


def forward(place, image_flat, text_flat, image_w, text_w, samples):
    width = image_w.shape[1]
    depth = image_w.shape[0]
    rows_i, rows_t = image_flat.shape[0], text_flat.shape[0]
    jobs = (rows_i + rows_t) // JOB_ROWS
    return pl.pallas_call(
        functools.partial(forward_kernel, (rows_i // samples, rows_t // samples)),
        out_shape=(
            jax.ShapeDtypeStruct((2 * samples, width), F32),
            jax.ShapeDtypeStruct((2 * samples, 128), F32),
            jax.ShapeDtypeStruct((rows_i, width), F32),
            jax.ShapeDtypeStruct((rows_t, width), F32),
        ),
        in_specs=[smem()] + [hbm()] * 4,
        out_specs=(vmem(), vmem(), hbm(), hbm()),
        scratch_shapes=[
            pltpu.VMEM((rows_i, depth), BF16),
            pltpu.VMEM((rows_t, depth), BF16),
            pltpu.VMEM((depth, width), BF16),
            pltpu.VMEM((depth, width), BF16),
            pltpu.VMEM((rows_i, width), F32),
            pltpu.VMEM((rows_t, width), F32),
            pltpu.SemaphoreType.DMA((jobs,)),
            pltpu.SemaphoreType.DMA((2,)),
            pltpu.SemaphoreType.DMA((jobs,)),
        ],
        compiler_params=params(63),
        cost_estimate=pl.CostEstimate(
            flops=2 * (rows_i + rows_t) * depth * width,
            bytes_accessed=2 * (rows_i + rows_t) * (depth + 2 * width) + 4 * depth * width,
            transcendentals=(rows_i + rows_t) * width,
        ),
    )(place, image_flat, text_flat, image_w, text_w)


def unit_kernel(count_ref, pooled_ref, own_ref, other_ref, unit_ref, sent_ref, norm_ref):
    both = pooled_ref.shape[0]
    norm = jnp.sqrt(own_ref[...] + other_ref[...] + 1e-06)
    norm_ref[...] = norm
    unit = pooled_ref[...] / norm[:, :1]
    unit_ref[...] = unit
    row = lax.broadcasted_iota(jnp.int32, unit.shape, 0) % (both // 2)
    sent_ref[...] = jnp.where(row < count_ref[0], unit, UNUSABLE).astype(BF16)


def units(count, pooled, own, other):
    return pl.pallas_call(
        unit_kernel,
        out_shape=(
            jax.ShapeDtypeStruct(pooled.shape, F32),
            jax.ShapeDtypeStruct(pooled.shape, BF16),
            jax.ShapeDtypeStruct(own.shape, F32),
        ),
        in_specs=[smem()] + [vmem()] * 3,
        out_specs=(vmem(),) * 3,
        compiler_params=params(4),
    )(count, pooled, own, other)


def stack_kernel(_, *refs):
    *parts, out_ref = refs
    for n, part in enumerate(parts):
        out_ref[n] = part[...]


def stack(parts, after):
    return pl.pallas_call(
        stack_kernel,
        out_shape=jax.ShapeDtypeStruct((len(parts), *parts[0].shape), parts[0].dtype),
        in_specs=[anyplace()] + [vmem()] * len(parts),
        out_specs=vmem(),
        compiler_params=params(4),
    )(after, *parts)


def prepare_kernel(source_ref, tokens_ref, pre_ref, _, turned_ref, most_ref, slope_ref, turned):
    def one(i, here, columns):
        slope_ref[here, columns] = gelu_slope(pre_ref[here, columns])

    in_strips(*pre_ref.shape, 32, one)
    turned[...] = tokens_ref[...].T
    largest = jnp.max(jnp.abs(tokens_ref[...]).astype(F32), axis=0, keepdims=True)
    largest = jnp.broadcast_to(jnp.max(largest, axis=1, keepdims=True), most_ref.shape)

    @pl.when(pl.program_id(0) == 0)
    def _():
        most_ref[...] = jnp.zeros_like(most_ref)

    most_ref[...] = jnp.maximum(most_ref[...], largest)
    blocks = source_ref.shape[0]
    height = turned_ref.shape[0] // blocks
    for q in range(blocks):
        source = pl.multiple_of(source_ref[q] * height, height)
        turned_ref[q * height : (q + 1) * height, :] = turned[pl.ds(source, height), :]


def prepare(sources, flat, pre, after):
    rows, depth = flat.shape
    width = pre.shape[1]
    blocks = sources.shape[0]
    odd = (depth // blocks) % 16
    picked = jnp.arange(16, dtype=jnp.int32) if odd else sources
    turned, most, slope = pl.pallas_call(
        prepare_kernel,
        out_shape=(
            jax.ShapeDtypeStruct((depth, rows), flat.dtype),
            jax.ShapeDtypeStruct((8, 128), F32),
            jax.ShapeDtypeStruct((rows, width), F32),
        ),
        grid=(rows // ROWS,),
        in_specs=[
            smem(),
            pl.BlockSpec((ROWS, depth), lambda i: (i, 0)),
            pl.BlockSpec((ROWS, width), lambda i: (i, 0)),
            anyplace(),
        ],
        out_specs=(
            pl.BlockSpec((depth, ROWS), lambda i: (0, i)),
            pl.BlockSpec((8, 128), lambda i: (0, 0)),
            pl.BlockSpec((ROWS, width), lambda i: (i, 0)),
        ),
        scratch_shapes=[pltpu.VMEM((depth, ROWS), flat.dtype)],
        compiler_params=params(16),
        cost_estimate=pl.CostEstimate(
            flops=0, bytes_accessed=4 * rows * depth + 8 * rows * width, transcendentals=0
        ),
    )(picked, flat, pre, after)
    if odd:
        turned = turned.reshape(blocks, depth // blocks, rows)[sources].reshape(depth, rows)
    return turned, most, slope


def row_products(left, right):
    return lax.dot_general(left, right, (((1,), (1,)), ((), ())), preferred_element_type=F32)


def towers(blocks_ref, samples):
    blocks, _, width = blocks_ref.shape
    image = blocks_ref[:, :samples, :].reshape(blocks * samples, width)
    text = blocks_ref[:, samples:, :].reshape(blocks * samples, width)
    return image, text


def product_kernel(image_most_ref, text_most_ref, *refs):
    *block_refs, out_ref, mark_ref = refs
    near_ref = block_refs[0]
    samples = near_ref.shape[1] // 2
    own_image = near_ref[0, :samples, :]
    own_text = near_ref[0, samples:, :]
    lane = lax.broadcasted_iota(jnp.int32, own_image.shape, 1)
    first = jnp.where(lane == 0, 1.0, 0.0).astype(BF16)
    start = 0
    for ref in block_refs:
        image, text = towers(ref, samples)
        stop = start + image.shape[0]
        found = row_products(jnp.concatenate([own_image, first], axis=0), text)
        out_ref[:samples, start:stop] = found[:samples]
        mark_ref[:, start:stop] = found[samples : samples + 8]
        out_ref[samples:, start:stop] = row_products(own_text, image)
        start = stop


def products(blocks, mosts):
    both = blocks[0].shape[1]
    columns = sum(b.shape[0] for b in blocks) * (both // 2)
    return pl.pallas_call(
        product_kernel,
        out_shape=(
            jax.ShapeDtypeStruct((both, columns), F32),
            jax.ShapeDtypeStruct((8, columns), F32),
        ),
        in_specs=[anyplace()] * 2 + [vmem()] * len(blocks),
        out_specs=(vmem(),) * 2,
        compiler_params=params(8),
    )(*mosts, *blocks)


def middle_kernel(
    tokens_of,
    scale_ref,
    bias_ref,
    gain_ref,
    count_ref,
    own_ref,
    other_ref,
    mark_ref,
    unit_ref,
    norm_ref,
    image_most_ref,
    text_most_ref,
    *refs,
):
    *block_refs, grad_ref, stat_ref = refs
    samples = unit_ref.shape[0] // 2
    scale, bias = scale_ref[0], bias_ref[0]
    dots = own_ref[...] + other_ref[...]
    logits = scale * dots + bias
    row = lax.broadcasted_iota(jnp.int32, dots.shape, 0) % samples
    column = lax.broadcasted_iota(jnp.int32, dots.shape, 1)
    sign = jnp.where(row == column, 1.0, -1.0).astype(F32)
    usable = jnp.where(mark_ref[:1, :] < 1.5, 1.0, 0.0)
    total = jnp.sum(usable, axis=1, keepdims=True)
    used = (usable > 0.5) & (row < count_ref[0])
    margin = -sign * logits
    small = jnp.exp(-jnp.abs(margin))
    soft = jnp.maximum(margin, 0.0) + jnp.log1p(small)
    sigmoid = jnp.where(margin >= 0, 1.0, small) / (1.0 + small)
    part = jnp.where(used, soft, 0.0)[:samples, :]
    loss = jnp.sum(jnp.sum(part, axis=1, keepdims=True), axis=0, keepdims=True) / total
    coeff = gain_ref[0] / total
    dlogit = (jnp.where(used, -sign * sigmoid, 0.0) * coeff).astype(BF16)
    radial = scale * jnp.sum(dlogit.astype(F32) * dots, axis=1, keepdims=True)
    raws = [jnp.zeros((samples, unit_ref.shape[1]), F32) for _ in range(2)]
    start = 0
    for ref in block_refs:
        image, text = towers(ref, samples)
        stop = start + image.shape[0]
        raws[0] += jnp.dot(dlogit[:samples, start:stop], text, preferred_element_type=F32)
        raws[1] += jnp.dot(dlogit[samples:, start:stop], image, preferred_element_type=F32)
        start = stop
    limits = []
    for n, most_ref in enumerate((image_most_ref, text_most_ref)):
        here = slice(n * samples, (n + 1) * samples)
        inward = unit_ref[here, :] * radial[here, :]
        grad = (scale * raws[n] - inward) / norm_ref[here, :1] / tokens_of[n]
        grad_ref[here, :] = grad
        steep = jnp.max(jnp.max(jnp.abs(grad), axis=1, keepdims=True), axis=0, keepdims=True)
        limits.append(1.2 * samples * tokens_of[n] * most_ref[:1, :1] * steep)
    line = lax.broadcasted_iota(jnp.int32, stat_ref.shape, 0)
    stat_ref[...] = jnp.where(line == 0, loss, jnp.where(line == 1, limits[0], limits[1]))


def middle(tokens_of, scale, bias, gain, count, own, other, mark, unit, norm, mosts, blocks):
    return pl.pallas_call(
        functools.partial(middle_kernel, tokens_of),
        out_shape=(
            jax.ShapeDtypeStruct(unit.shape, F32),
            jax.ShapeDtypeStruct((8, unit.shape[1]), F32),
        ),
        in_specs=[smem()] * 4 + [vmem()] * (7 + len(blocks)),
        out_specs=(vmem(), vmem()),
        compiler_params=params(12),
    )(scale, bias, gain, count, own, other, mark, unit, norm, *mosts, *blocks)


def weight_kernel(base, chunk, carries, first, grad_ref, slope_hbm, turned_hbm, stat_ref, *refs):
    _, send_out, keep_out, grad_out, slope_v, turned_v, terms, slope_sem, in_sem, out_sem = refs
    _, height, width = terms.shape
    slope_copy = pltpu.make_async_copy(slope_hbm, slope_v if first else grad_out, slope_sem)
    slope_copy.start()
    copies = []
    for n in range(2):
        block = 2 * chunk + 1 - n
        copy = pltpu.make_async_copy(
            turned_hbm.at[pl.ds(block * height, height), :], turned_v.at[n], in_sem.at[n]
        )
        copy.start()
        copies.append(copy)
    out_copies = []
    if carries:
        copy = pltpu.make_async_copy(
            stat_ref, send_out.at[pl.ds(height, stat_ref.shape[0]), :], out_sem.at[2]
        )
        copy.start()
        out_copies.append(copy)
    slope_copy.wait()
    if first:
        samples = grad_ref.shape[0] // 2
        tok = slope_v.shape[0] // samples
        for sample in range(samples):
            here = slice(sample * tok, (sample + 1) * tok)
            row = base * samples + sample
            for column in range(0, width, 128):
                columns = slice(column, column + 128)
                slope = slope_v[here, columns]
                grad_out[here, columns] = (grad_ref[row : row + 1, columns] * slope).astype(BF16)
    for n, out in enumerate((send_out, keep_out)):
        copies[n].wait()
        terms[n] = jnp.dot(turned_v[n], grad_out[...], preferred_element_type=F32)
        copy = pltpu.make_async_copy(terms.at[n], out.at[pl.ds(0, height), :], out_sem.at[n])
        copy.start()
        out_copies.append(copy)
    for copy in out_copies:
        copy.wait()


def weight_terms(grad, slope, turned, stat, base, chunk, carries, first, after):
    depth, rows = turned.shape
    width = slope.shape[1]
    height = depth // (2 * CHUNKS)
    sent = height + (stat.shape[0] if carries else 0)
    return pl.pallas_call(
        functools.partial(weight_kernel, base, chunk, carries, first),
        out_shape=(
            jax.ShapeDtypeStruct((sent, width), F32),
            jax.ShapeDtypeStruct((height, width), F32),
            jax.ShapeDtypeStruct((rows, width), BF16),
        ),
        in_specs=[vmem(), anyplace(), anyplace(), vmem(), anyplace()],
        out_specs=(anyplace(), anyplace(), vmem()),
        scratch_shapes=[
            pltpu.VMEM((rows if first else 8, width), F32),
            pltpu.VMEM((2, height, rows), BF16),
            pltpu.VMEM((2, height, width), F32),
            pltpu.SemaphoreType.DMA,
            pltpu.SemaphoreType.DMA((2,)),
            pltpu.SemaphoreType.DMA((3,)),
        ],
        compiler_params=params(14),
        cost_estimate=pl.CostEstimate(
            flops=depth * rows * width,
            bytes_accessed=depth * rows + 4 * rows * width + 2 * depth * width,
            transcendentals=0,
        ),
    )(grad, slope, turned, stat, after)


def sum_of(terms):
    total = None
    for term, unit in terms:
        value = term if unit is None else term.astype(F32) * unit
        total = value if total is None else total + value
    return total


def body(
    image_tokens,
    text_tokens,
    image_weight,
    text_weight,
    logit_scale,
    logit_bias,
    loss_scale,
    valid_count,
):
    samples, image_tok, depth = image_tokens.shape
    text_tok = text_tokens.shape[1]
    width = image_weight.shape[1]
    cycle = lax.axis_size("dp")
    bits = cycle.bit_length() - 1
    place = lax.axis_index("dp")

    def swap(array, mask):
        return lax.ppermute(array, "dp", [(i, i ^ mask) for i in range(cycle)])

    def swap_halves(array):
        return lax.ppermute(array, "mp", [(0, 1), (1, 0)])

    def picked(order):
        owners = [
            sum(((q >> (bits - 1 - i)) & 1) << b for i, b in enumerate(order)) for q in range(cycle)
        ]
        return jnp.asarray(owners, jnp.int32) ^ place

    image_flat = image_tokens.reshape(-1, depth)
    text_flat = text_tokens.reshape(-1, depth)
    near_first = list(range(bits))
    far_first = [0] + list(range(2, bits)) + [1]
    text_orders, image_orders = (near_first, far_first), (near_first, near_first)

    def sources(orders):
        return jnp.concatenate([picked(order) * CHUNKS + c for c, order in enumerate(orders)])

    model_place = lax.axis_index("mp").astype(jnp.int32).reshape(1)
    pooled, square, image_pre, text_pre = forward(
        model_place, image_flat, text_flat, image_weight, text_weight, samples
    )
    unit, sent, norm = units(valid_count, pooled, square, swap_halves(square))

    low = max(bits - 2, 1)
    tops = [1 << b for b in reversed(range(low, bits))]
    masks = tops + [tops[0] | tops[1]] if len(tops) == 2 else tops
    arrived = [swap(sent, mask) for mask in masks]
    image_turned, image_most, image_slope = prepare(
        sources(image_orders), image_flat, image_pre, sent
    )
    gathered = stack([sent] + arrived, image_most)
    text_turned, text_most, text_slope = prepare(
        sources(text_orders), text_flat, text_pre, gathered
    )
    blocks = [gathered]
    for b in reversed(range(1, low)):
        blocks = blocks + [swap(block, 1 << b) for block in blocks]
    far = [swap(block, 1) for block in blocks[:1]]
    for block in blocks[1:]:
        far.append(swap(stack([block], text_most)[0], 1))
    blocks = blocks + far

    own_dots, mark = products(blocks, (image_most, text_most))
    grad, stat = middle(
        (image_tok, text_tok),
        logit_scale,
        logit_bias,
        loss_scale,
        valid_count,
        own_dots,
        swap_halves(own_dots),
        mark,
        unit,
        norm,
        (image_most, text_most),
        blocks,
    )

    def terms_of(slope, turned, base, chunk, carries, after):
        first = chunk == 0
        return weight_terms(grad, slope, turned, stat, base, chunk, carries, first, after)

    def split(sent, kept):
        height = kept.shape[0]
        there = swap(sent, 1)
        return [(kept, None), (there[:height], None)], there[height:]

    def level(terms, line, bit, here, there, after):
        half = terms[0][0].shape[0] // 2
        leaving = sum_of([(term[half:], unit) for term, unit in terms])
        factor = HALF_MAX / jnp.maximum(here[line : line + 1], 1e-30)
        for array in after:
            factor = factor + 0.0 * array[:1].astype(F32)
        coded = (leaving * factor).astype(jnp.float16)
        coming = swap(coded, 1 << bit)
        unit = jnp.maximum(there[line : line + 1], 1e-30) / HALF_MAX
        return [(term[:half], u) for term, u in terms] + [(coming, unit)], coded, coming

    send, keep, text_grad = terms_of(text_slope, text_turned, 1, 0, True, grad)
    text0, stat_there = split(send, keep)
    near_stats = [stat + stat_there]
    near_theres = [swap(near_stats[0], 1 << near_first[1])]
    far_stats = [near_stats[0]]
    far_theres = [swap(far_stats[0], 1 << far_first[1])]
    text0, coded, text0_in = level(text0, 2, near_first[1], near_stats[0], near_theres[0], ())

    send, keep, _ = terms_of(text_grad, text_turned, 1, 1, False, text_grad)
    text1, _ = split(send, keep)
    after = coded[:8].astype(F32)
    text1, coded, text1_in = level(text1, 2, far_first[1], far_stats[0], far_theres[0], (coded,))

    send, keep, image_grad = terms_of(image_slope, image_turned, 0, 0, False, after)
    image0, _ = split(send, keep)
    after = coded[:8].astype(F32)
    image0, coded, _ = level(
        image0, 1, near_first[1], near_stats[0], near_theres[0], (coded,)
    )
    send, keep, _ = terms_of(image_grad, image_turned, 0, 1, False, after)
    image1, _ = split(send, keep)

    for step in range(2, bits):
        last = step == bits - 1
        near_stats.append(near_stats[-1] + near_theres[-1] + 0.0 * text0_in[:8].astype(F32))
        near_theres.append(swap(near_stats[-1], 1 << near_first[step]))
        if not last:
            far_stats.append(far_stats[-1] + far_theres[-1] + 0.0 * text1_in[:8].astype(F32))
            far_theres.append(swap(far_stats[-1], 1 << far_first[step]))
            text1, coded, text1_in = level(
                text1, 2, far_first[step], far_stats[-1], far_theres[-1], (coded,)
            )
        text0, coded, text0_in = level(
            text0, 2, near_first[step], near_stats[-1], near_theres[-1], (coded,)
        )
        if step == 2:
            image1, coded, _ = level(
                image1, 1, near_first[1], near_stats[0], near_theres[0], (coded, text0_in)
            )
    full = near_stats[-1] + near_theres[-1]
    loss = full[0, 0]
    text1, coded, _ = level(text1, 2, far_first[-1], full, full, (coded,))
    for step in range(2, bits):
        image0, coded, _ = level(
            image0, 1, near_first[step], near_stats[step - 1], near_theres[step - 1], (coded,)
        )
    for step in range(2, bits):
        image1, coded, _ = level(
            image1, 1, near_first[step], near_stats[step - 1], near_theres[step - 1], (coded,)
        )
    text = jnp.concatenate([sum_of(text0), sum_of(text1)])
    image = jnp.concatenate([sum_of(image0), sum_of(image1)])
    return (loss, image, text)


def solution(mesh):
    placed = (
        P("dp", None, None),
        P("dp", None, None),
        P(None, "mp"),
        P(None, "mp"),
        P(),
        P(),
        P(),
        P("dp"),
    )
    return jax.shard_map(
        body,
        mesh=mesh,
        in_specs=placed,
        out_specs=(P(), P("dp", "mp"), P("dp", "mp")),
        check_vma=False,
    )
```

time: 164 us -> 106 us (0.65)
  other arithmetic: 22.7 us -> 3.02 us
  local copies, waits for them, and re-layouts: 21.8 us -> 5.92 us
  between operations: 10.9 us -> 3.69 us
  Pallas kernels: 36.5 us -> 30.1 us
  starting transfers between devices: 37.7 us -> 33.1 us
  waiting for transfers between devices: 33.4 us -> 30.1 us
    unnamed x41 -> x16, local copies, waits for them, and re-layouts: 14.8 us -> 5.41 us
    concatenate x9 -> x3, other arithmetic: 7.37 us -> 1.54 us  [the longest x1 0.73 us: body(): image = jnp.concatenate([sum_of(image0), sum_of(image1)])]
    ppermute x33 -> x27, starting transfers between devices: 34.2 us -> 28.4 us  [swap(): return lax.ppermute(array, 'dp', [(i, i ^ mask) for i in range(cycle)])]
    mul x5 -> x1, other arithmetic: 5.74 us -> 0.01 us  [sources(): picked(order) * CHUNKS + c]
    pallas_call x7 -> x10, Pallas kernels: 24.4 us -> 20.4 us  [the longest x4 12.3 us: weight_terms(): pl.pallas_call(functools.partial(weight_kernel, base, chunk, carries, fir...]
    reduce_sum x3 -> x0, other arithmetic: 3.8 us -> none  [body(): total = jnp.sum(counts).astype(F32)]
    ppermute x33 -> x27, waiting for transfers between devices: 31.6 us -> 28.5 us  [swap(): return lax.ppermute(array, 'dp', [(i, i ^ mask) for i in range(cycle)])]
    slice x8 -> x1, local copies, waits for them, and re-layouts: 2.98 us -> 0.51 us  [body(): loss = full[0, 0]]
  transfers between devices with their start and end apart: 35 -> 29, of which waited for: 17 -> 11; matrix products, arithmetic and copies ran while one was open for 19% -> 3% of each run, Pallas kernels for 4% -> 17%
where the time goes in v2:
time: 106 us
  starting transfers between devices  33.1 us (31%)
  Pallas kernels  30.1 us (28%)
  waiting for transfers between devices  30.1 us (28%)
  local copies, waits for them, and re-layouts  5.92 us (6%)
  between operations  3.69 us (3%)
  other arithmetic  3.02 us (3%)
    ppermute x27, waiting for transfers between devices, swap(): return lax.ppermute(array, 'dp', [(i, i ^ mask) for i in range(cycle)])  28.5 us
    ppermute x27, starting transfers between devices, swap(): return lax.ppermute(array, 'dp', [(i, i ^ mask) for i in range(cycle)])  28.4 us
    pallas_call x4, Pallas kernels, weight_terms(): pl.pallas_call(functools.partial(weight_kernel, base, chunk, carries, fir...  12.3 us
    pallas_call x1, Pallas kernels, forward(): pl.pallas_call(functools.partial(forward_kernel, (rows_i // samples, rows...  9.2 us
    pallas_call x2, Pallas kernels, prepare(): pl.pallas_call(prepare_kernel, out_shape=(jax.ShapeDtypeStruct((depth, ro...  7.6 us
    unnamed x16, local copies, waits for them, and re-layouts  5.41 us
    ppermute x2, starting transfers between devices, swap_halves(): return lax.ppermute(array, 'mp', [(0, 1), (1, 0)])  4.67 us
  transfers between devices with their start and end apart: 29, of which 11 were waited for; matrix products, arithmetic and copies ran while one was open for 3% of the time, Pallas kernels for 17%

profile of v2, /device:TPU:0, one launch (start us, length us, event | category | flops | bytes accessed | tf_op | source)
XLA Modules:
  0.0 105.9 jit_solution(2386497373020765669)
XLA Ops:
  0.7 9.2 %shard_map.139 = (f32[32,768]{1,0:T(8,128)}, f32[32,128]{1,0:T(8,128)}, f32[1024,768]{1,0:T(8,128)}, f32[512,768]{1,0:T(8,128)}) custom-call(s32[1]{0:T(128)} %bitcast.1.place_ref, bf16[1024,1536]{1,0:T(8,128)(2,1)} %bitcast.5, bf16[512,1536]{1,0:T(8,128)(2,1)} %bitcast.7, bf16[1536,768]{1,0:T(8,128)(2,1)} %image_w_hbm.1, bf16[1536,768]{1,0:T(8,128)(2,1)} %text_w_hbm.1), custom_call_target="tpu_custom_call" | custom-call | flops 3623878656 | bytes 14155776 | tf_op jit(solution)/shard_map/pallas_call | solution.py:142
  9.9 3.0 %collective-permute-start = (f32[32,128]{1,0:T(8,128)}, f32[32,128]{1,0:T(8,128)S(1)}, u32[]{:S(2)}, u32[]{:S(2)}) collective-permute-start(f32[32,128]{1,0:T(8,128)} %get-tuple-element.32.own_ref), channel_id=1, source_target_pairs={{0,1},{1,0},{2,3},{3,2},{4,5},{5,4},{6,7},{7,6},{8,9},{9,8},{10,11... | collective-permute-start | bytes 49160 | tf_op jit(solution)/shard_map/ppermute | solution.py:483
  13.5 1.3 %collective-permute-done.other_ref = f32[32,128]{1,0:T(8,128)S(1)} collective-permute-done((f32[32,128]{1,0:T(8,128)}, f32[32,128]{1,0:T(8,128)S(1)}, u32[]{:S(2)}, u32[]{:S(2)}) %collective-permute-start) | collective-permute-done | bytes 16416 | tf_op jit(solution)/shard_map/ppermute | solution.py:483
  14.8 0.9 copy-done.4
  15.7 0.7 copy-done.5
  16.5 4.2 %collective-permute-start.3 = (bf16[32,768]{1,0:T(8,128)(2,1)S(1)}, bf16[32,768]{1,0:T(8,128)(2,1)S(1)}, u32[]{:S(2)}, u32[]{:S(2)}) collective-permute-start(bf16[32,768]{1,0:T(8,128)(2,1)S(1)} %get-tuple-element.33._.refs_0_), channel_id=1, source_target_pairs={{0,24},{2,26},{4,28},{6,30},{8,16},{10,18},{12,20},{14,22},{16,8},... | collective-permute-start | bytes 147464 | tf_op jit(solution)/shard_map/ppermute | solution.py:480
  20.7 0.6 collective-permute-start.1
  21.4 1.9 %copy-done = bf16[16,64,1536]{2,1,0:T(8,128)(2,1)S(1)} copy-done((bf16[16,64,1536]{2,1,0:T(8,128)(2,1)S(1)}, bf16[16,64,1536]{2,1,0:T(8,128)(2,1)}, u32[]{:S(2)}) %copy-start) | copy-done | bytes 3145752
  23.3 1.9 %copy-done.1 = f32[1024,768]{1,0:T(8,128)S(1)} copy-done((f32[1024,768]{1,0:T(8,128)S(1)}, f32[1024,768]{1,0:T(8,128)}, u32[]{:S(2)}) %copy-start.1) | copy-done | bytes 3145752
  25.2 4.9 %shard_map.141 = (bf16[1536,1024]{1,0:T(8,128)(2,1)S(1)}, f32[8,128]{1,0:T(8,128)S(1)}, f32[1024,768]{1,0:T(8,128)S(1)}) custom-call(s32[32]{0:T(128)S(1)} %get-tuple-element.78.source_ref, bf16[1024,1536]{1,0:T(8,128)(2,1)S(1)} %bitcast.6, f32[1024,768]{1,0:T(8,128)S(1)} %copy-done.1, bf16[32,768]{1,0:T(8,128)(2,1)S(1)} %get-tuple-element.33._.refs_0_), custom_call_target="tpu_custom_call" | custom-call | bytes 12582912 | tf_op jit(solution)/shard_map/pallas_call | solution.py:239
  30.2 1.7 %collective-permute-start.4 = (bf16[4,32,768]{2,1,0:T(8,128)(2,1)S(1)}, bf16[4,32,768]{2,1,0:T(8,128)(2,1)S(1)}, u32[]{:S(2)}, u32[]{:S(2)}) collective-permute-start(bf16[4,32,768]{2,1,0:T(8,128)(2,1)S(1)} %shard_map.142._.refs_0_), channel_id=1, source_target_pairs={{0,4},{2,6},{4,0},{6,2},{8,12},{10,14},{12,8},{14,10},{16,20},{18,... | collective-permute-start | bytes 589832 | tf_op jit(solution)/shard_map/ppermute | solution.py:480
  31.9 2.7 %shard_map.143 = (bf16[1536,512]{1,0:T(8,128)(2,1)S(1)}, f32[8,128]{1,0:T(8,128)S(1)}, f32[512,768]{1,0:T(8,128)S(1)}) custom-call(s32[32]{0:T(128)S(1)} %get-tuple-element.77.source_ref, bf16[512,1536]{1,0:T(8,128)(2,1)S(1)} %bitcast.8, f32[512,768]{1,0:T(8,128)S(1)} %copy-done.3, bf16[4,32,768]{2,1,0:T(8,128)(2,1)S(1)} %shard_map.142._.refs_0_), custom_call_target="tpu_custom_call" | custom-call | bytes 6291456 | tf_op jit(solution)/shard_map/pallas_call | solution.py:239
  34.6 1.3 %collective-permute-done.4.refs_0_.refs_1_ = bf16[4,32,768]{2,1,0:T(8,128)(2,1)S(1)} collective-permute-done((bf16[4,32,768]{2,1,0:T(8,128)(2,1)S(1)}, bf16[4,32,768]{2,1,0:T(8,128)(2,1)S(1)}, u32[]{:S(2)}, u32[]{:S(2)}) %collective-permute-start.4) | collective-permute-done | bytes 196640 | tf_op jit(solution)/shard_map/ppermute | solution.py:480
  36.0 1.4 %collective-permute-done.6.refs_3_ = bf16[4,32,768]{2,1,0:T(8,128)(2,1)S(1)} collective-permute-done((bf16[4,32,768]{2,1,0:T(8,128)(2,1)S(1)}, bf16[4,32,768]{2,1,0:T(8,128)(2,1)S(1)}, u32[]{:S(2)}, u32[]{:S(2)}) %collective-permute-start.6) | collective-permute-done | bytes 196640 | tf_op jit(solution)/shard_map/ppermute | solution.py:480
  37.5 0.4 shard_map.145
  37.8 1.7 %collective-permute-start.7 = (f32[32,256]{1,0:T(8,128)S(1)}, f32[32,256]{1,0:T(8,128)S(1)}, u32[]{:S(2)}, u32[]{:S(2)}) collective-permute-start(f32[32,256]{1,0:T(8,128)S(1)} %get-tuple-element.37.own_ref), channel_id=1, source_target_pairs={{0,1},{1,0},{2,3},{3,2},{4,5},{5,4},{6,7},{7,6},{8,9},{9,8},{10,11... | collective-permute-start | bytes 98312 | tf_op jit(solution)/shard_map/ppermute | solution.py:483
  41.4 0.3 collective-permute-done.7.other_ref
  41.8 0.5 shard_map.146
  42.3 2.4 %shard_map.147 = (f32[392,768]{1,0:T(8,128)S(1)}, f32[384,768]{1,0:T(8,128)S(1)}, bf16[512,768]{1,0:T(8,128)(2,1)S(1)}) custom-call(f32[32,768]{1,0:T(8,128)S(1)} %get-tuple-element.42.grad_ref.refs_0_, f32[512,768]{1,0:T(8,128)S(1)} %get-tuple-element.43.slope_hbm, bf16[1536,512]{1,0:T(8,128)(2,1)S(1)} %get-tuple-element.44.turned_hbm, ...), custom_call_target="tpu_custom_call" | custom-call | flops 603979776 | bytes 4718592 | tf_op jit(solution)/shard_map/pallas_call | solution.py:428
  44.7 3.0 %shard_map.148 = (f32[384,768]{1,0:T(8,128)S(1)}, f32[384,768]{1,0:T(8,128)S(1)}, bf16[512,768]{1,0:T(8,128)(2,1)}) custom-call(f32[32,768]{1,0:T(8,128)S(1)} %get-tuple-element.42.grad_ref.refs_0_, bf16[512,768]{1,0:T(8,128)(2,1)S(1)} %get-tuple-element.47.slope_hbm.refs_0_, bf16[1536,512]{1,0:T(8,128)(2,1)S(1)} %get-tuple-element.44.turned_hbm, ...), custom_call_target="tpu_custom_call" | custom-call | flops 603979776 | bytes 4718592 | tf_op jit(solution)/shard_map/pallas_call | solution.py:428
  47.7 0.6 collective-permute-start.12
  48.3 1.5 %collective-permute-start.14 = (f32[8,768]{1,0:T(8,128)S(1)}, f32[8,768]{1,0:T(8,128)S(1)}, u32[]{:S(2)}, u32[]{:S(2)}) collective-permute-start(f32[8,768]{1,0:T(8,128)S(1)} %slice_add_fusion.16), channel_id=1, source_target_pairs={{0,8},{2,10},{4,12},{6,14},{8,0},{10,2},{12,4},{14,6},{16,24},{18,... | collective-permute-start | bytes 73736 | tf_op jit(solution)/shard_map/ppermute | solution.py:480
  49.8 1.5 %collective-permute-start.9 = (f32[8,768]{1,0:T(8,128)S(1)}, f32[8,768]{1,0:T(8,128)S(1)}, u32[]{:S(2)}, u32[]{:S(2)}) collective-permute-start(f32[8,768]{1,0:T(8,128)S(1)} %slice_add_fusion.16), channel_id=1, source_target_pairs={{0,4},{2,6},{4,0},{6,2},{8,12},{10,14},{12,8},{14,10},{16,20},{18,... | collective-permute-start | bytes 73736 | tf_op jit(solution)/shard_map/ppermute | solution.py:480
  51.4 0.6 collective-permute-start.10
  52.0 3.1 %shard_map.149 = (f32[384,768]{1,0:T(8,128)S(1)}, f32[384,768]{1,0:T(8,128)S(1)}, bf16[1024,768]{1,0:T(8,128)(2,1)S(1)}) custom-call(f32[32,768]{1,0:T(8,128)S(1)} %get-tuple-element.42.grad_ref.refs_0_, f32[1024,768]{1,0:T(8,128)S(1)} %get-tuple-element.50.slope_hbm, bf16[1536,1024]{1,0:T(8,128)(2,1)S(1)} %get-tuple-element.51.turned_hbm, ...), custom_call_target="tpu_custom_call" | custom-call | flops 1207959552 | bytes 7077888 | tf_op jit(solution)/shard_map/pallas_call | solution.py:428
  55.3 0.7 collective-permute-start.13
  56.0 3.9 %shard_map.150 = (f32[384,768]{1,0:T(8,128)S(1)}, f32[384,768]{1,0:T(8,128)S(1)}, bf16[1024,768]{1,0:T(8,128)(2,1)}) custom-call(f32[32,768]{1,0:T(8,128)S(1)} %get-tuple-element.42.grad_ref.refs_0_, bf16[1024,768]{1,0:T(8,128)(2,1)S(1)} %get-tuple-element.54.slope_hbm, bf16[1536,1024]{1,0:T(8,128)(2,1)S(1)} %get-tuple-element.51.turned_hbm, ...), custom_call_target="tpu_custom_call" | custom-call | flops 1207959552 | bytes 7077888 | tf_op jit(solution)/shard_map/pallas_call | solution.py:428
  59.9 0.3 collective-permute-start.21
  60.2 4.5 %collective-permute-done.13 = f16[192,768]{1,0:T(8,128)(2,1)S(1)} collective-permute-done((f16[192,768]{1,0:T(8,128)(2,1)S(1)}, f16[192,768]{1,0:T(8,128)(2,1)S(1)}, u32[]{:S(2)}, u32[]{:S(2)}) %collective-permute-start.13) | collective-permute-done | bytes 294944 | tf_op jit(solution)/shard_map/ppermute | solution.py:480
  64.7 3.0 %collective-permute-start.20 = (f32[8,768]{1,0:T(8,128)S(1)}, f32[8,768]{1,0:T(8,128)S(1)}, u32[]{:S(2)}, u32[]{:S(2)}) collective-permute-start(f32[8,768]{1,0:T(8,128)S(1)} %get-tuple-element.73), channel_id=1, source_target_pairs={{0,16},{2,18},{4,20},{6,22},{8,24},{10,26},{12,28},{14,30},{16,0},... | collective-permute-start | bytes 73736 | tf_op jit(solution)/shard_map/ppermute | solution.py:480
  67.7 0.3 collective-permute-start.11
  68.3 1.8 %collective-permute-start.16 = (f16[96,768]{1,0:T(8,128)(2,1)S(1)}, f16[96,768]{1,0:T(8,128)(2,1)S(1)}, u32[]{:S(2)}, u32[]{:S(2)}) collective-permute-start(f16[96,768]{1,0:T(8,128)(2,1)S(1)} %fusion.19), channel_id=1, source_target_pairs={{0,8},{2,10},{4,12},{6,14},{8,0},{10,2},{12,4},{14,6},{16,24},{18,... | collective-permute-start | bytes 442376 | tf_op jit(solution)/shard_map/ppermute | solution.py:480
  70.2 1.7 %collective-permute-done.11 = f32[8,768]{1,0:T(8,128)S(1)} collective-permute-done((f32[8,768]{1,0:T(8,128)S(1)}, f32[8,768]{1,0:T(8,128)S(1)}, u32[]{:S(2)}, u32[]{:S(2)}) %collective-permute-start.11) | collective-permute-done | bytes 24608 | tf_op jit(solution)/shard_map/ppermute | solution.py:480
  71.9 0.7 collective-permute-start.19
  72.6 1.5 %collective-permute-start.18 = (f16[192,768]{1,0:T(8,128)(2,1)S(1)}, f16[192,768]{1,0:T(8,128)(2,1)S(1)}, u32[]{:S(2)}, u32[]{:S(2)}) collective-permute-start(f16[192,768]{1,0:T(8,128)(2,1)S(1)} %fusion.3), channel_id=1, source_target_pairs={{0,4},{2,6},{4,0},{6,2},{8,12},{10,14},{12,8},{14,10},{16,20},{18,... | collective-permute-start | bytes 884744 | tf_op jit(solution)/shard_map/ppermute | solution.py:480
  74.1 0.2 collective-permute-done.16
  74.3 2.1 %collective-permute-start.17 = (f32[8,768]{1,0:T(8,128)S(1)}, f32[8,768]{1,0:T(8,128)S(1)}, u32[]{:S(2)}, u32[]{:S(2)}) collective-permute-start(f32[8,768]{1,0:T(8,128)S(1)} %multiply_add_fusion), channel_id=1, source_target_pairs={{0,16},{2,18},{4,20},{6,22},{8,24},{10,26},{12,28},{14,30},{16,0},... | collective-permute-start | bytes 73736 | tf_op jit(solution)/shard_map/ppermute | solution.py:480
  76.6 0.6 collective-permute-start.24
  77.2 1.9 %collective-permute-start.27 = (f16[48,768]{1,0:T(8,128)(2,1)S(1)}, f16[48,768]{1,0:T(8,128)(2,1)S(1)}, u32[]{:S(2)}, u32[]{:S(2)}) collective-permute-start(f16[48,768]{1,0:T(8,128)(2,1)S(1)} %fusion.40), channel_id=1, source_target_pairs={{0,16},{2,18},{4,20},{6,22},{8,24},{10,26},{12,28},{14,30},{16,0},... | collective-permute-start | bytes 221192 | tf_op jit(solution)/shard_map/ppermute | solution.py:480
  79.1 3.3 %collective-permute-done.17 = f32[8,768]{1,0:T(8,128)S(1)} collective-permute-done((f32[8,768]{1,0:T(8,128)S(1)}, f32[8,768]{1,0:T(8,128)S(1)}, u32[]{:S(2)}, u32[]{:S(2)}) %collective-permute-start.17) | collective-permute-done | bytes 24608 | tf_op jit(solution)/shard_map/ppermute | solution.py:480
  82.4 0.5 slice.441
  83.1 2.3 %collective-permute-start.28 = (f16[48,768]{1,0:T(8,128)(2,1)S(1)}, f16[48,768]{1,0:T(8,128)(2,1)S(1)}, u32[]{:S(2)}, u32[]{:S(2)}) collective-permute-start(f16[48,768]{1,0:T(8,128)(2,1)S(1)} %fusion.44), channel_id=1, source_target_pairs={{0,4},{2,6},{4,0},{6,2},{8,12},{10,14},{12,8},{14,10},{16,20},{18,... | collective-permute-start | bytes 221192 | tf_op jit(solution)/shard_map/ppermute | solution.py:480
  85.7 7.0 %collective-permute-done.22 = f16[96,768]{1,0:T(8,128)(2,1)S(1)} collective-permute-done((f16[96,768]{1,0:T(8,128)(2,1)S(1)}, f16[96,768]{1,0:T(8,128)(2,1)S(1)}, u32[]{:S(2)}, u32[]{:S(2)}) %collective-permute-start.22) | collective-permute-done | bytes 147488 | tf_op jit(solution)/shard_map/ppermute | solution.py:480
  93.0 2.1 %collective-permute-start.23 = (f16[48,768]{1,0:T(8,128)(2,1)S(1)}, f16[48,768]{1,0:T(8,128)(2,1)S(1)}, u32[]{:S(2)}, u32[]{:S(2)}) collective-permute-start(f16[48,768]{1,0:T(8,128)(2,1)S(1)} %fusion.36), channel_id=1, source_target_pairs={{0,16},{2,18},{4,20},{6,22},{8,24},{10,26},{12,28},{14,30},{16,0},... | collective-permute-start | bytes 221192 | tf_op jit(solution)/shard_map/ppermute | solution.py:480
  95.1 4.5 %collective-permute-done.25 = f16[96,768]{1,0:T(8,128)(2,1)S(1)} collective-permute-done((f16[96,768]{1,0:T(8,128)(2,1)S(1)}, f16[96,768]{1,0:T(8,128)(2,1)S(1)}, u32[]{:S(2)}, u32[]{:S(2)}) %collective-permute-start.25) | collective-permute-done | bytes 147488 | tf_op jit(solution)/shard_map/ppermute | solution.py:480
  99.8 0.7 pad_maximum_fusion.1
  100.5 4.5 %collective-permute-done.26 = f16[48,768]{1,0:T(8,128)(2,1)S(1)} collective-permute-done((f16[48,768]{1,0:T(8,128)(2,1)S(1)}, f16[48,768]{1,0:T(8,128)(2,1)S(1)}, u32[]{:S(2)}, u32[]{:S(2)}) %collective-permute-start.26) | collective-permute-done | bytes 73760 | tf_op jit(solution)/shard_map/ppermute | solution.py:480
  105.1 0.7 pad_maximum_fusion
  (81 shorter events, 2.2 us)
Async XLA Ops:
  0.6 12.2 %copy-start.6 = (s32[16]{0:T(128)S(1)}, s32[16]{0:T(128)}, u32[]{:S(2)}) copy-start(s32[16]{0:T(128)} %constant.34.clone) | copy-start | bytes 196
  0.6 12.2 %copy-start.7 = (s32[16]{0:T(128)S(1)}, s32[16]{0:T(128)}, u32[]{:S(2)}) copy-start(s32[16]{0:T(128)} %constant.33.clone) | copy-start | bytes 196
  9.9 4.9 %collective-permute-start = (f32[32,128]{1,0:T(8,128)}, f32[32,128]{1,0:T(8,128)S(1)}, u32[]{:S(2)}, u32[]{:S(2)}) collective-permute-start(f32[32,128]{1,0:T(8,128)} %get-tuple-element.32.own_ref), channel_id=1, source_target_pairs={{0,1},{1,0},{2,3},{3,2},{4,5},{5,4},{6,7},{7,6},{8,9},{9,8},{10,11... | collective-permute-start | bytes 49160 | tf_op jit(solution)/shard_map/ppermute | solution.py:483
  14.8 0.9 copy-start.4
  15.7 0.7 copy-start.5
  16.5 13.6 %collective-permute-start.3 = (bf16[32,768]{1,0:T(8,128)(2,1)S(1)}, bf16[32,768]{1,0:T(8,128)(2,1)S(1)}, u32[]{:S(2)}, u32[]{:S(2)}) collective-permute-start(bf16[32,768]{1,0:T(8,128)(2,1)S(1)} %get-tuple-element.33._.refs_0_), channel_id=1, source_target_pairs={{0,24},{2,26},{4,28},{6,30},{8,16},{10,18},{12,20},{14,22},{16,8},... | collective-permute-start | bytes 147464 | tf_op jit(solution)/shard_map/ppermute | solution.py:480
  20.7 9.4 %collective-permute-start.2 = (bf16[32,768]{1,0:T(8,128)(2,1)S(1)}, bf16[32,768]{1,0:T(8,128)(2,1)S(1)}, u32[]{:S(2)}, u32[]{:S(2)}) collective-permute-start(bf16[32,768]{1,0:T(8,128)(2,1)S(1)} %get-tuple-element.33._.refs_0_), channel_id=1, source_target_pairs={{0,8},{2,10},{4,12},{6,14},{8,0},{10,2},{12,4},{14,6},{16,24},{18,... | collective-permute-start | bytes 147464 | tf_op jit(solution)/shard_map/ppermute | solution.py:480
  20.7 9.5 %collective-permute-start.1 = (bf16[32,768]{1,0:T(8,128)(2,1)S(1)}, bf16[32,768]{1,0:T(8,128)(2,1)S(1)}, u32[]{:S(2)}, u32[]{:S(2)}) collective-permute-start(bf16[32,768]{1,0:T(8,128)(2,1)S(1)} %get-tuple-element.33._.refs_0_), channel_id=1, source_target_pairs={{0,16},{2,18},{4,20},{6,22},{8,24},{10,26},{12,28},{14,30},{16,0},... | collective-permute-start | bytes 147464 | tf_op jit(solution)/shard_map/ppermute | solution.py:480
  21.4 1.9 %copy-start = (bf16[16,64,1536]{2,1,0:T(8,128)(2,1)S(1)}, bf16[16,64,1536]{2,1,0:T(8,128)(2,1)}, u32[]{:S(2)}) copy-start(bf16[16,64,1536]{2,1,0:T(8,128)(2,1)} %param.12) | copy-start | bytes 9437188
  23.3 1.9 %copy-start.1 = (f32[1024,768]{1,0:T(8,128)S(1)}, f32[1024,768]{1,0:T(8,128)}, u32[]{:S(2)}) copy-start(f32[1024,768]{1,0:T(8,128)} %get-tuple-element.30.pre_ref) | copy-start | bytes 9437188
  25.2 6.7 %copy-start.2 = (bf16[16,32,1536]{2,1,0:T(8,128)(2,1)S(1)}, bf16[16,32,1536]{2,1,0:T(8,128)(2,1)}, u32[]{:S(2)}) copy-start(bf16[16,32,1536]{2,1,0:T(8,128)(2,1)} %param.13) | copy-start | bytes 4718596
  25.2 6.7 %copy-start.3 = (f32[512,768]{1,0:T(8,128)S(1)}, f32[512,768]{1,0:T(8,128)}, u32[]{:S(2)}) copy-start(f32[512,768]{1,0:T(8,128)} %get-tuple-element.35.pre_ref) | copy-start | bytes 4718596
  30.2 5.7 %collective-permute-start.4 = (bf16[4,32,768]{2,1,0:T(8,128)(2,1)S(1)}, bf16[4,32,768]{2,1,0:T(8,128)(2,1)S(1)}, u32[]{:S(2)}, u32[]{:S(2)}) collective-permute-start(bf16[4,32,768]{2,1,0:T(8,128)(2,1)S(1)} %shard_map.142._.refs_0_), channel_id=1, source_target_pairs={{0,4},{2,6},{4,0},{6,2},{8,12},{10,14},{12,8},{14,10},{16,20},{18,... | collective-permute-start | bytes 589832 | tf_op jit(solution)/shard_map/ppermute | solution.py:480
  31.9 4.1 %collective-permute-start.5 = (bf16[4,32,768]{2,1,0:T(8,128)(2,1)S(1)}, bf16[4,32,768]{2,1,0:T(8,128)(2,1)S(1)}, u32[]{:S(2)}, u32[]{:S(2)}) collective-permute-start(bf16[4,32,768]{2,1,0:T(8,128)(2,1)S(1)} %shard_map.142._.refs_0_), channel_id=1, source_target_pairs={{0,2},{2,0},{4,6},{6,4},{8,10},{10,8},{12,14},{14,12},{16,18},{18,... | collective-permute-start | bytes 589832 | tf_op jit(solution)/shard_map/ppermute | solution.py:480
  36.0 1.5 %collective-permute-start.6 = (bf16[4,32,768]{2,1,0:T(8,128)(2,1)S(1)}, bf16[4,32,768]{2,1,0:T(8,128)(2,1)S(1)}, u32[]{:S(2)}, u32[]{:S(2)}) collective-permute-start(bf16[4,32,768]{2,1,0:T(8,128)(2,1)S(1)} %bitcast.9), channel_id=1, source_target_pairs={{0,2},{2,0},{4,6},{6,4},{8,10},{10,8},{12,14},{14,12},{16,18},{18,... | collective-permute-start | bytes 589832 | tf_op jit(solution)/shard_map/ppermute | solution.py:480
  37.8 3.9 %collective-permute-start.7 = (f32[32,256]{1,0:T(8,128)S(1)}, f32[32,256]{1,0:T(8,128)S(1)}, u32[]{:S(2)}, u32[]{:S(2)}) collective-permute-start(f32[32,256]{1,0:T(8,128)S(1)} %get-tuple-element.37.own_ref), channel_id=1, source_target_pairs={{0,1},{1,0},{2,3},{3,2},{4,5},{5,4},{6,7},{7,6},{8,9},{9,8},{10,11... | collective-permute-start | bytes 98312 | tf_op jit(solution)/shard_map/ppermute | solution.py:483
  44.7 3.6 %collective-permute-start.8 = (f32[392,768]{1,0:T(8,128)S(1)}, f32[392,768]{1,0:T(8,128)S(1)}, u32[]{:S(2)}, u32[]{:S(2)}) collective-permute-start(f32[392,768]{1,0:T(8,128)S(1)} %get-tuple-element.45), channel_id=1, source_target_pairs={{0,2},{2,0},{4,6},{6,4},{8,10},{10,8},{12,14},{14,12},{16,18},{18,... | collective-permute-start | bytes 3612680 | tf_op jit(solution)/shard_map/ppermute | solution.py:480
  47.7 7.4 %collective-permute-start.12 = (f32[384,768]{1,0:T(8,128)S(1)}, f32[384,768]{1,0:T(8,128)S(1)}, u32[]{:S(2)}, u32[]{:S(2)}) collective-permute-start(f32[384,768]{1,0:T(8,128)S(1)} %get-tuple-element.49), channel_id=1, source_target_pairs={{0,2},{2,0},{4,6},{6,4},{8,10},{10,8},{12,14},{14,12},{16,18},{18,... | collective-permute-start | bytes 3538952 | tf_op jit(solution)/shard_map/ppermute | solution.py:480
  48.3 11.6 %collective-permute-start.14 = (f32[8,768]{1,0:T(8,128)S(1)}, f32[8,768]{1,0:T(8,128)S(1)}, u32[]{:S(2)}, u32[]{:S(2)}) collective-permute-start(f32[8,768]{1,0:T(8,128)S(1)} %slice_add_fusion.16), channel_id=1, source_target_pairs={{0,8},{2,10},{4,12},{6,14},{8,0},{10,2},{12,4},{14,6},{16,24},{18,... | collective-permute-start | bytes 73736 | tf_op jit(solution)/shard_map/ppermute | solution.py:480
  49.8 10.4 %collective-permute-start.9 = (f32[8,768]{1,0:T(8,128)S(1)}, f32[8,768]{1,0:T(8,128)S(1)}, u32[]{:S(2)}, u32[]{:S(2)}) collective-permute-start(f32[8,768]{1,0:T(8,128)S(1)} %slice_add_fusion.16), channel_id=1, source_target_pairs={{0,4},{2,6},{4,0},{6,2},{8,12},{10,14},{12,8},{14,10},{16,20},{18,... | collective-permute-start | bytes 73736 | tf_op jit(solution)/shard_map/ppermute | solution.py:480
  51.4 8.8 %collective-permute-start.10 = (f16[192,768]{1,0:T(8,128)(2,1)S(1)}, f16[192,768]{1,0:T(8,128)(2,1)S(1)}, u32[]{:S(2)}, u32[]{:S(2)}) collective-permute-start(f16[192,768]{1,0:T(8,128)(2,1)S(1)} %fusion.7), channel_id=1, source_target_pairs={{0,4},{2,6},{4,0},{6,2},{8,12},{10,14},{12,8},{14,10},{16,20},{18,... | collective-permute-start | bytes 884744 | tf_op jit(solution)/shard_map/ppermute | solution.py:480
  55.1 13.0 %collective-permute-start.15 = (f32[384,768]{1,0:T(8,128)S(1)}, f32[384,768]{1,0:T(8,128)S(1)}, u32[]{:S(2)}, u32[]{:S(2)}) collective-permute-start(f32[384,768]{1,0:T(8,128)S(1)} %get-tuple-element.53), channel_id=1, source_target_pairs={{0,2},{2,0},{4,6},{6,4},{8,10},{10,8},{12,14},{14,12},{16,18},{18,... | collective-permute-start | bytes 3538952 | tf_op jit(solution)/shard_map/ppermute | solution.py:480
  55.3 9.5 %collective-permute-start.13 = (f16[192,768]{1,0:T(8,128)(2,1)S(1)}, f16[192,768]{1,0:T(8,128)(2,1)S(1)}, u32[]{:S(2)}, u32[]{:S(2)}) collective-permute-start(f16[192,768]{1,0:T(8,128)(2,1)S(1)} %fusion.5), channel_id=1, source_target_pairs={{0,8},{2,10},{4,12},{6,14},{8,0},{10,2},{12,4},{14,6},{16,24},{18,... | collective-permute-start | bytes 884744 | tf_op jit(solution)/shard_map/ppermute | solution.py:480
  59.9 16.6 %collective-permute-start.21 = (f32[384,768]{1,0:T(8,128)S(1)}, f32[384,768]{1,0:T(8,128)S(1)}, u32[]{:S(2)}, u32[]{:S(2)}) collective-permute-start(f32[384,768]{1,0:T(8,128)S(1)} %get-tuple-element.56), channel_id=1, source_target_pairs={{0,2},{2,0},{4,6},{6,4},{8,10},{10,8},{12,14},{14,12},{16,18},{18,... | collective-permute-start | bytes 3538952 | tf_op jit(solution)/shard_map/ppermute | solution.py:480
  64.7 5.4 %collective-permute-start.20 = (f32[8,768]{1,0:T(8,128)S(1)}, f32[8,768]{1,0:T(8,128)S(1)}, u32[]{:S(2)}, u32[]{:S(2)}) collective-permute-start(f32[8,768]{1,0:T(8,128)S(1)} %get-tuple-element.73), channel_id=1, source_target_pairs={{0,16},{2,18},{4,20},{6,22},{8,24},{10,26},{12,28},{14,30},{16,0},... | collective-permute-start | bytes 73736 | tf_op jit(solution)/shard_map/ppermute | solution.py:480
  67.7 4.1 %collective-permute-start.11 = (f32[8,768]{1,0:T(8,128)S(1)}, f32[8,768]{1,0:T(8,128)S(1)}, u32[]{:S(2)}, u32[]{:S(2)}) collective-permute-start(f32[8,768]{1,0:T(8,128)S(1)} %get-tuple-element.74), channel_id=1, source_target_pairs={{0,8},{2,10},{4,12},{6,14},{8,0},{10,2},{12,4},{14,6},{16,24},{18,... | collective-permute-start | bytes 73736 | tf_op jit(solution)/shard_map/ppermute | solution.py:480
  68.3 6.0 %collective-permute-start.16 = (f16[96,768]{1,0:T(8,128)(2,1)S(1)}, f16[96,768]{1,0:T(8,128)(2,1)S(1)}, u32[]{:S(2)}, u32[]{:S(2)}) collective-permute-start(f16[96,768]{1,0:T(8,128)(2,1)S(1)} %fusion.19), channel_id=1, source_target_pairs={{0,8},{2,10},{4,12},{6,14},{8,0},{10,2},{12,4},{14,6},{16,24},{18,... | collective-permute-start | bytes 442376 | tf_op jit(solution)/shard_map/ppermute | solution.py:480
  71.9 11.1 %collective-permute-start.19 = (f16[96,768]{1,0:T(8,128)(2,1)S(1)}, f16[96,768]{1,0:T(8,128)(2,1)S(1)}, u32[]{:S(2)}, u32[]{:S(2)}) collective-permute-start(f16[96,768]{1,0:T(8,128)(2,1)S(1)} %fusion.16), channel_id=1, source_target_pairs={{0,16},{2,18},{4,20},{6,22},{8,24},{10,26},{12,28},{14,30},{16,0},... | collective-permute-start | bytes 442376 | tf_op jit(solution)/shard_map/ppermute | solution.py:480
  72.6 12.9 %collective-permute-start.18 = (f16[192,768]{1,0:T(8,128)(2,1)S(1)}, f16[192,768]{1,0:T(8,128)(2,1)S(1)}, u32[]{:S(2)}, u32[]{:S(2)}) collective-permute-start(f16[192,768]{1,0:T(8,128)(2,1)S(1)} %fusion.3), channel_id=1, source_target_pairs={{0,4},{2,6},{4,0},{6,2},{8,12},{10,14},{12,8},{14,10},{16,20},{18,... | collective-permute-start | bytes 884744 | tf_op jit(solution)/shard_map/ppermute | solution.py:480
  74.3 8.1 %collective-permute-start.17 = (f32[8,768]{1,0:T(8,128)S(1)}, f32[8,768]{1,0:T(8,128)S(1)}, u32[]{:S(2)}, u32[]{:S(2)}) collective-permute-start(f32[8,768]{1,0:T(8,128)S(1)} %multiply_add_fusion), channel_id=1, source_target_pairs={{0,16},{2,18},{4,20},{6,22},{8,24},{10,26},{12,28},{14,30},{16,0},... | collective-permute-start | bytes 73736 | tf_op jit(solution)/shard_map/ppermute | solution.py:480
  76.6 16.2 %collective-permute-start.24 = (f16[192,768]{1,0:T(8,128)(2,1)S(1)}, f16[192,768]{1,0:T(8,128)(2,1)S(1)}, u32[]{:S(2)}, u32[]{:S(2)}) collective-permute-start(f16[192,768]{1,0:T(8,128)(2,1)S(1)} %fusion.1), channel_id=1, source_target_pairs={{0,4},{2,6},{4,0},{6,2},{8,12},{10,14},{12,8},{14,10},{16,20},{18,... | collective-permute-start | bytes 884744 | tf_op jit(solution)/shard_map/ppermute | solution.py:480
  77.2 8.2 %collective-permute-start.27 = (f16[48,768]{1,0:T(8,128)(2,1)S(1)}, f16[48,768]{1,0:T(8,128)(2,1)S(1)}, u32[]{:S(2)}, u32[]{:S(2)}) collective-permute-start(f16[48,768]{1,0:T(8,128)(2,1)S(1)} %fusion.40), channel_id=1, source_target_pairs={{0,16},{2,18},{4,20},{6,22},{8,24},{10,26},{12,28},{14,30},{16,0},... | collective-permute-start | bytes 221192 | tf_op jit(solution)/shard_map/ppermute | solution.py:480
  83.1 9.9 %collective-permute-start.28 = (f16[48,768]{1,0:T(8,128)(2,1)S(1)}, f16[48,768]{1,0:T(8,128)(2,1)S(1)}, u32[]{:S(2)}, u32[]{:S(2)}) collective-permute-start(f16[48,768]{1,0:T(8,128)(2,1)S(1)} %fusion.44), channel_id=1, source_target_pairs={{0,4},{2,6},{4,0},{6,2},{8,12},{10,14},{12,8},{14,10},{16,20},{18,... | collective-permute-start | bytes 221192 | tf_op jit(solution)/shard_map/ppermute | solution.py:480
  85.6 7.1 %collective-permute-start.22 = (f16[96,768]{1,0:T(8,128)(2,1)S(1)}, f16[96,768]{1,0:T(8,128)(2,1)S(1)}, u32[]{:S(2)}, u32[]{:S(2)}) collective-permute-start(f16[96,768]{1,0:T(8,128)(2,1)S(1)} %fusion.13), channel_id=1, source_target_pairs={{0,8},{2,10},{4,12},{6,14},{8,0},{10,2},{12,4},{14,6},{16,24},{18,... | collective-permute-start | bytes 442376 | tf_op jit(solution)/shard_map/ppermute | solution.py:480
  92.9 6.8 %collective-permute-start.25 = (f16[96,768]{1,0:T(8,128)(2,1)S(1)}, f16[96,768]{1,0:T(8,128)(2,1)S(1)}, u32[]{:S(2)}, u32[]{:S(2)}) collective-permute-start(f16[96,768]{1,0:T(8,128)(2,1)S(1)} %fusion.10), channel_id=1, source_target_pairs={{0,8},{2,10},{4,12},{6,14},{8,0},{10,2},{12,4},{14,6},{16,24},{18,... | collective-permute-start | bytes 442376 | tf_op jit(solution)/shard_map/ppermute | solution.py:480
  93.0 7.5 %collective-permute-start.23 = (f16[48,768]{1,0:T(8,128)(2,1)S(1)}, f16[48,768]{1,0:T(8,128)(2,1)S(1)}, u32[]{:S(2)}, u32[]{:S(2)}) collective-permute-start(f16[48,768]{1,0:T(8,128)(2,1)S(1)} %fusion.36), channel_id=1, source_target_pairs={{0,16},{2,18},{4,20},{6,22},{8,24},{10,26},{12,28},{14,30},{16,0},... | collective-permute-start | bytes 221192 | tf_op jit(solution)/shard_map/ppermute | solution.py:480
  99.7 5.3 %collective-permute-start.26 = (f16[48,768]{1,0:T(8,128)(2,1)S(1)}, f16[48,768]{1,0:T(8,128)(2,1)S(1)}, u32[]{:S(2)}, u32[]{:S(2)}) collective-permute-start(f16[48,768]{1,0:T(8,128)(2,1)S(1)} %fusion.29), channel_id=1, source_target_pairs={{0,16},{2,18},{4,20},{6,22},{8,24},{10,26},{12,28},{14,30},{16,0},... | collective-permute-start | bytes 221192 | tf_op jit(solution)/shard_map/ppermute | solution.py:480

commit v3 on v2

v3 whole, which is shorter than its diff:
```python
import functools

import jax
import jax.numpy as jnp
from jax import lax
from jax.experimental import pallas as pl
from jax.experimental.pallas import tpu as pltpu
from jax.sharding import PartitionSpec as P

F32 = jnp.float32
BF16 = jnp.bfloat16
ROWS = 256
JOB_ROWS = 512
JOB_COLUMNS = 256
STRIP = 64
ROOT = 0.7978845608028654
HALF_MAX = 16384.0
UNUSABLE = 2.0


def vmem():
    return pl.BlockSpec(memory_space=pltpu.VMEM)


def smem():
    return pl.BlockSpec(memory_space=pltpu.SMEM)


def anyplace():
    return pl.BlockSpec(memory_space=pl.ANY)


def hbm():
    return pl.BlockSpec(memory_space=pltpu.HBM)


def params(mib):
    return pltpu.CompilerParams(vmem_limit_bytes=mib * 2**20)


def gelu_and_slope(x):
    square = x * x
    cdf = 0.5 + 0.5 * jnp.tanh(x * (ROOT + (0.044715 * ROOT) * square))
    value = x * cdf
    rise = (value - value * cdf) * (2 * ROOT + (6 * 0.044715 * ROOT) * square)
    return value, cdf + rise


def forward_kernel(
    tokens_of,
    place_ref,
    image_hbm,
    text_hbm,
    image_w_hbm,
    text_w_hbm,
    pooled_ref,
    square_ref,
    image_slope_hbm,
    text_slope_hbm,
    image_v,
    text_v,
    image_w,
    text_w,
    image_slope,
    text_slope,
    in_sem,
    w_sem,
    out_sem,
):
    width = image_w.shape[1]
    samples = pooled_ref.shape[0] // 2
    towers_here = (
        (text_hbm, text_v, text_w_hbm, text_w, text_slope, text_slope_hbm, tokens_of[1], samples),
        (image_hbm, image_v, image_w_hbm, image_w, image_slope, image_slope_hbm, tokens_of[0], 0),
    )
    waits, tiles = [], []
    for t, (source, buf, w_source, w, _, _, _, _) in enumerate(towers_here):
        here = [
            pltpu.make_async_copy(w_source, w, w_sem.at[t]),
            pltpu.make_async_copy(source, buf, in_sem.at[t]),
        ]
        for copy in here:
            copy.start()
        waits.append(here)
        for start in range(0, buf.shape[0], JOB_ROWS):
            for column in range(0, width, JOB_COLUMNS):
                tiles.append((t, start, column))
    first = place_ref[0] * width

    def project(n):
        t, start, column = tiles[n]
        _, buf, _, w, slope, _, _, _ = towers_here[t]
        if start == 0 and column == 0:
            for copy in waits[t]:
                copy.wait()
        rows, columns = slice(start, start + JOB_ROWS), slice(column, column + JOB_COLUMNS)
        slope[rows, columns] = jnp.dot(buf[rows, :], w[:, columns], preferred_element_type=F32)

    out_copies = []
    project(0)
    for n, (t, start, tile_column) in enumerate(tiles):
        _, buf, _, _, slope, slope_out, tok, base = towers_here[t]
        if n + 1 < len(tiles):
            project(n + 1)
        for row in range(start, start + JOB_ROWS, STRIP):
            rows = slice(row, row + STRIP)
            here = (rows, slice(tile_column, tile_column + JOB_COLUMNS))
            token_columns = pl.ds(pl.multiple_of(first + tile_column, 128), JOB_COLUMNS)
            value, slant = gelu_and_slope(slope[here])
            slope[here] = slant
            hidden = buf[rows, token_columns].astype(F32) + value
            for part in range(0, STRIP, tok):
                sample = base + (row + part) // tok
                pooled_ref[sample : sample + 1, here[1]] = (
                    jnp.sum(hidden[part : part + tok], axis=0, keepdims=True) / tok
                )
        if tile_column + JOB_COLUMNS == width:
            part = pl.ds(start, JOB_ROWS)
            copy = pltpu.make_async_copy(
                slope.at[part, :], slope_out.at[part, :], out_sem.at[len(out_copies)]
            )
            copy.start()
            out_copies.append(copy)
    pooled = pooled_ref[...]
    total = jnp.sum(pooled * pooled, axis=1, keepdims=True)
    square_ref[...] = jnp.broadcast_to(total, square_ref.shape)
    for copy in out_copies:
        copy.wait()


def forward(place, image_flat, text_flat, image_w, text_w, samples):
    width = image_w.shape[1]
    depth = image_w.shape[0]
    rows_i, rows_t = image_flat.shape[0], text_flat.shape[0]
    jobs = (rows_i + rows_t) // JOB_ROWS
    return pl.pallas_call(
        functools.partial(forward_kernel, (rows_i // samples, rows_t // samples)),
        out_shape=(
            jax.ShapeDtypeStruct((2 * samples, width), F32),
            jax.ShapeDtypeStruct((2 * samples, 128), F32),
            jax.ShapeDtypeStruct((rows_i, width), F32),
            jax.ShapeDtypeStruct((rows_t, width), F32),
        ),
        in_specs=[smem()] + [hbm()] * 4,
        out_specs=(vmem(), vmem(), hbm(), hbm()),
        scratch_shapes=[
            pltpu.VMEM((rows_i, depth), BF16),
            pltpu.VMEM((rows_t, depth), BF16),
            pltpu.VMEM((depth, width), BF16),
            pltpu.VMEM((depth, width), BF16),
            pltpu.VMEM((rows_i, width), F32),
            pltpu.VMEM((rows_t, width), F32),
            pltpu.SemaphoreType.DMA((2,)),
            pltpu.SemaphoreType.DMA((2,)),
            pltpu.SemaphoreType.DMA((jobs,)),
        ],
        compiler_params=params(53),
        cost_estimate=pl.CostEstimate(
            flops=2 * (rows_i + rows_t) * depth * width,
            bytes_accessed=2 * (rows_i + rows_t) * (depth + 2 * width) + 4 * depth * width,
            transcendentals=(rows_i + rows_t) * width,
        ),
    )(place, image_flat, text_flat, image_w, text_w)


def unit_kernel(count_ref, pooled_ref, own_ref, other_ref, unit_ref, sent_ref, norm_ref):
    both = pooled_ref.shape[0]
    norm = jnp.sqrt(own_ref[...] + other_ref[...] + 1e-06)
    norm_ref[...] = norm
    unit = pooled_ref[...] / norm[:, :1]
    unit_ref[...] = unit
    row = lax.broadcasted_iota(jnp.int32, unit.shape, 0) % (both // 2)
    sent_ref[...] = jnp.where(row < count_ref[0], unit, UNUSABLE).astype(BF16)


def units(count, pooled, own, other):
    return pl.pallas_call(
        unit_kernel,
        out_shape=(
            jax.ShapeDtypeStruct(pooled.shape, F32),
            jax.ShapeDtypeStruct(pooled.shape, BF16),
            jax.ShapeDtypeStruct(own.shape, F32),
        ),
        in_specs=[smem()] + [pl.BlockSpec()] * 3,
        out_specs=(vmem(),) * 3,
        compiler_params=params(4),
    )(count, pooled, own, other)


def stack_kernel(afters, *refs):
    parts, out_ref = refs[afters:-1], refs[-1]
    for n, part in enumerate(parts):
        out_ref[n] = part[...]


def stack(parts, *afters):
    return pl.pallas_call(
        functools.partial(stack_kernel, len(afters)),
        out_shape=jax.ShapeDtypeStruct((len(parts), *parts[0].shape), parts[0].dtype),
        in_specs=[anyplace()] * len(afters) + [vmem()] * len(parts),
        out_specs=vmem(),
        compiler_params=params(4),
    )(*afters, *parts)


def turn_kernel(source_ref, tokens_ref, _, turned_ref, most_ref, turned):
    rows, _ = tokens_ref.shape
    blocks = source_ref.shape[0]
    height = turned_ref.shape[0] // blocks
    largest = None
    for start in range(0, rows, ROWS):
        tokens = tokens_ref[start : start + ROWS, :]
        turned[...] = tokens.T
        most = jnp.max(jnp.abs(tokens).astype(F32), axis=0, keepdims=True)
        largest = most if largest is None else jnp.maximum(largest, most)
        for q in range(blocks):
            source = pl.multiple_of(source_ref[q] * height, height)
            turned_ref[q * height : (q + 1) * height, start : start + ROWS] = turned[
                pl.ds(source, height), :
            ]
    most_ref[...] = jnp.broadcast_to(jnp.max(largest, axis=1, keepdims=True), most_ref.shape)


def turn(sources, flat, after):
    rows, depth = flat.shape
    blocks = sources.shape[0]
    odd = (depth // blocks) % 16
    picked = jnp.arange(16, dtype=jnp.int32) if odd else sources
    turned, most = pl.pallas_call(
        turn_kernel,
        out_shape=(
            jax.ShapeDtypeStruct((depth, rows), flat.dtype),
            jax.ShapeDtypeStruct((8, 128), F32),
        ),
        in_specs=[smem(), vmem(), anyplace()],
        out_specs=(vmem(), vmem()),
        scratch_shapes=[pltpu.VMEM((depth, ROWS), flat.dtype)],
        compiler_params=params(8),
        cost_estimate=pl.CostEstimate(
            flops=0, bytes_accessed=4 * rows * depth, transcendentals=0
        ),
    )(picked, flat, after)
    if odd:
        turned = turned.reshape(blocks, depth // blocks, rows)[sources].reshape(depth, rows)
    return turned, most


def row_products(left, right):
    return lax.dot_general(left, right, (((1,), (1,)), ((), ())), preferred_element_type=F32)


def towers(blocks_ref, samples):
    blocks, _, width = blocks_ref.shape
    image = blocks_ref[:, :samples, :].reshape(blocks * samples, width)
    text = blocks_ref[:, samples:, :].reshape(blocks * samples, width)
    return image, text


def product_kernel(image_most_ref, text_most_ref, *refs):
    *block_refs, out_ref, mark_ref = refs
    near_ref = block_refs[0]
    samples = near_ref.shape[1] // 2
    own_image = near_ref[0, :samples, :]
    own_text = near_ref[0, samples:, :]
    lane = lax.broadcasted_iota(jnp.int32, own_image.shape, 1)
    first = jnp.where(lane == 0, 1.0, 0.0).astype(BF16)
    start = 0
    for ref in block_refs:
        image, text = towers(ref, samples)
        stop = start + image.shape[0]
        found = row_products(jnp.concatenate([own_image, first], axis=0), text)
        out_ref[:samples, start:stop] = found[:samples]
        mark_ref[:, start:stop] = found[samples : samples + 8]
        out_ref[samples:, start:stop] = row_products(own_text, image)
        start = stop


def products(blocks, mosts):
    both = blocks[0].shape[1]
    columns = sum(b.shape[0] for b in blocks) * (both // 2)
    return pl.pallas_call(
        product_kernel,
        out_shape=(
            jax.ShapeDtypeStruct((both, columns), F32),
            jax.ShapeDtypeStruct((8, columns), F32),
        ),
        in_specs=[anyplace()] * 2 + [vmem()] * len(blocks),
        out_specs=(vmem(),) * 2,
        compiler_params=params(8),
    )(*mosts, *blocks)


def middle_kernel(
    tokens_of,
    scale_ref,
    bias_ref,
    gain_ref,
    count_ref,
    own_ref,
    other_ref,
    mark_ref,
    unit_ref,
    norm_ref,
    image_most_ref,
    text_most_ref,
    *refs,
):
    *block_refs, grad_ref, stat_ref = refs
    samples = unit_ref.shape[0] // 2
    scale, bias = scale_ref[0], bias_ref[0]
    dots = own_ref[...] + other_ref[...]
    logits = scale * dots + bias
    row = lax.broadcasted_iota(jnp.int32, dots.shape, 0) % samples
    column = lax.broadcasted_iota(jnp.int32, dots.shape, 1)
    sign = jnp.where(row == column, 1.0, -1.0).astype(F32)
    usable = jnp.where(mark_ref[:1, :] < 1.5, 1.0, 0.0)
    total = jnp.sum(usable, axis=1, keepdims=True)
    used = (usable > 0.5) & (row < count_ref[0])
    margin = -sign * logits
    small = jnp.exp(-jnp.abs(margin))
    soft = jnp.maximum(margin, 0.0) + jnp.log1p(small)
    sigmoid = jnp.where(margin >= 0, 1.0, small) / (1.0 + small)
    part = jnp.where(used, soft, 0.0)[:samples, :]
    loss = jnp.sum(jnp.sum(part, axis=1, keepdims=True), axis=0, keepdims=True) / total
    coeff = gain_ref[0] / total
    dlogit = (jnp.where(used, -sign * sigmoid, 0.0) * coeff).astype(BF16)
    radial = scale * jnp.sum(dlogit.astype(F32) * dots, axis=1, keepdims=True)
    raws = [jnp.zeros((samples, unit_ref.shape[1]), F32) for _ in range(2)]
    start = 0
    for ref in block_refs:
        image, text = towers(ref, samples)
        stop = start + image.shape[0]
        raws[0] += jnp.dot(dlogit[:samples, start:stop], text, preferred_element_type=F32)
        raws[1] += jnp.dot(dlogit[samples:, start:stop], image, preferred_element_type=F32)
        start = stop
    limits = []
    for n, most_ref in enumerate((image_most_ref, text_most_ref)):
        here = slice(n * samples, (n + 1) * samples)
        inward = unit_ref[here, :] * radial[here, :]
        grad = (scale * raws[n] - inward) / norm_ref[here, :1] / tokens_of[n]
        grad_ref[here, :] = grad
        steep = jnp.max(jnp.max(jnp.abs(grad), axis=1, keepdims=True), axis=0, keepdims=True)
        limits.append(1.2 * samples * tokens_of[n] * most_ref[:1, :1] * steep)
    line = lax.broadcasted_iota(jnp.int32, stat_ref.shape, 0)
    stat_ref[...] = jnp.where(line == 0, loss, jnp.where(line == 1, limits[0], limits[1]))


def middle(tokens_of, scale, bias, gain, count, own, other, mark, unit, norm, mosts, blocks):
    return pl.pallas_call(
        functools.partial(middle_kernel, tokens_of),
        out_shape=(
            jax.ShapeDtypeStruct(unit.shape, F32),
            jax.ShapeDtypeStruct((8, unit.shape[1]), F32),
        ),
        in_specs=[smem()] * 4 + [vmem()] * (7 + len(blocks)),
        out_specs=(vmem(), vmem()),
        compiler_params=params(12),
    )(scale, bias, gain, count, own, other, mark, unit, norm, *mosts, *blocks)


def weight_kernel(
    base, carries, grad_ref, slope_ref, turned_ref, stat_ref, _, soon_ref, late_ref, keep_ref, preact_grad
):
    rows, width = slope_ref.shape
    samples = grad_ref.shape[0] // 2
    tok = rows // samples
    for sample in range(samples):
        here = slice(sample * tok, (sample + 1) * tok)
        row = base * samples + sample
        for column in range(0, width, 128):
            columns = slice(column, column + 128)
            slope = slope_ref[here, columns]
            preact_grad[here, columns] = (grad_ref[row : row + 1, columns] * slope).astype(BF16)
    height = late_ref.shape[0]
    if carries:
        soon_ref[height:, :] = stat_ref[...]
    for n, (out, start) in enumerate(
        ((soon_ref, 0), (late_ref, 0), (keep_ref, 0), (keep_ref, height))
    ):
        out[start : start + height, :] = jnp.dot(
            turned_ref[n * height : (n + 1) * height, :],
            preact_grad[...],
            preferred_element_type=F32,
        )


def weight_terms(grad, slope, turned, stat, base, carries, after):
    depth, rows = turned.shape
    width = slope.shape[1]
    quarter = depth // 4
    soon = quarter + (stat.shape[0] if carries else 0)
    return pl.pallas_call(
        functools.partial(weight_kernel, base, carries),
        out_shape=tuple(jax.ShapeDtypeStruct((n, width), F32) for n in (soon, quarter, 2 * quarter)),
        in_specs=[vmem()] * 4 + [anyplace()],
        out_specs=(vmem(),) * 3,
        scratch_shapes=[pltpu.VMEM((rows, width), BF16)],
        compiler_params=params(8),
        cost_estimate=pl.CostEstimate(
            flops=2 * depth * rows * width,
            bytes_accessed=2 * depth * rows + 4 * rows * width + 4 * depth * width,
            transcendentals=0,
        ),
    )(grad, slope, turned, stat, after)


def sum_of(terms):
    total = None
    for term, unit in terms:
        value = term if unit is None else term.astype(F32) * unit
        total = value if total is None else total + value
    return total


def body(
    image_tokens,
    text_tokens,
    image_weight,
    text_weight,
    logit_scale,
    logit_bias,
    loss_scale,
    valid_count,
):
    samples, image_tok, depth = image_tokens.shape
    text_tok = text_tokens.shape[1]
    width = image_weight.shape[1]
    cycle = lax.axis_size("dp")
    bits = cycle.bit_length() - 1
    place = lax.axis_index("dp")

    def swap(array, mask):
        return lax.ppermute(array, "dp", [(i, i ^ mask) for i in range(cycle)])

    def swap_halves(array):
        return lax.ppermute(array, "mp", [(0, 1), (1, 0)])

    def bits_of(value, order):
        return sum(((value >> (len(order) - 1 - i)) & 1) << b for i, b in enumerate(order))

    image_flat = image_tokens.reshape(-1, depth)
    text_flat = text_tokens.reshape(-1, depth)
    text_orders = [list(range(2, bits)), list(range(3, bits)) + [2]]
    image_order = [2, 1] + list(range(3, bits))
    later = [(c, q) for c in range(2) for q in range(cycle // 4)]
    text_blocks = [
        2 * (high + bits_of(q, text_orders[c])) + c for high in (3, 1, 0, 2) for c, q in later
    ]
    image_blocks = [
        high + bits_of(q, image_order[1:])
        for high in (5, 1, 0, 4)
        for q in range(cycle // 4)
    ]
    text_blocks = jnp.asarray(text_blocks, jnp.int32) ^ (2 * place)
    image_blocks = jnp.asarray(image_blocks, jnp.int32) ^ place

    model_place = lax.axis_index("mp").astype(jnp.int32).reshape(1)
    pooled, square, image_slope, text_slope = forward(
        model_place, image_flat, text_flat, image_weight, text_weight, samples
    )
    unit, sent, norm = units(valid_count, pooled, square, swap_halves(square))

    low = max(bits - 2, 1)
    tops = [1 << b for b in reversed(range(low, bits))]
    masks = tops + [tops[0] | tops[1]] if len(tops) == 2 else tops
    arrived = [swap(sent, mask) for mask in masks]
    image_turned, image_most = turn(image_blocks, image_flat, sent)
    gathered = stack([sent] + arrived, image_most)
    text_turned, text_most = turn(text_blocks, text_flat, gathered)
    blocks = [gathered]
    for b in reversed(range(1, low)):
        blocks = blocks + [swap(block, 1 << b) for block in blocks]
    far = [swap(block, 1) for block in blocks[:1]]
    for block in blocks[1:]:
        far.append(swap(stack([block], text_most)[0], 1))
    blocks = blocks + far

    own_dots, mark = products(blocks, (image_most, text_most))
    grad, stat = middle(
        (image_tok, text_tok),
        logit_scale,
        logit_bias,
        loss_scale,
        valid_count,
        own_dots,
        swap_halves(own_dots),
        mark,
        unit,
        norm,
        (image_most, text_most),
        blocks,
    )

    lines = lax.broadcasted_iota(jnp.int32, (16, width), 0)

    def footer(exponents, stat):
        rows = list(exponents)
        rest = stat[:1]
        for _ in range(3):
            part = lax.reduce_precision(rest, 5, 10)
            rows.append(part)
            rest = (rest - part) * 2048.0
        found = jnp.zeros((16, width), F32)
        for n, row in enumerate(rows):
            found = jnp.where(lines == n, row, found)
        return found

    def exponents_of(stat):
        return [jnp.ceil(jnp.log2(jnp.maximum(stat[n : n + 1], 1e-30))) for n in (1, 2)]

    def merged(stat, message):
        foot = message[-16:].astype(F32)
        loss = (foot[4:5] / 2048.0 + foot[3:4]) / 2048.0 + foot[2:3]
        there = [foot[:1], foot[1:2]]
        add = [loss, jnp.exp2(there[0]), jnp.exp2(there[1])]
        total = [stat[n : n + 1] + row for n, row in enumerate(add)]
        return jnp.concatenate(total), there

    def halves(terms):
        half = terms[0][0].shape[0] // 2
        return [[(term[rows], unit) for term, unit in terms] for rows in (slice(half), slice(half, None))]

    def leave(terms, stat, tower, bit, after):
        rows = terms[0][0].shape[0]
        exponents = exponents_of(stat)
        factor = HALF_MAX * jnp.exp2(-exponents[tower]) + 0.0 * after[:1].astype(F32)
        coded = sum_of(terms) * factor
        foot = footer(exponents, stat) + 0.0 * coded[:1]
        coded = jnp.pad(coded, ((0, 16), (0, 0))) + jnp.pad(foot, ((rows, 0), (0, 0)))
        coded = coded.astype(jnp.float16)
        return coded, swap(coded, 1 << bit)

    def take(terms, stat, tower, coming):
        stat, there = merged(stat, coming)
        return terms + [(coming[:-16], jnp.exp2(there[tower]) / HALF_MAX)], stat

    def core_step(soon, late, keep):
        height = late.shape[0]
        there = swap(soon, 1)
        stays = [(keep[:height], None), (swap(late, 1), None)]
        return stays, [(keep[height:], None), (there[:height], None)], there[height:]

    text_terms = weight_terms(grad, text_slope, text_turned, stat, 1, True, stat)
    text, text_leaves, stat_there = core_step(*text_terms)
    start_stat = stat[:3] + stat_there[:3]
    image_terms = weight_terms(grad, image_slope, image_turned, stat, 0, False, text_terms[0])
    image, image_leaves, _ = core_step(*image_terms)

    coded, text_in = leave(text_leaves, start_stat, 1, 1, start_stat)
    coded, image_in = leave(image_leaves, start_stat, 0, image_order[0], coded)
    text, text_stat = take(text, start_stat, 1, text_in)
    parts = [(terms, text_stat) for terms in halves(text)]
    image, image_stat = take(image, start_stat, 0, image_in)
    for step in range(bits - 2):
        last = step == bits - 3
        image, image_leaves = halves(image)
        if last:
            coded, image_in = leave(image_leaves, image_stat, 0, image_order[step + 1], coded)
        arrivals = []
        for order, (terms, terms_stat) in zip(text_orders, parts):
            terms, leaves = halves(terms)
            coded, arrival = leave(leaves, terms_stat, 1, order[step], coded)
            arrivals.append((terms, terms_stat, arrival))
        if not last:
            coded, image_in = leave(image_leaves, image_stat, 0, image_order[step + 1], coded)
        parts = [take(terms, old, 1, arrival) for terms, old, arrival in arrivals]
        image, image_stat = take(image, image_stat, 0, image_in)
    text = jnp.concatenate([sum_of(terms) for terms, _ in parts])
    loss = jnp.max(parts[0][1][0] + 0.0 * coded[0].astype(F32))
    return (loss, sum_of(image), text)


def solution(mesh):
    placed = (
        P("dp", None, None),
        P("dp", None, None),
        P(None, "mp"),
        P(None, "mp"),
        P(),
        P(),
        P(),
        P("dp"),
    )
    return jax.shard_map(
        body,
        mesh=mesh,
        in_specs=placed,
        out_specs=(P(), P("dp", "mp"), P("dp", "mp")),
        check_vma=False,
    )
```

time: 106 us -> 87.4 us (0.82)
  Pallas kernels: 30.1 us -> 18.7 us
  starting transfers between devices: 33.1 us -> 23.4 us
  waiting for transfers between devices: 30.1 us -> 36.1 us
  local copies, waits for them, and re-layouts: 5.92 us -> 0.31 us
  other arithmetic: 3.02 us -> 5 us
    pallas_call x8 -> x6, Pallas kernels: 19.9 us -> 8.27 us  [the longest x2 4.17 us: weight_terms(): pl.pallas_call(functools.partial(weight_kernel, base, carries), out_shape...]
    ppermute x27 -> x18, starting transfers between devices: 28.4 us -> 18.9 us  [swap(): return lax.ppermute(array, 'dp', [(i, i ^ mask) for i in range(cycle)])]
    ppermute x27 -> x18, waiting for transfers between devices: 28.5 us -> 34.6 us  [swap(): return lax.ppermute(array, 'dp', [(i, i ^ mask) for i in range(cycle)])]
    unnamed x16 -> x12, local copies, waits for them, and re-layouts: 5.41 us -> 0.31 us
  transfers between devices with their start and end apart: 29 -> 20, of which waited for: 11 -> 10; matrix products, arithmetic and copies ran while one was open for 3% -> 4% of each run, Pallas kernels for 17% -> 8%
where the time goes in v3:
time: 87.4 us; the launch traced here: 87.2 us
  waiting for transfers between devices  36.1 us (41%)
  starting transfers between devices  23.4 us (27%)
  Pallas kernels  18.7 us (21%)
  other arithmetic  5 us (6%)
  between operations  3.75 us (4%)
    ppermute x18, waiting for transfers between devices, swap(): return lax.ppermute(array, 'dp', [(i, i ^ mask) for i in range(cycle)])  34.6 us
    ppermute x18, starting transfers between devices, swap(): return lax.ppermute(array, 'dp', [(i, i ^ mask) for i in range(cycle)])  18.9 us
    pallas_call x1, Pallas kernels, forward(): pl.pallas_call(functools.partial(forward_kernel, (rows_i // samples, rows...  9.42 us
    ppermute x2, starting transfers between devices, swap_halves(): return lax.ppermute(array, 'mp', [(0, 1), (1, 0)])  4.52 us
    pallas_call x2, Pallas kernels, weight_terms(): pl.pallas_call(functools.partial(weight_kernel, base, carries), out_shape...  4.17 us
    pallas_call x2, Pallas kernels, turn(): pl.pallas_call(turn_kernel, out_shape=(jax.ShapeDtypeStruct((depth, rows)...  4.07 us
  transfers between devices with their start and end apart: 20, of which 10 were waited for; matrix products, arithmetic and copies ran while one was open for 4% of the time, Pallas kernels for 8%

profile of v3, /device:TPU:0, one launch (start us, length us, event | category | flops | bytes accessed | tf_op | source)
XLA Modules:
  0.0 87.2 jit_solution(7434973798996745198)
XLA Ops:
  0.7 9.4 %shard_map.121 = (f32[32,768]{1,0:T(8,128)S(1)}, f32[32,128]{1,0:T(8,128)S(1)}, f32[1024,768]{1,0:T(8,128)}, f32[512,768]{1,0:T(8,128)}) custom-call(s32[1]{0:T(128)} %bitcast.1.place_ref, bf16[1024,1536]{1,0:T(8,128)(2,1)} %bitcast.4, bf16[512,1536]{1,0:T(8,128)(2,1)} %bitcast.6, bf16[1536,768]{1,0:T(8,128)(2,1)} %image_w_hbm.1, bf16[1536,768]{1,0:T(8,128)(2,1)} %text_w_hbm.1), custom_call_target="tpu_custom_call" | custom-call | flops 3623878656 | bytes 14155776 | tf_op jit(solution)/shard_map/pallas_call | solution.py:136
  10.1 3.0 %collective-permute-start = (f32[32,128]{1,0:T(8,128)S(1)}, f32[32,128]{1,0:T(8,128)S(1)}, u32[]{:S(2)}, u32[]{:S(2)}) collective-permute-start(f32[32,128]{1,0:T(8,128)S(1)} %get-tuple-element.25.own_ref), channel_id=1, source_target_pairs={{0,1},{1,0},{2,3},{3,2},{4,5},{5,4},{6,7},{7,6},{8,9},{9,8},{10,11... | collective-permute-start | bytes 49160 | tf_op jit(solution)/shard_map/ppermute | solution.py:436
  13.7 1.1 %collective-permute-done.other_ref = f32[32,128]{1,0:T(8,128)S(1)} collective-permute-done((f32[32,128]{1,0:T(8,128)S(1)}, f32[32,128]{1,0:T(8,128)S(1)}, u32[]{:S(2)}, u32[]{:S(2)}) %collective-permute-start) | collective-permute-done | bytes 16416 | tf_op jit(solution)/shard_map/ppermute | solution.py:436
  14.8 0.1 shard_map.122
  14.9 4.2 %collective-permute-start.3 = (bf16[32,768]{1,0:T(8,128)(2,1)S(1)}, bf16[32,768]{1,0:T(8,128)(2,1)S(1)}, u32[]{:S(2)}, u32[]{:S(2)}) collective-permute-start(bf16[32,768]{1,0:T(8,128)(2,1)S(1)} %get-tuple-element.26._.refs_1_), channel_id=1, source_target_pairs={{0,24},{2,26},{4,28},{6,30},{8,16},{10,18},{12,20},{14,22},{16,8},... | collective-permute-start | bytes 147464 | tf_op jit(solution)/shard_map/ppermute | solution.py:433
  19.1 0.6 collective-permute-start.1
  19.8 2.6 %shard_map.123 = (bf16[1536,1024]{1,0:T(8,128)(2,1)S(1)}, f32[8,128]{1,0:T(8,128)S(1)}) custom-call(s32[16]{0:T(128)S(1)} %broadcast_xor_fusion.1.source_ref, bf16[1024,1536]{1,0:T(8,128)(2,1)S(1)} %bitcast.5, bf16[32,768]{1,0:T(8,128)(2,1)S(1)} %get-tuple-element.26._.refs_1_), custom_call_target="tpu_custom_call" | custom-call | bytes 6291456 | tf_op jit(solution)/shard_map/pallas_call | solution.py:229
  22.4 0.8 collective-permute-done.2.refs_3_
  23.2 0.9 %collective-permute-done.1.refs_2_ = bf16[32,768]{1,0:T(8,128)(2,1)S(1)} collective-permute-done((bf16[32,768]{1,0:T(8,128)(2,1)S(1)}, bf16[32,768]{1,0:T(8,128)(2,1)S(1)}, u32[]{:S(2)}, u32[]{:S(2)}) %collective-permute-start.1) | collective-permute-done | bytes 49184 | tf_op jit(solution)/shard_map/ppermute | solution.py:433
  24.1 1.6 %collective-permute-start.4 = (bf16[4,32,768]{2,1,0:T(8,128)(2,1)S(1)}, bf16[4,32,768]{2,1,0:T(8,128)(2,1)S(1)}, u32[]{:S(2)}, u32[]{:S(2)}) collective-permute-start(bf16[4,32,768]{2,1,0:T(8,128)(2,1)S(1)} %shard_map.124._.refs_0_), channel_id=1, source_target_pairs={{0,4},{2,6},{4,0},{6,2},{8,12},{10,14},{12,8},{14,10},{16,20},{18,... | collective-permute-start | bytes 589832 | tf_op jit(solution)/shard_map/ppermute | solution.py:433
  25.7 1.5 %shard_map.125 = (bf16[1536,512]{1,0:T(8,128)(2,1)S(1)}, f32[8,128]{1,0:T(8,128)S(1)}) custom-call(s32[32]{0:T(128)S(1)} %broadcast_xor_fusion.source_ref, bf16[512,1536]{1,0:T(8,128)(2,1)S(1)} %bitcast.7, bf16[4,32,768]{2,1,0:T(8,128)(2,1)S(1)} %shard_map.124._.refs_0_), custom_call_target="tpu_custom_call" | custom-call | bytes 3145728 | tf_op jit(solution)/shard_map/pallas_call | solution.py:229
  27.2 2.6 %collective-permute-done.4.refs_1_ = bf16[4,32,768]{2,1,0:T(8,128)(2,1)S(1)} collective-permute-done((bf16[4,32,768]{2,1,0:T(8,128)(2,1)S(1)}, bf16[4,32,768]{2,1,0:T(8,128)(2,1)S(1)}, u32[]{:S(2)}, u32[]{:S(2)}) %collective-permute-start.4) | collective-permute-done | bytes 196640 | tf_op jit(solution)/shard_map/ppermute | solution.py:433
  30.0 1.4 %collective-permute-done.6.refs_3_ = bf16[4,32,768]{2,1,0:T(8,128)(2,1)S(1)} collective-permute-done((bf16[4,32,768]{2,1,0:T(8,128)(2,1)S(1)}, bf16[4,32,768]{2,1,0:T(8,128)(2,1)S(1)}, u32[]{:S(2)}, u32[]{:S(2)}) %collective-permute-start.6) | collective-permute-done | bytes 196640 | tf_op jit(solution)/shard_map/ppermute | solution.py:433
  31.4 0.4 shard_map.127
  31.7 1.5 %collective-permute-start.7 = (f32[32,256]{1,0:T(8,128)S(1)}, f32[32,256]{1,0:T(8,128)S(1)}, u32[]{:S(2)}, u32[]{:S(2)}) collective-permute-start(f32[32,256]{1,0:T(8,128)S(1)} %get-tuple-element.29.own_ref), channel_id=1, source_target_pairs={{0,1},{1,0},{2,3},{3,2},{4,5},{5,4},{6,7},{7,6},{8,9},{9,8},{10,11... | collective-permute-start | bytes 98312 | tf_op jit(solution)/shard_map/ppermute | solution.py:436
  35.2 0.5 collective-permute-done.7.other_ref
  35.7 0.5 shard_map.128
  36.2 1.5 %shard_map.129 = (f32[392,768]{1,0:T(8,128)S(1)}, f32[384,768]{1,0:T(8,128)S(1)}, f32[768,768]{1,0:T(8,128)S(1)}) custom-call(f32[32,768]{1,0:T(8,128)S(1)} %get-tuple-element.34.grad_ref, f32[512,768]{1,0:T(8,128)S(1)} %copy-done.3, bf16[1536,512]{1,0:T(8,128)(2,1)S(1)} %get-tuple-element.36.turned_ref, f32[8,768]{1,0:T(8,128)S(1)} %get-tuple-element.33.stat_ref._, ...), custom_call_target="tpu_custom_call" | custom-call | flops 1207959552 | bytes 7864320 | tf_op jit(solution)/shard_map/pallas_call | solution.py:392
  37.8 0.3 copy-done.2
  38.1 2.7 %shard_map.130 = (f32[384,768]{1,0:T(8,128)S(1)}, f32[384,768]{1,0:T(8,128)S(1)}, f32[768,768]{1,0:T(8,128)S(1)}) custom-call(f32[32,768]{1,0:T(8,128)S(1)} %get-tuple-element.34.grad_ref, f32[1024,768]{1,0:T(8,128)S(1)} %copy-done.2, bf16[1536,1024]{1,0:T(8,128)(2,1)S(1)} %get-tuple-element.41.turned_ref, f32[8,768]{1,0:T(8,128)S(1)} %get-tuple-element.33.stat_ref._, ...), custom_call_target="tpu_custom_call" | custom-call | flops 2415919104 | bytes 11010048 | tf_op jit(solution)/shard_map/pallas_call | solution.py:392
  40.8 0.3 collective-permute-start.11
  41.1 0.3 collective-permute-start.13
  41.4 0.3 collective-permute-start.10
  41.7 0.1 fusion.32
  41.8 0.1 fusion
  41.9 0.1 fusion.28
  42.1 1.6 %collective-permute-start.9 = (f16[400,768]{1,0:T(8,128)(2,1)S(1)}, f16[400,768]{1,0:T(8,128)(2,1)S(1)}, u32[]{:S(2)}, u32[]{:S(2)}) collective-permute-start(f16[400,768]{1,0:T(8,128)(2,1)S(1)} %add_convert_fusion.1), channel_id=1, source_target_pairs={{0,4},{2,6},{4,0},{6,2},{8,12},{10,14},{12,8},{14,10},{16,20},{18,... | collective-permute-start | bytes 1843208 | tf_op jit(solution)/shard_map/ppermute | solution.py:433
  43.7 0.1 add_multiply_fusion
  44.1 2.1 %collective-permute-start.14 = (f16[400,768]{1,0:T(8,128)(2,1)S(1)}, f16[400,768]{1,0:T(8,128)(2,1)S(1)}, u32[]{:S(2)}, u32[]{:S(2)}) collective-permute-start(f16[400,768]{1,0:T(8,128)(2,1)S(1)} %add_convert_fusion), channel_id=1, source_target_pairs={{0,8},{2,10},{4,12},{6,14},{8,0},{10,2},{12,4},{14,6},{16,24},{18,... | collective-permute-start | bytes 1843208 | tf_op jit(solution)/shard_map/ppermute | solution.py:433
  46.2 12.0 %collective-permute-done.9 = f16[400,768]{1,0:T(8,128)(2,1)S(1)} collective-permute-done((f16[400,768]{1,0:T(8,128)(2,1)S(1)}, f16[400,768]{1,0:T(8,128)(2,1)S(1)}, u32[]{:S(2)}, u32[]{:S(2)}) %collective-permute-start.9) | collective-permute-done | bytes 614432 | tf_op jit(solution)/shard_map/ppermute | solution.py:433
  58.2 0.1 fusion.36
  58.5 2.1 %collective-permute-start.12 = (f16[112,768]{1,0:T(8,128)(2,1)S(1)}, f16[112,768]{1,0:T(8,128)(2,1)S(1)}, u32[]{:S(2)}, u32[]{:S(2)}) collective-permute-start(f16[112,768]{1,0:T(8,128)(2,1)S(1)} %add_convert_fusion.5), channel_id=1, source_target_pairs={{0,8},{2,10},{4,12},{6,14},{8,0},{10,2},{12,4},{14,6},{16,24},{18,... | collective-permute-start | bytes 516104 | tf_op jit(solution)/shard_map/ppermute | solution.py:433
  60.9 0.7 collective-permute-start.17
  61.5 0.1 fusion.40
  61.7 0.1 fusion.2
  61.9 1.6 %collective-permute-start.15 = (f16[208,768]{1,0:T(8,128)(2,1)S(1)}, f16[208,768]{1,0:T(8,128)(2,1)S(1)}, u32[]{:S(2)}, u32[]{:S(2)}) collective-permute-start(f16[208,768]{1,0:T(8,128)(2,1)S(1)} %add_convert_fusion.2), channel_id=1, source_target_pairs={{0,4},{2,6},{4,0},{6,2},{8,12},{10,14},{12,8},{14,10},{16,20},{18,... | collective-permute-start | bytes 958472 | tf_op jit(solution)/shard_map/ppermute | solution.py:433
  63.5 2.1 %collective-permute-done.12 = f16[112,768]{1,0:T(8,128)(2,1)S(1)} collective-permute-done((f16[112,768]{1,0:T(8,128)(2,1)S(1)}, f16[112,768]{1,0:T(8,128)(2,1)S(1)}, u32[]{:S(2)}, u32[]{:S(2)}) %collective-permute-start.12) | collective-permute-done | bytes 172064 | tf_op jit(solution)/shard_map/ppermute | solution.py:433
  65.6 5.2 %collective-permute-done.17 = f16[112,768]{1,0:T(8,128)(2,1)S(1)} collective-permute-done((f16[112,768]{1,0:T(8,128)(2,1)S(1)}, f16[112,768]{1,0:T(8,128)(2,1)S(1)}, u32[]{:S(2)}, u32[]{:S(2)}) %collective-permute-start.17) | collective-permute-done | bytes 172064 | tf_op jit(solution)/shard_map/ppermute | solution.py:433
  70.8 0.1 ceil_reduce_fusion
  71.2 0.1 fusion.10
  71.4 1.7 %collective-permute-start.18 = (f16[112,768]{1,0:T(8,128)(2,1)S(1)}, f16[112,768]{1,0:T(8,128)(2,1)S(1)}, u32[]{:S(2)}, u32[]{:S(2)}) collective-permute-start(f16[112,768]{1,0:T(8,128)(2,1)S(1)} %add_convert_fusion.3), channel_id=1, source_target_pairs={{0,16},{2,18},{4,20},{6,22},{8,24},{10,26},{12,28},{14,30},{16,0},... | collective-permute-start | bytes 516104 | tf_op jit(solution)/shard_map/ppermute | solution.py:433
  73.3 1.4 %collective-permute-start.16 = (f16[64,768]{1,0:T(8,128)(2,1)S(1)}, f16[64,768]{1,0:T(8,128)(2,1)S(1)}, u32[]{:S(2)}, u32[]{:S(2)}) collective-permute-start(f16[64,768]{1,0:T(8,128)(2,1)S(1)} %add_convert_fusion.7), channel_id=1, source_target_pairs={{0,16},{2,18},{4,20},{6,22},{8,24},{10,26},{12,28},{14,30},{16,0},... | collective-permute-start | bytes 294920 | tf_op jit(solution)/shard_map/ppermute | solution.py:433
  74.9 0.4 collective-permute-start.19
  75.4 9.5 %collective-permute-done.16 = f16[64,768]{1,0:T(8,128)(2,1)S(1)} collective-permute-done((f16[64,768]{1,0:T(8,128)(2,1)S(1)}, f16[64,768]{1,0:T(8,128)(2,1)S(1)}, u32[]{:S(2)}, u32[]{:S(2)}) %collective-permute-start.16) | collective-permute-done | bytes 98336 | tf_op jit(solution)/shard_map/ppermute | solution.py:433
  84.8 0.6 fusion.59
  85.5 0.1 fusion.18
  85.6 0.7 pad_maximum_fusion
  86.4 0.8 fusion.5
  (76 shorter events, 1.9 us)
Async XLA Ops:
  0.6 19.1 %copy-start.5 = (s32[16]{0:T(128)S(1)}, s32[16]{0:T(128)}, u32[]{:S(2)}) copy-start(s32[16]{0:T(128)} %constant.64.clone) | copy-start | bytes 196
  0.6 19.1 %copy-start = (bf16[16,64,1536]{2,1,0:T(8,128)(2,1)S(1)}, bf16[16,64,1536]{2,1,0:T(8,128)(2,1)}, u32[]{:S(2)}) copy-start(bf16[16,64,1536]{2,1,0:T(8,128)(2,1)} %param.10) | copy-start | bytes 9437188
  10.1 4.7 %collective-permute-start = (f32[32,128]{1,0:T(8,128)S(1)}, f32[32,128]{1,0:T(8,128)S(1)}, u32[]{:S(2)}, u32[]{:S(2)}) collective-permute-start(f32[32,128]{1,0:T(8,128)S(1)} %get-tuple-element.25.own_ref), channel_id=1, source_target_pairs={{0,1},{1,0},{2,3},{3,2},{4,5},{5,4},{6,7},{7,6},{8,9},{9,8},{10,11... | collective-permute-start | bytes 49160 | tf_op jit(solution)/shard_map/ppermute | solution.py:436
  14.9 7.5 %collective-permute-start.3 = (bf16[32,768]{1,0:T(8,128)(2,1)S(1)}, bf16[32,768]{1,0:T(8,128)(2,1)S(1)}, u32[]{:S(2)}, u32[]{:S(2)}) collective-permute-start(bf16[32,768]{1,0:T(8,128)(2,1)S(1)} %get-tuple-element.26._.refs_1_), channel_id=1, source_target_pairs={{0,24},{2,26},{4,28},{6,30},{8,16},{10,18},{12,20},{14,22},{16,8},... | collective-permute-start | bytes 147464 | tf_op jit(solution)/shard_map/ppermute | solution.py:433
  19.1 4.1 %collective-permute-start.2 = (bf16[32,768]{1,0:T(8,128)(2,1)S(1)}, bf16[32,768]{1,0:T(8,128)(2,1)S(1)}, u32[]{:S(2)}, u32[]{:S(2)}) collective-permute-start(bf16[32,768]{1,0:T(8,128)(2,1)S(1)} %get-tuple-element.26._.refs_1_), channel_id=1, source_target_pairs={{0,8},{2,10},{4,12},{6,14},{8,0},{10,2},{12,4},{14,6},{16,24},{18,... | collective-permute-start | bytes 147464 | tf_op jit(solution)/shard_map/ppermute | solution.py:433
  19.1 5.0 %collective-permute-start.1 = (bf16[32,768]{1,0:T(8,128)(2,1)S(1)}, bf16[32,768]{1,0:T(8,128)(2,1)S(1)}, u32[]{:S(2)}, u32[]{:S(2)}) collective-permute-start(bf16[32,768]{1,0:T(8,128)(2,1)S(1)} %get-tuple-element.26._.refs_1_), channel_id=1, source_target_pairs={{0,16},{2,18},{4,20},{6,22},{8,24},{10,26},{12,28},{14,30},{16,0},... | collective-permute-start | bytes 147464 | tf_op jit(solution)/shard_map/ppermute | solution.py:433
  19.8 5.9 %copy-start.4 = (s32[32]{0:T(128)S(1)}, s32[32]{0:T(128)}, u32[]{:S(2)}) copy-start(s32[32]{0:T(128)} %constant.63.clone) | copy-start | bytes 388
  19.8 5.9 %copy-start.1 = (bf16[16,32,1536]{2,1,0:T(8,128)(2,1)S(1)}, bf16[16,32,1536]{2,1,0:T(8,128)(2,1)}, u32[]{:S(2)}) copy-start(bf16[16,32,1536]{2,1,0:T(8,128)(2,1)} %param.11) | copy-start | bytes 4718596
  24.1 5.7 %collective-permute-start.4 = (bf16[4,32,768]{2,1,0:T(8,128)(2,1)S(1)}, bf16[4,32,768]{2,1,0:T(8,128)(2,1)S(1)}, u32[]{:S(2)}, u32[]{:S(2)}) collective-permute-start(bf16[4,32,768]{2,1,0:T(8,128)(2,1)S(1)} %shard_map.124._.refs_0_), channel_id=1, source_target_pairs={{0,4},{2,6},{4,0},{6,2},{8,12},{10,14},{12,8},{14,10},{16,20},{18,... | collective-permute-start | bytes 589832 | tf_op jit(solution)/shard_map/ppermute | solution.py:433
  25.7 4.2 %collective-permute-start.5 = (bf16[4,32,768]{2,1,0:T(8,128)(2,1)S(1)}, bf16[4,32,768]{2,1,0:T(8,128)(2,1)S(1)}, u32[]{:S(2)}, u32[]{:S(2)}) collective-permute-start(bf16[4,32,768]{2,1,0:T(8,128)(2,1)S(1)} %shard_map.124._.refs_0_), channel_id=1, source_target_pairs={{0,2},{2,0},{4,6},{6,4},{8,10},{10,8},{12,14},{14,12},{16,18},{18,... | collective-permute-start | bytes 589832 | tf_op jit(solution)/shard_map/ppermute | solution.py:433
  27.2 9.0 %copy-start.3 = (f32[512,768]{1,0:T(8,128)S(1)}, f32[512,768]{1,0:T(8,128)}, u32[]{:S(2)}) copy-start(f32[512,768]{1,0:T(8,128)} %get-tuple-element.35.slope_ref) | copy-start | bytes 4718596
  29.9 1.5 %collective-permute-start.6 = (bf16[4,32,768]{2,1,0:T(8,128)(2,1)S(1)}, bf16[4,32,768]{2,1,0:T(8,128)(2,1)S(1)}, u32[]{:S(2)}, u32[]{:S(2)}) collective-permute-start(bf16[4,32,768]{2,1,0:T(8,128)(2,1)S(1)} %bitcast.8), channel_id=1, source_target_pairs={{0,2},{2,0},{4,6},{6,4},{8,10},{10,8},{12,14},{14,12},{16,18},{18,... | collective-permute-start | bytes 589832 | tf_op jit(solution)/shard_map/ppermute | solution.py:433
  31.7 3.9 %collective-permute-start.7 = (f32[32,256]{1,0:T(8,128)S(1)}, f32[32,256]{1,0:T(8,128)S(1)}, u32[]{:S(2)}, u32[]{:S(2)}) collective-permute-start(f32[32,256]{1,0:T(8,128)S(1)} %get-tuple-element.29.own_ref), channel_id=1, source_target_pairs={{0,1},{1,0},{2,3},{3,2},{4,5},{5,4},{6,7},{7,6},{8,9},{9,8},{10,11... | collective-permute-start | bytes 98312 | tf_op jit(solution)/shard_map/ppermute | solution.py:436
  36.2 1.9 %copy-start.2 = (f32[1024,768]{1,0:T(8,128)S(1)}, f32[1024,768]{1,0:T(8,128)}, u32[]{:S(2)}) copy-start(f32[1024,768]{1,0:T(8,128)} %get-tuple-element.40.slope_ref) | copy-start | bytes 9437188
  37.7 3.9 %collective-permute-start.8 = (f32[392,768]{1,0:T(8,128)S(1)}, f32[392,768]{1,0:T(8,128)S(1)}, u32[]{:S(2)}, u32[]{:S(2)}) collective-permute-start(f32[392,768]{1,0:T(8,128)S(1)} %get-tuple-element.37._), channel_id=1, source_target_pairs={{0,2},{2,0},{4,6},{6,4},{8,10},{10,8},{12,14},{14,12},{16,18},{18,... | collective-permute-start | bytes 3612680 | tf_op jit(solution)/shard_map/ppermute | solution.py:433
  40.8 2.9 %collective-permute-start.11 = (f32[384,768]{1,0:T(8,128)S(1)}, f32[384,768]{1,0:T(8,128)S(1)}, u32[]{:S(2)}, u32[]{:S(2)}) collective-permute-start(f32[384,768]{1,0:T(8,128)S(1)} %get-tuple-element.43), channel_id=1, source_target_pairs={{0,2},{2,0},{4,6},{6,4},{8,10},{10,8},{12,14},{14,12},{16,18},{18,... | collective-permute-start | bytes 3538952 | tf_op jit(solution)/shard_map/ppermute | solution.py:433
  41.1 20.6 %collective-permute-start.13 = (f32[384,768]{1,0:T(8,128)S(1)}, f32[384,768]{1,0:T(8,128)S(1)}, u32[]{:S(2)}, u32[]{:S(2)}) collective-permute-start(f32[384,768]{1,0:T(8,128)S(1)} %get-tuple-element.44), channel_id=1, source_target_pairs={{0,2},{2,0},{4,6},{6,4},{8,10},{10,8},{12,14},{14,12},{16,18},{18,... | collective-permute-start | bytes 3538952 | tf_op jit(solution)/shard_map/ppermute | solution.py:433
  41.4 16.9 %collective-permute-start.10 = (f32[384,768]{1,0:T(8,128)S(1)}, f32[384,768]{1,0:T(8,128)S(1)}, u32[]{:S(2)}, u32[]{:S(2)}) collective-permute-start(f32[384,768]{1,0:T(8,128)S(1)} %get-tuple-element.39), channel_id=1, source_target_pairs={{0,2},{2,0},{4,6},{6,4},{8,10},{10,8},{12,14},{14,12},{16,18},{18,... | collective-permute-start | bytes 3538952 | tf_op jit(solution)/shard_map/ppermute | solution.py:433
  42.1 16.1 %collective-permute-start.9 = (f16[400,768]{1,0:T(8,128)(2,1)S(1)}, f16[400,768]{1,0:T(8,128)(2,1)S(1)}, u32[]{:S(2)}, u32[]{:S(2)}) collective-permute-start(f16[400,768]{1,0:T(8,128)(2,1)S(1)} %add_convert_fusion.1), channel_id=1, source_target_pairs={{0,4},{2,6},{4,0},{6,2},{8,12},{10,14},{12,8},{14,10},{16,20},{18,... | collective-permute-start | bytes 1843208 | tf_op jit(solution)/shard_map/ppermute | solution.py:433
  44.1 17.4 %collective-permute-start.14 = (f16[400,768]{1,0:T(8,128)(2,1)S(1)}, f16[400,768]{1,0:T(8,128)(2,1)S(1)}, u32[]{:S(2)}, u32[]{:S(2)}) collective-permute-start(f16[400,768]{1,0:T(8,128)(2,1)S(1)} %add_convert_fusion), channel_id=1, source_target_pairs={{0,8},{2,10},{4,12},{6,14},{8,0},{10,2},{12,4},{14,6},{16,24},{18,... | collective-permute-start | bytes 1843208 | tf_op jit(solution)/shard_map/ppermute | solution.py:433
  58.5 7.1 %collective-permute-start.12 = (f16[112,768]{1,0:T(8,128)(2,1)S(1)}, f16[112,768]{1,0:T(8,128)(2,1)S(1)}, u32[]{:S(2)}, u32[]{:S(2)}) collective-permute-start(f16[112,768]{1,0:T(8,128)(2,1)S(1)} %add_convert_fusion.5), channel_id=1, source_target_pairs={{0,8},{2,10},{4,12},{6,14},{8,0},{10,2},{12,4},{14,6},{16,24},{18,... | collective-permute-start | bytes 516104 | tf_op jit(solution)/shard_map/ppermute | solution.py:433
  60.9 9.9 %collective-permute-start.17 = (f16[112,768]{1,0:T(8,128)(2,1)S(1)}, f16[112,768]{1,0:T(8,128)(2,1)S(1)}, u32[]{:S(2)}, u32[]{:S(2)}) collective-permute-start(f16[112,768]{1,0:T(8,128)(2,1)S(1)} %add_convert_fusion.4), channel_id=1, source_target_pairs={{0,16},{2,18},{4,20},{6,22},{8,24},{10,26},{12,28},{14,30},{16,0},... | collective-permute-start | bytes 516104 | tf_op jit(solution)/shard_map/ppermute | solution.py:433
  61.9 9.1 %collective-permute-start.15 = (f16[208,768]{1,0:T(8,128)(2,1)S(1)}, f16[208,768]{1,0:T(8,128)(2,1)S(1)}, u32[]{:S(2)}, u32[]{:S(2)}) collective-permute-start(f16[208,768]{1,0:T(8,128)(2,1)S(1)} %add_convert_fusion.2), channel_id=1, source_target_pairs={{0,4},{2,6},{4,0},{6,2},{8,12},{10,14},{12,8},{14,10},{16,20},{18,... | collective-permute-start | bytes 958472 | tf_op jit(solution)/shard_map/ppermute | solution.py:433
  71.4 14.9 %collective-permute-start.18 = (f16[112,768]{1,0:T(8,128)(2,1)S(1)}, f16[112,768]{1,0:T(8,128)(2,1)S(1)}, u32[]{:S(2)}, u32[]{:S(2)}) collective-permute-start(f16[112,768]{1,0:T(8,128)(2,1)S(1)} %add_convert_fusion.3), channel_id=1, source_target_pairs={{0,16},{2,18},{4,20},{6,22},{8,24},{10,26},{12,28},{14,30},{16,0},... | collective-permute-start | bytes 516104 | tf_op jit(solution)/shard_map/ppermute | solution.py:433
  73.3 11.5 %collective-permute-start.16 = (f16[64,768]{1,0:T(8,128)(2,1)S(1)}, f16[64,768]{1,0:T(8,128)(2,1)S(1)}, u32[]{:S(2)}, u32[]{:S(2)}) collective-permute-start(f16[64,768]{1,0:T(8,128)(2,1)S(1)} %add_convert_fusion.7), channel_id=1, source_target_pairs={{0,16},{2,18},{4,20},{6,22},{8,24},{10,26},{12,28},{14,30},{16,0},... | collective-permute-start | bytes 294920 | tf_op jit(solution)/shard_map/ppermute | solution.py:433
  74.9 10.5 %collective-permute-start.19 = (f16[64,768]{1,0:T(8,128)(2,1)S(1)}, f16[64,768]{1,0:T(8,128)(2,1)S(1)}, u32[]{:S(2)}, u32[]{:S(2)}) collective-permute-start(f16[64,768]{1,0:T(8,128)(2,1)S(1)} %add_convert_fusion.6), channel_id=1, source_target_pairs={{0,8},{2,10},{4,12},{6,14},{8,0},{10,2},{12,4},{14,6},{16,24},{18,... | collective-permute-start | bytes 294920 | tf_op jit(solution)/shard_map/ppermute | solution.py:433

commit v4 on v3

--- a/solution.py
+++ b/solution.py
@@ -10,11 +10,12 @@
 F32 = jnp.float32
 BF16 = jnp.bfloat16
 ROWS = 256
-JOB_ROWS = 512
+JOB_ROWS = 256
 JOB_COLUMNS = 256
 STRIP = 64
 ROOT = 0.7978845608028654
 HALF_MAX = 16384.0
+FOOT = 8
 UNUSABLE = 2.0
 
 
@@ -491,7 +492,7 @@
         blocks,
     )
 
-    lines = lax.broadcasted_iota(jnp.int32, (16, width), 0)
+    lines = lax.broadcasted_iota(jnp.int32, (FOOT, width), 0)
 
     def footer(exponents, stat):
         rows = list(exponents)
@@ -500,7 +501,7 @@
             part = lax.reduce_precision(rest, 5, 10)
             rows.append(part)
             rest = (rest - part) * 2048.0
-        found = jnp.zeros((16, width), F32)
+        found = jnp.zeros((FOOT, width), F32)
         for n, row in enumerate(rows):
             found = jnp.where(lines == n, row, found)
         return found
@@ -509,7 +510,7 @@
         return [jnp.ceil(jnp.log2(jnp.maximum(stat[n : n + 1], 1e-30))) for n in (1, 2)]
 
     def merged(stat, message):
-        foot = message[-16:].astype(F32)
+        foot = message[-FOOT:].astype(F32)
         loss = (foot[4:5] / 2048.0 + foot[3:4]) / 2048.0 + foot[2:3]
         there = [foot[:1], foot[1:2]]
         add = [loss, jnp.exp2(there[0]), jnp.exp2(there[1])]
@@ -526,13 +527,13 @@
         factor = HALF_MAX * jnp.exp2(-exponents[tower]) + 0.0 * after[:1].astype(F32)
         coded = sum_of(terms) * factor
         foot = footer(exponents, stat) + 0.0 * coded[:1]
-        coded = jnp.pad(coded, ((0, 16), (0, 0))) + jnp.pad(foot, ((rows, 0), (0, 0)))
+        coded = jnp.pad(coded, ((0, FOOT), (0, 0))) + jnp.pad(foot, ((rows, 0), (0, 0)))
         coded = coded.astype(jnp.float16)
         return coded, swap(coded, 1 << bit)
 
     def take(terms, stat, tower, coming):
         stat, there = merged(stat, coming)
-        return terms + [(coming[:-16], jnp.exp2(there[tower]) / HALF_MAX)], stat
+        return terms + [(coming[:-FOOT], jnp.exp2(there[tower]) / HALF_MAX)], stat
 
     def core_step(soon, late, keep):
         height = late.shape[0]
@@ -552,21 +553,19 @@
     parts = [(terms, text_stat) for terms in halves(text)]
     image, image_stat = take(image, start_stat, 0, image_in)
     for step in range(bits - 2):
-        last = step == bits - 3
         image, image_leaves = halves(image)
-        if last:
-            coded, image_in = leave(image_leaves, image_stat, 0, image_order[step + 1], coded)
-        arrivals = []
+        arrivals, before = [], coded
         for order, (terms, terms_stat) in zip(text_orders, parts):
             terms, leaves = halves(terms)
-            coded, arrival = leave(leaves, terms_stat, 1, order[step], coded)
+            last, arrival = leave(leaves, terms_stat, 1, order[step], before)
+            before = last if step == 0 else before
             arrivals.append((terms, terms_stat, arrival))
-        if not last:
-            coded, image_in = leave(image_leaves, image_stat, 0, image_order[step + 1], coded)
+        coded, image_in = leave(image_leaves, image_stat, 0, image_order[step + 1], before)
         parts = [take(terms, old, 1, arrival) for terms, old, arrival in arrivals]
         image, image_stat = take(image, image_stat, 0, image_in)
-    text = jnp.concatenate([sum_of(terms) for terms, _ in parts])
-    loss = jnp.max(parts[0][1][0] + 0.0 * coded[0].astype(F32))
+    row = 0.0 * coded[:1].astype(F32)
+    text = jnp.concatenate([sum_of(terms) + row for terms, _ in parts])
+    loss = jnp.max(parts[0][1][:1] + row)
     return (loss, sum_of(image), text)
 
 

time: 87.4 us -> 86.5 us (0.990)
  starting transfers between devices: 23.4 us -> 19.4 us
  waiting for transfers between devices: 36.1 us -> 39.3 us
    ppermute x18, starting transfers between devices: 18.9 us -> 14.9 us  [swap(): return lax.ppermute(array, 'dp', [(i, i ^ mask) for i in range(cycle)])]
    ppermute x18, waiting for transfers between devices: 34.6 us -> 37.8 us  [swap(): return lax.ppermute(array, 'dp', [(i, i ^ mask) for i in range(cycle)])]
  transfers between devices with their start and end apart: 20 -> 20, of which waited for: 10 -> 12; matrix products, arithmetic and copies ran while one was open for 4% -> 4% of each run, Pallas kernels for 8% -> 8%
where the time goes in v4:
time: 86.5 us; the launch traced here: 86.3 us
  waiting for transfers between devices  39.3 us (45%)
  starting transfers between devices  19.4 us (22%)
  Pallas kernels  18.7 us (22%)
  other arithmetic  4.87 us (6%)
  between operations  3.7 us (4%)
    ppermute x18, waiting for transfers between devices, swap(): return lax.ppermute(array, 'dp', [(i, i ^ mask) for i in range(cycle)])  37.8 us
    ppermute x18, starting transfers between devices, swap(): return lax.ppermute(array, 'dp', [(i, i ^ mask) for i in range(cycle)])  14.9 us
    pallas_call x1, Pallas kernels, forward(): pl.pallas_call(functools.partial(forward_kernel, (rows_i // samples, rows...  9.24 us
    ppermute x2, starting transfers between devices, swap_halves(): return lax.ppermute(array, 'mp', [(0, 1), (1, 0)])  4.55 us
    pallas_call x2, Pallas kernels, weight_terms(): pl.pallas_call(functools.partial(weight_kernel, base, carries), out_shape...  4.36 us
    pallas_call x2, Pallas kernels, turn(): pl.pallas_call(turn_kernel, out_shape=(jax.ShapeDtypeStruct((depth, rows)...  4.07 us
  transfers between devices with their start and end apart: 20, of which 12 were waited for; matrix products, arithmetic and copies ran while one was open for 4% of the time, Pallas kernels for 8%

profile of v4, /device:TPU:0, one launch (start us, length us, event | category | flops | bytes accessed | tf_op | source)
XLA Modules:
  0.0 86.3 jit_solution(16532387348119317048)
XLA Ops:
  0.7 9.2 %shard_map.121 = (f32[32,768]{1,0:T(8,128)S(1)}, f32[32,128]{1,0:T(8,128)S(1)}, f32[1024,768]{1,0:T(8,128)}, f32[512,768]{1,0:T(8,128)}) custom-call(s32[1]{0:T(128)} %bitcast.1.place_ref, bf16[1024,1536]{1,0:T(8,128)(2,1)} %bitcast.4, bf16[512,1536]{1,0:T(8,128)(2,1)} %bitcast.6, bf16[1536,768]{1,0:T(8,128)(2,1)} %image_w_hbm.1, bf16[1536,768]{1,0:T(8,128)(2,1)} %text_w_hbm.1), custom_call_target="tpu_custom_call" | custom-call | flops 3623878656 | bytes 14155776 | tf_op jit(solution)/shard_map/pallas_call | solution.py:137
  9.9 3.0 %collective-permute-start = (f32[32,128]{1,0:T(8,128)S(1)}, f32[32,128]{1,0:T(8,128)S(1)}, u32[]{:S(2)}, u32[]{:S(2)}) collective-permute-start(f32[32,128]{1,0:T(8,128)S(1)} %get-tuple-element.25.own_ref), channel_id=1, source_target_pairs={{0,1},{1,0},{2,3},{3,2},{4,5},{5,4},{6,7},{7,6},{8,9},{9,8},{10,11... | collective-permute-start | bytes 49160 | tf_op jit(solution)/shard_map/ppermute | solution.py:437
  13.6 1.1 %collective-permute-done.other_ref = f32[32,128]{1,0:T(8,128)S(1)} collective-permute-done((f32[32,128]{1,0:T(8,128)S(1)}, f32[32,128]{1,0:T(8,128)S(1)}, u32[]{:S(2)}, u32[]{:S(2)}) %collective-permute-start) | collective-permute-done | bytes 16416 | tf_op jit(solution)/shard_map/ppermute | solution.py:437
  14.6 0.1 shard_map.122
  14.7 3.2 %collective-permute-start.1 = (bf16[32,768]{1,0:T(8,128)(2,1)S(1)}, bf16[32,768]{1,0:T(8,128)(2,1)S(1)}, u32[]{:S(2)}, u32[]{:S(2)}) collective-permute-start(bf16[32,768]{1,0:T(8,128)(2,1)S(1)} %get-tuple-element.26._.refs_1_), channel_id=1, source_target_pairs={{0,16},{2,18},{4,20},{6,22},{8,24},{10,26},{12,28},{14,30},{16,0},... | collective-permute-start | bytes 147464 | tf_op jit(solution)/shard_map/ppermute | solution.py:434
  17.9 1.6 %collective-permute-start.2 = (bf16[32,768]{1,0:T(8,128)(2,1)S(1)}, bf16[32,768]{1,0:T(8,128)(2,1)S(1)}, u32[]{:S(2)}, u32[]{:S(2)}) collective-permute-start(bf16[32,768]{1,0:T(8,128)(2,1)S(1)} %get-tuple-element.26._.refs_1_), channel_id=1, source_target_pairs={{0,8},{2,10},{4,12},{6,14},{8,0},{10,2},{12,4},{14,6},{16,24},{18,... | collective-permute-start | bytes 147464 | tf_op jit(solution)/shard_map/ppermute | solution.py:434
  19.5 2.6 %shard_map.123 = (bf16[1536,1024]{1,0:T(8,128)(2,1)S(1)}, f32[8,128]{1,0:T(8,128)S(1)}) custom-call(s32[16]{0:T(128)S(1)} %broadcast_xor_fusion.1.source_ref, bf16[1024,1536]{1,0:T(8,128)(2,1)S(1)} %bitcast.5, bf16[32,768]{1,0:T(8,128)(2,1)S(1)} %get-tuple-element.26._.refs_1_), custom_call_target="tpu_custom_call" | custom-call | bytes 6291456 | tf_op jit(solution)/shard_map/pallas_call | solution.py:230
  22.1 3.2 %collective-permute-done.3.refs_4_ = bf16[32,768]{1,0:T(8,128)(2,1)S(1)} collective-permute-done((bf16[32,768]{1,0:T(8,128)(2,1)S(1)}, bf16[32,768]{1,0:T(8,128)(2,1)S(1)}, u32[]{:S(2)}, u32[]{:S(2)}) %collective-permute-start.3) | collective-permute-done | bytes 49184 | tf_op jit(solution)/shard_map/ppermute | solution.py:434
  25.4 1.6 %collective-permute-start.4 = (bf16[4,32,768]{2,1,0:T(8,128)(2,1)S(1)}, bf16[4,32,768]{2,1,0:T(8,128)(2,1)S(1)}, u32[]{:S(2)}, u32[]{:S(2)}) collective-permute-start(bf16[4,32,768]{2,1,0:T(8,128)(2,1)S(1)} %shard_map.124._.refs_0_), channel_id=1, source_target_pairs={{0,4},{2,6},{4,0},{6,2},{8,12},{10,14},{12,8},{14,10},{16,20},{18,... | collective-permute-start | bytes 589832 | tf_op jit(solution)/shard_map/ppermute | solution.py:434
  27.0 1.5 %shard_map.125 = (bf16[1536,512]{1,0:T(8,128)(2,1)S(1)}, f32[8,128]{1,0:T(8,128)S(1)}) custom-call(s32[32]{0:T(128)S(1)} %broadcast_xor_fusion.source_ref, bf16[512,1536]{1,0:T(8,128)(2,1)S(1)} %bitcast.7, bf16[4,32,768]{2,1,0:T(8,128)(2,1)S(1)} %shard_map.124._.refs_0_), custom_call_target="tpu_custom_call" | custom-call | bytes 3145728 | tf_op jit(solution)/shard_map/pallas_call | solution.py:230
  28.5 2.6 %collective-permute-done.4.refs_1_ = bf16[4,32,768]{2,1,0:T(8,128)(2,1)S(1)} collective-permute-done((bf16[4,32,768]{2,1,0:T(8,128)(2,1)S(1)}, bf16[4,32,768]{2,1,0:T(8,128)(2,1)S(1)}, u32[]{:S(2)}, u32[]{:S(2)}) %collective-permute-start.4) | collective-permute-done | bytes 196640 | tf_op jit(solution)/shard_map/ppermute | solution.py:434
  31.2 1.4 %collective-permute-done.6.refs_3_ = bf16[4,32,768]{2,1,0:T(8,128)(2,1)S(1)} collective-permute-done((bf16[4,32,768]{2,1,0:T(8,128)(2,1)S(1)}, bf16[4,32,768]{2,1,0:T(8,128)(2,1)S(1)}, u32[]{:S(2)}, u32[]{:S(2)}) %collective-permute-start.6) | collective-permute-done | bytes 196640 | tf_op jit(solution)/shard_map/ppermute | solution.py:434
  32.7 0.4 shard_map.127
  33.0 1.5 %collective-permute-start.7 = (f32[32,256]{1,0:T(8,128)S(1)}, f32[32,256]{1,0:T(8,128)S(1)}, u32[]{:S(2)}, u32[]{:S(2)}) collective-permute-start(f32[32,256]{1,0:T(8,128)S(1)} %get-tuple-element.29.own_ref), channel_id=1, source_target_pairs={{0,1},{1,0},{2,3},{3,2},{4,5},{5,4},{6,7},{7,6},{8,9},{9,8},{10,11... | collective-permute-start | bytes 98312 | tf_op jit(solution)/shard_map/ppermute | solution.py:437
  36.5 0.5 collective-permute-done.7.other_ref
  37.0 0.5 shard_map.128
  37.5 1.5 %shard_map.129 = (f32[392,768]{1,0:T(8,128)S(1)}, f32[384,768]{1,0:T(8,128)S(1)}, f32[768,768]{1,0:T(8,128)S(1)}) custom-call(f32[32,768]{1,0:T(8,128)S(1)} %get-tuple-element.34.grad_ref, f32[512,768]{1,0:T(8,128)S(1)} %copy-done.3, bf16[1536,512]{1,0:T(8,128)(2,1)S(1)} %get-tuple-element.36.turned_ref, f32[8,768]{1,0:T(8,128)S(1)} %get-tuple-element.33.stat_ref._, ...), custom_call_target="tpu_custom_call" | custom-call | flops 1207959552 | bytes 7864320 | tf_op jit(solution)/shard_map/pallas_call | solution.py:393
  39.1 0.3 copy-done.2
  39.4 2.9 %shard_map.130 = (f32[384,768]{1,0:T(8,128)S(1)}, f32[384,768]{1,0:T(8,128)S(1)}, f32[768,768]{1,0:T(8,128)S(1)}) custom-call(f32[32,768]{1,0:T(8,128)S(1)} %get-tuple-element.34.grad_ref, f32[1024,768]{1,0:T(8,128)S(1)} %copy-done.2, bf16[1536,1024]{1,0:T(8,128)(2,1)S(1)} %get-tuple-element.41.turned_ref, f32[8,768]{1,0:T(8,128)S(1)} %get-tuple-element.33.stat_ref._, ...), custom_call_target="tpu_custom_call" | custom-call | flops 2415919104 | bytes 11010048 | tf_op jit(solution)/shard_map/pallas_call | solution.py:393
  42.3 0.3 collective-permute-start.13
  42.6 0.3 collective-permute-start.11
  42.9 0.2 collective-permute-start.10
  43.1 0.1 fusion.34
  43.2 0.1 fusion
  43.5 1.6 %collective-permute-start.9 = (f16[392,768]{1,0:T(8,128)(2,1)S(1)}, f16[392,768]{1,0:T(8,128)(2,1)S(1)}, u32[]{:S(2)}, u32[]{:S(2)}) collective-permute-start(f16[392,768]{1,0:T(8,128)(2,1)S(1)} %add_convert_fusion.1), channel_id=1, source_target_pairs={{0,4},{2,6},{4,0},{6,2},{8,12},{10,14},{12,8},{14,10},{16,20},{18,... | collective-permute-start | bytes 1806344 | tf_op jit(solution)/shard_map/ppermute | solution.py:434
  45.1 1.7 %collective-permute-done.11 = f32[384,768]{1,0:T(8,128)S(1)} collective-permute-done((f32[384,768]{1,0:T(8,128)S(1)}, f32[384,768]{1,0:T(8,128)S(1)}, u32[]{:S(2)}, u32[]{:S(2)}) %collective-permute-start.11) | collective-permute-done | bytes 1179680 | tf_op jit(solution)/shard_map/ppermute | solution.py:434
  46.9 0.1 add_multiply_fusion
  47.0 0.1 fusion.29
  47.3 12.1 %collective-permute-done.9 = f16[392,768]{1,0:T(8,128)(2,1)S(1)} collective-permute-done((f16[392,768]{1,0:T(8,128)(2,1)S(1)}, f16[392,768]{1,0:T(8,128)(2,1)S(1)}, u32[]{:S(2)}, u32[]{:S(2)}) %collective-permute-start.9) | collective-permute-done | bytes 602144 | tf_op jit(solution)/shard_map/ppermute | solution.py:434
  59.4 0.1 fusion.38
  60.0 1.2 %collective-permute-start.18 = (f16[104,768]{1,0:T(8,128)(2,1)S(1)}, f16[104,768]{1,0:T(8,128)(2,1)S(1)}, u32[]{:S(2)}, u32[]{:S(2)}) collective-permute-start(f16[104,768]{1,0:T(8,128)(2,1)S(1)} %add_convert_fusion.4), channel_id=1, source_target_pairs={{0,16},{2,18},{4,20},{6,22},{8,24},{10,26},{12,28},{14,30},{16,0},... | collective-permute-start | bytes 479240 | tf_op jit(solution)/shard_map/ppermute | solution.py:434
  61.2 4.7 %collective-permute-done.14 = f16[392,768]{1,0:T(8,128)(2,1)S(1)} collective-permute-done((f16[392,768]{1,0:T(8,128)(2,1)S(1)}, f16[392,768]{1,0:T(8,128)(2,1)S(1)}, u32[]{:S(2)}, u32[]{:S(2)}) %collective-permute-start.14) | collective-permute-done | bytes 602144 | tf_op jit(solution)/shard_map/ppermute | solution.py:434
  65.9 0.1 fusion.42
  66.1 0.1 fusion.2
  66.3 1.6 %collective-permute-start.16 = (f16[200,768]{1,0:T(8,128)(2,1)S(1)}, f16[200,768]{1,0:T(8,128)(2,1)S(1)}, u32[]{:S(2)}, u32[]{:S(2)}) collective-permute-start(f16[200,768]{1,0:T(8,128)(2,1)S(1)} %add_convert_fusion.2), channel_id=1, source_target_pairs={{0,4},{2,6},{4,0},{6,2},{8,12},{10,14},{12,8},{14,10},{16,20},{18,... | collective-permute-start | bytes 921608 | tf_op jit(solution)/shard_map/ppermute | solution.py:434
  67.9 2.0 %collective-permute-done.18 = f16[104,768]{1,0:T(8,128)(2,1)S(1)} collective-permute-done((f16[104,768]{1,0:T(8,128)(2,1)S(1)}, f16[104,768]{1,0:T(8,128)(2,1)S(1)}, u32[]{:S(2)}, u32[]{:S(2)}) %collective-permute-start.18) | collective-permute-done | bytes 159776 | tf_op jit(solution)/shard_map/ppermute | solution.py:434
  70.0 0.1 ceil_reduce_fusion
  70.2 3.1 %collective-permute-done.16 = f16[200,768]{1,0:T(8,128)(2,1)S(1)} collective-permute-done((f16[200,768]{1,0:T(8,128)(2,1)S(1)}, f16[200,768]{1,0:T(8,128)(2,1)S(1)}, u32[]{:S(2)}, u32[]{:S(2)}) %collective-permute-start.16) | collective-permute-done | bytes 307232 | tf_op jit(solution)/shard_map/ppermute | solution.py:434
  73.4 0.1 fusion.8
  73.7 0.1 fusion.15
  73.8 0.1 select_add_fusion
  74.0 2.9 %collective-permute-start.17 = (f16[104,768]{1,0:T(8,128)(2,1)S(1)}, f16[104,768]{1,0:T(8,128)(2,1)S(1)}, u32[]{:S(2)}, u32[]{:S(2)}) collective-permute-start(f16[104,768]{1,0:T(8,128)(2,1)S(1)} %add_convert_fusion.3), channel_id=1, source_target_pairs={{0,16},{2,18},{4,20},{6,22},{8,24},{10,26},{12,28},{14,30},{16,0},... | collective-permute-start | bytes 479240 | tf_op jit(solution)/shard_map/ppermute | solution.py:434
  77.0 5.0 %collective-permute-done.15 = f16[56,768]{1,0:T(8,128)(2,1)S(1)} collective-permute-done((f16[56,768]{1,0:T(8,128)(2,1)S(1)}, f16[56,768]{1,0:T(8,128)(2,1)S(1)}, u32[]{:S(2)}, u32[]{:S(2)}) %collective-permute-start.15) | collective-permute-done | bytes 86048 | tf_op jit(solution)/shard_map/ppermute | solution.py:434
  82.0 0.6 fusion.117
  82.6 1.9 %collective-permute-done.19 = f16[56,768]{1,0:T(8,128)(2,1)S(1)} collective-permute-done((f16[56,768]{1,0:T(8,128)(2,1)S(1)}, f16[56,768]{1,0:T(8,128)(2,1)S(1)}, u32[]{:S(2)}, u32[]{:S(2)}) %collective-permute-start.19) | collective-permute-done | bytes 86048 | tf_op jit(solution)/shard_map/ppermute | solution.py:434
  84.6 0.1 fusion.23
  84.7 0.7 pad_maximum_fusion
  85.5 0.8 fusion.5
  (72 shorter events, 1.8 us)
Async XLA Ops:
  0.6 18.9 %copy-start.5 = (s32[16]{0:T(128)S(1)}, s32[16]{0:T(128)}, u32[]{:S(2)}) copy-start(s32[16]{0:T(128)} %constant.63.clone) | copy-start | bytes 196
  0.6 18.9 %copy-start = (bf16[16,64,1536]{2,1,0:T(8,128)(2,1)S(1)}, bf16[16,64,1536]{2,1,0:T(8,128)(2,1)}, u32[]{:S(2)}) copy-start(bf16[16,64,1536]{2,1,0:T(8,128)(2,1)} %param.10) | copy-start | bytes 9437188
  9.9 4.7 %collective-permute-start = (f32[32,128]{1,0:T(8,128)S(1)}, f32[32,128]{1,0:T(8,128)S(1)}, u32[]{:S(2)}, u32[]{:S(2)}) collective-permute-start(f32[32,128]{1,0:T(8,128)S(1)} %get-tuple-element.25.own_ref), channel_id=1, source_target_pairs={{0,1},{1,0},{2,3},{3,2},{4,5},{5,4},{6,7},{7,6},{8,9},{9,8},{10,11... | collective-permute-start | bytes 49160 | tf_op jit(solution)/shard_map/ppermute | solution.py:437
  14.7 7.4 %collective-permute-start.1 = (bf16[32,768]{1,0:T(8,128)(2,1)S(1)}, bf16[32,768]{1,0:T(8,128)(2,1)S(1)}, u32[]{:S(2)}, u32[]{:S(2)}) collective-permute-start(bf16[32,768]{1,0:T(8,128)(2,1)S(1)} %get-tuple-element.26._.refs_1_), channel_id=1, source_target_pairs={{0,16},{2,18},{4,20},{6,22},{8,24},{10,26},{12,28},{14,30},{16,0},... | collective-permute-start | bytes 147464 | tf_op jit(solution)/shard_map/ppermute | solution.py:434
  17.9 4.2 %collective-permute-start.2 = (bf16[32,768]{1,0:T(8,128)(2,1)S(1)}, bf16[32,768]{1,0:T(8,128)(2,1)S(1)}, u32[]{:S(2)}, u32[]{:S(2)}) collective-permute-start(bf16[32,768]{1,0:T(8,128)(2,1)S(1)} %get-tuple-element.26._.refs_1_), channel_id=1, source_target_pairs={{0,8},{2,10},{4,12},{6,14},{8,0},{10,2},{12,4},{14,6},{16,24},{18,... | collective-permute-start | bytes 147464 | tf_op jit(solution)/shard_map/ppermute | solution.py:434
  19.5 5.9 %collective-permute-start.3 = (bf16[32,768]{1,0:T(8,128)(2,1)S(1)}, bf16[32,768]{1,0:T(8,128)(2,1)S(1)}, u32[]{:S(2)}, u32[]{:S(2)}) collective-permute-start(bf16[32,768]{1,0:T(8,128)(2,1)S(1)} %get-tuple-element.26._.refs_1_), channel_id=1, source_target_pairs={{0,24},{2,26},{4,28},{6,30},{8,16},{10,18},{12,20},{14,22},{16,8},... | collective-permute-start | bytes 147464 | tf_op jit(solution)/shard_map/ppermute | solution.py:434
  19.5 7.5 %copy-start.4 = (s32[32]{0:T(128)S(1)}, s32[32]{0:T(128)}, u32[]{:S(2)}) copy-start(s32[32]{0:T(128)} %constant.62.clone) | copy-start | bytes 388
  19.5 7.5 %copy-start.1 = (bf16[16,32,1536]{2,1,0:T(8,128)(2,1)S(1)}, bf16[16,32,1536]{2,1,0:T(8,128)(2,1)}, u32[]{:S(2)}) copy-start(bf16[16,32,1536]{2,1,0:T(8,128)(2,1)} %param.11) | copy-start | bytes 4718596
  25.4 5.7 %collective-permute-start.4 = (bf16[4,32,768]{2,1,0:T(8,128)(2,1)S(1)}, bf16[4,32,768]{2,1,0:T(8,128)(2,1)S(1)}, u32[]{:S(2)}, u32[]{:S(2)}) collective-permute-start(bf16[4,32,768]{2,1,0:T(8,128)(2,1)S(1)} %shard_map.124._.refs_0_), channel_id=1, source_target_pairs={{0,4},{2,6},{4,0},{6,2},{8,12},{10,14},{12,8},{14,10},{16,20},{18,... | collective-permute-start | bytes 589832 | tf_op jit(solution)/shard_map/ppermute | solution.py:434
  27.0 4.2 %collective-permute-start.5 = (bf16[4,32,768]{2,1,0:T(8,128)(2,1)S(1)}, bf16[4,32,768]{2,1,0:T(8,128)(2,1)S(1)}, u32[]{:S(2)}, u32[]{:S(2)}) collective-permute-start(bf16[4,32,768]{2,1,0:T(8,128)(2,1)S(1)} %shard_map.124._.refs_0_), channel_id=1, source_target_pairs={{0,2},{2,0},{4,6},{6,4},{8,10},{10,8},{12,14},{14,12},{16,18},{18,... | collective-permute-start | bytes 589832 | tf_op jit(solution)/shard_map/ppermute | solution.py:434
  28.5 9.0 %copy-start.3 = (f32[512,768]{1,0:T(8,128)S(1)}, f32[512,768]{1,0:T(8,128)}, u32[]{:S(2)}) copy-start(f32[512,768]{1,0:T(8,128)} %get-tuple-element.35.slope_ref) | copy-start | bytes 4718596
  31.1 1.5 %collective-permute-start.6 = (bf16[4,32,768]{2,1,0:T(8,128)(2,1)S(1)}, bf16[4,32,768]{2,1,0:T(8,128)(2,1)S(1)}, u32[]{:S(2)}, u32[]{:S(2)}) collective-permute-start(bf16[4,32,768]{2,1,0:T(8,128)(2,1)S(1)} %bitcast.8), channel_id=1, source_target_pairs={{0,2},{2,0},{4,6},{6,4},{8,10},{10,8},{12,14},{14,12},{16,18},{18,... | collective-permute-start | bytes 589832 | tf_op jit(solution)/shard_map/ppermute | solution.py:434
  33.0 3.9 %collective-permute-start.7 = (f32[32,256]{1,0:T(8,128)S(1)}, f32[32,256]{1,0:T(8,128)S(1)}, u32[]{:S(2)}, u32[]{:S(2)}) collective-permute-start(f32[32,256]{1,0:T(8,128)S(1)} %get-tuple-element.29.own_ref), channel_id=1, source_target_pairs={{0,1},{1,0},{2,3},{3,2},{4,5},{5,4},{6,7},{7,6},{8,9},{9,8},{10,11... | collective-permute-start | bytes 98312 | tf_op jit(solution)/shard_map/ppermute | solution.py:437
  37.5 1.9 %copy-start.2 = (f32[1024,768]{1,0:T(8,128)S(1)}, f32[1024,768]{1,0:T(8,128)}, u32[]{:S(2)}) copy-start(f32[1024,768]{1,0:T(8,128)} %get-tuple-element.40.slope_ref) | copy-start | bytes 9437188
  39.0 4.1 %collective-permute-start.8 = (f32[392,768]{1,0:T(8,128)S(1)}, f32[392,768]{1,0:T(8,128)S(1)}, u32[]{:S(2)}, u32[]{:S(2)}) collective-permute-start(f32[392,768]{1,0:T(8,128)S(1)} %get-tuple-element.37._), channel_id=1, source_target_pairs={{0,2},{2,0},{4,6},{6,4},{8,10},{10,8},{12,14},{14,12},{16,18},{18,... | collective-permute-start | bytes 3612680 | tf_op jit(solution)/shard_map/ppermute | solution.py:434
  42.3 23.8 %collective-permute-start.13 = (f32[384,768]{1,0:T(8,128)S(1)}, f32[384,768]{1,0:T(8,128)S(1)}, u32[]{:S(2)}, u32[]{:S(2)}) collective-permute-start(f32[384,768]{1,0:T(8,128)S(1)} %get-tuple-element.44), channel_id=1, source_target_pairs={{0,2},{2,0},{4,6},{6,4},{8,10},{10,8},{12,14},{14,12},{16,18},{18,... | collective-permute-start | bytes 3538952 | tf_op jit(solution)/shard_map/ppermute | solution.py:434
  42.6 4.3 %collective-permute-start.11 = (f32[384,768]{1,0:T(8,128)S(1)}, f32[384,768]{1,0:T(8,128)S(1)}, u32[]{:S(2)}, u32[]{:S(2)}) collective-permute-start(f32[384,768]{1,0:T(8,128)S(1)} %get-tuple-element.43), channel_id=1, source_target_pairs={{0,2},{2,0},{4,6},{6,4},{8,10},{10,8},{12,14},{14,12},{16,18},{18,... | collective-permute-start | bytes 3538952 | tf_op jit(solution)/shard_map/ppermute | solution.py:434
  42.9 16.6 %collective-permute-start.10 = (f32[384,768]{1,0:T(8,128)S(1)}, f32[384,768]{1,0:T(8,128)S(1)}, u32[]{:S(2)}, u32[]{:S(2)}) collective-permute-start(f32[384,768]{1,0:T(8,128)S(1)} %get-tuple-element.39), channel_id=1, source_target_pairs={{0,2},{2,0},{4,6},{6,4},{8,10},{10,8},{12,14},{14,12},{16,18},{18,... | collective-permute-start | bytes 3538952 | tf_op jit(solution)/shard_map/ppermute | solution.py:434
  43.5 15.9 %collective-permute-start.9 = (f16[392,768]{1,0:T(8,128)(2,1)S(1)}, f16[392,768]{1,0:T(8,128)(2,1)S(1)}, u32[]{:S(2)}, u32[]{:S(2)}) collective-permute-start(f16[392,768]{1,0:T(8,128)(2,1)S(1)} %add_convert_fusion.1), channel_id=1, source_target_pairs={{0,4},{2,6},{4,0},{6,2},{8,12},{10,14},{12,8},{14,10},{16,20},{18,... | collective-permute-start | bytes 1806344 | tf_op jit(solution)/shard_map/ppermute | solution.py:434
  47.2 18.7 %collective-permute-start.14 = (f16[392,768]{1,0:T(8,128)(2,1)S(1)}, f16[392,768]{1,0:T(8,128)(2,1)S(1)}, u32[]{:S(2)}, u32[]{:S(2)}) collective-permute-start(f16[392,768]{1,0:T(8,128)(2,1)S(1)} %add_convert_fusion), channel_id=1, source_target_pairs={{0,8},{2,10},{4,12},{6,14},{8,0},{10,2},{12,4},{14,6},{16,24},{18,... | collective-permute-start | bytes 1806344 | tf_op jit(solution)/shard_map/ppermute | solution.py:434
  59.7 10.3 %collective-permute-start.12 = (f16[104,768]{1,0:T(8,128)(2,1)S(1)}, f16[104,768]{1,0:T(8,128)(2,1)S(1)}, u32[]{:S(2)}, u32[]{:S(2)}) collective-permute-start(f16[104,768]{1,0:T(8,128)(2,1)S(1)} %add_convert_fusion.5), channel_id=1, source_target_pairs={{0,8},{2,10},{4,12},{6,14},{8,0},{10,2},{12,4},{14,6},{16,24},{18,... | collective-permute-start | bytes 479240 | tf_op jit(solution)/shard_map/ppermute | solution.py:434
  60.0 9.9 %collective-permute-start.18 = (f16[104,768]{1,0:T(8,128)(2,1)S(1)}, f16[104,768]{1,0:T(8,128)(2,1)S(1)}, u32[]{:S(2)}, u32[]{:S(2)}) collective-permute-start(f16[104,768]{1,0:T(8,128)(2,1)S(1)} %add_convert_fusion.4), channel_id=1, source_target_pairs={{0,16},{2,18},{4,20},{6,22},{8,24},{10,26},{12,28},{14,30},{16,0},... | collective-permute-start | bytes 479240 | tf_op jit(solution)/shard_map/ppermute | solution.py:434
  66.3 6.9 %collective-permute-start.16 = (f16[200,768]{1,0:T(8,128)(2,1)S(1)}, f16[200,768]{1,0:T(8,128)(2,1)S(1)}, u32[]{:S(2)}, u32[]{:S(2)}) collective-permute-start(f16[200,768]{1,0:T(8,128)(2,1)S(1)} %add_convert_fusion.2), channel_id=1, source_target_pairs={{0,4},{2,6},{4,0},{6,2},{8,12},{10,14},{12,8},{14,10},{16,20},{18,... | collective-permute-start | bytes 921608 | tf_op jit(solution)/shard_map/ppermute | solution.py:434
  73.9 8.1 %collective-permute-start.15 = (f16[56,768]{1,0:T(8,128)(2,1)S(1)}, f16[56,768]{1,0:T(8,128)(2,1)S(1)}, u32[]{:S(2)}, u32[]{:S(2)}) collective-permute-start(f16[56,768]{1,0:T(8,128)(2,1)S(1)} %add_convert_fusion.7), channel_id=1, source_target_pairs={{0,16},{2,18},{4,20},{6,22},{8,24},{10,26},{12,28},{14,30},{16,0},... | collective-permute-start | bytes 258056 | tf_op jit(solution)/shard_map/ppermute | solution.py:434
  74.0 11.4 %collective-permute-start.17 = (f16[104,768]{1,0:T(8,128)(2,1)S(1)}, f16[104,768]{1,0:T(8,128)(2,1)S(1)}, u32[]{:S(2)}, u32[]{:S(2)}) collective-permute-start(f16[104,768]{1,0:T(8,128)(2,1)S(1)} %add_convert_fusion.3), channel_id=1, source_target_pairs={{0,16},{2,18},{4,20},{6,22},{8,24},{10,26},{12,28},{14,30},{16,0},... | collective-permute-start | bytes 479240 | tf_op jit(solution)/shard_map/ppermute | solution.py:434
  76.9 7.6 %collective-permute-start.19 = (f16[56,768]{1,0:T(8,128)(2,1)S(1)}, f16[56,768]{1,0:T(8,128)(2,1)S(1)}, u32[]{:S(2)}, u32[]{:S(2)}) collective-permute-start(f16[56,768]{1,0:T(8,128)(2,1)S(1)} %add_convert_fusion.6), channel_id=1, source_target_pairs={{0,8},{2,10},{4,12},{6,14},{8,0},{10,2},{12,4},{14,6},{16,24},{18,... | collective-permute-start | bytes 258056 | tf_op jit(solution)/shard_map/ppermute | solution.py:434

commit v5 on v4

--- a/solution.py
+++ b/solution.py
@@ -463,7 +463,7 @@
 
     low = max(bits - 2, 1)
     tops = [1 << b for b in reversed(range(low, bits))]
-    masks = tops + [tops[0] | tops[1]] if len(tops) == 2 else tops
+    masks = [tops[0] | tops[1], *tops] if len(tops) == 2 else tops
     arrived = [swap(sent, mask) for mask in masks]
     image_turned, image_most = turn(image_blocks, image_flat, sent)
     gathered = stack([sent] + arrived, image_most)
@@ -541,26 +541,25 @@
         stays = [(keep[:height], None), (swap(late, 1), None)]
         return stays, [(keep[height:], None), (there[:height], None)], there[height:]
 
-    text_terms = weight_terms(grad, text_slope, text_turned, stat, 1, True, stat)
-    text, text_leaves, stat_there = core_step(*text_terms)
+    image_terms = weight_terms(grad, image_slope, image_turned, stat, 0, True, stat)
+    image, image_leaves, stat_there = core_step(*image_terms)
     start_stat = stat[:3] + stat_there[:3]
-    image_terms = weight_terms(grad, image_slope, image_turned, stat, 0, False, text_terms[0])
-    image, image_leaves, _ = core_step(*image_terms)
-
-    coded, text_in = leave(text_leaves, start_stat, 1, 1, start_stat)
-    coded, image_in = leave(image_leaves, start_stat, 0, image_order[0], coded)
+    text_terms = weight_terms(grad, text_slope, text_turned, stat, 1, False, image_terms[0])
+    text, text_leaves, _ = core_step(*text_terms)
+
+    coded, image_in = leave(image_leaves, start_stat, 0, image_order[0], start_stat)
+    coded, text_in = leave(text_leaves, start_stat, 1, 1, coded)
     text, text_stat = take(text, start_stat, 1, text_in)
     parts = [(terms, text_stat) for terms in halves(text)]
     image, image_stat = take(image, start_stat, 0, image_in)
     for step in range(bits - 2):
         image, image_leaves = halves(image)
         arrivals, before = [], coded
+        coded, image_in = leave(image_leaves, image_stat, 0, image_order[step + 1], before)
         for order, (terms, terms_stat) in zip(text_orders, parts):
             terms, leaves = halves(terms)
-            last, arrival = leave(leaves, terms_stat, 1, order[step], before)
-            before = last if step == 0 else before
+            last, arrival = leave(leaves, terms_stat, 1, order[step], coded if step == 0 else before)
             arrivals.append((terms, terms_stat, arrival))
-        coded, image_in = leave(image_leaves, image_stat, 0, image_order[step + 1], before)
         parts = [take(terms, old, 1, arrival) for terms, old, arrival in arrivals]
         image, image_stat = take(image, image_stat, 0, image_in)
     row = 0.0 * coded[:1].astype(F32)

time: 86.5 us -> 88 us (1.017)
  starting transfers between devices: 19.4 us -> 22 us
    ppermute x18, starting transfers between devices: 14.9 us -> 17.5 us  [swap(): return lax.ppermute(array, 'dp', [(i, i ^ mask) for i in range(cycle)])]
  transfers between devices with their start and end apart: 20 -> 20, of which waited for: 12 -> 13; matrix products, arithmetic and copies ran while one was open for 4% -> 4% of each run, Pallas kernels for 8% -> 7%
where the time goes in v5:
time: 88 us; the launch traced here: 87.8 us
  waiting for transfers between devices  38.5 us (44%)
  starting transfers between devices  22 us (25%)
  Pallas kernels  18.7 us (21%)
  other arithmetic  4.87 us (6%)
  between operations  3.65 us (4%)
    ppermute x18, waiting for transfers between devices, swap(): return lax.ppermute(array, 'dp', [(i, i ^ mask) for i in range(cycle)])  37 us
    ppermute x18, starting transfers between devices, swap(): return lax.ppermute(array, 'dp', [(i, i ^ mask) for i in range(cycle)])  17.5 us
    pallas_call x1, Pallas kernels, forward(): pl.pallas_call(functools.partial(forward_kernel, (rows_i // samples, rows...  9.24 us
    ppermute x2, starting transfers between devices, swap_halves(): return lax.ppermute(array, 'mp', [(0, 1), (1, 0)])  4.55 us
    pallas_call x2, Pallas kernels, weight_terms(): pl.pallas_call(functools.partial(weight_kernel, base, carries), out_shape...  4.42 us
    pallas_call x2, Pallas kernels, turn(): pl.pallas_call(turn_kernel, out_shape=(jax.ShapeDtypeStruct((depth, rows)...  4.07 us
  transfers between devices with their start and end apart: 20, of which 13 were waited for; matrix products, arithmetic and copies ran while one was open for 4% of the time, Pallas kernels for 7%

profile of v5, /device:TPU:0, one launch (start us, length us, event | category | flops | bytes accessed | tf_op | source)
XLA Modules:
  0.0 87.8 jit_solution(16031708130420732924)
XLA Ops:
  0.7 9.2 %shard_map.121 = (f32[32,768]{1,0:T(8,128)S(1)}, f32[32,128]{1,0:T(8,128)S(1)}, f32[1024,768]{1,0:T(8,128)}, f32[512,768]{1,0:T(8,128)}) custom-call(s32[1]{0:T(128)} %bitcast.1.place_ref, bf16[1024,1536]{1,0:T(8,128)(2,1)} %bitcast.4, bf16[512,1536]{1,0:T(8,128)(2,1)} %bitcast.6, bf16[1536,768]{1,0:T(8,128)(2,1)} %image_w_hbm.1, bf16[1536,768]{1,0:T(8,128)(2,1)} %text_w_hbm.1), custom_call_target="tpu_custom_call" | custom-call | flops 3623878656 | bytes 14155776 | tf_op jit(solution)/shard_map/pallas_call | solution.py:137
  9.9 3.0 %collective-permute-start = (f32[32,128]{1,0:T(8,128)S(1)}, f32[32,128]{1,0:T(8,128)S(1)}, u32[]{:S(2)}, u32[]{:S(2)}) collective-permute-start(f32[32,128]{1,0:T(8,128)S(1)} %get-tuple-element.25.own_ref), channel_id=1, source_target_pairs={{0,1},{1,0},{2,3},{3,2},{4,5},{5,4},{6,7},{7,6},{8,9},{9,8},{10,11... | collective-permute-start | bytes 49160 | tf_op jit(solution)/shard_map/ppermute | solution.py:437
  13.6 1.1 %collective-permute-done.other_ref = f32[32,128]{1,0:T(8,128)S(1)} collective-permute-done((f32[32,128]{1,0:T(8,128)S(1)}, f32[32,128]{1,0:T(8,128)S(1)}, u32[]{:S(2)}, u32[]{:S(2)}) %collective-permute-start) | collective-permute-done | bytes 16416 | tf_op jit(solution)/shard_map/ppermute | solution.py:437
  14.7 4.2 %collective-permute-start.1 = (bf16[32,768]{1,0:T(8,128)(2,1)S(1)}, bf16[32,768]{1,0:T(8,128)(2,1)S(1)}, u32[]{:S(2)}, u32[]{:S(2)}) collective-permute-start(bf16[32,768]{1,0:T(8,128)(2,1)S(1)} %get-tuple-element.26._.refs_1_), channel_id=1, source_target_pairs={{0,24},{2,26},{4,28},{6,30},{8,16},{10,18},{12,20},{14,22},{16,8},... | collective-permute-start | bytes 147464 | tf_op jit(solution)/shard_map/ppermute | solution.py:434
  18.9 0.6 collective-permute-start.3
  19.6 2.6 %shard_map.123 = (bf16[1536,1024]{1,0:T(8,128)(2,1)S(1)}, f32[8,128]{1,0:T(8,128)S(1)}) custom-call(s32[16]{0:T(128)S(1)} %broadcast_xor_fusion.1.source_ref, bf16[1024,1536]{1,0:T(8,128)(2,1)S(1)} %bitcast.5, bf16[32,768]{1,0:T(8,128)(2,1)S(1)} %get-tuple-element.26._.refs_1_), custom_call_target="tpu_custom_call" | custom-call | bytes 6291456 | tf_op jit(solution)/shard_map/pallas_call | solution.py:230
  22.2 1.7 %collective-permute-done.2.refs_3_ = bf16[32,768]{1,0:T(8,128)(2,1)S(1)} collective-permute-done((bf16[32,768]{1,0:T(8,128)(2,1)S(1)}, bf16[32,768]{1,0:T(8,128)(2,1)S(1)}, u32[]{:S(2)}, u32[]{:S(2)}) %collective-permute-start.2) | collective-permute-done | bytes 49184 | tf_op jit(solution)/shard_map/ppermute | solution.py:434
  23.9 1.6 %collective-permute-start.4 = (bf16[4,32,768]{2,1,0:T(8,128)(2,1)S(1)}, bf16[4,32,768]{2,1,0:T(8,128)(2,1)S(1)}, u32[]{:S(2)}, u32[]{:S(2)}) collective-permute-start(bf16[4,32,768]{2,1,0:T(8,128)(2,1)S(1)} %shard_map.124._.refs_0_), channel_id=1, source_target_pairs={{0,4},{2,6},{4,0},{6,2},{8,12},{10,14},{12,8},{14,10},{16,20},{18,... | collective-permute-start | bytes 589832 | tf_op jit(solution)/shard_map/ppermute | solution.py:434
  25.6 1.5 %shard_map.125 = (bf16[1536,512]{1,0:T(8,128)(2,1)S(1)}, f32[8,128]{1,0:T(8,128)S(1)}) custom-call(s32[32]{0:T(128)S(1)} %broadcast_xor_fusion.source_ref, bf16[512,1536]{1,0:T(8,128)(2,1)S(1)} %bitcast.7, bf16[4,32,768]{2,1,0:T(8,128)(2,1)S(1)} %shard_map.124._.refs_0_), custom_call_target="tpu_custom_call" | custom-call | bytes 3145728 | tf_op jit(solution)/shard_map/pallas_call | solution.py:230
  27.1 2.6 %collective-permute-done.4.refs_1_ = bf16[4,32,768]{2,1,0:T(8,128)(2,1)S(1)} collective-permute-done((bf16[4,32,768]{2,1,0:T(8,128)(2,1)S(1)}, bf16[4,32,768]{2,1,0:T(8,128)(2,1)S(1)}, u32[]{:S(2)}, u32[]{:S(2)}) %collective-permute-start.4) | collective-permute-done | bytes 196640 | tf_op jit(solution)/shard_map/ppermute | solution.py:434
  29.8 1.4 %collective-permute-done.6.refs_3_ = bf16[4,32,768]{2,1,0:T(8,128)(2,1)S(1)} collective-permute-done((bf16[4,32,768]{2,1,0:T(8,128)(2,1)S(1)}, bf16[4,32,768]{2,1,0:T(8,128)(2,1)S(1)}, u32[]{:S(2)}, u32[]{:S(2)}) %collective-permute-start.6) | collective-permute-done | bytes 196640 | tf_op jit(solution)/shard_map/ppermute | solution.py:434
  31.2 0.4 shard_map.127
  31.6 1.5 %collective-permute-start.7 = (f32[32,256]{1,0:T(8,128)S(1)}, f32[32,256]{1,0:T(8,128)S(1)}, u32[]{:S(2)}, u32[]{:S(2)}) collective-permute-start(f32[32,256]{1,0:T(8,128)S(1)} %get-tuple-element.29.own_ref), channel_id=1, source_target_pairs={{0,1},{1,0},{2,3},{3,2},{4,5},{5,4},{6,7},{7,6},{8,9},{9,8},{10,11... | collective-permute-start | bytes 98312 | tf_op jit(solution)/shard_map/ppermute | solution.py:437
  35.0 0.5 collective-permute-done.7.other_ref
  35.5 0.5 shard_map.128
  36.0 2.8 %shard_map.129 = (f32[392,768]{1,0:T(8,128)S(1)}, f32[384,768]{1,0:T(8,128)S(1)}, f32[768,768]{1,0:T(8,128)S(1)}) custom-call(f32[32,768]{1,0:T(8,128)S(1)} %get-tuple-element.34.grad_ref, f32[1024,768]{1,0:T(8,128)S(1)} %copy-done.3, bf16[1536,1024]{1,0:T(8,128)(2,1)S(1)} %get-tuple-element.36.turned_ref, f32[8,768]{1,0:T(8,128)S(1)} %get-tuple-element.33.stat_ref._, ...), custom_call_target="tpu_custom_call" | custom-call | flops 2415919104 | bytes 11010048 | tf_op jit(solution)/shard_map/pallas_call | solution.py:393
  39.0 1.6 %shard_map.130 = (f32[384,768]{1,0:T(8,128)S(1)}, f32[384,768]{1,0:T(8,128)S(1)}, f32[768,768]{1,0:T(8,128)S(1)}) custom-call(f32[32,768]{1,0:T(8,128)S(1)} %get-tuple-element.34.grad_ref, f32[512,768]{1,0:T(8,128)S(1)} %copy-done.1, bf16[1536,512]{1,0:T(8,128)(2,1)S(1)} %get-tuple-element.39.turned_ref, f32[8,768]{1,0:T(8,128)S(1)} %get-tuple-element.33.stat_ref._, ...), custom_call_target="tpu_custom_call" | custom-call | flops 1207959552 | bytes 7864320 | tf_op jit(solution)/shard_map/pallas_call | solution.py:393
  40.6 0.5 collective-permute-start.9
  41.2 0.4 collective-permute-start.11
  41.7 0.1 collective-permute-done.8
  41.8 0.1 fusion.34
  41.9 0.2 fusion
  42.3 0.2 collective-permute-start.13
  42.5 1.1 %collective-permute-done.9 = f32[384,768]{1,0:T(8,128)S(1)} collective-permute-done((f32[384,768]{1,0:T(8,128)S(1)}, f32[384,768]{1,0:T(8,128)S(1)}, u32[]{:S(2)}, u32[]{:S(2)}) %collective-permute-start.9) | collective-permute-done | bytes 1179680 | tf_op jit(solution)/shard_map/ppermute | solution.py:434
  43.6 0.1 add_multiply_fusion
  43.9 1.6 %collective-permute-start.10 = (f16[392,768]{1,0:T(8,128)(2,1)S(1)}, f16[392,768]{1,0:T(8,128)(2,1)S(1)}, u32[]{:S(2)}, u32[]{:S(2)}) collective-permute-start(f16[392,768]{1,0:T(8,128)(2,1)S(1)} %add_convert_fusion), channel_id=1, source_target_pairs={{0,4},{2,6},{4,0},{6,2},{8,12},{10,14},{12,8},{14,10},{16,20},{18,... | collective-permute-start | bytes 1806344 | tf_op jit(solution)/shard_map/ppermute | solution.py:434
  45.6 12.4 %collective-permute-done.13 = f16[392,768]{1,0:T(8,128)(2,1)S(1)} collective-permute-done((f16[392,768]{1,0:T(8,128)(2,1)S(1)}, f16[392,768]{1,0:T(8,128)(2,1)S(1)}, u32[]{:S(2)}, u32[]{:S(2)}) %collective-permute-start.13) | collective-permute-done | bytes 602144 | tf_op jit(solution)/shard_map/ppermute | solution.py:434
  58.0 0.1 fusion.38
  58.1 0.1 fusion.2
  58.4 1.5 %collective-permute-done.10 = f16[392,768]{1,0:T(8,128)(2,1)S(1)} collective-permute-done((f16[392,768]{1,0:T(8,128)(2,1)S(1)}, f16[392,768]{1,0:T(8,128)(2,1)S(1)}, u32[]{:S(2)}, u32[]{:S(2)}) %collective-permute-start.10) | collective-permute-done | bytes 602144 | tf_op jit(solution)/shard_map/ppermute | solution.py:434
  59.9 0.1 fusion.42
  60.0 0.1 fusion.12
  60.3 0.4 collective-permute-start.14
  60.6 1.5 %collective-permute-start.16 = (f16[200,768]{1,0:T(8,128)(2,1)S(1)}, f16[200,768]{1,0:T(8,128)(2,1)S(1)}, u32[]{:S(2)}, u32[]{:S(2)}) collective-permute-start(f16[200,768]{1,0:T(8,128)(2,1)S(1)} %add_convert_fusion.2), channel_id=1, source_target_pairs={{0,4},{2,6},{4,0},{6,2},{8,12},{10,14},{12,8},{14,10},{16,20},{18,... | collective-permute-start | bytes 921608 | tf_op jit(solution)/shard_map/ppermute | solution.py:434
  62.2 2.4 %collective-permute-start.18 = (f16[104,768]{1,0:T(8,128)(2,1)S(1)}, f16[104,768]{1,0:T(8,128)(2,1)S(1)}, u32[]{:S(2)}, u32[]{:S(2)}) collective-permute-start(f16[104,768]{1,0:T(8,128)(2,1)S(1)} %add_convert_fusion.3), channel_id=1, source_target_pairs={{0,16},{2,18},{4,20},{6,22},{8,24},{10,26},{12,28},{14,30},{16,0},... | collective-permute-start | bytes 479240 | tf_op jit(solution)/shard_map/ppermute | solution.py:434
  64.6 3.5 %collective-permute-done.14 = f16[104,768]{1,0:T(8,128)(2,1)S(1)} collective-permute-done((f16[104,768]{1,0:T(8,128)(2,1)S(1)}, f16[104,768]{1,0:T(8,128)(2,1)S(1)}, u32[]{:S(2)}, u32[]{:S(2)}) %collective-permute-start.14) | collective-permute-done | bytes 159776 | tf_op jit(solution)/shard_map/ppermute | solution.py:434
  68.1 3.7 %collective-permute-done.18 = f16[104,768]{1,0:T(8,128)(2,1)S(1)} collective-permute-done((f16[104,768]{1,0:T(8,128)(2,1)S(1)}, f16[104,768]{1,0:T(8,128)(2,1)S(1)}, u32[]{:S(2)}, u32[]{:S(2)}) %collective-permute-start.18) | collective-permute-done | bytes 159776 | tf_op jit(solution)/shard_map/ppermute | solution.py:434
  71.7 0.1 ceil_reduce_fusion
  72.1 0.1 fusion.15
  72.3 0.3 collective-permute-start.19
  72.6 3.4 %collective-permute-start.15 = (f16[56,768]{1,0:T(8,128)(2,1)S(1)}, f16[56,768]{1,0:T(8,128)(2,1)S(1)}, u32[]{:S(2)}, u32[]{:S(2)}) collective-permute-start(f16[56,768]{1,0:T(8,128)(2,1)S(1)} %add_convert_fusion.7), channel_id=1, source_target_pairs={{0,16},{2,18},{4,20},{6,22},{8,24},{10,26},{12,28},{14,30},{16,0},... | collective-permute-start | bytes 258056 | tf_op jit(solution)/shard_map/ppermute | solution.py:434
  76.1 0.1 fusion.10
  76.4 7.3 %collective-permute-done.15 = f16[56,768]{1,0:T(8,128)(2,1)S(1)} collective-permute-done((f16[56,768]{1,0:T(8,128)(2,1)S(1)}, f16[56,768]{1,0:T(8,128)(2,1)S(1)}, u32[]{:S(2)}, u32[]{:S(2)}) %collective-permute-start.15) | collective-permute-done | bytes 86048 | tf_op jit(solution)/shard_map/ppermute | solution.py:434
  83.7 0.6 fusion.111
  84.4 0.1 fusion.23
  84.5 0.7 pad_maximum_fusion
  85.3 1.7 %collective-permute-done.17 = f16[104,768]{1,0:T(8,128)(2,1)S(1)} collective-permute-done((f16[104,768]{1,0:T(8,128)(2,1)S(1)}, f16[104,768]{1,0:T(8,128)(2,1)S(1)}, u32[]{:S(2)}, u32[]{:S(2)}) %collective-permute-start.17) | collective-permute-done | bytes 159776 | tf_op jit(solution)/shard_map/ppermute | solution.py:434
  87.0 0.8 fusion.7
  (69 shorter events, 1.7 us)
Async XLA Ops:
  0.6 18.9 %copy-start.5 = (s32[16]{0:T(128)S(1)}, s32[16]{0:T(128)}, u32[]{:S(2)}) copy-start(s32[16]{0:T(128)} %constant.63.clone) | copy-start | bytes 196
  0.6 18.9 %copy-start = (bf16[16,64,1536]{2,1,0:T(8,128)(2,1)S(1)}, bf16[16,64,1536]{2,1,0:T(8,128)(2,1)}, u32[]{:S(2)}) copy-start(bf16[16,64,1536]{2,1,0:T(8,128)(2,1)} %param.10) | copy-start | bytes 9437188
  9.9 4.7 %collective-permute-start = (f32[32,128]{1,0:T(8,128)S(1)}, f32[32,128]{1,0:T(8,128)S(1)}, u32[]{:S(2)}, u32[]{:S(2)}) collective-permute-start(f32[32,128]{1,0:T(8,128)S(1)} %get-tuple-element.25.own_ref), channel_id=1, source_target_pairs={{0,1},{1,0},{2,3},{3,2},{4,5},{5,4},{6,7},{7,6},{8,9},{9,8},{10,11... | collective-permute-start | bytes 49160 | tf_op jit(solution)/shard_map/ppermute | solution.py:437
  14.7 7.4 %collective-permute-start.1 = (bf16[32,768]{1,0:T(8,128)(2,1)S(1)}, bf16[32,768]{1,0:T(8,128)(2,1)S(1)}, u32[]{:S(2)}, u32[]{:S(2)}) collective-permute-start(bf16[32,768]{1,0:T(8,128)(2,1)S(1)} %get-tuple-element.26._.refs_1_), channel_id=1, source_target_pairs={{0,24},{2,26},{4,28},{6,30},{8,16},{10,18},{12,20},{14,22},{16,8},... | collective-permute-start | bytes 147464 | tf_op jit(solution)/shard_map/ppermute | solution.py:434
  18.9 5.0 %collective-permute-start.2 = (bf16[32,768]{1,0:T(8,128)(2,1)S(1)}, bf16[32,768]{1,0:T(8,128)(2,1)S(1)}, u32[]{:S(2)}, u32[]{:S(2)}) collective-permute-start(bf16[32,768]{1,0:T(8,128)(2,1)S(1)} %get-tuple-element.26._.refs_1_), channel_id=1, source_target_pairs={{0,16},{2,18},{4,20},{6,22},{8,24},{10,26},{12,28},{14,30},{16,0},... | collective-permute-start | bytes 147464 | tf_op jit(solution)/shard_map/ppermute | solution.py:434
  18.9 5.0 %collective-permute-start.3 = (bf16[32,768]{1,0:T(8,128)(2,1)S(1)}, bf16[32,768]{1,0:T(8,128)(2,1)S(1)}, u32[]{:S(2)}, u32[]{:S(2)}) collective-permute-start(bf16[32,768]{1,0:T(8,128)(2,1)S(1)} %get-tuple-element.26._.refs_1_), channel_id=1, source_target_pairs={{0,8},{2,10},{4,12},{6,14},{8,0},{10,2},{12,4},{14,6},{16,24},{18,... | collective-permute-start | bytes 147464 | tf_op jit(solution)/shard_map/ppermute | solution.py:434
  19.6 6.0 %copy-start.4 = (s32[32]{0:T(128)S(1)}, s32[32]{0:T(128)}, u32[]{:S(2)}) copy-start(s32[32]{0:T(128)} %constant.62.clone) | copy-start | bytes 388
  19.6 6.0 %copy-start.2 = (bf16[16,32,1536]{2,1,0:T(8,128)(2,1)S(1)}, bf16[16,32,1536]{2,1,0:T(8,128)(2,1)}, u32[]{:S(2)}) copy-start(bf16[16,32,1536]{2,1,0:T(8,128)(2,1)} %param.11) | copy-start | bytes 4718596
  23.9 5.7 %collective-permute-start.4 = (bf16[4,32,768]{2,1,0:T(8,128)(2,1)S(1)}, bf16[4,32,768]{2,1,0:T(8,128)(2,1)S(1)}, u32[]{:S(2)}, u32[]{:S(2)}) collective-permute-start(bf16[4,32,768]{2,1,0:T(8,128)(2,1)S(1)} %shard_map.124._.refs_0_), channel_id=1, source_target_pairs={{0,4},{2,6},{4,0},{6,2},{8,12},{10,14},{12,8},{14,10},{16,20},{18,... | collective-permute-start | bytes 589832 | tf_op jit(solution)/shard_map/ppermute | solution.py:434
  25.5 4.2 %collective-permute-start.5 = (bf16[4,32,768]{2,1,0:T(8,128)(2,1)S(1)}, bf16[4,32,768]{2,1,0:T(8,128)(2,1)S(1)}, u32[]{:S(2)}, u32[]{:S(2)}) collective-permute-start(bf16[4,32,768]{2,1,0:T(8,128)(2,1)S(1)} %shard_map.124._.refs_0_), channel_id=1, source_target_pairs={{0,2},{2,0},{4,6},{6,4},{8,10},{10,8},{12,14},{14,12},{16,18},{18,... | collective-permute-start | bytes 589832 | tf_op jit(solution)/shard_map/ppermute | solution.py:434
  25.5 10.5 %copy-start.3 = (f32[1024,768]{1,0:T(8,128)S(1)}, f32[1024,768]{1,0:T(8,128)}, u32[]{:S(2)}) copy-start(f32[1024,768]{1,0:T(8,128)} %get-tuple-element.35.slope_ref) | copy-start | bytes 9437188
  29.7 1.5 %collective-permute-start.6 = (bf16[4,32,768]{2,1,0:T(8,128)(2,1)S(1)}, bf16[4,32,768]{2,1,0:T(8,128)(2,1)S(1)}, u32[]{:S(2)}, u32[]{:S(2)}) collective-permute-start(bf16[4,32,768]{2,1,0:T(8,128)(2,1)S(1)} %bitcast.8), channel_id=1, source_target_pairs={{0,2},{2,0},{4,6},{6,4},{8,10},{10,8},{12,14},{14,12},{16,18},{18,... | collective-permute-start | bytes 589832 | tf_op jit(solution)/shard_map/ppermute | solution.py:434
  31.6 3.9 %collective-permute-start.7 = (f32[32,256]{1,0:T(8,128)S(1)}, f32[32,256]{1,0:T(8,128)S(1)}, u32[]{:S(2)}, u32[]{:S(2)}) collective-permute-start(f32[32,256]{1,0:T(8,128)S(1)} %get-tuple-element.29.own_ref), channel_id=1, source_target_pairs={{0,1},{1,0},{2,3},{3,2},{4,5},{5,4},{6,7},{7,6},{8,9},{9,8},{10,11... | collective-permute-start | bytes 98312 | tf_op jit(solution)/shard_map/ppermute | solution.py:437
  36.0 2.9 %copy-start.1 = (f32[512,768]{1,0:T(8,128)S(1)}, f32[512,768]{1,0:T(8,128)}, u32[]{:S(2)}) copy-start(f32[512,768]{1,0:T(8,128)} %get-tuple-element.38.slope_ref) | copy-start | bytes 4718596
  38.8 2.9 %collective-permute-start.8 = (f32[392,768]{1,0:T(8,128)S(1)}, f32[392,768]{1,0:T(8,128)S(1)}, u32[]{:S(2)}, u32[]{:S(2)}) collective-permute-start(f32[392,768]{1,0:T(8,128)S(1)} %get-tuple-element.37._), channel_id=1, source_target_pairs={{0,2},{2,0},{4,6},{6,4},{8,10},{10,8},{12,14},{14,12},{16,18},{18,... | collective-permute-start | bytes 3612680 | tf_op jit(solution)/shard_map/ppermute | solution.py:434
  40.6 3.0 %collective-permute-start.9 = (f32[384,768]{1,0:T(8,128)S(1)}, f32[384,768]{1,0:T(8,128)S(1)}, u32[]{:S(2)}, u32[]{:S(2)}) collective-permute-start(f32[384,768]{1,0:T(8,128)S(1)} %get-tuple-element.41), channel_id=1, source_target_pairs={{0,2},{2,0},{4,6},{6,4},{8,10},{10,8},{12,14},{14,12},{16,18},{18,... | collective-permute-start | bytes 3538952 | tf_op jit(solution)/shard_map/ppermute | solution.py:434
  41.2 17.0 %collective-permute-start.12 = (f32[384,768]{1,0:T(8,128)S(1)}, f32[384,768]{1,0:T(8,128)S(1)}, u32[]{:S(2)}, u32[]{:S(2)}) collective-permute-start(f32[384,768]{1,0:T(8,128)S(1)} %get-tuple-element.44), channel_id=1, source_target_pairs={{0,2},{2,0},{4,6},{6,4},{8,10},{10,8},{12,14},{14,12},{16,18},{18,... | collective-permute-start | bytes 3538952 | tf_op jit(solution)/shard_map/ppermute | solution.py:434
  41.2 18.8 %collective-permute-start.11 = (f32[384,768]{1,0:T(8,128)S(1)}, f32[384,768]{1,0:T(8,128)S(1)}, u32[]{:S(2)}, u32[]{:S(2)}) collective-permute-start(f32[384,768]{1,0:T(8,128)S(1)} %get-tuple-element.43), channel_id=1, source_target_pairs={{0,2},{2,0},{4,6},{6,4},{8,10},{10,8},{12,14},{14,12},{16,18},{18,... | collective-permute-start | bytes 3538952 | tf_op jit(solution)/shard_map/ppermute | solution.py:434
  42.3 15.7 %collective-permute-start.13 = (f16[392,768]{1,0:T(8,128)(2,1)S(1)}, f16[392,768]{1,0:T(8,128)(2,1)S(1)}, u32[]{:S(2)}, u32[]{:S(2)}) collective-permute-start(f16[392,768]{1,0:T(8,128)(2,1)S(1)} %add_convert_fusion.1), channel_id=1, source_target_pairs={{0,8},{2,10},{4,12},{6,14},{8,0},{10,2},{12,4},{14,6},{16,24},{18,... | collective-permute-start | bytes 1806344 | tf_op jit(solution)/shard_map/ppermute | solution.py:434
  43.9 15.9 %collective-permute-start.10 = (f16[392,768]{1,0:T(8,128)(2,1)S(1)}, f16[392,768]{1,0:T(8,128)(2,1)S(1)}, u32[]{:S(2)}, u32[]{:S(2)}) collective-permute-start(f16[392,768]{1,0:T(8,128)(2,1)S(1)} %add_convert_fusion), channel_id=1, source_target_pairs={{0,4},{2,6},{4,0},{6,2},{8,12},{10,14},{12,8},{14,10},{16,20},{18,... | collective-permute-start | bytes 1806344 | tf_op jit(solution)/shard_map/ppermute | solution.py:434
  60.3 7.8 %collective-permute-start.14 = (f16[104,768]{1,0:T(8,128)(2,1)S(1)}, f16[104,768]{1,0:T(8,128)(2,1)S(1)}, u32[]{:S(2)}, u32[]{:S(2)}) collective-permute-start(f16[104,768]{1,0:T(8,128)(2,1)S(1)} %add_convert_fusion.5), channel_id=1, source_target_pairs={{0,8},{2,10},{4,12},{6,14},{8,0},{10,2},{12,4},{14,6},{16,24},{18,... | collective-permute-start | bytes 479240 | tf_op jit(solution)/shard_map/ppermute | solution.py:434
  60.6 11.3 %collective-permute-start.16 = (f16[200,768]{1,0:T(8,128)(2,1)S(1)}, f16[200,768]{1,0:T(8,128)(2,1)S(1)}, u32[]{:S(2)}, u32[]{:S(2)}) collective-permute-start(f16[200,768]{1,0:T(8,128)(2,1)S(1)} %add_convert_fusion.2), channel_id=1, source_target_pairs={{0,4},{2,6},{4,0},{6,2},{8,12},{10,14},{12,8},{14,10},{16,20},{18,... | collective-permute-start | bytes 921608 | tf_op jit(solution)/shard_map/ppermute | solution.py:434
  62.2 9.5 %collective-permute-start.18 = (f16[104,768]{1,0:T(8,128)(2,1)S(1)}, f16[104,768]{1,0:T(8,128)(2,1)S(1)}, u32[]{:S(2)}, u32[]{:S(2)}) collective-permute-start(f16[104,768]{1,0:T(8,128)(2,1)S(1)} %add_convert_fusion.3), channel_id=1, source_target_pairs={{0,16},{2,18},{4,20},{6,22},{8,24},{10,26},{12,28},{14,30},{16,0},... | collective-permute-start | bytes 479240 | tf_op jit(solution)/shard_map/ppermute | solution.py:434
  72.3 12.0 %collective-permute-start.19 = (f16[56,768]{1,0:T(8,128)(2,1)S(1)}, f16[56,768]{1,0:T(8,128)(2,1)S(1)}, u32[]{:S(2)}, u32[]{:S(2)}) collective-permute-start(f16[56,768]{1,0:T(8,128)(2,1)S(1)} %add_convert_fusion.6), channel_id=1, source_target_pairs={{0,8},{2,10},{4,12},{6,14},{8,0},{10,2},{12,4},{14,6},{16,24},{18,... | collective-permute-start | bytes 258056 | tf_op jit(solution)/shard_map/ppermute | solution.py:434
  72.6 11.1 %collective-permute-start.15 = (f16[56,768]{1,0:T(8,128)(2,1)S(1)}, f16[56,768]{1,0:T(8,128)(2,1)S(1)}, u32[]{:S(2)}, u32[]{:S(2)}) collective-permute-start(f16[56,768]{1,0:T(8,128)(2,1)S(1)} %add_convert_fusion.7), channel_id=1, source_target_pairs={{0,16},{2,18},{4,20},{6,22},{8,24},{10,26},{12,28},{14,30},{16,0},... | collective-permute-start | bytes 258056 | tf_op jit(solution)/shard_map/ppermute | solution.py:434
  76.4 10.6 %collective-permute-start.17 = (f16[104,768]{1,0:T(8,128)(2,1)S(1)}, f16[104,768]{1,0:T(8,128)(2,1)S(1)}, u32[]{:S(2)}, u32[]{:S(2)}) collective-permute-start(f16[104,768]{1,0:T(8,128)(2,1)S(1)} %add_convert_fusion.4), channel_id=1, source_target_pairs={{0,16},{2,18},{4,20},{6,22},{8,24},{10,26},{12,28},{14,30},{16,0},... | collective-permute-start | bytes 479240 | tf_op jit(solution)/shard_map/ppermute | solution.py:434

commit v6 on v5

--- a/solution.py
+++ b/solution.py
@@ -521,14 +521,18 @@
         half = terms[0][0].shape[0] // 2
         return [[(term[rows], unit) for term, unit in terms] for rows in (slice(half), slice(half, None))]
 
-    def leave(terms, stat, tower, bit, after):
-        rows = terms[0][0].shape[0]
-        exponents = exponents_of(stat)
-        factor = HALF_MAX * jnp.exp2(-exponents[tower]) + 0.0 * after[:1].astype(F32)
-        coded = sum_of(terms) * factor
+    def coded_of(terms, stat, tower, after):
+        factor = HALF_MAX * jnp.exp2(-exponents_of(stat)[tower]) + 0.0 * after[:1].astype(F32)
+        return sum_of(terms) * factor
+
+    def with_foot(coded, exponents, stat):
+        rows = coded.shape[0]
         foot = footer(exponents, stat) + 0.0 * coded[:1]
         coded = jnp.pad(coded, ((0, FOOT), (0, 0))) + jnp.pad(foot, ((rows, 0), (0, 0)))
-        coded = coded.astype(jnp.float16)
+        return coded.astype(jnp.float16)
+
+    def leave(terms, stat, tower, bit, after):
+        coded = with_foot(coded_of(terms, stat, tower, after), exponents_of(stat), stat)
         return coded, swap(coded, 1 << bit)
 
     def take(terms, stat, tower, coming):
@@ -551,20 +555,43 @@
     coded, text_in = leave(text_leaves, start_stat, 1, 1, coded)
     text, text_stat = take(text, start_stat, 1, text_in)
     parts = [(terms, text_stat) for terms in halves(text)]
+    image_in = image_in.astype(F32) + 0.0 * coded[:1].astype(F32)
     image, image_stat = take(image, start_stat, 0, image_in)
-    for step in range(bits - 2):
+    for step in range(bits - 3):
         image, image_leaves = halves(image)
-        arrivals, before = [], coded
-        coded, image_in = leave(image_leaves, image_stat, 0, image_order[step + 1], before)
-        for order, (terms, terms_stat) in zip(text_orders, parts):
-            terms, leaves = halves(terms)
-            last, arrival = leave(leaves, terms_stat, 1, order[step], coded if step == 0 else before)
-            arrivals.append((terms, terms_stat, arrival))
-        parts = [take(terms, old, 1, arrival) for terms, old, arrival in arrivals]
+        (first, first_stat), (second, second_stat) = parts
+        first, first_leaves = halves(first)
+        second, second_leaves = halves(second)
+        coded, image_in = leave(image_leaves, image_stat, 0, image_order[step + 1], coded)
+        coded, second_in = leave(second_leaves, second_stat, 1, text_orders[1][step], coded)
+        coded, first_in = leave(first_leaves, first_stat, 1, text_orders[0][step], coded)
+        parts = [(first, first_stat, first_in), (second, second_stat, second_in)]
+        if step < bits - 4:
+            parts = [take(terms, old, 1, arrival) for terms, old, arrival in parts]
         image, image_stat = take(image, image_stat, 0, image_in)
+
+    (first, first_stat, first_in), (second, second_stat, second_in) = parts
+    first, first_stat = take(first, first_stat, 1, first_in)
+    first, first_leaves = halves(first)
+    image, image_leaves = halves(image)
+    image_coded = coded_of(image_leaves, image_stat, 0, coded)
+    first_coded = coded_of(first_leaves, first_stat, 1, coded)
+    exponents = [exponents_of(image_stat)[0], exponents_of(first_stat)[1]]
+    rows = image_coded.shape[0]
+    both = jnp.pad(image_coded, ((0, first_coded.shape[0]), (0, 0)))
+    both = both + jnp.pad(first_coded, ((rows, 0), (0, 0)))
+    both = with_foot(both, exponents, first_stat)
+    both_in = swap(both, 1 << image_order[-1])
+    second_in = second_in.astype(F32) + 0.0 * both[:1].astype(F32)
+    second, second_stat = take(second, second_stat, 1, second_in)
+    second, second_leaves = halves(second)
+    coded, second_in = leave(second_leaves, second_stat, 1, text_orders[1][-1], coded)
+    second, _ = take(second, second_stat, 1, second_in)
+    first, first_stat = take(first, first_stat, 1, both_in[rows:])
+    image, _ = take(image, image_stat, 0, jnp.concatenate([both_in[:rows], both_in[-FOOT:]]))
     row = 0.0 * coded[:1].astype(F32)
-    text = jnp.concatenate([sum_of(terms) + row for terms, _ in parts])
-    loss = jnp.max(parts[0][1][:1] + row)
+    text = jnp.concatenate([sum_of(first) + row, sum_of(second)])
+    loss = jnp.max(first_stat[:1] + row)
     return (loss, sum_of(image), text)
 
 

time: 88 us -> 87.5 us (level)
  starting transfers between devices: 22 us -> 20.7 us
    ppermute x18 -> x17, starting transfers between devices: 17.5 us -> 16.1 us  [swap(): return lax.ppermute(array, 'dp', [(i, i ^ mask) for i in range(cycle)])]
    ppermute x18 -> x17, waiting for transfers between devices: 37 us -> 37.7 us  [swap(): return lax.ppermute(array, 'dp', [(i, i ^ mask) for i in range(cycle)])]
  transfers between devices with their start and end apart: 20 -> 19, of which waited for: 13 -> 13; matrix products, arithmetic and copies ran while one was open for 4% -> 3% of each run, Pallas kernels for 7% -> 7%
where the time goes in v6:
time: 87.5 us; the launch traced here: 87.4 us
  waiting for transfers between devices  39.3 us (45%)
  starting transfers between devices  20.7 us (24%)
  Pallas kernels  18.7 us (21%)
  other arithmetic  5 us (6%)
  between operations  3.66 us (4%)
    ppermute x17, waiting for transfers between devices, swap(): return lax.ppermute(array, 'dp', [(i, i ^ mask) for i in range(cycle)])  37.7 us
    ppermute x17, starting transfers between devices, swap(): return lax.ppermute(array, 'dp', [(i, i ^ mask) for i in range(cycle)])  16.1 us
    pallas_call x1, Pallas kernels, forward(): pl.pallas_call(functools.partial(forward_kernel, (rows_i // samples, rows...  9.24 us
    ppermute x2, starting transfers between devices, swap_halves(): return lax.ppermute(array, 'mp', [(0, 1), (1, 0)])  4.55 us
    pallas_call x2, Pallas kernels, weight_terms(): pl.pallas_call(functools.partial(weight_kernel, base, carries), out_shape...  4.42 us
    pallas_call x2, Pallas kernels, turn(): pl.pallas_call(turn_kernel, out_shape=(jax.ShapeDtypeStruct((depth, rows)...  4.07 us
  transfers between devices with their start and end apart: 19, of which 13 were waited for; matrix products, arithmetic and copies ran while one was open for 3% of the time, Pallas kernels for 7%

profile of v6, /device:TPU:0, one launch (start us, length us, event | category | flops | bytes accessed | tf_op | source)
XLA Modules:
  0.0 87.4 jit_solution(16182766988017750632)
XLA Ops:
  0.7 9.2 %shard_map.121 = (f32[32,768]{1,0:T(8,128)S(1)}, f32[32,128]{1,0:T(8,128)S(1)}, f32[1024,768]{1,0:T(8,128)}, f32[512,768]{1,0:T(8,128)}) custom-call(s32[1]{0:T(128)} %bitcast.1.place_ref, bf16[1024,1536]{1,0:T(8,128)(2,1)} %bitcast.4, bf16[512,1536]{1,0:T(8,128)(2,1)} %bitcast.6, bf16[1536,768]{1,0:T(8,128)(2,1)} %image_w_hbm.1, bf16[1536,768]{1,0:T(8,128)(2,1)} %text_w_hbm.1), custom_call_target="tpu_custom_call" | custom-call | flops 3623878656 | bytes 14155776 | tf_op jit(solution)/shard_map/pallas_call | solution.py:137
  9.9 3.0 %collective-permute-start = (f32[32,128]{1,0:T(8,128)S(1)}, f32[32,128]{1,0:T(8,128)S(1)}, u32[]{:S(2)}, u32[]{:S(2)}) collective-permute-start(f32[32,128]{1,0:T(8,128)S(1)} %get-tuple-element.25.own_ref), channel_id=1, source_target_pairs={{0,1},{1,0},{2,3},{3,2},{4,5},{5,4},{6,7},{7,6},{8,9},{9,8},{10,11... | collective-permute-start | bytes 49160 | tf_op jit(solution)/shard_map/ppermute | solution.py:437
  13.6 1.1 %collective-permute-done.other_ref = f32[32,128]{1,0:T(8,128)S(1)} collective-permute-done((f32[32,128]{1,0:T(8,128)S(1)}, f32[32,128]{1,0:T(8,128)S(1)}, u32[]{:S(2)}, u32[]{:S(2)}) %collective-permute-start) | collective-permute-done | bytes 16416 | tf_op jit(solution)/shard_map/ppermute | solution.py:437
  14.6 0.1 shard_map.122
  14.7 4.2 %collective-permute-start.1 = (bf16[32,768]{1,0:T(8,128)(2,1)S(1)}, bf16[32,768]{1,0:T(8,128)(2,1)S(1)}, u32[]{:S(2)}, u32[]{:S(2)}) collective-permute-start(bf16[32,768]{1,0:T(8,128)(2,1)S(1)} %get-tuple-element.26._.refs_1_), channel_id=1, source_target_pairs={{0,24},{2,26},{4,28},{6,30},{8,16},{10,18},{12,20},{14,22},{16,8},... | collective-permute-start | bytes 147464 | tf_op jit(solution)/shard_map/ppermute | solution.py:434
  18.9 0.6 collective-permute-start.3
  19.6 2.6 %shard_map.123 = (bf16[1536,1024]{1,0:T(8,128)(2,1)S(1)}, f32[8,128]{1,0:T(8,128)S(1)}) custom-call(s32[16]{0:T(128)S(1)} %broadcast_xor_fusion.1.source_ref, bf16[1024,1536]{1,0:T(8,128)(2,1)S(1)} %bitcast.5, bf16[32,768]{1,0:T(8,128)(2,1)S(1)} %get-tuple-element.26._.refs_1_), custom_call_target="tpu_custom_call" | custom-call | bytes 6291456 | tf_op jit(solution)/shard_map/pallas_call | solution.py:230
  22.2 1.7 %collective-permute-done.2.refs_3_ = bf16[32,768]{1,0:T(8,128)(2,1)S(1)} collective-permute-done((bf16[32,768]{1,0:T(8,128)(2,1)S(1)}, bf16[32,768]{1,0:T(8,128)(2,1)S(1)}, u32[]{:S(2)}, u32[]{:S(2)}) %collective-permute-start.2) | collective-permute-done | bytes 49184 | tf_op jit(solution)/shard_map/ppermute | solution.py:434
  23.9 1.6 %collective-permute-start.4 = (bf16[4,32,768]{2,1,0:T(8,128)(2,1)S(1)}, bf16[4,32,768]{2,1,0:T(8,128)(2,1)S(1)}, u32[]{:S(2)}, u32[]{:S(2)}) collective-permute-start(bf16[4,32,768]{2,1,0:T(8,128)(2,1)S(1)} %shard_map.124._.refs_0_), channel_id=1, source_target_pairs={{0,4},{2,6},{4,0},{6,2},{8,12},{10,14},{12,8},{14,10},{16,20},{18,... | collective-permute-start | bytes 589832 | tf_op jit(solution)/shard_map/ppermute | solution.py:434
  25.6 1.5 %shard_map.125 = (bf16[1536,512]{1,0:T(8,128)(2,1)S(1)}, f32[8,128]{1,0:T(8,128)S(1)}) custom-call(s32[32]{0:T(128)S(1)} %broadcast_xor_fusion.source_ref, bf16[512,1536]{1,0:T(8,128)(2,1)S(1)} %bitcast.7, bf16[4,32,768]{2,1,0:T(8,128)(2,1)S(1)} %shard_map.124._.refs_0_), custom_call_target="tpu_custom_call" | custom-call | bytes 3145728 | tf_op jit(solution)/shard_map/pallas_call | solution.py:230
  27.1 2.6 %collective-permute-done.4.refs_1_ = bf16[4,32,768]{2,1,0:T(8,128)(2,1)S(1)} collective-permute-done((bf16[4,32,768]{2,1,0:T(8,128)(2,1)S(1)}, bf16[4,32,768]{2,1,0:T(8,128)(2,1)S(1)}, u32[]{:S(2)}, u32[]{:S(2)}) %collective-permute-start.4) | collective-permute-done | bytes 196640 | tf_op jit(solution)/shard_map/ppermute | solution.py:434
  29.8 1.4 %collective-permute-done.6.refs_3_ = bf16[4,32,768]{2,1,0:T(8,128)(2,1)S(1)} collective-permute-done((bf16[4,32,768]{2,1,0:T(8,128)(2,1)S(1)}, bf16[4,32,768]{2,1,0:T(8,128)(2,1)S(1)}, u32[]{:S(2)}, u32[]{:S(2)}) %collective-permute-start.6) | collective-permute-done | bytes 196640 | tf_op jit(solution)/shard_map/ppermute | solution.py:434
  31.2 0.4 shard_map.127
  31.6 1.5 %collective-permute-start.7 = (f32[32,256]{1,0:T(8,128)S(1)}, f32[32,256]{1,0:T(8,128)S(1)}, u32[]{:S(2)}, u32[]{:S(2)}) collective-permute-start(f32[32,256]{1,0:T(8,128)S(1)} %get-tuple-element.29.own_ref), channel_id=1, source_target_pairs={{0,1},{1,0},{2,3},{3,2},{4,5},{5,4},{6,7},{7,6},{8,9},{9,8},{10,11... | collective-permute-start | bytes 98312 | tf_op jit(solution)/shard_map/ppermute | solution.py:437
  35.0 0.5 collective-permute-done.7.other_ref
  35.5 0.5 shard_map.128
  36.0 2.8 %shard_map.129 = (f32[392,768]{1,0:T(8,128)S(1)}, f32[384,768]{1,0:T(8,128)S(1)}, f32[768,768]{1,0:T(8,128)S(1)}) custom-call(f32[32,768]{1,0:T(8,128)S(1)} %get-tuple-element.34.grad_ref, f32[1024,768]{1,0:T(8,128)S(1)} %copy-done.3, bf16[1536,1024]{1,0:T(8,128)(2,1)S(1)} %get-tuple-element.36.turned_ref, f32[8,768]{1,0:T(8,128)S(1)} %get-tuple-element.33.stat_ref._, ...), custom_call_target="tpu_custom_call" | custom-call | flops 2415919104 | bytes 11010048 | tf_op jit(solution)/shard_map/pallas_call | solution.py:393
  39.0 1.6 %shard_map.130 = (f32[384,768]{1,0:T(8,128)S(1)}, f32[384,768]{1,0:T(8,128)S(1)}, f32[768,768]{1,0:T(8,128)S(1)}) custom-call(f32[32,768]{1,0:T(8,128)S(1)} %get-tuple-element.34.grad_ref, f32[512,768]{1,0:T(8,128)S(1)} %copy-done.1, bf16[1536,512]{1,0:T(8,128)(2,1)S(1)} %get-tuple-element.39.turned_ref, f32[8,768]{1,0:T(8,128)S(1)} %get-tuple-element.33.stat_ref._, ...), custom_call_target="tpu_custom_call" | custom-call | flops 1207959552 | bytes 7864320 | tf_op jit(solution)/shard_map/pallas_call | solution.py:393
  40.6 0.5 collective-permute-start.11
  41.2 0.4 collective-permute-start.12
  41.7 0.1 collective-permute-done.8
  41.8 0.1 fusion.34
  41.9 0.2 fusion
  42.1 0.1 fusion.29
  42.3 0.2 collective-permute-start.13
  42.5 2.8 %collective-permute-done.9 = f32[384,768]{1,0:T(8,128)S(1)} collective-permute-done((f32[384,768]{1,0:T(8,128)S(1)}, f32[384,768]{1,0:T(8,128)S(1)}, u32[]{:S(2)}, u32[]{:S(2)}) %collective-permute-start.9) | collective-permute-done | bytes 1179680 | tf_op jit(solution)/shard_map/ppermute | solution.py:434
  45.3 0.1 add_multiply_fusion
  45.5 0.1 fusion.28
  45.6 1.6 %collective-permute-start.10 = (f16[392,768]{1,0:T(8,128)(2,1)S(1)}, f16[392,768]{1,0:T(8,128)(2,1)S(1)}, u32[]{:S(2)}, u32[]{:S(2)}) collective-permute-start(f16[392,768]{1,0:T(8,128)(2,1)S(1)} %add_convert_fusion), channel_id=1, source_target_pairs={{0,4},{2,6},{4,0},{6,2},{8,12},{10,14},{12,8},{14,10},{16,20},{18,... | collective-permute-start | bytes 1806344 | tf_op jit(solution)/shard_map/ppermute | solution.py:434
  47.3 10.7 %collective-permute-done.13 = f16[392,768]{1,0:T(8,128)(2,1)S(1)} collective-permute-done((f16[392,768]{1,0:T(8,128)(2,1)S(1)}, f16[392,768]{1,0:T(8,128)(2,1)S(1)}, u32[]{:S(2)}, u32[]{:S(2)}) %collective-permute-start.13) | collective-permute-done | bytes 602144 | tf_op jit(solution)/shard_map/ppermute | solution.py:434
  58.0 0.1 convert_add_fusion
  58.2 0.1 fusion.2
  58.5 3.1 %collective-permute-done.10 = f16[392,768]{1,0:T(8,128)(2,1)S(1)} collective-permute-done((f16[392,768]{1,0:T(8,128)(2,1)S(1)}, f16[392,768]{1,0:T(8,128)(2,1)S(1)}, u32[]{:S(2)}, u32[]{:S(2)}) %collective-permute-start.10) | collective-permute-done | bytes 602144 | tf_op jit(solution)/shard_map/ppermute | solution.py:434
  61.6 0.1 fusion.42
  62.1 0.2 collective-permute-start.14
  62.4 2.5 %collective-permute-start.17 = (f16[104,768]{1,0:T(8,128)(2,1)S(1)}, f16[104,768]{1,0:T(8,128)(2,1)S(1)}, u32[]{:S(2)}, u32[]{:S(2)}) collective-permute-start(f16[104,768]{1,0:T(8,128)(2,1)S(1)} %add_convert_fusion.5), channel_id=1, source_target_pairs={{0,16},{2,18},{4,20},{6,22},{8,24},{10,26},{12,28},{14,30},{16,0},... | collective-permute-start | bytes 479240 | tf_op jit(solution)/shard_map/ppermute | solution.py:434
  64.8 1.5 %collective-permute-start.15 = (f16[200,768]{1,0:T(8,128)(2,1)S(1)}, f16[200,768]{1,0:T(8,128)(2,1)S(1)}, u32[]{:S(2)}, u32[]{:S(2)}) collective-permute-start(f16[200,768]{1,0:T(8,128)(2,1)S(1)} %add_convert_fusion.2), channel_id=1, source_target_pairs={{0,4},{2,6},{4,0},{6,2},{8,12},{10,14},{12,8},{14,10},{16,20},{18,... | collective-permute-start | bytes 921608 | tf_op jit(solution)/shard_map/ppermute | solution.py:434
  66.4 4.9 %collective-permute-done.14 = f16[104,768]{1,0:T(8,128)(2,1)S(1)} collective-permute-done((f16[104,768]{1,0:T(8,128)(2,1)S(1)}, f16[104,768]{1,0:T(8,128)(2,1)S(1)}, u32[]{:S(2)}, u32[]{:S(2)}) %collective-permute-start.14) | collective-permute-done | bytes 159776 | tf_op jit(solution)/shard_map/ppermute | solution.py:434
  71.2 0.1 fusion.46
  71.3 1.7 %collective-permute-done.15 = f16[200,768]{1,0:T(8,128)(2,1)S(1)} collective-permute-done((f16[200,768]{1,0:T(8,128)(2,1)S(1)}, f16[200,768]{1,0:T(8,128)(2,1)S(1)}, u32[]{:S(2)}, u32[]{:S(2)}) %collective-permute-start.15) | collective-permute-done | bytes 307232 | tf_op jit(solution)/shard_map/ppermute | solution.py:434
  73.4 0.7 collective-permute-start.16
  74.5 1.7 %collective-permute-start.18 = (f16[56,768]{1,0:T(8,128)(2,1)S(1)}, f16[56,768]{1,0:T(8,128)(2,1)S(1)}, u32[]{:S(2)}, u32[]{:S(2)}) collective-permute-start(f16[56,768]{1,0:T(8,128)(2,1)S(1)} %add_convert_fusion.6), channel_id=1, source_target_pairs={{0,8},{2,10},{4,12},{6,14},{8,0},{10,2},{12,4},{14,6},{16,24},{18,... | collective-permute-start | bytes 258056 | tf_op jit(solution)/shard_map/ppermute | solution.py:434
  76.3 3.7 %collective-permute-done.18 = f16[56,768]{1,0:T(8,128)(2,1)S(1)} collective-permute-done((f16[56,768]{1,0:T(8,128)(2,1)S(1)}, f16[56,768]{1,0:T(8,128)(2,1)S(1)}, u32[]{:S(2)}, u32[]{:S(2)}) %collective-permute-start.18) | collective-permute-done | bytes 86048 | tf_op jit(solution)/shard_map/ppermute | solution.py:434
  80.0 5.1 %collective-permute-done.16 = f16[152,768]{1,0:T(8,128)(2,1)S(1)} collective-permute-done((f16[152,768]{1,0:T(8,128)(2,1)S(1)}, f16[152,768]{1,0:T(8,128)(2,1)S(1)}, u32[]{:S(2)}, u32[]{:S(2)}) %collective-permute-start.16) | collective-permute-done | bytes 233504 | tf_op jit(solution)/shard_map/ppermute | solution.py:434
  85.0 0.6 fusion.106
  85.7 0.1 fusion.19
  85.8 0.7 pad_maximum_fusion
  86.5 0.8 fusion.5
  (72 shorter events, 2.0 us)
Async XLA Ops:
  0.6 18.9 %copy-start.5 = (s32[16]{0:T(128)S(1)}, s32[16]{0:T(128)}, u32[]{:S(2)}) copy-start(s32[16]{0:T(128)} %constant.61.clone) | copy-start | bytes 196
  0.6 18.9 %copy-start = (bf16[16,64,1536]{2,1,0:T(8,128)(2,1)S(1)}, bf16[16,64,1536]{2,1,0:T(8,128)(2,1)}, u32[]{:S(2)}) copy-start(bf16[16,64,1536]{2,1,0:T(8,128)(2,1)} %param.10) | copy-start | bytes 9437188
  9.9 4.7 %collective-permute-start = (f32[32,128]{1,0:T(8,128)S(1)}, f32[32,128]{1,0:T(8,128)S(1)}, u32[]{:S(2)}, u32[]{:S(2)}) collective-permute-start(f32[32,128]{1,0:T(8,128)S(1)} %get-tuple-element.25.own_ref), channel_id=1, source_target_pairs={{0,1},{1,0},{2,3},{3,2},{4,5},{5,4},{6,7},{7,6},{8,9},{9,8},{10,11... | collective-permute-start | bytes 49160 | tf_op jit(solution)/shard_map/ppermute | solution.py:437
  14.7 7.4 %collective-permute-start.1 = (bf16[32,768]{1,0:T(8,128)(2,1)S(1)}, bf16[32,768]{1,0:T(8,128)(2,1)S(1)}, u32[]{:S(2)}, u32[]{:S(2)}) collective-permute-start(bf16[32,768]{1,0:T(8,128)(2,1)S(1)} %get-tuple-element.26._.refs_1_), channel_id=1, source_target_pairs={{0,24},{2,26},{4,28},{6,30},{8,16},{10,18},{12,20},{14,22},{16,8},... | collective-permute-start | bytes 147464 | tf_op jit(solution)/shard_map/ppermute | solution.py:434
  18.9 5.0 %collective-permute-start.2 = (bf16[32,768]{1,0:T(8,128)(2,1)S(1)}, bf16[32,768]{1,0:T(8,128)(2,1)S(1)}, u32[]{:S(2)}, u32[]{:S(2)}) collective-permute-start(bf16[32,768]{1,0:T(8,128)(2,1)S(1)} %get-tuple-element.26._.refs_1_), channel_id=1, source_target_pairs={{0,16},{2,18},{4,20},{6,22},{8,24},{10,26},{12,28},{14,30},{16,0},... | collective-permute-start | bytes 147464 | tf_op jit(solution)/shard_map/ppermute | solution.py:434
  18.9 5.0 %collective-permute-start.3 = (bf16[32,768]{1,0:T(8,128)(2,1)S(1)}, bf16[32,768]{1,0:T(8,128)(2,1)S(1)}, u32[]{:S(2)}, u32[]{:S(2)}) collective-permute-start(bf16[32,768]{1,0:T(8,128)(2,1)S(1)} %get-tuple-element.26._.refs_1_), channel_id=1, source_target_pairs={{0,8},{2,10},{4,12},{6,14},{8,0},{10,2},{12,4},{14,6},{16,24},{18,... | collective-permute-start | bytes 147464 | tf_op jit(solution)/shard_map/ppermute | solution.py:434
  19.6 6.0 %copy-start.4 = (s32[32]{0:T(128)S(1)}, s32[32]{0:T(128)}, u32[]{:S(2)}) copy-start(s32[32]{0:T(128)} %constant.60.clone) | copy-start | bytes 388
  19.6 6.0 %copy-start.2 = (bf16[16,32,1536]{2,1,0:T(8,128)(2,1)S(1)}, bf16[16,32,1536]{2,1,0:T(8,128)(2,1)}, u32[]{:S(2)}) copy-start(bf16[16,32,1536]{2,1,0:T(8,128)(2,1)} %param.11) | copy-start | bytes 4718596
  23.9 5.7 %collective-permute-start.4 = (bf16[4,32,768]{2,1,0:T(8,128)(2,1)S(1)}, bf16[4,32,768]{2,1,0:T(8,128)(2,1)S(1)}, u32[]{:S(2)}, u32[]{:S(2)}) collective-permute-start(bf16[4,32,768]{2,1,0:T(8,128)(2,1)S(1)} %shard_map.124._.refs_0_), channel_id=1, source_target_pairs={{0,4},{2,6},{4,0},{6,2},{8,12},{10,14},{12,8},{14,10},{16,20},{18,... | collective-permute-start | bytes 589832 | tf_op jit(solution)/shard_map/ppermute | solution.py:434
  25.5 4.2 %collective-permute-start.5 = (bf16[4,32,768]{2,1,0:T(8,128)(2,1)S(1)}, bf16[4,32,768]{2,1,0:T(8,128)(2,1)S(1)}, u32[]{:S(2)}, u32[]{:S(2)}) collective-permute-start(bf16[4,32,768]{2,1,0:T(8,128)(2,1)S(1)} %shard_map.124._.refs_0_), channel_id=1, source_target_pairs={{0,2},{2,0},{4,6},{6,4},{8,10},{10,8},{12,14},{14,12},{16,18},{18,... | collective-permute-start | bytes 589832 | tf_op jit(solution)/shard_map/ppermute | solution.py:434
  25.5 10.5 %copy-start.3 = (f32[1024,768]{1,0:T(8,128)S(1)}, f32[1024,768]{1,0:T(8,128)}, u32[]{:S(2)}) copy-start(f32[1024,768]{1,0:T(8,128)} %get-tuple-element.35.slope_ref) | copy-start | bytes 9437188
  29.7 1.5 %collective-permute-start.6 = (bf16[4,32,768]{2,1,0:T(8,128)(2,1)S(1)}, bf16[4,32,768]{2,1,0:T(8,128)(2,1)S(1)}, u32[]{:S(2)}, u32[]{:S(2)}) collective-permute-start(bf16[4,32,768]{2,1,0:T(8,128)(2,1)S(1)} %bitcast.8), channel_id=1, source_target_pairs={{0,2},{2,0},{4,6},{6,4},{8,10},{10,8},{12,14},{14,12},{16,18},{18,... | collective-permute-start | bytes 589832 | tf_op jit(solution)/shard_map/ppermute | solution.py:434
  31.6 3.9 %collective-permute-start.7 = (f32[32,256]{1,0:T(8,128)S(1)}, f32[32,256]{1,0:T(8,128)S(1)}, u32[]{:S(2)}, u32[]{:S(2)}) collective-permute-start(f32[32,256]{1,0:T(8,128)S(1)} %get-tuple-element.29.own_ref), channel_id=1, source_target_pairs={{0,1},{1,0},{2,3},{3,2},{4,5},{5,4},{6,7},{7,6},{8,9},{9,8},{10,11... | collective-permute-start | bytes 98312 | tf_op jit(solution)/shard_map/ppermute | solution.py:437
  36.0 2.9 %copy-start.1 = (f32[512,768]{1,0:T(8,128)S(1)}, f32[512,768]{1,0:T(8,128)}, u32[]{:S(2)}) copy-start(f32[512,768]{1,0:T(8,128)} %get-tuple-element.38.slope_ref) | copy-start | bytes 4718596
  38.8 2.9 %collective-permute-start.8 = (f32[392,768]{1,0:T(8,128)S(1)}, f32[392,768]{1,0:T(8,128)S(1)}, u32[]{:S(2)}, u32[]{:S(2)}) collective-permute-start(f32[392,768]{1,0:T(8,128)S(1)} %get-tuple-element.37._), channel_id=1, source_target_pairs={{0,2},{2,0},{4,6},{6,4},{8,10},{10,8},{12,14},{14,12},{16,18},{18,... | collective-permute-start | bytes 3612680 | tf_op jit(solution)/shard_map/ppermute | solution.py:434
  40.6 21.1 %collective-permute-start.11 = (f32[384,768]{1,0:T(8,128)S(1)}, f32[384,768]{1,0:T(8,128)S(1)}, u32[]{:S(2)}, u32[]{:S(2)}) collective-permute-start(f32[384,768]{1,0:T(8,128)S(1)} %get-tuple-element.43), channel_id=1, source_target_pairs={{0,2},{2,0},{4,6},{6,4},{8,10},{10,8},{12,14},{14,12},{16,18},{18,... | collective-permute-start | bytes 3538952 | tf_op jit(solution)/shard_map/ppermute | solution.py:434
  41.2 4.2 %collective-permute-start.9 = (f32[384,768]{1,0:T(8,128)S(1)}, f32[384,768]{1,0:T(8,128)S(1)}, u32[]{:S(2)}, u32[]{:S(2)}) collective-permute-start(f32[384,768]{1,0:T(8,128)S(1)} %get-tuple-element.41), channel_id=1, source_target_pairs={{0,2},{2,0},{4,6},{6,4},{8,10},{10,8},{12,14},{14,12},{16,18},{18,... | collective-permute-start | bytes 3538952 | tf_op jit(solution)/shard_map/ppermute | solution.py:434
  41.2 16.9 %collective-permute-start.12 = (f32[384,768]{1,0:T(8,128)S(1)}, f32[384,768]{1,0:T(8,128)S(1)}, u32[]{:S(2)}, u32[]{:S(2)}) collective-permute-start(f32[384,768]{1,0:T(8,128)S(1)} %get-tuple-element.44), channel_id=1, source_target_pairs={{0,2},{2,0},{4,6},{6,4},{8,10},{10,8},{12,14},{14,12},{16,18},{18,... | collective-permute-start | bytes 3538952 | tf_op jit(solution)/shard_map/ppermute | solution.py:434
  42.3 15.7 %collective-permute-start.13 = (f16[392,768]{1,0:T(8,128)(2,1)S(1)}, f16[392,768]{1,0:T(8,128)(2,1)S(1)}, u32[]{:S(2)}, u32[]{:S(2)}) collective-permute-start(f16[392,768]{1,0:T(8,128)(2,1)S(1)} %add_convert_fusion.1), channel_id=1, source_target_pairs={{0,8},{2,10},{4,12},{6,14},{8,0},{10,2},{12,4},{14,6},{16,24},{18,... | collective-permute-start | bytes 1806344 | tf_op jit(solution)/shard_map/ppermute | solution.py:434
  45.6 15.9 %collective-permute-start.10 = (f16[392,768]{1,0:T(8,128)(2,1)S(1)}, f16[392,768]{1,0:T(8,128)(2,1)S(1)}, u32[]{:S(2)}, u32[]{:S(2)}) collective-permute-start(f16[392,768]{1,0:T(8,128)(2,1)S(1)} %add_convert_fusion), channel_id=1, source_target_pairs={{0,4},{2,6},{4,0},{6,2},{8,12},{10,14},{12,8},{14,10},{16,20},{18,... | collective-permute-start | bytes 1806344 | tf_op jit(solution)/shard_map/ppermute | solution.py:434
  62.1 9.1 %collective-permute-start.14 = (f16[104,768]{1,0:T(8,128)(2,1)S(1)}, f16[104,768]{1,0:T(8,128)(2,1)S(1)}, u32[]{:S(2)}, u32[]{:S(2)}) collective-permute-start(f16[104,768]{1,0:T(8,128)(2,1)S(1)} %add_convert_fusion.4), channel_id=1, source_target_pairs={{0,8},{2,10},{4,12},{6,14},{8,0},{10,2},{12,4},{14,6},{16,24},{18,... | collective-permute-start | bytes 479240 | tf_op jit(solution)/shard_map/ppermute | solution.py:434
  62.4 11.8 %collective-permute-start.17 = (f16[104,768]{1,0:T(8,128)(2,1)S(1)}, f16[104,768]{1,0:T(8,128)(2,1)S(1)}, u32[]{:S(2)}, u32[]{:S(2)}) collective-permute-start(f16[104,768]{1,0:T(8,128)(2,1)S(1)} %add_convert_fusion.5), channel_id=1, source_target_pairs={{0,16},{2,18},{4,20},{6,22},{8,24},{10,26},{12,28},{14,30},{16,0},... | collective-permute-start | bytes 479240 | tf_op jit(solution)/shard_map/ppermute | solution.py:434
  64.8 8.2 %collective-permute-start.15 = (f16[200,768]{1,0:T(8,128)(2,1)S(1)}, f16[200,768]{1,0:T(8,128)(2,1)S(1)}, u32[]{:S(2)}, u32[]{:S(2)}) collective-permute-start(f16[200,768]{1,0:T(8,128)(2,1)S(1)} %add_convert_fusion.2), channel_id=1, source_target_pairs={{0,4},{2,6},{4,0},{6,2},{8,12},{10,14},{12,8},{14,10},{16,20},{18,... | collective-permute-start | bytes 921608 | tf_op jit(solution)/shard_map/ppermute | solution.py:434
  73.4 11.6 %collective-permute-start.16 = (f16[152,768]{1,0:T(8,128)(2,1)S(1)}, f16[152,768]{1,0:T(8,128)(2,1)S(1)}, u32[]{:S(2)}, u32[]{:S(2)}) collective-permute-start(f16[152,768]{1,0:T(8,128)(2,1)S(1)} %add_convert_fusion.3), channel_id=1, source_target_pairs={{0,16},{2,18},{4,20},{6,22},{8,24},{10,26},{12,28},{14,30},{16,0},... | collective-permute-start | bytes 700424 | tf_op jit(solution)/shard_map/ppermute | solution.py:434
  74.5 5.4 %collective-permute-start.18 = (f16[56,768]{1,0:T(8,128)(2,1)S(1)}, f16[56,768]{1,0:T(8,128)(2,1)S(1)}, u32[]{:S(2)}, u32[]{:S(2)}) collective-permute-start(f16[56,768]{1,0:T(8,128)(2,1)S(1)} %add_convert_fusion.6), channel_id=1, source_target_pairs={{0,8},{2,10},{4,12},{6,14},{8,0},{10,2},{12,4},{14,6},{16,24},{18,... | collective-permute-start | bytes 258056 | tf_op jit(solution)/shard_map/ppermute | solution.py:434

commit v7 on v6

--- a/solution.py
+++ b/solution.py
@@ -39,12 +39,16 @@
     return pltpu.CompilerParams(vmem_limit_bytes=mib * 2**20)
 
 
-def gelu_and_slope(x):
+def gelu(x):
     square = x * x
-    cdf = 0.5 + 0.5 * jnp.tanh(x * (ROOT + (0.044715 * ROOT) * square))
-    value = x * cdf
-    rise = (value - value * cdf) * (2 * ROOT + (6 * 0.044715 * ROOT) * square)
-    return value, cdf + rise
+    return x * (0.5 + 0.5 * jnp.tanh(x * (ROOT + (0.044715 * ROOT) * square)))
+
+
+def gelu_slope(x):
+    square = x * x
+    t = jnp.tanh(x * (ROOT + (0.044715 * ROOT) * square))
+    rise = (1.0 - t) * (x * (ROOT + (3 * 0.044715 * ROOT) * square))
+    return (0.5 + 0.5 * t) * (1.0 + rise)
 
 
 def forward_kernel(
@@ -56,14 +60,14 @@
     text_w_hbm,
     pooled_ref,
     square_ref,
-    image_slope_hbm,
-    text_slope_hbm,
+    image_preact_hbm,
+    text_preact_hbm,
     image_v,
     text_v,
     image_w,
     text_w,
-    image_slope,
-    text_slope,
+    image_preact,
+    text_preact,
     in_sem,
     w_sem,
     out_sem,
@@ -71,8 +75,8 @@
     width = image_w.shape[1]
     samples = pooled_ref.shape[0] // 2
     towers_here = (
-        (text_hbm, text_v, text_w_hbm, text_w, text_slope, text_slope_hbm, tokens_of[1], samples),
-        (image_hbm, image_v, image_w_hbm, image_w, image_slope, image_slope_hbm, tokens_of[0], 0),
+        (text_hbm, text_v, text_w_hbm, text_w, text_preact, text_preact_hbm, tokens_of[1], samples),
+        (image_hbm, image_v, image_w_hbm, image_w, image_preact, image_preact_hbm, tokens_of[0], 0),
     )
     waits, tiles = [], []
     for t, (source, buf, w_source, w, _, _, _, _) in enumerate(towers_here):
@@ -90,26 +94,24 @@
 
     def project(n):
         t, start, column = tiles[n]
-        _, buf, _, w, slope, _, _, _ = towers_here[t]
+        _, buf, _, w, preact, _, _, _ = towers_here[t]
         if start == 0 and column == 0:
             for copy in waits[t]:
                 copy.wait()
         rows, columns = slice(start, start + JOB_ROWS), slice(column, column + JOB_COLUMNS)
-        slope[rows, columns] = jnp.dot(buf[rows, :], w[:, columns], preferred_element_type=F32)
+        preact[rows, columns] = jnp.dot(buf[rows, :], w[:, columns], preferred_element_type=F32)
 
     out_copies = []
     project(0)
     for n, (t, start, tile_column) in enumerate(tiles):
-        _, buf, _, _, slope, slope_out, tok, base = towers_here[t]
+        _, buf, _, _, preact, preact_out, tok, base = towers_here[t]
         if n + 1 < len(tiles):
             project(n + 1)
         for row in range(start, start + JOB_ROWS, STRIP):
             rows = slice(row, row + STRIP)
             here = (rows, slice(tile_column, tile_column + JOB_COLUMNS))
             token_columns = pl.ds(pl.multiple_of(first + tile_column, 128), JOB_COLUMNS)
-            value, slant = gelu_and_slope(slope[here])
-            slope[here] = slant
-            hidden = buf[rows, token_columns].astype(F32) + value
+            hidden = buf[rows, token_columns].astype(F32) + gelu(preact[here])
             for part in range(0, STRIP, tok):
                 sample = base + (row + part) // tok
                 pooled_ref[sample : sample + 1, here[1]] = (
@@ -118,7 +120,7 @@
         if tile_column + JOB_COLUMNS == width:
             part = pl.ds(start, JOB_ROWS)
             copy = pltpu.make_async_copy(
-                slope.at[part, :], slope_out.at[part, :], out_sem.at[len(out_copies)]
+                preact.at[part, :], preact_out.at[part, :], out_sem.at[len(out_copies)]
             )
             copy.start()
             out_copies.append(copy)
@@ -204,6 +206,27 @@
     )(*afters, *parts)
 
 
+def slope_kernel(preact_ref, _, slope_ref):
+    rows, width = preact_ref.shape
+    for row in range(0, rows, STRIP):
+        for column in range(0, width, JOB_COLUMNS):
+            here = (slice(row, row + STRIP), slice(column, column + JOB_COLUMNS))
+            slope_ref[here] = gelu_slope(preact_ref[here])
+
+
+def slopes(preact, after):
+    return pl.pallas_call(
+        slope_kernel,
+        out_shape=jax.ShapeDtypeStruct(preact.shape, F32),
+        in_specs=[vmem(), anyplace()],
+        out_specs=vmem(),
+        compiler_params=params(4),
+        cost_estimate=pl.CostEstimate(
+            flops=0, bytes_accessed=8 * preact.size, transcendentals=preact.size
+        ),
+    )(preact, after)
+
+
 def turn_kernel(source_ref, tokens_ref, _, turned_ref, most_ref, turned):
     rows, _ = tokens_ref.shape
     blocks = source_ref.shape[0]
@@ -257,7 +280,7 @@
     return image, text
 
 
-def product_kernel(image_most_ref, text_most_ref, *refs):
+def product_kernel(*refs):
     *block_refs, out_ref, mark_ref = refs
     near_ref = block_refs[0]
     samples = near_ref.shape[1] // 2
@@ -276,7 +299,7 @@
         start = stop
 
 
-def products(blocks, mosts):
+def products(blocks):
     both = blocks[0].shape[1]
     columns = sum(b.shape[0] for b in blocks) * (both // 2)
     return pl.pallas_call(
@@ -285,10 +308,10 @@
             jax.ShapeDtypeStruct((both, columns), F32),
             jax.ShapeDtypeStruct((8, columns), F32),
         ),
-        in_specs=[anyplace()] * 2 + [vmem()] * len(blocks),
+        in_specs=[vmem()] * len(blocks),
         out_specs=(vmem(),) * 2,
         compiler_params=params(8),
-    )(*mosts, *blocks)
+    )(*blocks)
 
 
 def middle_kernel(
@@ -456,27 +479,29 @@
     image_blocks = jnp.asarray(image_blocks, jnp.int32) ^ place
 
     model_place = lax.axis_index("mp").astype(jnp.int32).reshape(1)
-    pooled, square, image_slope, text_slope = forward(
+    pooled, square, image_preact, text_preact = forward(
         model_place, image_flat, text_flat, image_weight, text_weight, samples
     )
     unit, sent, norm = units(valid_count, pooled, square, swap_halves(square))
 
     low = max(bits - 2, 1)
     tops = [1 << b for b in reversed(range(low, bits))]
-    masks = [tops[0] | tops[1], *tops] if len(tops) == 2 else tops
+    masks = tops + [tops[0] | tops[1]] if len(tops) == 2 else tops
     arrived = [swap(sent, mask) for mask in masks]
     image_turned, image_most = turn(image_blocks, image_flat, sent)
-    gathered = stack([sent] + arrived, image_most)
-    text_turned, text_most = turn(text_blocks, text_flat, gathered)
+    text_slope = slopes(text_preact, image_most)
+    gathered = stack([sent] + arrived, text_slope)
+    image_slope = slopes(image_preact, gathered)
     blocks = [gathered]
     for b in reversed(range(1, low)):
         blocks = blocks + [swap(block, 1 << b) for block in blocks]
     far = [swap(block, 1) for block in blocks[:1]]
     for block in blocks[1:]:
-        far.append(swap(stack([block], text_most)[0], 1))
+        far.append(swap(stack([block], image_slope)[0], 1))
     blocks = blocks + far
 
-    own_dots, mark = products(blocks, (image_most, text_most))
+    own_dots, mark = products(blocks)
+    text_turned, text_most = turn(text_blocks, text_flat, own_dots)
     grad, stat = middle(
         (image_tok, text_tok),
         logit_scale,
@@ -545,26 +570,25 @@
         stays = [(keep[:height], None), (swap(late, 1), None)]
         return stays, [(keep[height:], None), (there[:height], None)], there[height:]
 
-    image_terms = weight_terms(grad, image_slope, image_turned, stat, 0, True, stat)
-    image, image_leaves, stat_there = core_step(*image_terms)
+    text_terms = weight_terms(grad, text_slope, text_turned, stat, 1, True, stat)
+    text, text_leaves, stat_there = core_step(*text_terms)
     start_stat = stat[:3] + stat_there[:3]
-    text_terms = weight_terms(grad, text_slope, text_turned, stat, 1, False, image_terms[0])
-    text, text_leaves, _ = core_step(*text_terms)
-
-    coded, image_in = leave(image_leaves, start_stat, 0, image_order[0], start_stat)
-    coded, text_in = leave(text_leaves, start_stat, 1, 1, coded)
+    image_terms = weight_terms(grad, image_slope, image_turned, stat, 0, False, text_terms[0])
+    image, image_leaves, _ = core_step(*image_terms)
+
+    coded, text_in = leave(text_leaves, start_stat, 1, 1, start_stat)
+    coded, image_in = leave(image_leaves, start_stat, 0, image_order[0], coded)
     text, text_stat = take(text, start_stat, 1, text_in)
     parts = [(terms, text_stat) for terms in halves(text)]
-    image_in = image_in.astype(F32) + 0.0 * coded[:1].astype(F32)
     image, image_stat = take(image, start_stat, 0, image_in)
     for step in range(bits - 3):
         image, image_leaves = halves(image)
         (first, first_stat), (second, second_stat) = parts
         first, first_leaves = halves(first)
         second, second_leaves = halves(second)
-        coded, image_in = leave(image_leaves, image_stat, 0, image_order[step + 1], coded)
         coded, second_in = leave(second_leaves, second_stat, 1, text_orders[1][step], coded)
         coded, first_in = leave(first_leaves, first_stat, 1, text_orders[0][step], coded)
+        coded, image_in = leave(image_leaves, image_stat, 0, image_order[step + 1], coded)
         parts = [(first, first_stat, first_in), (second, second_stat, second_in)]
         if step < bits - 4:
             parts = [take(terms, old, 1, arrival) for terms, old, arrival in parts]

time: 87.5 us -> 91.4 us (1.045)
  waiting for transfers between devices: 39.3 us -> 33.2 us
  Pallas kernels: 18.7 us -> 22.1 us
  local copies, waits for them, and re-layouts: 0.03 us -> 3.37 us
  starting transfers between devices: 20.7 us -> 23.2 us
    ppermute x17, waiting for transfers between devices: 37.7 us -> 32.1 us  [swap(): return lax.ppermute(array, 'dp', [(i, i ^ mask) for i in range(cycle)])]
    unnamed x12 -> x26, local copies, waits for them, and re-layouts: 0.03 us -> 3.37 us
    ppermute x17, starting transfers between devices: 16.1 us -> 18.6 us  [swap(): return lax.ppermute(array, 'dp', [(i, i ^ mask) for i in range(cycle)])]
    pallas_call x0 -> x2, Pallas kernels: none -> 2.14 us  [slopes(): pl.pallas_call(slope_kernel, out_shape=jax.ShapeDtypeStruct(preact.shape,...]
    pallas_call x1, Pallas kernels: 9.24 us -> 7.83 us  [forward(): pl.pallas_call(functools.partial(forward_kernel, (rows_i // samples, rows...]
    pallas_call x1, Pallas kernels: 0.51 us -> 1.54 us  [middle(): pl.pallas_call(functools.partial(middle_kernel, tokens_of), out_shape=(ja...]
    pallas_call x1, Pallas kernels: 0.36 us -> 1.38 us  [products(): pl.pallas_call(product_kernel, out_shape=(jax.ShapeDtypeStruct((both, col...]
  transfers between devices with their start and end apart: 19 -> 19, of which waited for: 13 -> 10; matrix products, arithmetic and copies ran while one was open for 3% -> 4% of each run, Pallas kernels for 7% -> 11%
where the time goes in v7:
time: 91.4 us; the launch traced here: 91.1 us
  waiting for transfers between devices  33.2 us (36%)
  starting transfers between devices  23.2 us (25%)
  Pallas kernels  22.1 us (24%)
  other arithmetic  5.59 us (6%)
  between operations  3.7 us (4%)
  local copies, waits for them, and re-layouts  3.37 us (4%)
    ppermute x17, waiting for transfers between devices, swap(): return lax.ppermute(array, 'dp', [(i, i ^ mask) for i in range(cycle)])  32.1 us
    ppermute x17, starting transfers between devices, swap(): return lax.ppermute(array, 'dp', [(i, i ^ mask) for i in range(cycle)])  18.6 us
    pallas_call x1, Pallas kernels, forward(): pl.pallas_call(functools.partial(forward_kernel, (rows_i // samples, rows...  7.83 us
    ppermute x2, starting transfers between devices, swap_halves(): return lax.ppermute(array, 'mp', [(0, 1), (1, 0)])  4.64 us
    pallas_call x2, Pallas kernels, weight_terms(): pl.pallas_call(functools.partial(weight_kernel, base, carries), out_shape...  4.35 us
    pallas_call x2, Pallas kernels, turn(): pl.pallas_call(turn_kernel, out_shape=(jax.ShapeDtypeStruct((depth, rows)...  4.07 us
    unnamed x26, local copies, waits for them, and re-layouts  3.37 us
    pallas_call x2, Pallas kernels, slopes(): pl.pallas_call(slope_kernel, out_shape=jax.ShapeDtypeStruct(preact.shape,...  2.14 us
  transfers between devices with their start and end apart: 19, of which 10 were waited for; matrix products, arithmetic and copies ran while one was open for 4% of the time, Pallas kernels for 11%

profile of v7, /device:TPU:0, one launch (start us, length us, event | category | flops | bytes accessed | tf_op | source)
XLA Modules:
  0.0 91.1 jit_solution(6841495658959767254)
XLA Ops:
  0.7 7.8 %shard_map.121 = (f32[32,768]{1,0:T(8,128)S(1)}, f32[32,128]{1,0:T(8,128)S(1)}, f32[1024,768]{1,0:T(8,128)}, f32[512,768]{1,0:T(8,128)}) custom-call(s32[1]{0:T(128)} %bitcast.place_ref, bf16[1024,1536]{1,0:T(8,128)(2,1)} %bitcast.4, bf16[512,1536]{1,0:T(8,128)(2,1)} %bitcast.6, bf16[1536,768]{1,0:T(8,128)(2,1)} %image_w_hbm.1, bf16[1536,768]{1,0:T(8,128)(2,1)} %text_w_hbm.1), custom_call_target="tpu_custom_call" | custom-call | flops 3623878656 | bytes 14155776 | tf_op jit(solution)/shard_map/pallas_call | solution.py:139
  8.5 3.0 %collective-permute-start = (f32[32,128]{1,0:T(8,128)S(1)}, f32[32,128]{1,0:T(8,128)S(1)}, u32[]{:S(2)}, u32[]{:S(2)}) collective-permute-start(f32[32,128]{1,0:T(8,128)S(1)} %get-tuple-element.26.own_ref), channel_id=1, source_target_pairs={{0,1},{1,0},{2,3},{3,2},{4,5},{5,4},{6,7},{7,6},{8,9},{9,8},{10,11... | collective-permute-start | bytes 49160 | tf_op jit(solution)/shard_map/ppermute | solution.py:460
  12.2 1.1 %collective-permute-done.other_ref = f32[32,128]{1,0:T(8,128)S(1)} collective-permute-done((f32[32,128]{1,0:T(8,128)S(1)}, f32[32,128]{1,0:T(8,128)S(1)}, u32[]{:S(2)}, u32[]{:S(2)}) %collective-permute-start) | collective-permute-done | bytes 16416 | tf_op jit(solution)/shard_map/ppermute | solution.py:460
  13.3 0.6 copy-done.6
  14.0 4.1 %collective-permute-start.3 = (bf16[32,768]{1,0:T(8,128)(2,1)S(1)}, bf16[32,768]{1,0:T(8,128)(2,1)S(1)}, u32[]{:S(2)}, u32[]{:S(2)}) collective-permute-start(bf16[32,768]{1,0:T(8,128)(2,1)S(1)} %get-tuple-element.27._.refs_1_), channel_id=1, source_target_pairs={{0,24},{2,26},{4,28},{6,30},{8,16},{10,18},{12,20},{14,22},{16,8},... | collective-permute-start | bytes 147464 | tf_op jit(solution)/shard_map/ppermute | solution.py:457
  18.1 0.6 collective-permute-start.1
  18.7 2.6 %shard_map.123 = (bf16[1536,1024]{1,0:T(8,128)(2,1)S(1)}, f32[8,128]{1,0:T(8,128)S(1)}) custom-call(s32[16]{0:T(128)S(1)} %broadcast_xor_fusion.1.source_ref, bf16[1024,1536]{1,0:T(8,128)(2,1)S(1)} %bitcast.5, bf16[32,768]{1,0:T(8,128)(2,1)S(1)} %get-tuple-element.27._.refs_1_), custom_call_target="tpu_custom_call" | custom-call | bytes 6291456 | tf_op jit(solution)/shard_map/pallas_call | solution.py:253
  21.3 0.7 shard_map.124.refs_0_.slope_ref
  22.0 0.9 copy-done.10
  23.0 0.1 collective-permute-done.1.refs_2_
  23.1 1.7 %collective-permute-start.4 = (bf16[4,32,768]{2,1,0:T(8,128)(2,1)S(1)}, bf16[4,32,768]{2,1,0:T(8,128)(2,1)S(1)}, u32[]{:S(2)}, u32[]{:S(2)}) collective-permute-start(bf16[4,32,768]{2,1,0:T(8,128)(2,1)S(1)} %shard_map.125._.refs_0_), channel_id=1, source_target_pairs={{0,4},{2,6},{4,0},{6,2},{8,12},{10,14},{12,8},{14,10},{16,20},{18,... | collective-permute-start | bytes 589832 | tf_op jit(solution)/shard_map/ppermute | solution.py:457
  24.9 1.4 %shard_map.126.refs_0_.slope_ref = f32[1024,768]{1,0:T(8,128)S(1)} custom-call(f32[1024,768]{1,0:T(8,128)S(1)} %copy-done.2, bf16[4,32,768]{2,1,0:T(8,128)(2,1)S(1)} %shard_map.125._.refs_0_), custom_call_target="tpu_custom_call" | custom-call | bytes 6291456 | tf_op jit(solution)/shard_map/pallas_call | solution.py:218
  26.3 2.5 %collective-permute-done.4.refs_1_ = bf16[4,32,768]{2,1,0:T(8,128)(2,1)S(1)} collective-permute-done((bf16[4,32,768]{2,1,0:T(8,128)(2,1)S(1)}, bf16[4,32,768]{2,1,0:T(8,128)(2,1)S(1)}, u32[]{:S(2)}, u32[]{:S(2)}) %collective-permute-start.4) | collective-permute-done | bytes 196640 | tf_op jit(solution)/shard_map/ppermute | solution.py:457
  28.8 0.7 shard_map.127
  29.5 1.8 %collective-permute-done.6.refs_3_ = bf16[4,32,768]{2,1,0:T(8,128)(2,1)} collective-permute-done((bf16[4,32,768]{2,1,0:T(8,128)(2,1)}, bf16[4,32,768]{2,1,0:T(8,128)(2,1)}, u32[]{:S(2)}, u32[]{:S(2)}) %collective-permute-start.6) | collective-permute-done | bytes 196640 | tf_op jit(solution)/shard_map/ppermute | solution.py:457
  31.3 1.4 %shard_map.128 = (f32[32,256]{1,0:T(8,128)S(1)}, f32[8,256]{1,0:T(8,128)S(1)}) custom-call(bf16[4,32,768]{2,1,0:T(8,128)(2,1)S(1)} %shard_map.125._.refs_0_, bf16[4,32,768]{2,1,0:T(8,128)(2,1)S(1)} %collective-permute-done.4.refs_1_, bf16[4,32,768]{2,1,0:T(8,128)(2,1)} %collective-permute-done.5.refs_2_, bf16[4,32,768]{2,1,0:T(8,128)(2,1)} %collective-permute-done.6.refs_3_), custom_call_target="tpu_custom_call" | custom-call | tf_op jit(solution)/shard_map/pallas_call | solution.py:305
  32.7 1.6 %collective-permute-start.7 = (f32[32,256]{1,0:T(8,128)S(1)}, f32[32,256]{1,0:T(8,128)S(1)}, u32[]{:S(2)}, u32[]{:S(2)}) collective-permute-start(f32[32,256]{1,0:T(8,128)S(1)} %get-tuple-element.30._.own_ref), channel_id=1, source_target_pairs={{0,1},{1,0},{2,3},{3,2},{4,5},{5,4},{6,7},{7,6},{8,9},{9,8},{10,11... | collective-permute-start | bytes 98312 | tf_op jit(solution)/shard_map/ppermute | solution.py:460
  34.3 0.7 broadcast_xor_fusion.source_ref
  36.9 1.4 %copy-done.4 = bf16[16,32,1536]{2,1,0:T(8,128)(2,1)S(1)} copy-done((bf16[16,32,1536]{2,1,0:T(8,128)(2,1)S(1)}, bf16[16,32,1536]{2,1,0:T(8,128)(2,1)}, u32[]{:S(2)}) %copy-start.4) | copy-done | bytes 1572888
  38.3 1.5 %shard_map.129 = (bf16[1536,512]{1,0:T(8,128)(2,1)S(1)}, f32[8,128]{1,0:T(8,128)S(1)}) custom-call(s32[32]{0:T(128)S(1)} %broadcast_xor_fusion.source_ref, bf16[512,1536]{1,0:T(8,128)(2,1)S(1)} %bitcast.7, f32[32,256]{1,0:T(8,128)S(1)} %get-tuple-element.30._.own_ref), custom_call_target="tpu_custom_call" | custom-call | bytes 3145728 | tf_op jit(solution)/shard_map/pallas_call | solution.py:253
  39.9 1.5 %shard_map.130 = (f32[32,768]{1,0:T(8,128)S(1)}, f32[8,768]{1,0:T(8,128)S(1)}) custom-call(f32[1]{0:T(128)S(6)} %copy.13.scale_ref, f32[1]{0:T(128)S(6)} %copy.14.bias_ref, f32[1]{0:T(128)S(6)} %copy.15.gain_ref, s32[1]{0:T(128)S(6)} %copy.16.count_ref, f32[32,256]{1,0:T(8,128)S(1)} %get-tuple-element.30._.own_ref, ...), custom_call_target="tpu_custom_call" | custom-call | tf_op jit(solution)/shard_map/pallas_call | solution.py:373
  41.4 1.5 %shard_map.131 = (f32[392,768]{1,0:T(8,128)S(1)}, f32[384,768]{1,0:T(8,128)S(1)}, f32[768,768]{1,0:T(8,128)S(1)}) custom-call(f32[32,768]{1,0:T(8,128)S(1)} %get-tuple-element.36.grad_ref, f32[512,768]{1,0:T(8,128)S(1)} %copy-done.1, bf16[1536,512]{1,0:T(8,128)(2,1)S(1)} %get-tuple-element.37.turned_ref, f32[8,768]{1,0:T(8,128)S(1)} %get-tuple-element.35.stat_ref._, ...), custom_call_target="tpu_custom_call" | custom-call | flops 1207959552 | bytes 7864320 | tf_op jit(solution)/shard_map/pallas_call | solution.py:416
  43.0 0.3 copy-done.11
  43.3 2.9 %shard_map.132 = (f32[384,768]{1,0:T(8,128)S(1)}, f32[384,768]{1,0:T(8,128)S(1)}, f32[768,768]{1,0:T(8,128)S(1)}) custom-call(f32[32,768]{1,0:T(8,128)S(1)} %get-tuple-element.36.grad_ref, f32[1024,768]{1,0:T(8,128)S(1)} %shard_map.126.refs_0_.slope_ref, bf16[1536,1024]{1,0:T(8,128)(2,1)S(1)} %copy-done.11, f32[8,768]{1,0:T(8,128)S(1)} %get-tuple-element.35.stat_ref._, ...), custom_call_target="tpu_custom_call" | custom-call | flops 2415919104 | bytes 11010048 | tf_op jit(solution)/shard_map/pallas_call | solution.py:416
  46.2 0.3 collective-permute-start.11
  46.5 0.3 collective-permute-start.13
  46.8 0.2 collective-permute-start.10
  47.0 0.1 fusion.34
  47.1 0.1 fusion
  47.4 1.6 %collective-permute-start.9 = (f16[392,768]{1,0:T(8,128)(2,1)S(1)}, f16[392,768]{1,0:T(8,128)(2,1)S(1)}, u32[]{:S(2)}, u32[]{:S(2)}) collective-permute-start(f16[392,768]{1,0:T(8,128)(2,1)S(1)} %add_convert_fusion.1), channel_id=1, source_target_pairs={{0,4},{2,6},{4,0},{6,2},{8,12},{10,14},{12,8},{14,10},{16,20},{18,... | collective-permute-start | bytes 1806344 | tf_op jit(solution)/shard_map/ppermute | solution.py:457
  49.1 0.2 add_multiply_fusion
  49.5 2.0 %collective-permute-start.14 = (f16[392,768]{1,0:T(8,128)(2,1)S(1)}, f16[392,768]{1,0:T(8,128)(2,1)S(1)}, u32[]{:S(2)}, u32[]{:S(2)}) collective-permute-start(f16[392,768]{1,0:T(8,128)(2,1)S(1)} %add_convert_fusion), channel_id=1, source_target_pairs={{0,8},{2,10},{4,12},{6,14},{8,0},{10,2},{12,4},{14,6},{16,24},{18,... | collective-permute-start | bytes 1806344 | tf_op jit(solution)/shard_map/ppermute | solution.py:457
  51.5 11.8 %collective-permute-done.9 = f16[392,768]{1,0:T(8,128)(2,1)S(1)} collective-permute-done((f16[392,768]{1,0:T(8,128)(2,1)S(1)}, f16[392,768]{1,0:T(8,128)(2,1)S(1)}, u32[]{:S(2)}, u32[]{:S(2)}) %collective-permute-start.9) | collective-permute-done | bytes 602144 | tf_op jit(solution)/shard_map/ppermute | solution.py:457
  63.3 0.1 fusion.38
  63.6 2.2 %collective-permute-start.17 = (f16[104,768]{1,0:T(8,128)(2,1)S(1)}, f16[104,768]{1,0:T(8,128)(2,1)S(1)}, u32[]{:S(2)}, u32[]{:S(2)}) collective-permute-start(f16[104,768]{1,0:T(8,128)(2,1)S(1)} %add_convert_fusion.5), channel_id=1, source_target_pairs={{0,16},{2,18},{4,20},{6,22},{8,24},{10,26},{12,28},{14,30},{16,0},... | collective-permute-start | bytes 479240 | tf_op jit(solution)/shard_map/ppermute | solution.py:457
  66.1 2.1 %collective-permute-start.12 = (f16[104,768]{1,0:T(8,128)(2,1)S(1)}, f16[104,768]{1,0:T(8,128)(2,1)S(1)}, u32[]{:S(2)}, u32[]{:S(2)}) collective-permute-start(f16[104,768]{1,0:T(8,128)(2,1)S(1)} %add_convert_fusion.4), channel_id=1, source_target_pairs={{0,8},{2,10},{4,12},{6,14},{8,0},{10,2},{12,4},{14,6},{16,24},{18,... | collective-permute-start | bytes 479240 | tf_op jit(solution)/shard_map/ppermute | solution.py:457
  68.4 0.1 fusion.2
  68.6 1.6 %collective-permute-start.15 = (f16[200,768]{1,0:T(8,128)(2,1)S(1)}, f16[200,768]{1,0:T(8,128)(2,1)S(1)}, u32[]{:S(2)}, u32[]{:S(2)}) collective-permute-start(f16[200,768]{1,0:T(8,128)(2,1)S(1)} %add_convert_fusion.2), channel_id=1, source_target_pairs={{0,4},{2,6},{4,0},{6,2},{8,12},{10,14},{12,8},{14,10},{16,20},{18,... | collective-permute-start | bytes 921608 | tf_op jit(solution)/shard_map/ppermute | solution.py:457
  70.2 2.9 %collective-permute-done.12 = f16[104,768]{1,0:T(8,128)(2,1)S(1)} collective-permute-done((f16[104,768]{1,0:T(8,128)(2,1)S(1)}, f16[104,768]{1,0:T(8,128)(2,1)S(1)}, u32[]{:S(2)}, u32[]{:S(2)}) %collective-permute-start.12) | collective-permute-done | bytes 159776 | tf_op jit(solution)/shard_map/ppermute | solution.py:457
  73.2 3.6 %collective-permute-done.15 = f16[200,768]{1,0:T(8,128)(2,1)S(1)} collective-permute-done((f16[200,768]{1,0:T(8,128)(2,1)S(1)}, f16[200,768]{1,0:T(8,128)(2,1)S(1)}, u32[]{:S(2)}, u32[]{:S(2)}) %collective-permute-start.15) | collective-permute-done | bytes 307232 | tf_op jit(solution)/shard_map/ppermute | solution.py:457
  77.2 0.7 collective-permute-start.16
  78.4 1.1 %collective-permute-start.18 = (f16[56,768]{1,0:T(8,128)(2,1)S(1)}, f16[56,768]{1,0:T(8,128)(2,1)S(1)}, u32[]{:S(2)}, u32[]{:S(2)}) collective-permute-start(f16[56,768]{1,0:T(8,128)(2,1)S(1)} %add_convert_fusion.6), channel_id=1, source_target_pairs={{0,8},{2,10},{4,12},{6,14},{8,0},{10,2},{12,4},{14,6},{16,24},{18,... | collective-permute-start | bytes 258056 | tf_op jit(solution)/shard_map/ppermute | solution.py:457
  79.4 4.0 %collective-permute-done.18 = f16[56,768]{1,0:T(8,128)(2,1)S(1)} collective-permute-done((f16[56,768]{1,0:T(8,128)(2,1)S(1)}, f16[56,768]{1,0:T(8,128)(2,1)S(1)}, u32[]{:S(2)}, u32[]{:S(2)}) %collective-permute-start.18) | collective-permute-done | bytes 86048 | tf_op jit(solution)/shard_map/ppermute | solution.py:457
  83.5 5.3 %collective-permute-done.16 = f16[152,768]{1,0:T(8,128)(2,1)S(1)} collective-permute-done((f16[152,768]{1,0:T(8,128)(2,1)S(1)}, f16[152,768]{1,0:T(8,128)(2,1)S(1)}, u32[]{:S(2)}, u32[]{:S(2)}) %collective-permute-start.16) | collective-permute-done | bytes 233504 | tf_op jit(solution)/shard_map/ppermute | solution.py:457
  88.8 0.6 fusion.107
  89.4 0.1 fusion.19
  89.6 0.7 pad_maximum_fusion
  90.3 0.8 fusion.5
  (87 shorter events, 2.3 us)
Async XLA Ops:
  0.6 18.0 %copy-start.12 = (s32[16]{0:T(128)S(1)}, s32[16]{0:T(128)}, u32[]{:S(2)}) copy-start(s32[16]{0:T(128)} %constant.61.clone) | copy-start | bytes 196
  0.6 18.0 %copy-start.3 = (bf16[16,64,1536]{2,1,0:T(8,128)(2,1)S(1)}, bf16[16,64,1536]{2,1,0:T(8,128)(2,1)}, u32[]{:S(2)}) copy-start(bf16[16,64,1536]{2,1,0:T(8,128)(2,1)} %param.10) | copy-start | bytes 9437188
  8.5 4.7 %collective-permute-start = (f32[32,128]{1,0:T(8,128)S(1)}, f32[32,128]{1,0:T(8,128)S(1)}, u32[]{:S(2)}, u32[]{:S(2)}) collective-permute-start(f32[32,128]{1,0:T(8,128)S(1)} %get-tuple-element.26.own_ref), channel_id=1, source_target_pairs={{0,1},{1,0},{2,3},{3,2},{4,5},{5,4},{6,7},{7,6},{8,9},{9,8},{10,11... | collective-permute-start | bytes 49160 | tf_op jit(solution)/shard_map/ppermute | solution.py:460
  13.3 0.6 copy-start.6
  14.0 9.0 %collective-permute-start.3 = (bf16[32,768]{1,0:T(8,128)(2,1)S(1)}, bf16[32,768]{1,0:T(8,128)(2,1)S(1)}, u32[]{:S(2)}, u32[]{:S(2)}) collective-permute-start(bf16[32,768]{1,0:T(8,128)(2,1)S(1)} %get-tuple-element.27._.refs_1_), channel_id=1, source_target_pairs={{0,24},{2,26},{4,28},{6,30},{8,16},{10,18},{12,20},{14,22},{16,8},... | collective-permute-start | bytes 147464 | tf_op jit(solution)/shard_map/ppermute | solution.py:457
  18.1 4.9 %collective-permute-start.2 = (bf16[32,768]{1,0:T(8,128)(2,1)S(1)}, bf16[32,768]{1,0:T(8,128)(2,1)S(1)}, u32[]{:S(2)}, u32[]{:S(2)}) collective-permute-start(bf16[32,768]{1,0:T(8,128)(2,1)S(1)} %get-tuple-element.27._.refs_1_), channel_id=1, source_target_pairs={{0,8},{2,10},{4,12},{6,14},{8,0},{10,2},{12,4},{14,6},{16,24},{18,... | collective-permute-start | bytes 147464 | tf_op jit(solution)/shard_map/ppermute | solution.py:457
  18.1 5.0 %collective-permute-start.1 = (bf16[32,768]{1,0:T(8,128)(2,1)S(1)}, bf16[32,768]{1,0:T(8,128)(2,1)S(1)}, u32[]{:S(2)}, u32[]{:S(2)}) collective-permute-start(bf16[32,768]{1,0:T(8,128)(2,1)S(1)} %get-tuple-element.27._.refs_1_), channel_id=1, source_target_pairs={{0,16},{2,18},{4,20},{6,22},{8,24},{10,26},{12,28},{14,30},{16,0},... | collective-permute-start | bytes 147464 | tf_op jit(solution)/shard_map/ppermute | solution.py:457
  18.7 2.6 %copy-start.5 = (f32[512,768]{1,0:T(8,128)S(1)}, f32[512,768]{1,0:T(8,128)}, u32[]{:S(2)}) copy-start(f32[512,768]{1,0:T(8,128)} %get-tuple-element.24.preact_ref) | copy-start | bytes 4718596
  21.3 0.8 copy-start.8
  21.3 1.7 %copy-start.10 = (bf16[1536,1024]{1,0:T(8,128)(2,1)}, bf16[1536,1024]{1,0:T(8,128)(2,1)S(1)}, u32[]{:S(2)}) copy-start(bf16[1536,1024]{1,0:T(8,128)(2,1)S(1)} %get-tuple-element.41.turned_ref) | copy-start | bytes 9437188
  21.3 3.6 %copy-start.2 = (f32[1024,768]{1,0:T(8,128)S(1)}, f32[1024,768]{1,0:T(8,128)}, u32[]{:S(2)}) copy-start(f32[1024,768]{1,0:T(8,128)} %get-tuple-element.29.preact_ref) | copy-start | bytes 9437188
  22.9 1.9 %copy-start = (f32[512,768]{1,0:T(8,128)}, f32[512,768]{1,0:T(8,128)S(1)}, u32[]{:S(2)}) copy-start(f32[512,768]{1,0:T(8,128)S(1)} %shard_map.124.refs_0_.slope_ref) | copy-start | bytes 4718596
  23.1 5.7 %collective-permute-start.4 = (bf16[4,32,768]{2,1,0:T(8,128)(2,1)S(1)}, bf16[4,32,768]{2,1,0:T(8,128)(2,1)S(1)}, u32[]{:S(2)}, u32[]{:S(2)}) collective-permute-start(bf16[4,32,768]{2,1,0:T(8,128)(2,1)S(1)} %shard_map.125._.refs_0_), channel_id=1, source_target_pairs={{0,4},{2,6},{4,0},{6,2},{8,12},{10,14},{12,8},{14,10},{16,20},{18,... | collective-permute-start | bytes 589832 | tf_op jit(solution)/shard_map/ppermute | solution.py:457
  24.8 4.7 %collective-permute-start.5 = (bf16[4,32,768]{2,1,0:T(8,128)(2,1)S(1)}, bf16[4,32,768]{2,1,0:T(8,128)(2,1)}, u32[]{:S(2)}, u32[]{:S(2)}) collective-permute-start(bf16[4,32,768]{2,1,0:T(8,128)(2,1)S(1)} %shard_map.125._.refs_0_), channel_id=1, source_target_pairs={{0,2},{2,0},{4,6},{6,4},{8,10},{10,8},{12,14},{14,12},{16,18},{18,... | collective-permute-start | bytes 589832 | tf_op jit(solution)/shard_map/ppermute | solution.py:457
  29.5 1.8 %collective-permute-start.6 = (bf16[4,32,768]{2,1,0:T(8,128)(2,1)}, bf16[4,32,768]{2,1,0:T(8,128)(2,1)}, u32[]{:S(2)}, u32[]{:S(2)}) collective-permute-start(bf16[4,32,768]{2,1,0:T(8,128)(2,1)} %bitcast.3), channel_id=1, source_target_pairs={{0,2},{2,0},{4,6},{6,4},{8,10},{10,8},{12,14},{14,12},{16,18},{18,... | collective-permute-start | bytes 589832 | tf_op jit(solution)/shard_map/ppermute | solution.py:457
  29.5 10.3 %copy-start.7 = (f32[32,768]{1,0:T(8,128)S(1)}, f32[32,768]{1,0:T(8,128)}, u32[]{:S(2)}) copy-start(f32[32,768]{1,0:T(8,128)} %copy-done.6) | copy-start | bytes 294916
  29.5 10.3 %copy-start.9 = (f32[8,128]{1,0:T(8,128)S(1)}, f32[8,128]{1,0:T(8,128)}, u32[]{:S(2)}) copy-start(f32[8,128]{1,0:T(8,128)} %copy-done.8) | copy-start | bytes 12292
  32.7 7.1 %collective-permute-start.7 = (f32[32,256]{1,0:T(8,128)S(1)}, f32[32,256]{1,0:T(8,128)S(1)}, u32[]{:S(2)}, u32[]{:S(2)}) collective-permute-start(f32[32,256]{1,0:T(8,128)S(1)} %get-tuple-element.30._.own_ref), channel_id=1, source_target_pairs={{0,1},{1,0},{2,3},{3,2},{4,5},{5,4},{6,7},{7,6},{8,9},{9,8},{10,11... | collective-permute-start | bytes 98312 | tf_op jit(solution)/shard_map/ppermute | solution.py:460
  36.9 1.4 %copy-start.4 = (bf16[16,32,1536]{2,1,0:T(8,128)(2,1)S(1)}, bf16[16,32,1536]{2,1,0:T(8,128)(2,1)}, u32[]{:S(2)}) copy-start(bf16[16,32,1536]{2,1,0:T(8,128)(2,1)} %param.11) | copy-start | bytes 4718596
  38.3 3.1 %copy-start.1 = (f32[512,768]{1,0:T(8,128)S(1)}, f32[512,768]{1,0:T(8,128)}, u32[]{:S(2)}) copy-start(f32[512,768]{1,0:T(8,128)} %copy-done) | copy-start | bytes 4718596
  41.4 1.9 %copy-start.11 = (bf16[1536,1024]{1,0:T(8,128)(2,1)S(1)}, bf16[1536,1024]{1,0:T(8,128)(2,1)}, u32[]{:S(2)}) copy-start(bf16[1536,1024]{1,0:T(8,128)(2,1)} %copy-done.10) | copy-start | bytes 9437188
  42.9 4.1 %collective-permute-start.8 = (f32[392,768]{1,0:T(8,128)S(1)}, f32[392,768]{1,0:T(8,128)S(1)}, u32[]{:S(2)}, u32[]{:S(2)}) collective-permute-start(f32[392,768]{1,0:T(8,128)S(1)} %get-tuple-element.38._), channel_id=1, source_target_pairs={{0,2},{2,0},{4,6},{6,4},{8,10},{10,8},{12,14},{14,12},{16,18},{18,... | collective-permute-start | bytes 3612680 | tf_op jit(solution)/shard_map/ppermute | solution.py:457
  46.2 2.9 %collective-permute-start.11 = (f32[384,768]{1,0:T(8,128)S(1)}, f32[384,768]{1,0:T(8,128)S(1)}, u32[]{:S(2)}, u32[]{:S(2)}) collective-permute-start(f32[384,768]{1,0:T(8,128)S(1)} %get-tuple-element.43), channel_id=1, source_target_pairs={{0,2},{2,0},{4,6},{6,4},{8,10},{10,8},{12,14},{14,12},{16,18},{18,... | collective-permute-start | bytes 3538952 | tf_op jit(solution)/shard_map/ppermute | solution.py:457
  46.5 21.9 %collective-permute-start.13 = (f32[384,768]{1,0:T(8,128)S(1)}, f32[384,768]{1,0:T(8,128)S(1)}, u32[]{:S(2)}, u32[]{:S(2)}) collective-permute-start(f32[384,768]{1,0:T(8,128)S(1)} %get-tuple-element.44), channel_id=1, source_target_pairs={{0,2},{2,0},{4,6},{6,4},{8,10},{10,8},{12,14},{14,12},{16,18},{18,... | collective-permute-start | bytes 3538952 | tf_op jit(solution)/shard_map/ppermute | solution.py:457
  46.8 16.6 %collective-permute-start.10 = (f32[384,768]{1,0:T(8,128)S(1)}, f32[384,768]{1,0:T(8,128)S(1)}, u32[]{:S(2)}, u32[]{:S(2)}) collective-permute-start(f32[384,768]{1,0:T(8,128)S(1)} %get-tuple-element.40), channel_id=1, source_target_pairs={{0,2},{2,0},{4,6},{6,4},{8,10},{10,8},{12,14},{14,12},{16,18},{18,... | collective-permute-start | bytes 3538952 | tf_op jit(solution)/shard_map/ppermute | solution.py:457
  47.4 15.9 %collective-permute-start.9 = (f16[392,768]{1,0:T(8,128)(2,1)S(1)}, f16[392,768]{1,0:T(8,128)(2,1)S(1)}, u32[]{:S(2)}, u32[]{:S(2)}) collective-permute-start(f16[392,768]{1,0:T(8,128)(2,1)S(1)} %add_convert_fusion.1), channel_id=1, source_target_pairs={{0,4},{2,6},{4,0},{6,2},{8,12},{10,14},{12,8},{14,10},{16,20},{18,... | collective-permute-start | bytes 1806344 | tf_op jit(solution)/shard_map/ppermute | solution.py:457
  49.5 18.7 %collective-permute-start.14 = (f16[392,768]{1,0:T(8,128)(2,1)S(1)}, f16[392,768]{1,0:T(8,128)(2,1)S(1)}, u32[]{:S(2)}, u32[]{:S(2)}) collective-permute-start(f16[392,768]{1,0:T(8,128)(2,1)S(1)} %add_convert_fusion), channel_id=1, source_target_pairs={{0,8},{2,10},{4,12},{6,14},{8,0},{10,2},{12,4},{14,6},{16,24},{18,... | collective-permute-start | bytes 1806344 | tf_op jit(solution)/shard_map/ppermute | solution.py:457
  63.6 14.3 %collective-permute-start.17 = (f16[104,768]{1,0:T(8,128)(2,1)S(1)}, f16[104,768]{1,0:T(8,128)(2,1)S(1)}, u32[]{:S(2)}, u32[]{:S(2)}) collective-permute-start(f16[104,768]{1,0:T(8,128)(2,1)S(1)} %add_convert_fusion.5), channel_id=1, source_target_pairs={{0,16},{2,18},{4,20},{6,22},{8,24},{10,26},{12,28},{14,30},{16,0},... | collective-permute-start | bytes 479240 | tf_op jit(solution)/shard_map/ppermute | solution.py:457
  66.1 7.0 %collective-permute-start.12 = (f16[104,768]{1,0:T(8,128)(2,1)S(1)}, f16[104,768]{1,0:T(8,128)(2,1)S(1)}, u32[]{:S(2)}, u32[]{:S(2)}) collective-permute-start(f16[104,768]{1,0:T(8,128)(2,1)S(1)} %add_convert_fusion.4), channel_id=1, source_target_pairs={{0,8},{2,10},{4,12},{6,14},{8,0},{10,2},{12,4},{14,6},{16,24},{18,... | collective-permute-start | bytes 479240 | tf_op jit(solution)/shard_map/ppermute | solution.py:457
  68.6 8.2 %collective-permute-start.15 = (f16[200,768]{1,0:T(8,128)(2,1)S(1)}, f16[200,768]{1,0:T(8,128)(2,1)S(1)}, u32[]{:S(2)}, u32[]{:S(2)}) collective-permute-start(f16[200,768]{1,0:T(8,128)(2,1)S(1)} %add_convert_fusion.2), channel_id=1, source_target_pairs={{0,4},{2,6},{4,0},{6,2},{8,12},{10,14},{12,8},{14,10},{16,20},{18,... | collective-permute-start | bytes 921608 | tf_op jit(solution)/shard_map/ppermute | solution.py:457
  77.2 11.6 %collective-permute-start.16 = (f16[152,768]{1,0:T(8,128)(2,1)S(1)}, f16[152,768]{1,0:T(8,128)(2,1)S(1)}, u32[]{:S(2)}, u32[]{:S(2)}) collective-permute-start(f16[152,768]{1,0:T(8,128)(2,1)S(1)} %add_convert_fusion.3), channel_id=1, source_target_pairs={{0,16},{2,18},{4,20},{6,22},{8,24},{10,26},{12,28},{14,30},{16,0},... | collective-permute-start | bytes 700424 | tf_op jit(solution)/shard_map/ppermute | solution.py:457
  78.4 5.1 %collective-permute-start.18 = (f16[56,768]{1,0:T(8,128)(2,1)S(1)}, f16[56,768]{1,0:T(8,128)(2,1)S(1)}, u32[]{:S(2)}, u32[]{:S(2)}) collective-permute-start(f16[56,768]{1,0:T(8,128)(2,1)S(1)} %add_convert_fusion.6), channel_id=1, source_target_pairs={{0,8},{2,10},{4,12},{6,14},{8,0},{10,2},{12,4},{14,6},{16,24},{18,... | collective-permute-start | bytes 258056 | tf_op jit(solution)/shard_map/ppermute | solution.py:457

commit v8 on v4

--- a/solution.py
+++ b/solution.py
@@ -64,6 +64,8 @@
     text_w,
     image_slope,
     text_slope,
+    even,
+    odd,
     in_sem,
     w_sem,
     out_sem,
@@ -90,12 +92,13 @@
 
     def project(n):
         t, start, column = tiles[n]
-        _, buf, _, w, slope, _, _, _ = towers_here[t]
+        _, buf, _, w, _, _, _, _ = towers_here[t]
         if start == 0 and column == 0:
             for copy in waits[t]:
                 copy.wait()
         rows, columns = slice(start, start + JOB_ROWS), slice(column, column + JOB_COLUMNS)
-        slope[rows, columns] = jnp.dot(buf[rows, :], w[:, columns], preferred_element_type=F32)
+        target = (even, odd)[n % 2]
+        target[...] = jnp.dot(buf[rows, :], w[:, columns], preferred_element_type=F32)
 
     out_copies = []
     project(0)
@@ -107,7 +110,8 @@
             rows = slice(row, row + STRIP)
             here = (rows, slice(tile_column, tile_column + JOB_COLUMNS))
             token_columns = pl.ds(pl.multiple_of(first + tile_column, 128), JOB_COLUMNS)
-            value, slant = gelu_and_slope(slope[here])
+            preact = (even, odd)[n % 2][row - start : row - start + STRIP, :]
+            value, slant = gelu_and_slope(preact)
             slope[here] = slant
             hidden = buf[rows, token_columns].astype(F32) + value
             for part in range(0, STRIP, tok):
@@ -151,6 +155,8 @@
             pltpu.VMEM((depth, width), BF16),
             pltpu.VMEM((rows_i, width), F32),
             pltpu.VMEM((rows_t, width), F32),
+            pltpu.VMEM((JOB_ROWS, JOB_COLUMNS), F32),
+            pltpu.VMEM((JOB_ROWS, JOB_COLUMNS), F32),
             pltpu.SemaphoreType.DMA((2,)),
             pltpu.SemaphoreType.DMA((2,)),
             pltpu.SemaphoreType.DMA((jobs,)),
@@ -463,7 +469,7 @@
 
     low = max(bits - 2, 1)
     tops = [1 << b for b in reversed(range(low, bits))]
-    masks = tops + [tops[0] | tops[1]] if len(tops) == 2 else tops
+    masks = [tops[0] | tops[1], *tops] if len(tops) == 2 else tops
     arrived = [swap(sent, mask) for mask in masks]
     image_turned, image_most = turn(image_blocks, image_flat, sent)
     gathered = stack([sent] + arrived, image_most)

time: 86.5 us -> 86.2 us (level)
  waiting for transfers between devices: 39.3 us -> 37.4 us
  starting transfers between devices: 19.4 us -> 21.1 us
    ppermute x18, waiting for transfers between devices: 37.8 us -> 35.9 us  [swap(): return lax.ppermute(array, 'dp', [(i, i ^ mask) for i in range(cycle)])]
    ppermute x18, starting transfers between devices: 14.9 us -> 16.6 us  [swap(): return lax.ppermute(array, 'dp', [(i, i ^ mask) for i in range(cycle)])]
where the time goes in v8:
time: 86.2 us; the launch traced here: 86 us
  waiting for transfers between devices  37.4 us (43%)
  starting transfers between devices  21.1 us (24%)
  Pallas kernels  18.6 us (22%)
  other arithmetic  4.87 us (6%)
  between operations  3.66 us (4%)
    ppermute x18, waiting for transfers between devices, swap(): return lax.ppermute(array, 'dp', [(i, i ^ mask) for i in range(cycle)])  35.9 us
    ppermute x18, starting transfers between devices, swap(): return lax.ppermute(array, 'dp', [(i, i ^ mask) for i in range(cycle)])  16.6 us
    pallas_call x1, Pallas kernels, forward(): pl.pallas_call(functools.partial(forward_kernel, (rows_i // samples, rows...  9.25 us
    ppermute x2, starting transfers between devices, swap_halves(): return lax.ppermute(array, 'mp', [(0, 1), (1, 0)])  4.52 us
    pallas_call x2, Pallas kernels, weight_terms(): pl.pallas_call(functools.partial(weight_kernel, base, carries), out_shape...  4.32 us
    pallas_call x2, Pallas kernels, turn(): pl.pallas_call(turn_kernel, out_shape=(jax.ShapeDtypeStruct((depth, rows)...  4.07 us
  transfers between devices with their start and end apart: 20, of which 12 were waited for; matrix products, arithmetic and copies ran while one was open for 4% of the time, Pallas kernels for 8%

profile of v8, /device:TPU:0, one launch (start us, length us, event | category | flops | bytes accessed | tf_op | source)
XLA Modules:
  0.0 86.0 jit_solution(10449248564654535311)
XLA Ops:
  0.7 9.2 %shard_map.121 = (f32[32,768]{1,0:T(8,128)S(1)}, f32[32,128]{1,0:T(8,128)S(1)}, f32[1024,768]{1,0:T(8,128)}, f32[512,768]{1,0:T(8,128)}) custom-call(s32[1]{0:T(128)} %bitcast.1.place_ref, bf16[1024,1536]{1,0:T(8,128)(2,1)} %bitcast.4, bf16[512,1536]{1,0:T(8,128)(2,1)} %bitcast.6, bf16[1536,768]{1,0:T(8,128)(2,1)} %image_w_hbm.1, bf16[1536,768]{1,0:T(8,128)(2,1)} %text_w_hbm.1), custom_call_target="tpu_custom_call" | custom-call | flops 3623878656 | bytes 14155776 | tf_op jit(solution)/shard_map/pallas_call | solution.py:141
  9.9 3.0 %collective-permute-start = (f32[32,128]{1,0:T(8,128)S(1)}, f32[32,128]{1,0:T(8,128)S(1)}, u32[]{:S(2)}, u32[]{:S(2)}) collective-permute-start(f32[32,128]{1,0:T(8,128)S(1)} %get-tuple-element.25.own_ref), channel_id=1, source_target_pairs={{0,1},{1,0},{2,3},{3,2},{4,5},{5,4},{6,7},{7,6},{8,9},{9,8},{10,11... | collective-permute-start | bytes 49160 | tf_op jit(solution)/shard_map/ppermute | solution.py:443
  13.6 1.1 %collective-permute-done.other_ref = f32[32,128]{1,0:T(8,128)S(1)} collective-permute-done((f32[32,128]{1,0:T(8,128)S(1)}, f32[32,128]{1,0:T(8,128)S(1)}, u32[]{:S(2)}, u32[]{:S(2)}) %collective-permute-start) | collective-permute-done | bytes 16416 | tf_op jit(solution)/shard_map/ppermute | solution.py:443
  14.6 0.1 shard_map.122
  14.7 4.2 %collective-permute-start.1 = (bf16[32,768]{1,0:T(8,128)(2,1)S(1)}, bf16[32,768]{1,0:T(8,128)(2,1)S(1)}, u32[]{:S(2)}, u32[]{:S(2)}) collective-permute-start(bf16[32,768]{1,0:T(8,128)(2,1)S(1)} %get-tuple-element.26._.refs_1_), channel_id=1, source_target_pairs={{0,24},{2,26},{4,28},{6,30},{8,16},{10,18},{12,20},{14,22},{16,8},... | collective-permute-start | bytes 147464 | tf_op jit(solution)/shard_map/ppermute | solution.py:440
  19.0 0.6 collective-permute-start.3
  19.6 2.6 %shard_map.123 = (bf16[1536,1024]{1,0:T(8,128)(2,1)S(1)}, f32[8,128]{1,0:T(8,128)S(1)}) custom-call(s32[16]{0:T(128)S(1)} %broadcast_xor_fusion.1.source_ref, bf16[1024,1536]{1,0:T(8,128)(2,1)S(1)} %bitcast.5, bf16[32,768]{1,0:T(8,128)(2,1)S(1)} %get-tuple-element.26._.refs_1_), custom_call_target="tpu_custom_call" | custom-call | bytes 6291456 | tf_op jit(solution)/shard_map/pallas_call | solution.py:236
  22.2 1.7 %collective-permute-done.2.refs_3_ = bf16[32,768]{1,0:T(8,128)(2,1)S(1)} collective-permute-done((bf16[32,768]{1,0:T(8,128)(2,1)S(1)}, bf16[32,768]{1,0:T(8,128)(2,1)S(1)}, u32[]{:S(2)}, u32[]{:S(2)}) %collective-permute-start.2) | collective-permute-done | bytes 49184 | tf_op jit(solution)/shard_map/ppermute | solution.py:440
  24.0 1.6 %collective-permute-start.4 = (bf16[4,32,768]{2,1,0:T(8,128)(2,1)S(1)}, bf16[4,32,768]{2,1,0:T(8,128)(2,1)S(1)}, u32[]{:S(2)}, u32[]{:S(2)}) collective-permute-start(bf16[4,32,768]{2,1,0:T(8,128)(2,1)S(1)} %shard_map.124._.refs_0_), channel_id=1, source_target_pairs={{0,4},{2,6},{4,0},{6,2},{8,12},{10,14},{12,8},{14,10},{16,20},{18,... | collective-permute-start | bytes 589832 | tf_op jit(solution)/shard_map/ppermute | solution.py:440
  25.6 1.5 %shard_map.125 = (bf16[1536,512]{1,0:T(8,128)(2,1)S(1)}, f32[8,128]{1,0:T(8,128)S(1)}) custom-call(s32[32]{0:T(128)S(1)} %broadcast_xor_fusion.source_ref, bf16[512,1536]{1,0:T(8,128)(2,1)S(1)} %bitcast.7, bf16[4,32,768]{2,1,0:T(8,128)(2,1)S(1)} %shard_map.124._.refs_0_), custom_call_target="tpu_custom_call" | custom-call | bytes 3145728 | tf_op jit(solution)/shard_map/pallas_call | solution.py:236
  27.1 2.6 %collective-permute-done.4.refs_1_ = bf16[4,32,768]{2,1,0:T(8,128)(2,1)S(1)} collective-permute-done((bf16[4,32,768]{2,1,0:T(8,128)(2,1)S(1)}, bf16[4,32,768]{2,1,0:T(8,128)(2,1)S(1)}, u32[]{:S(2)}, u32[]{:S(2)}) %collective-permute-start.4) | collective-permute-done | bytes 196640 | tf_op jit(solution)/shard_map/ppermute | solution.py:440
  29.8 1.4 %collective-permute-done.6.refs_3_ = bf16[4,32,768]{2,1,0:T(8,128)(2,1)S(1)} collective-permute-done((bf16[4,32,768]{2,1,0:T(8,128)(2,1)S(1)}, bf16[4,32,768]{2,1,0:T(8,128)(2,1)S(1)}, u32[]{:S(2)}, u32[]{:S(2)}) %collective-permute-start.6) | collective-permute-done | bytes 196640 | tf_op jit(solution)/shard_map/ppermute | solution.py:440
  31.2 0.4 shard_map.127
  31.6 1.5 %collective-permute-start.7 = (f32[32,256]{1,0:T(8,128)S(1)}, f32[32,256]{1,0:T(8,128)S(1)}, u32[]{:S(2)}, u32[]{:S(2)}) collective-permute-start(f32[32,256]{1,0:T(8,128)S(1)} %get-tuple-element.29.own_ref), channel_id=1, source_target_pairs={{0,1},{1,0},{2,3},{3,2},{4,5},{5,4},{6,7},{7,6},{8,9},{9,8},{10,11... | collective-permute-start | bytes 98312 | tf_op jit(solution)/shard_map/ppermute | solution.py:443
  35.0 0.5 collective-permute-done.7.other_ref
  35.5 0.5 shard_map.128
  36.1 1.5 %shard_map.129 = (f32[392,768]{1,0:T(8,128)S(1)}, f32[384,768]{1,0:T(8,128)S(1)}, f32[768,768]{1,0:T(8,128)S(1)}) custom-call(f32[32,768]{1,0:T(8,128)S(1)} %get-tuple-element.34.grad_ref, f32[512,768]{1,0:T(8,128)S(1)} %copy-done.3, bf16[1536,512]{1,0:T(8,128)(2,1)S(1)} %get-tuple-element.36.turned_ref, f32[8,768]{1,0:T(8,128)S(1)} %get-tuple-element.33.stat_ref._, ...), custom_call_target="tpu_custom_call" | custom-call | flops 1207959552 | bytes 7864320 | tf_op jit(solution)/shard_map/pallas_call | solution.py:399
  37.7 0.3 copy-done.2
  38.0 2.8 %shard_map.130 = (f32[384,768]{1,0:T(8,128)S(1)}, f32[384,768]{1,0:T(8,128)S(1)}, f32[768,768]{1,0:T(8,128)S(1)}) custom-call(f32[32,768]{1,0:T(8,128)S(1)} %get-tuple-element.34.grad_ref, f32[1024,768]{1,0:T(8,128)S(1)} %copy-done.2, bf16[1536,1024]{1,0:T(8,128)(2,1)S(1)} %get-tuple-element.41.turned_ref, f32[8,768]{1,0:T(8,128)S(1)} %get-tuple-element.33.stat_ref._, ...), custom_call_target="tpu_custom_call" | custom-call | flops 2415919104 | bytes 11010048 | tf_op jit(solution)/shard_map/pallas_call | solution.py:399
  40.8 0.3 collective-permute-start.13
  41.1 0.3 collective-permute-start.11
  41.4 0.2 collective-permute-start.10
  41.6 0.1 fusion.34
  41.7 0.1 fusion
  42.0 1.6 %collective-permute-start.9 = (f16[392,768]{1,0:T(8,128)(2,1)S(1)}, f16[392,768]{1,0:T(8,128)(2,1)S(1)}, u32[]{:S(2)}, u32[]{:S(2)}) collective-permute-start(f16[392,768]{1,0:T(8,128)(2,1)S(1)} %add_convert_fusion.1), channel_id=1, source_target_pairs={{0,4},{2,6},{4,0},{6,2},{8,12},{10,14},{12,8},{14,10},{16,20},{18,... | collective-permute-start | bytes 1806344 | tf_op jit(solution)/shard_map/ppermute | solution.py:440
  43.7 1.7 %collective-permute-done.11 = f32[384,768]{1,0:T(8,128)S(1)} collective-permute-done((f32[384,768]{1,0:T(8,128)S(1)}, f32[384,768]{1,0:T(8,128)S(1)}, u32[]{:S(2)}, u32[]{:S(2)}) %collective-permute-start.11) | collective-permute-done | bytes 1179680 | tf_op jit(solution)/shard_map/ppermute | solution.py:440
  45.4 0.1 add_multiply_fusion
  45.7 0.2 collective-permute-start.14
  45.9 12.0 %collective-permute-done.9 = f16[392,768]{1,0:T(8,128)(2,1)S(1)} collective-permute-done((f16[392,768]{1,0:T(8,128)(2,1)S(1)}, f16[392,768]{1,0:T(8,128)(2,1)S(1)}, u32[]{:S(2)}, u32[]{:S(2)}) %collective-permute-start.9) | collective-permute-done | bytes 602144 | tf_op jit(solution)/shard_map/ppermute | solution.py:440
  57.9 0.1 fusion.38
  58.2 0.2 collective-permute-start.12
  58.7 2.5 %collective-permute-start.18 = (f16[104,768]{1,0:T(8,128)(2,1)S(1)}, f16[104,768]{1,0:T(8,128)(2,1)S(1)}, u32[]{:S(2)}, u32[]{:S(2)}) collective-permute-start(f16[104,768]{1,0:T(8,128)(2,1)S(1)} %add_convert_fusion.4), channel_id=1, source_target_pairs={{0,16},{2,18},{4,20},{6,22},{8,24},{10,26},{12,28},{14,30},{16,0},... | collective-permute-start | bytes 479240 | tf_op jit(solution)/shard_map/ppermute | solution.py:440
  61.2 4.4 %collective-permute-done.14 = f16[392,768]{1,0:T(8,128)(2,1)S(1)} collective-permute-done((f16[392,768]{1,0:T(8,128)(2,1)S(1)}, f16[392,768]{1,0:T(8,128)(2,1)S(1)}, u32[]{:S(2)}, u32[]{:S(2)}) %collective-permute-start.14) | collective-permute-done | bytes 602144 | tf_op jit(solution)/shard_map/ppermute | solution.py:440
  65.6 0.1 fusion.42
  65.8 0.1 fusion.2
  66.0 1.6 %collective-permute-start.16 = (f16[200,768]{1,0:T(8,128)(2,1)S(1)}, f16[200,768]{1,0:T(8,128)(2,1)S(1)}, u32[]{:S(2)}, u32[]{:S(2)}) collective-permute-start(f16[200,768]{1,0:T(8,128)(2,1)S(1)} %add_convert_fusion.2), channel_id=1, source_target_pairs={{0,4},{2,6},{4,0},{6,2},{8,12},{10,14},{12,8},{14,10},{16,20},{18,... | collective-permute-start | bytes 921608 | tf_op jit(solution)/shard_map/ppermute | solution.py:440
  67.6 0.7 collective-permute-done.12
  68.4 0.1 ceil_reduce_fusion
  68.6 4.4 %collective-permute-done.16 = f16[200,768]{1,0:T(8,128)(2,1)S(1)} collective-permute-done((f16[200,768]{1,0:T(8,128)(2,1)S(1)}, f16[200,768]{1,0:T(8,128)(2,1)S(1)}, u32[]{:S(2)}, u32[]{:S(2)}) %collective-permute-start.16) | collective-permute-done | bytes 307232 | tf_op jit(solution)/shard_map/ppermute | solution.py:440
  73.1 0.1 fusion.8
  73.4 0.1 fusion.15
  73.7 2.9 %collective-permute-start.17 = (f16[104,768]{1,0:T(8,128)(2,1)S(1)}, f16[104,768]{1,0:T(8,128)(2,1)S(1)}, u32[]{:S(2)}, u32[]{:S(2)}) collective-permute-start(f16[104,768]{1,0:T(8,128)(2,1)S(1)} %add_convert_fusion.3), channel_id=1, source_target_pairs={{0,16},{2,18},{4,20},{6,22},{8,24},{10,26},{12,28},{14,30},{16,0},... | collective-permute-start | bytes 479240 | tf_op jit(solution)/shard_map/ppermute | solution.py:440
  76.7 5.0 %collective-permute-done.15 = f16[56,768]{1,0:T(8,128)(2,1)S(1)} collective-permute-done((f16[56,768]{1,0:T(8,128)(2,1)S(1)}, f16[56,768]{1,0:T(8,128)(2,1)S(1)}, u32[]{:S(2)}, u32[]{:S(2)}) %collective-permute-start.15) | collective-permute-done | bytes 86048 | tf_op jit(solution)/shard_map/ppermute | solution.py:440
  81.7 0.6 fusion.117
  82.3 1.9 %collective-permute-done.19 = f16[56,768]{1,0:T(8,128)(2,1)S(1)} collective-permute-done((f16[56,768]{1,0:T(8,128)(2,1)S(1)}, f16[56,768]{1,0:T(8,128)(2,1)S(1)}, u32[]{:S(2)}, u32[]{:S(2)}) %collective-permute-start.19) | collective-permute-done | bytes 86048 | tf_op jit(solution)/shard_map/ppermute | solution.py:440
  84.3 0.1 fusion.23
  84.4 0.7 pad_maximum_fusion
  85.2 0.8 fusion.5
  (72 shorter events, 1.8 us)
Async XLA Ops:
  0.6 19.0 %copy-start.5 = (s32[16]{0:T(128)S(1)}, s32[16]{0:T(128)}, u32[]{:S(2)}) copy-start(s32[16]{0:T(128)} %constant.63.clone) | copy-start | bytes 196
  0.6 19.0 %copy-start = (bf16[16,64,1536]{2,1,0:T(8,128)(2,1)S(1)}, bf16[16,64,1536]{2,1,0:T(8,128)(2,1)}, u32[]{:S(2)}) copy-start(bf16[16,64,1536]{2,1,0:T(8,128)(2,1)} %param.10) | copy-start | bytes 9437188
  9.9 4.7 %collective-permute-start = (f32[32,128]{1,0:T(8,128)S(1)}, f32[32,128]{1,0:T(8,128)S(1)}, u32[]{:S(2)}, u32[]{:S(2)}) collective-permute-start(f32[32,128]{1,0:T(8,128)S(1)} %get-tuple-element.25.own_ref), channel_id=1, source_target_pairs={{0,1},{1,0},{2,3},{3,2},{4,5},{5,4},{6,7},{7,6},{8,9},{9,8},{10,11... | collective-permute-start | bytes 49160 | tf_op jit(solution)/shard_map/ppermute | solution.py:443
  14.7 7.5 %collective-permute-start.1 = (bf16[32,768]{1,0:T(8,128)(2,1)S(1)}, bf16[32,768]{1,0:T(8,128)(2,1)S(1)}, u32[]{:S(2)}, u32[]{:S(2)}) collective-permute-start(bf16[32,768]{1,0:T(8,128)(2,1)S(1)} %get-tuple-element.26._.refs_1_), channel_id=1, source_target_pairs={{0,24},{2,26},{4,28},{6,30},{8,16},{10,18},{12,20},{14,22},{16,8},... | collective-permute-start | bytes 147464 | tf_op jit(solution)/shard_map/ppermute | solution.py:440
  18.9 5.0 %collective-permute-start.2 = (bf16[32,768]{1,0:T(8,128)(2,1)S(1)}, bf16[32,768]{1,0:T(8,128)(2,1)S(1)}, u32[]{:S(2)}, u32[]{:S(2)}) collective-permute-start(bf16[32,768]{1,0:T(8,128)(2,1)S(1)} %get-tuple-element.26._.refs_1_), channel_id=1, source_target_pairs={{0,16},{2,18},{4,20},{6,22},{8,24},{10,26},{12,28},{14,30},{16,0},... | collective-permute-start | bytes 147464 | tf_op jit(solution)/shard_map/ppermute | solution.py:440
  19.0 5.0 %collective-permute-start.3 = (bf16[32,768]{1,0:T(8,128)(2,1)S(1)}, bf16[32,768]{1,0:T(8,128)(2,1)S(1)}, u32[]{:S(2)}, u32[]{:S(2)}) collective-permute-start(bf16[32,768]{1,0:T(8,128)(2,1)S(1)} %get-tuple-element.26._.refs_1_), channel_id=1, source_target_pairs={{0,8},{2,10},{4,12},{6,14},{8,0},{10,2},{12,4},{14,6},{16,24},{18,... | collective-permute-start | bytes 147464 | tf_op jit(solution)/shard_map/ppermute | solution.py:440
  19.6 6.0 %copy-start.4 = (s32[32]{0:T(128)S(1)}, s32[32]{0:T(128)}, u32[]{:S(2)}) copy-start(s32[32]{0:T(128)} %constant.62.clone) | copy-start | bytes 388
  19.6 6.0 %copy-start.1 = (bf16[16,32,1536]{2,1,0:T(8,128)(2,1)S(1)}, bf16[16,32,1536]{2,1,0:T(8,128)(2,1)}, u32[]{:S(2)}) copy-start(bf16[16,32,1536]{2,1,0:T(8,128)(2,1)} %param.11) | copy-start | bytes 4718596
  24.0 5.7 %collective-permute-start.4 = (bf16[4,32,768]{2,1,0:T(8,128)(2,1)S(1)}, bf16[4,32,768]{2,1,0:T(8,128)(2,1)S(1)}, u32[]{:S(2)}, u32[]{:S(2)}) collective-permute-start(bf16[4,32,768]{2,1,0:T(8,128)(2,1)S(1)} %shard_map.124._.refs_0_), channel_id=1, source_target_pairs={{0,4},{2,6},{4,0},{6,2},{8,12},{10,14},{12,8},{14,10},{16,20},{18,... | collective-permute-start | bytes 589832 | tf_op jit(solution)/shard_map/ppermute | solution.py:440
  25.6 4.2 %collective-permute-start.5 = (bf16[4,32,768]{2,1,0:T(8,128)(2,1)S(1)}, bf16[4,32,768]{2,1,0:T(8,128)(2,1)S(1)}, u32[]{:S(2)}, u32[]{:S(2)}) collective-permute-start(bf16[4,32,768]{2,1,0:T(8,128)(2,1)S(1)} %shard_map.124._.refs_0_), channel_id=1, source_target_pairs={{0,2},{2,0},{4,6},{6,4},{8,10},{10,8},{12,14},{14,12},{16,18},{18,... | collective-permute-start | bytes 589832 | tf_op jit(solution)/shard_map/ppermute | solution.py:440
  27.1 9.0 %copy-start.3 = (f32[512,768]{1,0:T(8,128)S(1)}, f32[512,768]{1,0:T(8,128)}, u32[]{:S(2)}) copy-start(f32[512,768]{1,0:T(8,128)} %get-tuple-element.35.slope_ref) | copy-start | bytes 4718596
  29.7 1.5 %collective-permute-start.6 = (bf16[4,32,768]{2,1,0:T(8,128)(2,1)S(1)}, bf16[4,32,768]{2,1,0:T(8,128)(2,1)S(1)}, u32[]{:S(2)}, u32[]{:S(2)}) collective-permute-start(bf16[4,32,768]{2,1,0:T(8,128)(2,1)S(1)} %bitcast.8), channel_id=1, source_target_pairs={{0,2},{2,0},{4,6},{6,4},{8,10},{10,8},{12,14},{14,12},{16,18},{18,... | collective-permute-start | bytes 589832 | tf_op jit(solution)/shard_map/ppermute | solution.py:440
  31.6 3.9 %collective-permute-start.7 = (f32[32,256]{1,0:T(8,128)S(1)}, f32[32,256]{1,0:T(8,128)S(1)}, u32[]{:S(2)}, u32[]{:S(2)}) collective-permute-start(f32[32,256]{1,0:T(8,128)S(1)} %get-tuple-element.29.own_ref), channel_id=1, source_target_pairs={{0,1},{1,0},{2,3},{3,2},{4,5},{5,4},{6,7},{7,6},{8,9},{9,8},{10,11... | collective-permute-start | bytes 98312 | tf_op jit(solution)/shard_map/ppermute | solution.py:443
  36.1 1.9 %copy-start.2 = (f32[1024,768]{1,0:T(8,128)S(1)}, f32[1024,768]{1,0:T(8,128)}, u32[]{:S(2)}) copy-start(f32[1024,768]{1,0:T(8,128)} %get-tuple-element.40.slope_ref) | copy-start | bytes 9437188
  37.6 4.0 %collective-permute-start.8 = (f32[392,768]{1,0:T(8,128)S(1)}, f32[392,768]{1,0:T(8,128)S(1)}, u32[]{:S(2)}, u32[]{:S(2)}) collective-permute-start(f32[392,768]{1,0:T(8,128)S(1)} %get-tuple-element.37._), channel_id=1, source_target_pairs={{0,2},{2,0},{4,6},{6,4},{8,10},{10,8},{12,14},{14,12},{16,18},{18,... | collective-permute-start | bytes 3612680 | tf_op jit(solution)/shard_map/ppermute | solution.py:440
  40.8 25.0 %collective-permute-start.13 = (f32[384,768]{1,0:T(8,128)S(1)}, f32[384,768]{1,0:T(8,128)S(1)}, u32[]{:S(2)}, u32[]{:S(2)}) collective-permute-start(f32[384,768]{1,0:T(8,128)S(1)} %get-tuple-element.44), channel_id=1, source_target_pairs={{0,2},{2,0},{4,6},{6,4},{8,10},{10,8},{12,14},{14,12},{16,18},{18,... | collective-permute-start | bytes 3538952 | tf_op jit(solution)/shard_map/ppermute | solution.py:440
  41.1 4.3 %collective-permute-start.11 = (f32[384,768]{1,0:T(8,128)S(1)}, f32[384,768]{1,0:T(8,128)S(1)}, u32[]{:S(2)}, u32[]{:S(2)}) collective-permute-start(f32[384,768]{1,0:T(8,128)S(1)} %get-tuple-element.43), channel_id=1, source_target_pairs={{0,2},{2,0},{4,6},{6,4},{8,10},{10,8},{12,14},{14,12},{16,18},{18,... | collective-permute-start | bytes 3538952 | tf_op jit(solution)/shard_map/ppermute | solution.py:440
  41.4 16.6 %collective-permute-start.10 = (f32[384,768]{1,0:T(8,128)S(1)}, f32[384,768]{1,0:T(8,128)S(1)}, u32[]{:S(2)}, u32[]{:S(2)}) collective-permute-start(f32[384,768]{1,0:T(8,128)S(1)} %get-tuple-element.39), channel_id=1, source_target_pairs={{0,2},{2,0},{4,6},{6,4},{8,10},{10,8},{12,14},{14,12},{16,18},{18,... | collective-permute-start | bytes 3538952 | tf_op jit(solution)/shard_map/ppermute | solution.py:440
  42.0 15.9 %collective-permute-start.9 = (f16[392,768]{1,0:T(8,128)(2,1)S(1)}, f16[392,768]{1,0:T(8,128)(2,1)S(1)}, u32[]{:S(2)}, u32[]{:S(2)}) collective-permute-start(f16[392,768]{1,0:T(8,128)(2,1)S(1)} %add_convert_fusion.1), channel_id=1, source_target_pairs={{0,4},{2,6},{4,0},{6,2},{8,12},{10,14},{12,8},{14,10},{16,20},{18,... | collective-permute-start | bytes 1806344 | tf_op jit(solution)/shard_map/ppermute | solution.py:440
  45.7 19.9 %collective-permute-start.14 = (f16[392,768]{1,0:T(8,128)(2,1)S(1)}, f16[392,768]{1,0:T(8,128)(2,1)S(1)}, u32[]{:S(2)}, u32[]{:S(2)}) collective-permute-start(f16[392,768]{1,0:T(8,128)(2,1)S(1)} %add_convert_fusion), channel_id=1, source_target_pairs={{0,8},{2,10},{4,12},{6,14},{8,0},{10,2},{12,4},{14,6},{16,24},{18,... | collective-permute-start | bytes 1806344 | tf_op jit(solution)/shard_map/ppermute | solution.py:440
  58.2 10.1 %collective-permute-start.12 = (f16[104,768]{1,0:T(8,128)(2,1)S(1)}, f16[104,768]{1,0:T(8,128)(2,1)S(1)}, u32[]{:S(2)}, u32[]{:S(2)}) collective-permute-start(f16[104,768]{1,0:T(8,128)(2,1)S(1)} %add_convert_fusion.5), channel_id=1, source_target_pairs={{0,8},{2,10},{4,12},{6,14},{8,0},{10,2},{12,4},{14,6},{16,24},{18,... | collective-permute-start | bytes 479240 | tf_op jit(solution)/shard_map/ppermute | solution.py:440
  58.7 9.0 %collective-permute-start.18 = (f16[104,768]{1,0:T(8,128)(2,1)S(1)}, f16[104,768]{1,0:T(8,128)(2,1)S(1)}, u32[]{:S(2)}, u32[]{:S(2)}) collective-permute-start(f16[104,768]{1,0:T(8,128)(2,1)S(1)} %add_convert_fusion.4), channel_id=1, source_target_pairs={{0,16},{2,18},{4,20},{6,22},{8,24},{10,26},{12,28},{14,30},{16,0},... | collective-permute-start | bytes 479240 | tf_op jit(solution)/shard_map/ppermute | solution.py:440
  66.0 6.9 %collective-permute-start.16 = (f16[200,768]{1,0:T(8,128)(2,1)S(1)}, f16[200,768]{1,0:T(8,128)(2,1)S(1)}, u32[]{:S(2)}, u32[]{:S(2)}) collective-permute-start(f16[200,768]{1,0:T(8,128)(2,1)S(1)} %add_convert_fusion.2), channel_id=1, source_target_pairs={{0,4},{2,6},{4,0},{6,2},{8,12},{10,14},{12,8},{14,10},{16,20},{18,... | collective-permute-start | bytes 921608 | tf_op jit(solution)/shard_map/ppermute | solution.py:440
  73.6 8.1 %collective-permute-start.15 = (f16[56,768]{1,0:T(8,128)(2,1)S(1)}, f16[56,768]{1,0:T(8,128)(2,1)S(1)}, u32[]{:S(2)}, u32[]{:S(2)}) collective-permute-start(f16[56,768]{1,0:T(8,128)(2,1)S(1)} %add_convert_fusion.7), channel_id=1, source_target_pairs={{0,16},{2,18},{4,20},{6,22},{8,24},{10,26},{12,28},{14,30},{16,0},... | collective-permute-start | bytes 258056 | tf_op jit(solution)/shard_map/ppermute | solution.py:440
  73.7 11.4 %collective-permute-start.17 = (f16[104,768]{1,0:T(8,128)(2,1)S(1)}, f16[104,768]{1,0:T(8,128)(2,1)S(1)}, u32[]{:S(2)}, u32[]{:S(2)}) collective-permute-start(f16[104,768]{1,0:T(8,128)(2,1)S(1)} %add_convert_fusion.3), channel_id=1, source_target_pairs={{0,16},{2,18},{4,20},{6,22},{8,24},{10,26},{12,28},{14,30},{16,0},... | collective-permute-start | bytes 479240 | tf_op jit(solution)/shard_map/ppermute | solution.py:440
  76.7 7.6 %collective-permute-start.19 = (f16[56,768]{1,0:T(8,128)(2,1)S(1)}, f16[56,768]{1,0:T(8,128)(2,1)S(1)}, u32[]{:S(2)}, u32[]{:S(2)}) collective-permute-start(f16[56,768]{1,0:T(8,128)(2,1)S(1)} %add_convert_fusion.6), channel_id=1, source_target_pairs={{0,8},{2,10},{4,12},{6,14},{8,0},{10,2},{12,4},{14,6},{16,24},{18,... | collective-permute-start | bytes 258056 | tf_op jit(solution)/shard_map/ppermute | solution.py:440

commit v9 on v8

--- a/solution.py
+++ b/solution.py
@@ -553,8 +553,14 @@
     image_terms = weight_terms(grad, image_slope, image_turned, stat, 0, False, text_terms[0])
     image, image_leaves, _ = core_step(*image_terms)
 
-    coded, text_in = leave(text_leaves, start_stat, 1, 1, start_stat)
-    coded, image_in = leave(image_leaves, start_stat, 0, image_order[0], coded)
+    text_coded, text_in = leave(text_leaves, start_stat, 1, 1, start_stat)
+    coded, image_in = leave(image_leaves, start_stat, 0, image_order[0], text_coded)
+    _, late, keep = image_terms
+    late = late + 0.0 * text_coded[:1].astype(F32)
+    image = [(keep[: late.shape[0]], None), (swap(late, 1), None)]
+    _, late, keep = text_terms
+    late = late + 0.0 * text_coded[:1].astype(F32)
+    text = [(keep[: late.shape[0]], None), (swap(late, 1), None)]
     text, text_stat = take(text, start_stat, 1, text_in)
     parts = [(terms, text_stat) for terms in halves(text)]
     image, image_stat = take(image, start_stat, 0, image_in)

time: 86.2 us -> 87.4 us (1.014)
  starting transfers between devices: 21.1 us -> 22.5 us
    ppermute x18, starting transfers between devices: 16.6 us -> 18 us  [swap(): return lax.ppermute(array, 'dp', [(i, i ^ mask) for i in range(cycle)])]
  transfers between devices with their start and end apart: 20 -> 20, of which waited for: 12 -> 13; matrix products, arithmetic and copies ran while one was open for 4% -> 4% of each run, Pallas kernels for 8% -> 8%
where the time goes in v9:
time: 87.4 us; the launch traced here: 87.2 us
  waiting for transfers between devices  36.9 us (42%)
  starting transfers between devices  22.5 us (26%)
  Pallas kernels  18.7 us (21%)
  other arithmetic  5.12 us (6%)
  between operations  3.64 us (4%)
    ppermute x18, waiting for transfers between devices, swap(): return lax.ppermute(array, 'dp', [(i, i ^ mask) for i in range(cycle)])  35.4 us
    ppermute x18, starting transfers between devices, swap(): return lax.ppermute(array, 'dp', [(i, i ^ mask) for i in range(cycle)])  18 us
    pallas_call x1, Pallas kernels, forward(): pl.pallas_call(functools.partial(forward_kernel, (rows_i // samples, rows...  9.25 us
    ppermute x2, starting transfers between devices, swap_halves(): return lax.ppermute(array, 'mp', [(0, 1), (1, 0)])  4.52 us
    pallas_call x2, Pallas kernels, weight_terms(): pl.pallas_call(functools.partial(weight_kernel, base, carries), out_shape...  4.38 us
    pallas_call x2, Pallas kernels, turn(): pl.pallas_call(turn_kernel, out_shape=(jax.ShapeDtypeStruct((depth, rows)...  4.08 us
  transfers between devices with their start and end apart: 20, of which 13 were waited for; matrix products, arithmetic and copies ran while one was open for 4% of the time, Pallas kernels for 8%

profile of v9, /device:TPU:0, one launch (start us, length us, event | category | flops | bytes accessed | tf_op | source)
XLA Modules:
  0.0 87.2 jit_solution(1183958476015290740)
XLA Ops:
  0.7 9.2 %shard_map.121 = (f32[32,768]{1,0:T(8,128)S(1)}, f32[32,128]{1,0:T(8,128)S(1)}, f32[1024,768]{1,0:T(8,128)}, f32[512,768]{1,0:T(8,128)}) custom-call(s32[1]{0:T(128)} %bitcast.1.place_ref, bf16[1024,1536]{1,0:T(8,128)(2,1)} %bitcast.4, bf16[512,1536]{1,0:T(8,128)(2,1)} %bitcast.6, bf16[1536,768]{1,0:T(8,128)(2,1)} %image_w_hbm.1, bf16[1536,768]{1,0:T(8,128)(2,1)} %text_w_hbm.1), custom_call_target="tpu_custom_call" | custom-call | flops 3623878656 | bytes 14155776 | tf_op jit(solution)/shard_map/pallas_call | solution.py:141
  9.9 3.0 %collective-permute-start = (f32[32,128]{1,0:T(8,128)S(1)}, f32[32,128]{1,0:T(8,128)S(1)}, u32[]{:S(2)}, u32[]{:S(2)}) collective-permute-start(f32[32,128]{1,0:T(8,128)S(1)} %get-tuple-element.25.own_ref), channel_id=1, source_target_pairs={{0,1},{1,0},{2,3},{3,2},{4,5},{5,4},{6,7},{7,6},{8,9},{9,8},{10,11... | collective-permute-start | bytes 49160 | tf_op jit(solution)/shard_map/ppermute | solution.py:443
  13.6 1.1 %collective-permute-done.other_ref = f32[32,128]{1,0:T(8,128)S(1)} collective-permute-done((f32[32,128]{1,0:T(8,128)S(1)}, f32[32,128]{1,0:T(8,128)S(1)}, u32[]{:S(2)}, u32[]{:S(2)}) %collective-permute-start) | collective-permute-done | bytes 16416 | tf_op jit(solution)/shard_map/ppermute | solution.py:443
  14.7 4.2 %collective-permute-start.1 = (bf16[32,768]{1,0:T(8,128)(2,1)S(1)}, bf16[32,768]{1,0:T(8,128)(2,1)S(1)}, u32[]{:S(2)}, u32[]{:S(2)}) collective-permute-start(bf16[32,768]{1,0:T(8,128)(2,1)S(1)} %get-tuple-element.26._.refs_1_), channel_id=1, source_target_pairs={{0,24},{2,26},{4,28},{6,30},{8,16},{10,18},{12,20},{14,22},{16,8},... | collective-permute-start | bytes 147464 | tf_op jit(solution)/shard_map/ppermute | solution.py:440
  19.0 0.6 collective-permute-start.3
  19.6 2.6 %shard_map.123 = (bf16[1536,1024]{1,0:T(8,128)(2,1)S(1)}, f32[8,128]{1,0:T(8,128)S(1)}) custom-call(s32[16]{0:T(128)S(1)} %broadcast_xor_fusion.1.source_ref, bf16[1024,1536]{1,0:T(8,128)(2,1)S(1)} %bitcast.5, bf16[32,768]{1,0:T(8,128)(2,1)S(1)} %get-tuple-element.26._.refs_1_), custom_call_target="tpu_custom_call" | custom-call | bytes 6291456 | tf_op jit(solution)/shard_map/pallas_call | solution.py:236
  22.2 1.7 %collective-permute-done.2.refs_3_ = bf16[32,768]{1,0:T(8,128)(2,1)S(1)} collective-permute-done((bf16[32,768]{1,0:T(8,128)(2,1)S(1)}, bf16[32,768]{1,0:T(8,128)(2,1)S(1)}, u32[]{:S(2)}, u32[]{:S(2)}) %collective-permute-start.2) | collective-permute-done | bytes 49184 | tf_op jit(solution)/shard_map/ppermute | solution.py:440
  24.0 1.6 %collective-permute-start.4 = (bf16[4,32,768]{2,1,0:T(8,128)(2,1)S(1)}, bf16[4,32,768]{2,1,0:T(8,128)(2,1)S(1)}, u32[]{:S(2)}, u32[]{:S(2)}) collective-permute-start(bf16[4,32,768]{2,1,0:T(8,128)(2,1)S(1)} %shard_map.124._.refs_0_), channel_id=1, source_target_pairs={{0,4},{2,6},{4,0},{6,2},{8,12},{10,14},{12,8},{14,10},{16,20},{18,... | collective-permute-start | bytes 589832 | tf_op jit(solution)/shard_map/ppermute | solution.py:440
  25.6 1.5 %shard_map.125 = (bf16[1536,512]{1,0:T(8,128)(2,1)S(1)}, f32[8,128]{1,0:T(8,128)S(1)}) custom-call(s32[32]{0:T(128)S(1)} %broadcast_xor_fusion.source_ref, bf16[512,1536]{1,0:T(8,128)(2,1)S(1)} %bitcast.7, bf16[4,32,768]{2,1,0:T(8,128)(2,1)S(1)} %shard_map.124._.refs_0_), custom_call_target="tpu_custom_call" | custom-call | bytes 3145728 | tf_op jit(solution)/shard_map/pallas_call | solution.py:236
  27.1 2.6 %collective-permute-done.4.refs_1_ = bf16[4,32,768]{2,1,0:T(8,128)(2,1)S(1)} collective-permute-done((bf16[4,32,768]{2,1,0:T(8,128)(2,1)S(1)}, bf16[4,32,768]{2,1,0:T(8,128)(2,1)S(1)}, u32[]{:S(2)}, u32[]{:S(2)}) %collective-permute-start.4) | collective-permute-done | bytes 196640 | tf_op jit(solution)/shard_map/ppermute | solution.py:440
  29.8 1.4 %collective-permute-done.6.refs_3_ = bf16[4,32,768]{2,1,0:T(8,128)(2,1)S(1)} collective-permute-done((bf16[4,32,768]{2,1,0:T(8,128)(2,1)S(1)}, bf16[4,32,768]{2,1,0:T(8,128)(2,1)S(1)}, u32[]{:S(2)}, u32[]{:S(2)}) %collective-permute-start.6) | collective-permute-done | bytes 196640 | tf_op jit(solution)/shard_map/ppermute | solution.py:440
  31.2 0.4 shard_map.127
  31.6 1.5 %collective-permute-start.7 = (f32[32,256]{1,0:T(8,128)S(1)}, f32[32,256]{1,0:T(8,128)S(1)}, u32[]{:S(2)}, u32[]{:S(2)}) collective-permute-start(f32[32,256]{1,0:T(8,128)S(1)} %get-tuple-element.29.own_ref), channel_id=1, source_target_pairs={{0,1},{1,0},{2,3},{3,2},{4,5},{5,4},{6,7},{7,6},{8,9},{9,8},{10,11... | collective-permute-start | bytes 98312 | tf_op jit(solution)/shard_map/ppermute | solution.py:443
  35.0 0.5 collective-permute-done.7.other_ref
  35.5 0.5 shard_map.128
  36.1 1.5 %shard_map.129 = (f32[392,768]{1,0:T(8,128)S(1)}, f32[384,768]{1,0:T(8,128)S(1)}, f32[768,768]{1,0:T(8,128)S(1)}) custom-call(f32[32,768]{1,0:T(8,128)S(1)} %get-tuple-element.34.grad_ref, f32[512,768]{1,0:T(8,128)S(1)} %copy-done.3, bf16[1536,512]{1,0:T(8,128)(2,1)S(1)} %get-tuple-element.36.turned_ref, f32[8,768]{1,0:T(8,128)S(1)} %get-tuple-element.33.stat_ref._, ...), custom_call_target="tpu_custom_call" | custom-call | flops 1207959552 | bytes 7864320 | tf_op jit(solution)/shard_map/pallas_call | solution.py:399
  37.7 0.3 copy-done.2
  38.0 2.9 %shard_map.130 = (f32[384,768]{1,0:T(8,128)S(1)}, f32[384,768]{1,0:T(8,128)S(1)}, f32[768,768]{1,0:T(8,128)S(1)}) custom-call(f32[32,768]{1,0:T(8,128)S(1)} %get-tuple-element.34.grad_ref, f32[1024,768]{1,0:T(8,128)S(1)} %copy-done.2, bf16[1536,1024]{1,0:T(8,128)(2,1)S(1)} %get-tuple-element.41.turned_ref, f32[8,768]{1,0:T(8,128)S(1)} %get-tuple-element.33.stat_ref._, ...), custom_call_target="tpu_custom_call" | custom-call | flops 2415919104 | bytes 11010048 | tf_op jit(solution)/shard_map/pallas_call | solution.py:399
  40.9 0.3 collective-permute-start.11
  41.3 0.1 fusion
  41.6 1.6 %collective-permute-start.9 = (f16[392,768]{1,0:T(8,128)(2,1)S(1)}, f16[392,768]{1,0:T(8,128)(2,1)S(1)}, u32[]{:S(2)}, u32[]{:S(2)}) collective-permute-start(f16[392,768]{1,0:T(8,128)(2,1)S(1)} %add_convert_fusion.1), channel_id=1, source_target_pairs={{0,4},{2,6},{4,0},{6,2},{8,12},{10,14},{12,8},{14,10},{16,20},{18,... | collective-permute-start | bytes 1806344 | tf_op jit(solution)/shard_map/ppermute | solution.py:440
  43.2 0.6 collective-permute-done.11
  43.8 0.1 add_multiply_fusion
  44.0 0.2 broadcast_add_fusion.1
  44.2 0.2 collective-permute-start.10
  44.5 0.2 collective-permute-start.14
  44.7 0.2 collective-permute-start.13
  45.0 12.5 %collective-permute-done.9 = f16[392,768]{1,0:T(8,128)(2,1)S(1)} collective-permute-done((f16[392,768]{1,0:T(8,128)(2,1)S(1)}, f16[392,768]{1,0:T(8,128)(2,1)S(1)}, u32[]{:S(2)}, u32[]{:S(2)}) %collective-permute-start.9) | collective-permute-done | bytes 602144 | tf_op jit(solution)/shard_map/ppermute | solution.py:440
  57.5 2.9 %collective-permute-done.14 = f16[392,768]{1,0:T(8,128)(2,1)S(1)} collective-permute-done((f16[392,768]{1,0:T(8,128)(2,1)S(1)}, f16[392,768]{1,0:T(8,128)(2,1)S(1)}, u32[]{:S(2)}, u32[]{:S(2)}) %collective-permute-start.14) | collective-permute-done | bytes 602144 | tf_op jit(solution)/shard_map/ppermute | solution.py:440
  60.4 0.1 fusion.38
  60.7 0.4 collective-permute-start.12
  61.3 2.4 %collective-permute-start.18 = (f16[104,768]{1,0:T(8,128)(2,1)S(1)}, f16[104,768]{1,0:T(8,128)(2,1)S(1)}, u32[]{:S(2)}, u32[]{:S(2)}) collective-permute-start(f16[104,768]{1,0:T(8,128)(2,1)S(1)} %add_convert_fusion.4), channel_id=1, source_target_pairs={{0,16},{2,18},{4,20},{6,22},{8,24},{10,26},{12,28},{14,30},{16,0},... | collective-permute-start | bytes 479240 | tf_op jit(solution)/shard_map/ppermute | solution.py:440
  63.7 0.1 fusion.42
  63.8 0.1 fusion.2
  64.1 1.6 %collective-permute-start.16 = (f16[200,768]{1,0:T(8,128)(2,1)S(1)}, f16[200,768]{1,0:T(8,128)(2,1)S(1)}, u32[]{:S(2)}, u32[]{:S(2)}) collective-permute-start(f16[200,768]{1,0:T(8,128)(2,1)S(1)} %add_convert_fusion.2), channel_id=1, source_target_pairs={{0,4},{2,6},{4,0},{6,2},{8,12},{10,14},{12,8},{14,10},{16,20},{18,... | collective-permute-start | bytes 921608 | tf_op jit(solution)/shard_map/ppermute | solution.py:440
  65.7 3.5 %collective-permute-done.18 = f16[104,768]{1,0:T(8,128)(2,1)S(1)} collective-permute-done((f16[104,768]{1,0:T(8,128)(2,1)S(1)}, f16[104,768]{1,0:T(8,128)(2,1)S(1)}, u32[]{:S(2)}, u32[]{:S(2)}) %collective-permute-start.18) | collective-permute-done | bytes 159776 | tf_op jit(solution)/shard_map/ppermute | solution.py:440
  69.2 0.5 collective-permute-done.12
  69.7 0.1 ceil_reduce_fusion
  70.0 2.4 %collective-permute-done.16 = f16[200,768]{1,0:T(8,128)(2,1)S(1)} collective-permute-done((f16[200,768]{1,0:T(8,128)(2,1)S(1)}, f16[200,768]{1,0:T(8,128)(2,1)S(1)}, u32[]{:S(2)}, u32[]{:S(2)}) %collective-permute-start.16) | collective-permute-done | bytes 307232 | tf_op jit(solution)/shard_map/ppermute | solution.py:440
  72.7 1.5 %collective-permute-start.19 = (f16[56,768]{1,0:T(8,128)(2,1)S(1)}, f16[56,768]{1,0:T(8,128)(2,1)S(1)}, u32[]{:S(2)}, u32[]{:S(2)}) collective-permute-start(f16[56,768]{1,0:T(8,128)(2,1)S(1)} %add_convert_fusion.6), channel_id=1, source_target_pairs={{0,8},{2,10},{4,12},{6,14},{8,0},{10,2},{12,4},{14,6},{16,24},{18,... | collective-permute-start | bytes 258056 | tf_op jit(solution)/shard_map/ppermute | solution.py:440
  74.2 1.3 %collective-permute-start.15 = (f16[56,768]{1,0:T(8,128)(2,1)S(1)}, f16[56,768]{1,0:T(8,128)(2,1)S(1)}, u32[]{:S(2)}, u32[]{:S(2)}) collective-permute-start(f16[56,768]{1,0:T(8,128)(2,1)S(1)} %add_convert_fusion.7), channel_id=1, source_target_pairs={{0,16},{2,18},{4,20},{6,22},{8,24},{10,26},{12,28},{14,30},{16,0},... | collective-permute-start | bytes 258056 | tf_op jit(solution)/shard_map/ppermute | solution.py:440
  75.8 1.8 %collective-permute-start.17 = (f16[104,768]{1,0:T(8,128)(2,1)S(1)}, f16[104,768]{1,0:T(8,128)(2,1)S(1)}, u32[]{:S(2)}, u32[]{:S(2)}) collective-permute-start(f16[104,768]{1,0:T(8,128)(2,1)S(1)} %add_convert_fusion.3), channel_id=1, source_target_pairs={{0,16},{2,18},{4,20},{6,22},{8,24},{10,26},{12,28},{14,30},{16,0},... | collective-permute-start | bytes 479240 | tf_op jit(solution)/shard_map/ppermute | solution.py:440
  77.6 6.4 %collective-permute-done.15 = f16[56,768]{1,0:T(8,128)(2,1)S(1)} collective-permute-done((f16[56,768]{1,0:T(8,128)(2,1)S(1)}, f16[56,768]{1,0:T(8,128)(2,1)S(1)}, u32[]{:S(2)}, u32[]{:S(2)}) %collective-permute-start.15) | collective-permute-done | bytes 86048 | tf_op jit(solution)/shard_map/ppermute | solution.py:440
  83.9 0.6 fusion.116
  84.6 0.1 fusion.23
  84.7 0.7 pad_maximum_fusion
  85.5 0.9 %collective-permute-done.17 = f16[104,768]{1,0:T(8,128)(2,1)S(1)} collective-permute-done((f16[104,768]{1,0:T(8,128)(2,1)S(1)}, f16[104,768]{1,0:T(8,128)(2,1)S(1)}, u32[]{:S(2)}, u32[]{:S(2)}) %collective-permute-start.17) | collective-permute-done | bytes 159776 | tf_op jit(solution)/shard_map/ppermute | solution.py:440
  86.4 0.8 fusion.5
  (73 shorter events, 2.1 us)
Async XLA Ops:
  0.6 19.0 %copy-start.5 = (s32[16]{0:T(128)S(1)}, s32[16]{0:T(128)}, u32[]{:S(2)}) copy-start(s32[16]{0:T(128)} %constant.63.clone) | copy-start | bytes 196
  0.6 19.0 %copy-start = (bf16[16,64,1536]{2,1,0:T(8,128)(2,1)S(1)}, bf16[16,64,1536]{2,1,0:T(8,128)(2,1)}, u32[]{:S(2)}) copy-start(bf16[16,64,1536]{2,1,0:T(8,128)(2,1)} %param.10) | copy-start | bytes 9437188
  9.9 4.7 %collective-permute-start = (f32[32,128]{1,0:T(8,128)S(1)}, f32[32,128]{1,0:T(8,128)S(1)}, u32[]{:S(2)}, u32[]{:S(2)}) collective-permute-start(f32[32,128]{1,0:T(8,128)S(1)} %get-tuple-element.25.own_ref), channel_id=1, source_target_pairs={{0,1},{1,0},{2,3},{3,2},{4,5},{5,4},{6,7},{7,6},{8,9},{9,8},{10,11... | collective-permute-start | bytes 49160 | tf_op jit(solution)/shard_map/ppermute | solution.py:443
  14.7 7.5 %collective-permute-start.1 = (bf16[32,768]{1,0:T(8,128)(2,1)S(1)}, bf16[32,768]{1,0:T(8,128)(2,1)S(1)}, u32[]{:S(2)}, u32[]{:S(2)}) collective-permute-start(bf16[32,768]{1,0:T(8,128)(2,1)S(1)} %get-tuple-element.26._.refs_1_), channel_id=1, source_target_pairs={{0,24},{2,26},{4,28},{6,30},{8,16},{10,18},{12,20},{14,22},{16,8},... | collective-permute-start | bytes 147464 | tf_op jit(solution)/shard_map/ppermute | solution.py:440
  18.9 5.0 %collective-permute-start.2 = (bf16[32,768]{1,0:T(8,128)(2,1)S(1)}, bf16[32,768]{1,0:T(8,128)(2,1)S(1)}, u32[]{:S(2)}, u32[]{:S(2)}) collective-permute-start(bf16[32,768]{1,0:T(8,128)(2,1)S(1)} %get-tuple-element.26._.refs_1_), channel_id=1, source_target_pairs={{0,16},{2,18},{4,20},{6,22},{8,24},{10,26},{12,28},{14,30},{16,0},... | collective-permute-start | bytes 147464 | tf_op jit(solution)/shard_map/ppermute | solution.py:440
  19.0 5.0 %collective-permute-start.3 = (bf16[32,768]{1,0:T(8,128)(2,1)S(1)}, bf16[32,768]{1,0:T(8,128)(2,1)S(1)}, u32[]{:S(2)}, u32[]{:S(2)}) collective-permute-start(bf16[32,768]{1,0:T(8,128)(2,1)S(1)} %get-tuple-element.26._.refs_1_), channel_id=1, source_target_pairs={{0,8},{2,10},{4,12},{6,14},{8,0},{10,2},{12,4},{14,6},{16,24},{18,... | collective-permute-start | bytes 147464 | tf_op jit(solution)/shard_map/ppermute | solution.py:440
  19.6 6.0 %copy-start.4 = (s32[32]{0:T(128)S(1)}, s32[32]{0:T(128)}, u32[]{:S(2)}) copy-start(s32[32]{0:T(128)} %constant.62.clone) | copy-start | bytes 388
  19.6 6.0 %copy-start.1 = (bf16[16,32,1536]{2,1,0:T(8,128)(2,1)S(1)}, bf16[16,32,1536]{2,1,0:T(8,128)(2,1)}, u32[]{:S(2)}) copy-start(bf16[16,32,1536]{2,1,0:T(8,128)(2,1)} %param.11) | copy-start | bytes 4718596
  24.0 5.7 %collective-permute-start.4 = (bf16[4,32,768]{2,1,0:T(8,128)(2,1)S(1)}, bf16[4,32,768]{2,1,0:T(8,128)(2,1)S(1)}, u32[]{:S(2)}, u32[]{:S(2)}) collective-permute-start(bf16[4,32,768]{2,1,0:T(8,128)(2,1)S(1)} %shard_map.124._.refs_0_), channel_id=1, source_target_pairs={{0,4},{2,6},{4,0},{6,2},{8,12},{10,14},{12,8},{14,10},{16,20},{18,... | collective-permute-start | bytes 589832 | tf_op jit(solution)/shard_map/ppermute | solution.py:440
  25.6 4.2 %collective-permute-start.5 = (bf16[4,32,768]{2,1,0:T(8,128)(2,1)S(1)}, bf16[4,32,768]{2,1,0:T(8,128)(2,1)S(1)}, u32[]{:S(2)}, u32[]{:S(2)}) collective-permute-start(bf16[4,32,768]{2,1,0:T(8,128)(2,1)S(1)} %shard_map.124._.refs_0_), channel_id=1, source_target_pairs={{0,2},{2,0},{4,6},{6,4},{8,10},{10,8},{12,14},{14,12},{16,18},{18,... | collective-permute-start | bytes 589832 | tf_op jit(solution)/shard_map/ppermute | solution.py:440
  27.1 9.0 %copy-start.3 = (f32[512,768]{1,0:T(8,128)S(1)}, f32[512,768]{1,0:T(8,128)}, u32[]{:S(2)}) copy-start(f32[512,768]{1,0:T(8,128)} %get-tuple-element.35.slope_ref) | copy-start | bytes 4718596
  29.7 1.5 %collective-permute-start.6 = (bf16[4,32,768]{2,1,0:T(8,128)(2,1)S(1)}, bf16[4,32,768]{2,1,0:T(8,128)(2,1)S(1)}, u32[]{:S(2)}, u32[]{:S(2)}) collective-permute-start(bf16[4,32,768]{2,1,0:T(8,128)(2,1)S(1)} %bitcast.8), channel_id=1, source_target_pairs={{0,2},{2,0},{4,6},{6,4},{8,10},{10,8},{12,14},{14,12},{16,18},{18,... | collective-permute-start | bytes 589832 | tf_op jit(solution)/shard_map/ppermute | solution.py:440
  31.6 3.9 %collective-permute-start.7 = (f32[32,256]{1,0:T(8,128)S(1)}, f32[32,256]{1,0:T(8,128)S(1)}, u32[]{:S(2)}, u32[]{:S(2)}) collective-permute-start(f32[32,256]{1,0:T(8,128)S(1)} %get-tuple-element.29.own_ref), channel_id=1, source_target_pairs={{0,1},{1,0},{2,3},{3,2},{4,5},{5,4},{6,7},{7,6},{8,9},{9,8},{10,11... | collective-permute-start | bytes 98312 | tf_op jit(solution)/shard_map/ppermute | solution.py:443
  36.1 1.9 %copy-start.2 = (f32[1024,768]{1,0:T(8,128)S(1)}, f32[1024,768]{1,0:T(8,128)}, u32[]{:S(2)}) copy-start(f32[1024,768]{1,0:T(8,128)} %get-tuple-element.40.slope_ref) | copy-start | bytes 9437188
  37.6 3.6 %collective-permute-start.8 = (f32[392,768]{1,0:T(8,128)S(1)}, f32[392,768]{1,0:T(8,128)S(1)}, u32[]{:S(2)}, u32[]{:S(2)}) collective-permute-start(f32[392,768]{1,0:T(8,128)S(1)} %get-tuple-element.37._), channel_id=1, source_target_pairs={{0,2},{2,0},{4,6},{6,4},{8,10},{10,8},{12,14},{14,12},{16,18},{18,... | collective-permute-start | bytes 3612680 | tf_op jit(solution)/shard_map/ppermute | solution.py:440
  40.9 2.9 %collective-permute-start.11 = (f32[384,768]{1,0:T(8,128)S(1)}, f32[384,768]{1,0:T(8,128)S(1)}, u32[]{:S(2)}, u32[]{:S(2)}) collective-permute-start(f32[384,768]{1,0:T(8,128)S(1)} %get-tuple-element.43), channel_id=1, source_target_pairs={{0,2},{2,0},{4,6},{6,4},{8,10},{10,8},{12,14},{14,12},{16,18},{18,... | collective-permute-start | bytes 3538952 | tf_op jit(solution)/shard_map/ppermute | solution.py:440
  41.6 15.9 %collective-permute-start.9 = (f16[392,768]{1,0:T(8,128)(2,1)S(1)}, f16[392,768]{1,0:T(8,128)(2,1)S(1)}, u32[]{:S(2)}, u32[]{:S(2)}) collective-permute-start(f16[392,768]{1,0:T(8,128)(2,1)S(1)} %add_convert_fusion.1), channel_id=1, source_target_pairs={{0,4},{2,6},{4,0},{6,2},{8,12},{10,14},{12,8},{14,10},{16,20},{18,... | collective-permute-start | bytes 1806344 | tf_op jit(solution)/shard_map/ppermute | solution.py:440
  44.2 16.3 %collective-permute-start.10 = (f32[384,768]{1,0:T(8,128)S(1)}, f32[384,768]{1,0:T(8,128)S(1)}, u32[]{:S(2)}, u32[]{:S(2)}) collective-permute-start(f32[384,768]{1,0:T(8,128)S(1)} %get-tuple-element.123), channel_id=1, source_target_pairs={{0,2},{2,0},{4,6},{6,4},{8,10},{10,8},{12,14},{14,12},{16,18},{18,... | collective-permute-start | bytes 3538952 | tf_op jit(solution)/shard_map/ppermute | solution.py:440
  44.5 15.9 %collective-permute-start.14 = (f16[392,768]{1,0:T(8,128)(2,1)S(1)}, f16[392,768]{1,0:T(8,128)(2,1)S(1)}, u32[]{:S(2)}, u32[]{:S(2)}) collective-permute-start(f16[392,768]{1,0:T(8,128)(2,1)S(1)} %add_convert_fusion), channel_id=1, source_target_pairs={{0,8},{2,10},{4,12},{6,14},{8,0},{10,2},{12,4},{14,6},{16,24},{18,... | collective-permute-start | bytes 1806344 | tf_op jit(solution)/shard_map/ppermute | solution.py:440
  44.7 19.1 %collective-permute-start.13 = (f32[384,768]{1,0:T(8,128)S(1)}, f32[384,768]{1,0:T(8,128)S(1)}, u32[]{:S(2)}, u32[]{:S(2)}) collective-permute-start(f32[384,768]{1,0:T(8,128)S(1)} %get-tuple-element.124), channel_id=1, source_target_pairs={{0,2},{2,0},{4,6},{6,4},{8,10},{10,8},{12,14},{14,12},{16,18},{18,... | collective-permute-start | bytes 3538952 | tf_op jit(solution)/shard_map/ppermute | solution.py:440
  60.7 9.0 %collective-permute-start.12 = (f16[104,768]{1,0:T(8,128)(2,1)S(1)}, f16[104,768]{1,0:T(8,128)(2,1)S(1)}, u32[]{:S(2)}, u32[]{:S(2)}) collective-permute-start(f16[104,768]{1,0:T(8,128)(2,1)S(1)} %add_convert_fusion.5), channel_id=1, source_target_pairs={{0,8},{2,10},{4,12},{6,14},{8,0},{10,2},{12,4},{14,6},{16,24},{18,... | collective-permute-start | bytes 479240 | tf_op jit(solution)/shard_map/ppermute | solution.py:440
  61.3 7.9 %collective-permute-start.18 = (f16[104,768]{1,0:T(8,128)(2,1)S(1)}, f16[104,768]{1,0:T(8,128)(2,1)S(1)}, u32[]{:S(2)}, u32[]{:S(2)}) collective-permute-start(f16[104,768]{1,0:T(8,128)(2,1)S(1)} %add_convert_fusion.4), channel_id=1, source_target_pairs={{0,16},{2,18},{4,20},{6,22},{8,24},{10,26},{12,28},{14,30},{16,0},... | collective-permute-start | bytes 479240 | tf_op jit(solution)/shard_map/ppermute | solution.py:440
  64.1 8.2 %collective-permute-start.16 = (f16[200,768]{1,0:T(8,128)(2,1)S(1)}, f16[200,768]{1,0:T(8,128)(2,1)S(1)}, u32[]{:S(2)}, u32[]{:S(2)}) collective-permute-start(f16[200,768]{1,0:T(8,128)(2,1)S(1)} %add_convert_fusion.2), channel_id=1, source_target_pairs={{0,4},{2,6},{4,0},{6,2},{8,12},{10,14},{12,8},{14,10},{16,20},{18,... | collective-permute-start | bytes 921608 | tf_op jit(solution)/shard_map/ppermute | solution.py:440
  72.7 11.9 %collective-permute-start.19 = (f16[56,768]{1,0:T(8,128)(2,1)S(1)}, f16[56,768]{1,0:T(8,128)(2,1)S(1)}, u32[]{:S(2)}, u32[]{:S(2)}) collective-permute-start(f16[56,768]{1,0:T(8,128)(2,1)S(1)} %add_convert_fusion.6), channel_id=1, source_target_pairs={{0,8},{2,10},{4,12},{6,14},{8,0},{10,2},{12,4},{14,6},{16,24},{18,... | collective-permute-start | bytes 258056 | tf_op jit(solution)/shard_map/ppermute | solution.py:440
  74.2 9.7 %collective-permute-start.15 = (f16[56,768]{1,0:T(8,128)(2,1)S(1)}, f16[56,768]{1,0:T(8,128)(2,1)S(1)}, u32[]{:S(2)}, u32[]{:S(2)}) collective-permute-start(f16[56,768]{1,0:T(8,128)(2,1)S(1)} %add_convert_fusion.7), channel_id=1, source_target_pairs={{0,16},{2,18},{4,20},{6,22},{8,24},{10,26},{12,28},{14,30},{16,0},... | collective-permute-start | bytes 258056 | tf_op jit(solution)/shard_map/ppermute | solution.py:440
  75.8 10.6 %collective-permute-start.17 = (f16[104,768]{1,0:T(8,128)(2,1)S(1)}, f16[104,768]{1,0:T(8,128)(2,1)S(1)}, u32[]{:S(2)}, u32[]{:S(2)}) collective-permute-start(f16[104,768]{1,0:T(8,128)(2,1)S(1)} %add_convert_fusion.3), channel_id=1, source_target_pairs={{0,16},{2,18},{4,20},{6,22},{8,24},{10,26},{12,28},{14,30},{16,0},... | collective-permute-start | bytes 479240 | tf_op jit(solution)/shard_map/ppermute | solution.py:440

commit v10 on v9

--- a/solution.py
+++ b/solution.py
@@ -566,13 +566,23 @@
     image, image_stat = take(image, start_stat, 0, image_in)
     for step in range(bits - 2):
         image, image_leaves = halves(image)
-        arrivals, before = [], coded
-        for order, (terms, terms_stat) in zip(text_orders, parts):
-            terms, leaves = halves(terms)
-            last, arrival = leave(leaves, terms_stat, 1, order[step], before)
-            before = last if step == 0 else before
-            arrivals.append((terms, terms_stat, arrival))
-        coded, image_in = leave(image_leaves, image_stat, 0, image_order[step + 1], before)
+        arrivals = [None, None]
+        if step < bits - 3:
+            terms, leaves = halves(parts[0][0])
+            made, arrival = leave(leaves, parts[0][1], 1, text_orders[0][step], coded)
+            arrivals[0] = (terms, parts[0][1], arrival)
+            terms, leaves = halves(parts[1][0])
+            made, arrival = leave(leaves, parts[1][1], 1, text_orders[1][step], made)
+            arrivals[1] = (terms, parts[1][1], arrival)
+            coded, image_in = leave(image_leaves, image_stat, 0, image_order[step + 1], made)
+        else:
+            coded, image_in = leave(image_leaves, image_stat, 0, image_order[step + 1], coded)
+            terms, leaves = halves(parts[0][0])
+            made, arrival = leave(leaves, parts[0][1], 1, text_orders[0][step], coded)
+            arrivals[0] = (terms, parts[0][1], arrival)
+            terms, leaves = halves(parts[1][0])
+            made, arrival = leave(leaves, parts[1][1], 1, text_orders[1][step], made)
+            arrivals[1] = (terms, parts[1][1], arrival)
         parts = [take(terms, old, 1, arrival) for terms, old, arrival in arrivals]
         image, image_stat = take(image, image_stat, 0, image_in)
     row = 0.0 * coded[:1].astype(F32)

time: 87.4 us -> 87.4 us (level)
  transfers between devices with their start and end apart: 20 -> 20, of which waited for: 13 -> 12; matrix products, arithmetic and copies ran while one was open for 4% -> 5% of each run, Pallas kernels for 8% -> 8%
where the time goes in v10:
time: 87.4 us; the launch traced here: 87.2 us
  waiting for transfers between devices  36.8 us (42%)
  starting transfers between devices  22.5 us (26%)
  Pallas kernels  18.7 us (21%)
  other arithmetic  5.21 us (6%)
  between operations  3.65 us (4%)
    ppermute x18, waiting for transfers between devices, swap(): return lax.ppermute(array, 'dp', [(i, i ^ mask) for i in range(cycle)])  35.3 us
    ppermute x18, starting transfers between devices, swap(): return lax.ppermute(array, 'dp', [(i, i ^ mask) for i in range(cycle)])  18 us
    pallas_call x1, Pallas kernels, forward(): pl.pallas_call(functools.partial(forward_kernel, (rows_i // samples, rows...  9.25 us
    ppermute x2, starting transfers between devices, swap_halves(): return lax.ppermute(array, 'mp', [(0, 1), (1, 0)])  4.52 us
    pallas_call x2, Pallas kernels, weight_terms(): pl.pallas_call(functools.partial(weight_kernel, base, carries), out_shape...  4.38 us
    pallas_call x2, Pallas kernels, turn(): pl.pallas_call(turn_kernel, out_shape=(jax.ShapeDtypeStruct((depth, rows)...  4.08 us
  transfers between devices with their start and end apart: 20, of which 12 were waited for; matrix products, arithmetic and copies ran while one was open for 5% of the time, Pallas kernels for 8%

profile of v10, /device:TPU:0, one launch (start us, length us, event | category | flops | bytes accessed | tf_op | source)
XLA Modules:
  0.0 87.2 jit_solution(7902768806013783212)
XLA Ops:
  0.7 9.2 %shard_map.121 = (f32[32,768]{1,0:T(8,128)S(1)}, f32[32,128]{1,0:T(8,128)S(1)}, f32[1024,768]{1,0:T(8,128)}, f32[512,768]{1,0:T(8,128)}) custom-call(s32[1]{0:T(128)} %bitcast.1.place_ref, bf16[1024,1536]{1,0:T(8,128)(2,1)} %bitcast.4, bf16[512,1536]{1,0:T(8,128)(2,1)} %bitcast.6, bf16[1536,768]{1,0:T(8,128)(2,1)} %image_w_hbm.1, bf16[1536,768]{1,0:T(8,128)(2,1)} %text_w_hbm.1), custom_call_target="tpu_custom_call" | custom-call | flops 3623878656 | bytes 14155776 | tf_op jit(solution)/shard_map/pallas_call | solution.py:141
  9.9 3.0 %collective-permute-start = (f32[32,128]{1,0:T(8,128)S(1)}, f32[32,128]{1,0:T(8,128)S(1)}, u32[]{:S(2)}, u32[]{:S(2)}) collective-permute-start(f32[32,128]{1,0:T(8,128)S(1)} %get-tuple-element.25.own_ref), channel_id=1, source_target_pairs={{0,1},{1,0},{2,3},{3,2},{4,5},{5,4},{6,7},{7,6},{8,9},{9,8},{10,11... | collective-permute-start | bytes 49160 | tf_op jit(solution)/shard_map/ppermute | solution.py:443
  13.6 1.1 %collective-permute-done.other_ref = f32[32,128]{1,0:T(8,128)S(1)} collective-permute-done((f32[32,128]{1,0:T(8,128)S(1)}, f32[32,128]{1,0:T(8,128)S(1)}, u32[]{:S(2)}, u32[]{:S(2)}) %collective-permute-start) | collective-permute-done | bytes 16416 | tf_op jit(solution)/shard_map/ppermute | solution.py:443
  14.7 4.2 %collective-permute-start.1 = (bf16[32,768]{1,0:T(8,128)(2,1)S(1)}, bf16[32,768]{1,0:T(8,128)(2,1)S(1)}, u32[]{:S(2)}, u32[]{:S(2)}) collective-permute-start(bf16[32,768]{1,0:T(8,128)(2,1)S(1)} %get-tuple-element.26._.refs_1_), channel_id=1, source_target_pairs={{0,24},{2,26},{4,28},{6,30},{8,16},{10,18},{12,20},{14,22},{16,8},... | collective-permute-start | bytes 147464 | tf_op jit(solution)/shard_map/ppermute | solution.py:440
  19.0 0.6 collective-permute-start.3
  19.6 2.6 %shard_map.123 = (bf16[1536,1024]{1,0:T(8,128)(2,1)S(1)}, f32[8,128]{1,0:T(8,128)S(1)}) custom-call(s32[16]{0:T(128)S(1)} %broadcast_xor_fusion.1.source_ref, bf16[1024,1536]{1,0:T(8,128)(2,1)S(1)} %bitcast.5, bf16[32,768]{1,0:T(8,128)(2,1)S(1)} %get-tuple-element.26._.refs_1_), custom_call_target="tpu_custom_call" | custom-call | bytes 6291456 | tf_op jit(solution)/shard_map/pallas_call | solution.py:236
  22.2 1.7 %collective-permute-done.2.refs_3_ = bf16[32,768]{1,0:T(8,128)(2,1)S(1)} collective-permute-done((bf16[32,768]{1,0:T(8,128)(2,1)S(1)}, bf16[32,768]{1,0:T(8,128)(2,1)S(1)}, u32[]{:S(2)}, u32[]{:S(2)}) %collective-permute-start.2) | collective-permute-done | bytes 49184 | tf_op jit(solution)/shard_map/ppermute | solution.py:440
  24.0 1.6 %collective-permute-start.4 = (bf16[4,32,768]{2,1,0:T(8,128)(2,1)S(1)}, bf16[4,32,768]{2,1,0:T(8,128)(2,1)S(1)}, u32[]{:S(2)}, u32[]{:S(2)}) collective-permute-start(bf16[4,32,768]{2,1,0:T(8,128)(2,1)S(1)} %shard_map.124._.refs_0_), channel_id=1, source_target_pairs={{0,4},{2,6},{4,0},{6,2},{8,12},{10,14},{12,8},{14,10},{16,20},{18,... | collective-permute-start | bytes 589832 | tf_op jit(solution)/shard_map/ppermute | solution.py:440
  25.6 1.5 %shard_map.125 = (bf16[1536,512]{1,0:T(8,128)(2,1)S(1)}, f32[8,128]{1,0:T(8,128)S(1)}) custom-call(s32[32]{0:T(128)S(1)} %broadcast_xor_fusion.source_ref, bf16[512,1536]{1,0:T(8,128)(2,1)S(1)} %bitcast.7, bf16[4,32,768]{2,1,0:T(8,128)(2,1)S(1)} %shard_map.124._.refs_0_), custom_call_target="tpu_custom_call" | custom-call | bytes 3145728 | tf_op jit(solution)/shard_map/pallas_call | solution.py:236
  27.1 2.6 %collective-permute-done.4.refs_1_ = bf16[4,32,768]{2,1,0:T(8,128)(2,1)S(1)} collective-permute-done((bf16[4,32,768]{2,1,0:T(8,128)(2,1)S(1)}, bf16[4,32,768]{2,1,0:T(8,128)(2,1)S(1)}, u32[]{:S(2)}, u32[]{:S(2)}) %collective-permute-start.4) | collective-permute-done | bytes 196640 | tf_op jit(solution)/shard_map/ppermute | solution.py:440
  29.8 1.4 %collective-permute-done.6.refs_3_ = bf16[4,32,768]{2,1,0:T(8,128)(2,1)S(1)} collective-permute-done((bf16[4,32,768]{2,1,0:T(8,128)(2,1)S(1)}, bf16[4,32,768]{2,1,0:T(8,128)(2,1)S(1)}, u32[]{:S(2)}, u32[]{:S(2)}) %collective-permute-start.6) | collective-permute-done | bytes 196640 | tf_op jit(solution)/shard_map/ppermute | solution.py:440
  31.2 0.4 shard_map.127
  31.6 1.5 %collective-permute-start.7 = (f32[32,256]{1,0:T(8,128)S(1)}, f32[32,256]{1,0:T(8,128)S(1)}, u32[]{:S(2)}, u32[]{:S(2)}) collective-permute-start(f32[32,256]{1,0:T(8,128)S(1)} %get-tuple-element.29.own_ref), channel_id=1, source_target_pairs={{0,1},{1,0},{2,3},{3,2},{4,5},{5,4},{6,7},{7,6},{8,9},{9,8},{10,11... | collective-permute-start | bytes 98312 | tf_op jit(solution)/shard_map/ppermute | solution.py:443
  35.0 0.5 collective-permute-done.7.other_ref
  35.5 0.5 shard_map.128
  36.1 1.5 %shard_map.129 = (f32[392,768]{1,0:T(8,128)S(1)}, f32[384,768]{1,0:T(8,128)S(1)}, f32[768,768]{1,0:T(8,128)S(1)}) custom-call(f32[32,768]{1,0:T(8,128)S(1)} %get-tuple-element.34.grad_ref, f32[512,768]{1,0:T(8,128)S(1)} %copy-done.3, bf16[1536,512]{1,0:T(8,128)(2,1)S(1)} %get-tuple-element.36.turned_ref, f32[8,768]{1,0:T(8,128)S(1)} %get-tuple-element.33.stat_ref._, ...), custom_call_target="tpu_custom_call" | custom-call | flops 1207959552 | bytes 7864320 | tf_op jit(solution)/shard_map/pallas_call | solution.py:399
  37.7 0.3 copy-done.2
  38.0 2.9 %shard_map.130 = (f32[384,768]{1,0:T(8,128)S(1)}, f32[384,768]{1,0:T(8,128)S(1)}, f32[768,768]{1,0:T(8,128)S(1)}) custom-call(f32[32,768]{1,0:T(8,128)S(1)} %get-tuple-element.34.grad_ref, f32[1024,768]{1,0:T(8,128)S(1)} %copy-done.2, bf16[1536,1024]{1,0:T(8,128)(2,1)S(1)} %get-tuple-element.41.turned_ref, f32[8,768]{1,0:T(8,128)S(1)} %get-tuple-element.33.stat_ref._, ...), custom_call_target="tpu_custom_call" | custom-call | flops 2415919104 | bytes 11010048 | tf_op jit(solution)/shard_map/pallas_call | solution.py:399
  40.9 0.3 collective-permute-start.11
  41.3 0.1 fusion
  41.6 1.6 %collective-permute-start.9 = (f16[392,768]{1,0:T(8,128)(2,1)S(1)}, f16[392,768]{1,0:T(8,128)(2,1)S(1)}, u32[]{:S(2)}, u32[]{:S(2)}) collective-permute-start(f16[392,768]{1,0:T(8,128)(2,1)S(1)} %add_convert_fusion.1), channel_id=1, source_target_pairs={{0,4},{2,6},{4,0},{6,2},{8,12},{10,14},{12,8},{14,10},{16,20},{18,... | collective-permute-start | bytes 1806344 | tf_op jit(solution)/shard_map/ppermute | solution.py:440
  43.2 0.6 collective-permute-done.11
  43.8 0.1 add_multiply_fusion
  44.0 0.2 broadcast_add_fusion.1
  44.2 0.2 collective-permute-start.10
  44.5 0.2 collective-permute-start.14
  44.7 0.2 collective-permute-start.13
  45.0 12.5 %collective-permute-done.9 = f16[392,768]{1,0:T(8,128)(2,1)S(1)} collective-permute-done((f16[392,768]{1,0:T(8,128)(2,1)S(1)}, f16[392,768]{1,0:T(8,128)(2,1)S(1)}, u32[]{:S(2)}, u32[]{:S(2)}) %collective-permute-start.9) | collective-permute-done | bytes 602144 | tf_op jit(solution)/shard_map/ppermute | solution.py:440
  57.5 2.9 %collective-permute-done.14 = f16[392,768]{1,0:T(8,128)(2,1)S(1)} collective-permute-done((f16[392,768]{1,0:T(8,128)(2,1)S(1)}, f16[392,768]{1,0:T(8,128)(2,1)S(1)}, u32[]{:S(2)}, u32[]{:S(2)}) %collective-permute-start.14) | collective-permute-done | bytes 602144 | tf_op jit(solution)/shard_map/ppermute | solution.py:440
  60.4 0.1 fusion.38
  60.7 0.4 collective-permute-start.12
  61.3 2.4 %collective-permute-start.18 = (f16[104,768]{1,0:T(8,128)(2,1)S(1)}, f16[104,768]{1,0:T(8,128)(2,1)S(1)}, u32[]{:S(2)}, u32[]{:S(2)}) collective-permute-start(f16[104,768]{1,0:T(8,128)(2,1)S(1)} %add_convert_fusion.4), channel_id=1, source_target_pairs={{0,16},{2,18},{4,20},{6,22},{8,24},{10,26},{12,28},{14,30},{16,0},... | collective-permute-start | bytes 479240 | tf_op jit(solution)/shard_map/ppermute | solution.py:440
  63.7 0.1 fusion.42
  63.8 0.1 fusion.2
  64.1 1.6 %collective-permute-start.15 = (f16[200,768]{1,0:T(8,128)(2,1)S(1)}, f16[200,768]{1,0:T(8,128)(2,1)S(1)}, u32[]{:S(2)}, u32[]{:S(2)}) collective-permute-start(f16[200,768]{1,0:T(8,128)(2,1)S(1)} %add_convert_fusion.2), channel_id=1, source_target_pairs={{0,4},{2,6},{4,0},{6,2},{8,12},{10,14},{12,8},{14,10},{16,20},{18,... | collective-permute-start | bytes 921608 | tf_op jit(solution)/shard_map/ppermute | solution.py:440
  65.7 3.5 %collective-permute-done.18 = f16[104,768]{1,0:T(8,128)(2,1)S(1)} collective-permute-done((f16[104,768]{1,0:T(8,128)(2,1)S(1)}, f16[104,768]{1,0:T(8,128)(2,1)S(1)}, u32[]{:S(2)}, u32[]{:S(2)}) %collective-permute-start.18) | collective-permute-done | bytes 159776 | tf_op jit(solution)/shard_map/ppermute | solution.py:440
  69.2 0.5 collective-permute-done.12
  69.7 0.1 ceil_reduce_fusion
  70.0 2.4 %collective-permute-done.15 = f16[200,768]{1,0:T(8,128)(2,1)S(1)} collective-permute-done((f16[200,768]{1,0:T(8,128)(2,1)S(1)}, f16[200,768]{1,0:T(8,128)(2,1)S(1)}, u32[]{:S(2)}, u32[]{:S(2)}) %collective-permute-start.15) | collective-permute-done | bytes 307232 | tf_op jit(solution)/shard_map/ppermute | solution.py:440
  72.4 0.1 fusion.10
  72.7 0.8 collective-permute-start.17
  73.7 2.2 %collective-permute-start.16 = (f16[56,768]{1,0:T(8,128)(2,1)S(1)}, f16[56,768]{1,0:T(8,128)(2,1)S(1)}, u32[]{:S(2)}, u32[]{:S(2)}) collective-permute-start(f16[56,768]{1,0:T(8,128)(2,1)S(1)} %add_convert_fusion.7), channel_id=1, source_target_pairs={{0,16},{2,18},{4,20},{6,22},{8,24},{10,26},{12,28},{14,30},{16,0},... | collective-permute-start | bytes 258056 | tf_op jit(solution)/shard_map/ppermute | solution.py:440
  76.2 1.5 %collective-permute-start.19 = (f16[56,768]{1,0:T(8,128)(2,1)S(1)}, f16[56,768]{1,0:T(8,128)(2,1)S(1)}, u32[]{:S(2)}, u32[]{:S(2)}) collective-permute-start(f16[56,768]{1,0:T(8,128)(2,1)S(1)} %add_convert_fusion.6), channel_id=1, source_target_pairs={{0,8},{2,10},{4,12},{6,14},{8,0},{10,2},{12,4},{14,6},{16,24},{18,... | collective-permute-start | bytes 258056 | tf_op jit(solution)/shard_map/ppermute | solution.py:440
  77.7 7.2 %collective-permute-done.16 = f16[56,768]{1,0:T(8,128)(2,1)S(1)} collective-permute-done((f16[56,768]{1,0:T(8,128)(2,1)S(1)}, f16[56,768]{1,0:T(8,128)(2,1)S(1)}, u32[]{:S(2)}, u32[]{:S(2)}) %collective-permute-start.16) | collective-permute-done | bytes 86048 | tf_op jit(solution)/shard_map/ppermute | solution.py:440
  84.8 0.6 fusion.121
  85.5 0.1 fusion.23
  85.6 0.7 pad_maximum_fusion
  86.4 0.8 fusion.5
  (77 shorter events, 2.1 us)
Async XLA Ops:
  0.6 19.0 %copy-start.5 = (s32[16]{0:T(128)S(1)}, s32[16]{0:T(128)}, u32[]{:S(2)}) copy-start(s32[16]{0:T(128)} %constant.63.clone) | copy-start | bytes 196
  0.6 19.0 %copy-start = (bf16[16,64,1536]{2,1,0:T(8,128)(2,1)S(1)}, bf16[16,64,1536]{2,1,0:T(8,128)(2,1)}, u32[]{:S(2)}) copy-start(bf16[16,64,1536]{2,1,0:T(8,128)(2,1)} %param.10) | copy-start | bytes 9437188
  9.9 4.7 %collective-permute-start = (f32[32,128]{1,0:T(8,128)S(1)}, f32[32,128]{1,0:T(8,128)S(1)}, u32[]{:S(2)}, u32[]{:S(2)}) collective-permute-start(f32[32,128]{1,0:T(8,128)S(1)} %get-tuple-element.25.own_ref), channel_id=1, source_target_pairs={{0,1},{1,0},{2,3},{3,2},{4,5},{5,4},{6,7},{7,6},{8,9},{9,8},{10,11... | collective-permute-start | bytes 49160 | tf_op jit(solution)/shard_map/ppermute | solution.py:443
  14.7 7.5 %collective-permute-start.1 = (bf16[32,768]{1,0:T(8,128)(2,1)S(1)}, bf16[32,768]{1,0:T(8,128)(2,1)S(1)}, u32[]{:S(2)}, u32[]{:S(2)}) collective-permute-start(bf16[32,768]{1,0:T(8,128)(2,1)S(1)} %get-tuple-element.26._.refs_1_), channel_id=1, source_target_pairs={{0,24},{2,26},{4,28},{6,30},{8,16},{10,18},{12,20},{14,22},{16,8},... | collective-permute-start | bytes 147464 | tf_op jit(solution)/shard_map/ppermute | solution.py:440
  18.9 5.0 %collective-permute-start.2 = (bf16[32,768]{1,0:T(8,128)(2,1)S(1)}, bf16[32,768]{1,0:T(8,128)(2,1)S(1)}, u32[]{:S(2)}, u32[]{:S(2)}) collective-permute-start(bf16[32,768]{1,0:T(8,128)(2,1)S(1)} %get-tuple-element.26._.refs_1_), channel_id=1, source_target_pairs={{0,16},{2,18},{4,20},{6,22},{8,24},{10,26},{12,28},{14,30},{16,0},... | collective-permute-start | bytes 147464 | tf_op jit(solution)/shard_map/ppermute | solution.py:440
  19.0 5.0 %collective-permute-start.3 = (bf16[32,768]{1,0:T(8,128)(2,1)S(1)}, bf16[32,768]{1,0:T(8,128)(2,1)S(1)}, u32[]{:S(2)}, u32[]{:S(2)}) collective-permute-start(bf16[32,768]{1,0:T(8,128)(2,1)S(1)} %get-tuple-element.26._.refs_1_), channel_id=1, source_target_pairs={{0,8},{2,10},{4,12},{6,14},{8,0},{10,2},{12,4},{14,6},{16,24},{18,... | collective-permute-start | bytes 147464 | tf_op jit(solution)/shard_map/ppermute | solution.py:440
  19.6 6.0 %copy-start.4 = (s32[32]{0:T(128)S(1)}, s32[32]{0:T(128)}, u32[]{:S(2)}) copy-start(s32[32]{0:T(128)} %constant.62.clone) | copy-start | bytes 388
  19.6 6.0 %copy-start.1 = (bf16[16,32,1536]{2,1,0:T(8,128)(2,1)S(1)}, bf16[16,32,1536]{2,1,0:T(8,128)(2,1)}, u32[]{:S(2)}) copy-start(bf16[16,32,1536]{2,1,0:T(8,128)(2,1)} %param.11) | copy-start | bytes 4718596
  24.0 5.7 %collective-permute-start.4 = (bf16[4,32,768]{2,1,0:T(8,128)(2,1)S(1)}, bf16[4,32,768]{2,1,0:T(8,128)(2,1)S(1)}, u32[]{:S(2)}, u32[]{:S(2)}) collective-permute-start(bf16[4,32,768]{2,1,0:T(8,128)(2,1)S(1)} %shard_map.124._.refs_0_), channel_id=1, source_target_pairs={{0,4},{2,6},{4,0},{6,2},{8,12},{10,14},{12,8},{14,10},{16,20},{18,... | collective-permute-start | bytes 589832 | tf_op jit(solution)/shard_map/ppermute | solution.py:440
  25.6 4.2 %collective-permute-start.5 = (bf16[4,32,768]{2,1,0:T(8,128)(2,1)S(1)}, bf16[4,32,768]{2,1,0:T(8,128)(2,1)S(1)}, u32[]{:S(2)}, u32[]{:S(2)}) collective-permute-start(bf16[4,32,768]{2,1,0:T(8,128)(2,1)S(1)} %shard_map.124._.refs_0_), channel_id=1, source_target_pairs={{0,2},{2,0},{4,6},{6,4},{8,10},{10,8},{12,14},{14,12},{16,18},{18,... | collective-permute-start | bytes 589832 | tf_op jit(solution)/shard_map/ppermute | solution.py:440
  27.1 9.0 %copy-start.3 = (f32[512,768]{1,0:T(8,128)S(1)}, f32[512,768]{1,0:T(8,128)}, u32[]{:S(2)}) copy-start(f32[512,768]{1,0:T(8,128)} %get-tuple-element.35.slope_ref) | copy-start | bytes 4718596
  29.7 1.5 %collective-permute-start.6 = (bf16[4,32,768]{2,1,0:T(8,128)(2,1)S(1)}, bf16[4,32,768]{2,1,0:T(8,128)(2,1)S(1)}, u32[]{:S(2)}, u32[]{:S(2)}) collective-permute-start(bf16[4,32,768]{2,1,0:T(8,128)(2,1)S(1)} %bitcast.8), channel_id=1, source_target_pairs={{0,2},{2,0},{4,6},{6,4},{8,10},{10,8},{12,14},{14,12},{16,18},{18,... | collective-permute-start | bytes 589832 | tf_op jit(solution)/shard_map/ppermute | solution.py:440
  31.6 3.9 %collective-permute-start.7 = (f32[32,256]{1,0:T(8,128)S(1)}, f32[32,256]{1,0:T(8,128)S(1)}, u32[]{:S(2)}, u32[]{:S(2)}) collective-permute-start(f32[32,256]{1,0:T(8,128)S(1)} %get-tuple-element.29.own_ref), channel_id=1, source_target_pairs={{0,1},{1,0},{2,3},{3,2},{4,5},{5,4},{6,7},{7,6},{8,9},{9,8},{10,11... | collective-permute-start | bytes 98312 | tf_op jit(solution)/shard_map/ppermute | solution.py:443
  36.1 1.9 %copy-start.2 = (f32[1024,768]{1,0:T(8,128)S(1)}, f32[1024,768]{1,0:T(8,128)}, u32[]{:S(2)}) copy-start(f32[1024,768]{1,0:T(8,128)} %get-tuple-element.40.slope_ref) | copy-start | bytes 9437188
  37.6 3.6 %collective-permute-start.8 = (f32[392,768]{1,0:T(8,128)S(1)}, f32[392,768]{1,0:T(8,128)S(1)}, u32[]{:S(2)}, u32[]{:S(2)}) collective-permute-start(f32[392,768]{1,0:T(8,128)S(1)} %get-tuple-element.37._), channel_id=1, source_target_pairs={{0,2},{2,0},{4,6},{6,4},{8,10},{10,8},{12,14},{14,12},{16,18},{18,... | collective-permute-start | bytes 3612680 | tf_op jit(solution)/shard_map/ppermute | solution.py:440
  40.9 2.9 %collective-permute-start.11 = (f32[384,768]{1,0:T(8,128)S(1)}, f32[384,768]{1,0:T(8,128)S(1)}, u32[]{:S(2)}, u32[]{:S(2)}) collective-permute-start(f32[384,768]{1,0:T(8,128)S(1)} %get-tuple-element.43), channel_id=1, source_target_pairs={{0,2},{2,0},{4,6},{6,4},{8,10},{10,8},{12,14},{14,12},{16,18},{18,... | collective-permute-start | bytes 3538952 | tf_op jit(solution)/shard_map/ppermute | solution.py:440
  41.6 15.9 %collective-permute-start.9 = (f16[392,768]{1,0:T(8,128)(2,1)S(1)}, f16[392,768]{1,0:T(8,128)(2,1)S(1)}, u32[]{:S(2)}, u32[]{:S(2)}) collective-permute-start(f16[392,768]{1,0:T(8,128)(2,1)S(1)} %add_convert_fusion.1), channel_id=1, source_target_pairs={{0,4},{2,6},{4,0},{6,2},{8,12},{10,14},{12,8},{14,10},{16,20},{18,... | collective-permute-start | bytes 1806344 | tf_op jit(solution)/shard_map/ppermute | solution.py:440
  44.2 16.3 %collective-permute-start.10 = (f32[384,768]{1,0:T(8,128)S(1)}, f32[384,768]{1,0:T(8,128)S(1)}, u32[]{:S(2)}, u32[]{:S(2)}) collective-permute-start(f32[384,768]{1,0:T(8,128)S(1)} %get-tuple-element.121), channel_id=1, source_target_pairs={{0,2},{2,0},{4,6},{6,4},{8,10},{10,8},{12,14},{14,12},{16,18},{18,... | collective-permute-start | bytes 3538952 | tf_op jit(solution)/shard_map/ppermute | solution.py:440
  44.5 15.9 %collective-permute-start.14 = (f16[392,768]{1,0:T(8,128)(2,1)S(1)}, f16[392,768]{1,0:T(8,128)(2,1)S(1)}, u32[]{:S(2)}, u32[]{:S(2)}) collective-permute-start(f16[392,768]{1,0:T(8,128)(2,1)S(1)} %add_convert_fusion), channel_id=1, source_target_pairs={{0,8},{2,10},{4,12},{6,14},{8,0},{10,2},{12,4},{14,6},{16,24},{18,... | collective-permute-start | bytes 1806344 | tf_op jit(solution)/shard_map/ppermute | solution.py:440
  44.7 19.1 %collective-permute-start.13 = (f32[384,768]{1,0:T(8,128)S(1)}, f32[384,768]{1,0:T(8,128)S(1)}, u32[]{:S(2)}, u32[]{:S(2)}) collective-permute-start(f32[384,768]{1,0:T(8,128)S(1)} %get-tuple-element.122), channel_id=1, source_target_pairs={{0,2},{2,0},{4,6},{6,4},{8,10},{10,8},{12,14},{14,12},{16,18},{18,... | collective-permute-start | bytes 3538952 | tf_op jit(solution)/shard_map/ppermute | solution.py:440
  60.7 9.0 %collective-permute-start.12 = (f16[104,768]{1,0:T(8,128)(2,1)S(1)}, f16[104,768]{1,0:T(8,128)(2,1)S(1)}, u32[]{:S(2)}, u32[]{:S(2)}) collective-permute-start(f16[104,768]{1,0:T(8,128)(2,1)S(1)} %add_convert_fusion.5), channel_id=1, source_target_pairs={{0,8},{2,10},{4,12},{6,14},{8,0},{10,2},{12,4},{14,6},{16,24},{18,... | collective-permute-start | bytes 479240 | tf_op jit(solution)/shard_map/ppermute | solution.py:440
  61.3 7.9 %collective-permute-start.18 = (f16[104,768]{1,0:T(8,128)(2,1)S(1)}, f16[104,768]{1,0:T(8,128)(2,1)S(1)}, u32[]{:S(2)}, u32[]{:S(2)}) collective-permute-start(f16[104,768]{1,0:T(8,128)(2,1)S(1)} %add_convert_fusion.4), channel_id=1, source_target_pairs={{0,16},{2,18},{4,20},{6,22},{8,24},{10,26},{12,28},{14,30},{16,0},... | collective-permute-start | bytes 479240 | tf_op jit(solution)/shard_map/ppermute | solution.py:440
  64.1 8.2 %collective-permute-start.15 = (f16[200,768]{1,0:T(8,128)(2,1)S(1)}, f16[200,768]{1,0:T(8,128)(2,1)S(1)}, u32[]{:S(2)}, u32[]{:S(2)}) collective-permute-start(f16[200,768]{1,0:T(8,128)(2,1)S(1)} %add_convert_fusion.2), channel_id=1, source_target_pairs={{0,4},{2,6},{4,0},{6,2},{8,12},{10,14},{12,8},{14,10},{16,20},{18,... | collective-permute-start | bytes 921608 | tf_op jit(solution)/shard_map/ppermute | solution.py:440
  72.7 13.7 %collective-permute-start.17 = (f16[104,768]{1,0:T(8,128)(2,1)S(1)}, f16[104,768]{1,0:T(8,128)(2,1)S(1)}, u32[]{:S(2)}, u32[]{:S(2)}) collective-permute-start(f16[104,768]{1,0:T(8,128)(2,1)S(1)} %add_convert_fusion.3), channel_id=1, source_target_pairs={{0,16},{2,18},{4,20},{6,22},{8,24},{10,26},{12,28},{14,30},{16,0},... | collective-permute-start | bytes 479240 | tf_op jit(solution)/shard_map/ppermute | solution.py:440
  73.7 11.1 %collective-permute-start.16 = (f16[56,768]{1,0:T(8,128)(2,1)S(1)}, f16[56,768]{1,0:T(8,128)(2,1)S(1)}, u32[]{:S(2)}, u32[]{:S(2)}) collective-permute-start(f16[56,768]{1,0:T(8,128)(2,1)S(1)} %add_convert_fusion.7), channel_id=1, source_target_pairs={{0,16},{2,18},{4,20},{6,22},{8,24},{10,26},{12,28},{14,30},{16,0},... | collective-permute-start | bytes 258056 | tf_op jit(solution)/shard_map/ppermute | solution.py:440
  76.2 9.3 %collective-permute-start.19 = (f16[56,768]{1,0:T(8,128)(2,1)S(1)}, f16[56,768]{1,0:T(8,128)(2,1)S(1)}, u32[]{:S(2)}, u32[]{:S(2)}) collective-permute-start(f16[56,768]{1,0:T(8,128)(2,1)S(1)} %add_convert_fusion.6), channel_id=1, source_target_pairs={{0,8},{2,10},{4,12},{6,14},{8,0},{10,2},{12,4},{14,6},{16,24},{18,... | collective-permute-start | bytes 258056 | tf_op jit(solution)/shard_map/ppermute | solution.py:440

commit v11 on v9

--- a/solution.py
+++ b/solution.py
@@ -563,15 +563,17 @@
     text = [(keep[: late.shape[0]], None), (swap(late, 1), None)]
     text, text_stat = take(text, start_stat, 1, text_in)
     parts = [(terms, text_stat) for terms in halves(text)]
-    image, image_stat = take(image, start_stat, 0, image_in)
     for step in range(bits - 2):
-        image, image_leaves = halves(image)
         arrivals, before = [], coded
         for order, (terms, terms_stat) in zip(text_orders, parts):
             terms, leaves = halves(terms)
             last, arrival = leave(leaves, terms_stat, 1, order[step], before)
             before = last if step == 0 else before
             arrivals.append((terms, terms_stat, arrival))
+        if step == 0:
+            image_in = image_in.astype(F32) + 0.0 * before[:1].astype(F32)
+            image, image_stat = take(image, start_stat, 0, image_in)
+        image, image_leaves = halves(image)
         coded, image_in = leave(image_leaves, image_stat, 0, image_order[step + 1], before)
         parts = [take(terms, old, 1, arrival) for terms, old, arrival in arrivals]
         image, image_stat = take(image, image_stat, 0, image_in)

time: 87.4 us -> 83.3 us (0.953)
  waiting for transfers between devices: 36.9 us -> 33.1 us
    ppermute x18, waiting for transfers between devices: 35.4 us -> 31.6 us  [swap(): return lax.ppermute(array, 'dp', [(i, i ^ mask) for i in range(cycle)])]
  transfers between devices with their start and end apart: 20 -> 20, of which waited for: 13 -> 12; matrix products, arithmetic and copies ran while one was open for 4% -> 4% of each run, Pallas kernels for 8% -> 8%
where the time goes in v11:
time: 83.3 us; the launch traced here: 83.1 us
  waiting for transfers between devices  33.1 us (40%)
  starting transfers between devices  22.2 us (27%)
  Pallas kernels  18.7 us (22%)
  other arithmetic  5.16 us (6%)
  between operations  3.66 us (4%)
    ppermute x18, waiting for transfers between devices, swap(): return lax.ppermute(array, 'dp', [(i, i ^ mask) for i in range(cycle)])  31.6 us
    ppermute x18, starting transfers between devices, swap(): return lax.ppermute(array, 'dp', [(i, i ^ mask) for i in range(cycle)])  17.7 us
    pallas_call x1, Pallas kernels, forward(): pl.pallas_call(functools.partial(forward_kernel, (rows_i // samples, rows...  9.25 us
    ppermute x2, starting transfers between devices, swap_halves(): return lax.ppermute(array, 'mp', [(0, 1), (1, 0)])  4.52 us
    pallas_call x2, Pallas kernels, weight_terms(): pl.pallas_call(functools.partial(weight_kernel, base, carries), out_shape...  4.38 us
    pallas_call x2, Pallas kernels, turn(): pl.pallas_call(turn_kernel, out_shape=(jax.ShapeDtypeStruct((depth, rows)...  4.08 us
  transfers between devices with their start and end apart: 20, of which 12 were waited for; matrix products, arithmetic and copies ran while one was open for 4% of the time, Pallas kernels for 8%

profile of v11, /device:TPU:0, one launch (start us, length us, event | category | flops | bytes accessed | tf_op | source)
XLA Modules:
  0.0 83.1 jit_solution(275969387693081)
XLA Ops:
  0.7 9.2 %shard_map.121 = (f32[32,768]{1,0:T(8,128)S(1)}, f32[32,128]{1,0:T(8,128)S(1)}, f32[1024,768]{1,0:T(8,128)}, f32[512,768]{1,0:T(8,128)}) custom-call(s32[1]{0:T(128)} %bitcast.1.place_ref, bf16[1024,1536]{1,0:T(8,128)(2,1)} %bitcast.4, bf16[512,1536]{1,0:T(8,128)(2,1)} %bitcast.6, bf16[1536,768]{1,0:T(8,128)(2,1)} %image_w_hbm.1, bf16[1536,768]{1,0:T(8,128)(2,1)} %text_w_hbm.1), custom_call_target="tpu_custom_call" | custom-call | flops 3623878656 | bytes 14155776 | tf_op jit(solution)/shard_map/pallas_call | solution.py:141
  9.9 3.0 %collective-permute-start = (f32[32,128]{1,0:T(8,128)S(1)}, f32[32,128]{1,0:T(8,128)S(1)}, u32[]{:S(2)}, u32[]{:S(2)}) collective-permute-start(f32[32,128]{1,0:T(8,128)S(1)} %get-tuple-element.25.own_ref), channel_id=1, source_target_pairs={{0,1},{1,0},{2,3},{3,2},{4,5},{5,4},{6,7},{7,6},{8,9},{9,8},{10,11... | collective-permute-start | bytes 49160 | tf_op jit(solution)/shard_map/ppermute | solution.py:443
  13.6 1.1 %collective-permute-done.other_ref = f32[32,128]{1,0:T(8,128)S(1)} collective-permute-done((f32[32,128]{1,0:T(8,128)S(1)}, f32[32,128]{1,0:T(8,128)S(1)}, u32[]{:S(2)}, u32[]{:S(2)}) %collective-permute-start) | collective-permute-done | bytes 16416 | tf_op jit(solution)/shard_map/ppermute | solution.py:443
  14.7 4.2 %collective-permute-start.1 = (bf16[32,768]{1,0:T(8,128)(2,1)S(1)}, bf16[32,768]{1,0:T(8,128)(2,1)S(1)}, u32[]{:S(2)}, u32[]{:S(2)}) collective-permute-start(bf16[32,768]{1,0:T(8,128)(2,1)S(1)} %get-tuple-element.26._.refs_1_), channel_id=1, source_target_pairs={{0,24},{2,26},{4,28},{6,30},{8,16},{10,18},{12,20},{14,22},{16,8},... | collective-permute-start | bytes 147464 | tf_op jit(solution)/shard_map/ppermute | solution.py:440
  19.0 0.6 collective-permute-start.3
  19.6 2.6 %shard_map.123 = (bf16[1536,1024]{1,0:T(8,128)(2,1)S(1)}, f32[8,128]{1,0:T(8,128)S(1)}) custom-call(s32[16]{0:T(128)S(1)} %broadcast_xor_fusion.1.source_ref, bf16[1024,1536]{1,0:T(8,128)(2,1)S(1)} %bitcast.5, bf16[32,768]{1,0:T(8,128)(2,1)S(1)} %get-tuple-element.26._.refs_1_), custom_call_target="tpu_custom_call" | custom-call | bytes 6291456 | tf_op jit(solution)/shard_map/pallas_call | solution.py:236
  22.2 1.7 %collective-permute-done.2.refs_3_ = bf16[32,768]{1,0:T(8,128)(2,1)S(1)} collective-permute-done((bf16[32,768]{1,0:T(8,128)(2,1)S(1)}, bf16[32,768]{1,0:T(8,128)(2,1)S(1)}, u32[]{:S(2)}, u32[]{:S(2)}) %collective-permute-start.2) | collective-permute-done | bytes 49184 | tf_op jit(solution)/shard_map/ppermute | solution.py:440
  24.0 1.6 %collective-permute-start.4 = (bf16[4,32,768]{2,1,0:T(8,128)(2,1)S(1)}, bf16[4,32,768]{2,1,0:T(8,128)(2,1)S(1)}, u32[]{:S(2)}, u32[]{:S(2)}) collective-permute-start(bf16[4,32,768]{2,1,0:T(8,128)(2,1)S(1)} %shard_map.124._.refs_0_), channel_id=1, source_target_pairs={{0,4},{2,6},{4,0},{6,2},{8,12},{10,14},{12,8},{14,10},{16,20},{18,... | collective-permute-start | bytes 589832 | tf_op jit(solution)/shard_map/ppermute | solution.py:440
  25.6 1.5 %shard_map.125 = (bf16[1536,512]{1,0:T(8,128)(2,1)S(1)}, f32[8,128]{1,0:T(8,128)S(1)}) custom-call(s32[32]{0:T(128)S(1)} %broadcast_xor_fusion.source_ref, bf16[512,1536]{1,0:T(8,128)(2,1)S(1)} %bitcast.7, bf16[4,32,768]{2,1,0:T(8,128)(2,1)S(1)} %shard_map.124._.refs_0_), custom_call_target="tpu_custom_call" | custom-call | bytes 3145728 | tf_op jit(solution)/shard_map/pallas_call | solution.py:236
  27.1 2.6 %collective-permute-done.4.refs_1_ = bf16[4,32,768]{2,1,0:T(8,128)(2,1)S(1)} collective-permute-done((bf16[4,32,768]{2,1,0:T(8,128)(2,1)S(1)}, bf16[4,32,768]{2,1,0:T(8,128)(2,1)S(1)}, u32[]{:S(2)}, u32[]{:S(2)}) %collective-permute-start.4) | collective-permute-done | bytes 196640 | tf_op jit(solution)/shard_map/ppermute | solution.py:440
  29.8 1.4 %collective-permute-done.6.refs_3_ = bf16[4,32,768]{2,1,0:T(8,128)(2,1)S(1)} collective-permute-done((bf16[4,32,768]{2,1,0:T(8,128)(2,1)S(1)}, bf16[4,32,768]{2,1,0:T(8,128)(2,1)S(1)}, u32[]{:S(2)}, u32[]{:S(2)}) %collective-permute-start.6) | collective-permute-done | bytes 196640 | tf_op jit(solution)/shard_map/ppermute | solution.py:440
  31.2 0.4 shard_map.127
  31.6 1.5 %collective-permute-start.7 = (f32[32,256]{1,0:T(8,128)S(1)}, f32[32,256]{1,0:T(8,128)S(1)}, u32[]{:S(2)}, u32[]{:S(2)}) collective-permute-start(f32[32,256]{1,0:T(8,128)S(1)} %get-tuple-element.29.own_ref), channel_id=1, source_target_pairs={{0,1},{1,0},{2,3},{3,2},{4,5},{5,4},{6,7},{7,6},{8,9},{9,8},{10,11... | collective-permute-start | bytes 98312 | tf_op jit(solution)/shard_map/ppermute | solution.py:443
  35.0 0.5 collective-permute-done.7.other_ref
  35.5 0.5 shard_map.128
  36.1 1.5 %shard_map.129 = (f32[392,768]{1,0:T(8,128)S(1)}, f32[384,768]{1,0:T(8,128)S(1)}, f32[768,768]{1,0:T(8,128)S(1)}) custom-call(f32[32,768]{1,0:T(8,128)S(1)} %get-tuple-element.34.grad_ref, f32[512,768]{1,0:T(8,128)S(1)} %copy-done.3, bf16[1536,512]{1,0:T(8,128)(2,1)S(1)} %get-tuple-element.36.turned_ref, f32[8,768]{1,0:T(8,128)S(1)} %get-tuple-element.33.stat_ref._, ...), custom_call_target="tpu_custom_call" | custom-call | flops 1207959552 | bytes 7864320 | tf_op jit(solution)/shard_map/pallas_call | solution.py:399
  37.7 0.3 copy-done.2
  38.0 2.9 %shard_map.130 = (f32[384,768]{1,0:T(8,128)S(1)}, f32[384,768]{1,0:T(8,128)S(1)}, f32[768,768]{1,0:T(8,128)S(1)}) custom-call(f32[32,768]{1,0:T(8,128)S(1)} %get-tuple-element.34.grad_ref, f32[1024,768]{1,0:T(8,128)S(1)} %copy-done.2, bf16[1536,1024]{1,0:T(8,128)(2,1)S(1)} %get-tuple-element.41.turned_ref, f32[8,768]{1,0:T(8,128)S(1)} %get-tuple-element.33.stat_ref._, ...), custom_call_target="tpu_custom_call" | custom-call | flops 2415919104 | bytes 11010048 | tf_op jit(solution)/shard_map/pallas_call | solution.py:399
  40.9 0.3 collective-permute-start.11
  41.1 0.1 fusion.34
  41.3 0.1 fusion
  41.6 1.6 %collective-permute-start.9 = (f16[392,768]{1,0:T(8,128)(2,1)S(1)}, f16[392,768]{1,0:T(8,128)(2,1)S(1)}, u32[]{:S(2)}, u32[]{:S(2)}) collective-permute-start(f16[392,768]{1,0:T(8,128)(2,1)S(1)} %add_convert_fusion.1), channel_id=1, source_target_pairs={{0,4},{2,6},{4,0},{6,2},{8,12},{10,14},{12,8},{14,10},{16,20},{18,... | collective-permute-start | bytes 1806344 | tf_op jit(solution)/shard_map/ppermute | solution.py:440
  43.2 0.2 broadcast_add_fusion
  43.5 0.3 collective-permute-done.11
  43.8 0.1 add_multiply_fusion
  44.1 0.2 collective-permute-start.14
  44.3 0.1 collective-permute-start.13
  44.4 13.0 %collective-permute-done.9 = f16[392,768]{1,0:T(8,128)(2,1)S(1)} collective-permute-done((f16[392,768]{1,0:T(8,128)(2,1)S(1)}, f16[392,768]{1,0:T(8,128)(2,1)S(1)}, u32[]{:S(2)}, u32[]{:S(2)}) %collective-permute-start.9) | collective-permute-done | bytes 602144 | tf_op jit(solution)/shard_map/ppermute | solution.py:440
  57.5 0.1 fusion.38
  57.8 0.2 collective-permute-start.12
  58.2 2.5 %collective-permute-start.18 = (f16[104,768]{1,0:T(8,128)(2,1)S(1)}, f16[104,768]{1,0:T(8,128)(2,1)S(1)}, u32[]{:S(2)}, u32[]{:S(2)}) collective-permute-start(f16[104,768]{1,0:T(8,128)(2,1)S(1)} %add_convert_fusion.4), channel_id=1, source_target_pairs={{0,16},{2,18},{4,20},{6,22},{8,24},{10,26},{12,28},{14,30},{16,0},... | collective-permute-start | bytes 479240 | tf_op jit(solution)/shard_map/ppermute | solution.py:440
  60.9 0.1 fusion.42
  61.0 0.1 fusion.2
  61.3 1.6 %collective-permute-start.16 = (f16[200,768]{1,0:T(8,128)(2,1)S(1)}, f16[200,768]{1,0:T(8,128)(2,1)S(1)}, u32[]{:S(2)}, u32[]{:S(2)}) collective-permute-start(f16[200,768]{1,0:T(8,128)(2,1)S(1)} %add_convert_fusion.2), channel_id=1, source_target_pairs={{0,4},{2,6},{4,0},{6,2},{8,12},{10,14},{12,8},{14,10},{16,20},{18,... | collective-permute-start | bytes 921608 | tf_op jit(solution)/shard_map/ppermute | solution.py:440
  62.9 3.1 %collective-permute-done.18 = f16[104,768]{1,0:T(8,128)(2,1)S(1)} collective-permute-done((f16[104,768]{1,0:T(8,128)(2,1)S(1)}, f16[104,768]{1,0:T(8,128)(2,1)S(1)}, u32[]{:S(2)}, u32[]{:S(2)}) %collective-permute-start.18) | collective-permute-done | bytes 159776 | tf_op jit(solution)/shard_map/ppermute | solution.py:440
  66.0 0.8 collective-permute-done.12
  66.8 0.1 ceil_reduce_fusion
  67.0 2.5 %collective-permute-done.16 = f16[200,768]{1,0:T(8,128)(2,1)S(1)} collective-permute-done((f16[200,768]{1,0:T(8,128)(2,1)S(1)}, f16[200,768]{1,0:T(8,128)(2,1)S(1)}, u32[]{:S(2)}, u32[]{:S(2)}) %collective-permute-start.16) | collective-permute-done | bytes 307232 | tf_op jit(solution)/shard_map/ppermute | solution.py:440
  69.9 0.1 fusion.15
  70.2 1.6 %collective-permute-start.15 = (f16[56,768]{1,0:T(8,128)(2,1)S(1)}, f16[56,768]{1,0:T(8,128)(2,1)S(1)}, u32[]{:S(2)}, u32[]{:S(2)}) collective-permute-start(f16[56,768]{1,0:T(8,128)(2,1)S(1)} %add_convert_fusion.7), channel_id=1, source_target_pairs={{0,16},{2,18},{4,20},{6,22},{8,24},{10,26},{12,28},{14,30},{16,0},... | collective-permute-start | bytes 258056 | tf_op jit(solution)/shard_map/ppermute | solution.py:440
  71.8 1.4 %collective-permute-start.17 = (f16[104,768]{1,0:T(8,128)(2,1)S(1)}, f16[104,768]{1,0:T(8,128)(2,1)S(1)}, u32[]{:S(2)}, u32[]{:S(2)}) collective-permute-start(f16[104,768]{1,0:T(8,128)(2,1)S(1)} %add_convert_fusion.3), channel_id=1, source_target_pairs={{0,16},{2,18},{4,20},{6,22},{8,24},{10,26},{12,28},{14,30},{16,0},... | collective-permute-start | bytes 479240 | tf_op jit(solution)/shard_map/ppermute | solution.py:440
  73.2 1.5 %collective-permute-start.19 = (f16[56,768]{1,0:T(8,128)(2,1)S(1)}, f16[56,768]{1,0:T(8,128)(2,1)S(1)}, u32[]{:S(2)}, u32[]{:S(2)}) collective-permute-start(f16[56,768]{1,0:T(8,128)(2,1)S(1)} %add_convert_fusion.6), channel_id=1, source_target_pairs={{0,8},{2,10},{4,12},{6,14},{8,0},{10,2},{12,4},{14,6},{16,24},{18,... | collective-permute-start | bytes 258056 | tf_op jit(solution)/shard_map/ppermute | solution.py:440
  74.6 5.9 %collective-permute-done.15 = f16[56,768]{1,0:T(8,128)(2,1)S(1)} collective-permute-done((f16[56,768]{1,0:T(8,128)(2,1)S(1)}, f16[56,768]{1,0:T(8,128)(2,1)S(1)}, u32[]{:S(2)}, u32[]{:S(2)}) %collective-permute-start.15) | collective-permute-done | bytes 86048 | tf_op jit(solution)/shard_map/ppermute | solution.py:440
  80.6 0.6 fusion.115
  81.2 0.1 fusion.23
  81.4 0.7 pad_maximum_fusion
  82.1 0.2 collective-permute-done.17
  82.3 0.8 %fusion.5 = f32[96,768]{1,0:T(8,128)} fusion(f32[392,768]{1,0:T(8,128)S(1)} %convert_add_fusion, f32[384,768]{1,0:T(8,128)S(1)} %collective-permute-done.13, f32[768,768]{1,0:T(8,128)S(1)} %get-tuple-element.42, f16[104,768]{1,0:T(8,128)(2,1)S(1)} %collective-permute-done.17, f16[200,768]{1,0:T(8,128)(2,1)S(1)} %collective-permute-done.16, ...), kind=kLoop, calls=%fused_computation.19 | loop fusion | flops 663552 | bytes 1483776 | tf_op jit(solution)/shard_map/add | solution.py:418
  (74 shorter events, 2.1 us)
Async XLA Ops:
  0.6 19.0 %copy-start.5 = (s32[16]{0:T(128)S(1)}, s32[16]{0:T(128)}, u32[]{:S(2)}) copy-start(s32[16]{0:T(128)} %constant.63.clone) | copy-start | bytes 196
  0.6 19.0 %copy-start = (bf16[16,64,1536]{2,1,0:T(8,128)(2,1)S(1)}, bf16[16,64,1536]{2,1,0:T(8,128)(2,1)}, u32[]{:S(2)}) copy-start(bf16[16,64,1536]{2,1,0:T(8,128)(2,1)} %param.10) | copy-start | bytes 9437188
  9.9 4.7 %collective-permute-start = (f32[32,128]{1,0:T(8,128)S(1)}, f32[32,128]{1,0:T(8,128)S(1)}, u32[]{:S(2)}, u32[]{:S(2)}) collective-permute-start(f32[32,128]{1,0:T(8,128)S(1)} %get-tuple-element.25.own_ref), channel_id=1, source_target_pairs={{0,1},{1,0},{2,3},{3,2},{4,5},{5,4},{6,7},{7,6},{8,9},{9,8},{10,11... | collective-permute-start | bytes 49160 | tf_op jit(solution)/shard_map/ppermute | solution.py:443
  14.7 7.5 %collective-permute-start.1 = (bf16[32,768]{1,0:T(8,128)(2,1)S(1)}, bf16[32,768]{1,0:T(8,128)(2,1)S(1)}, u32[]{:S(2)}, u32[]{:S(2)}) collective-permute-start(bf16[32,768]{1,0:T(8,128)(2,1)S(1)} %get-tuple-element.26._.refs_1_), channel_id=1, source_target_pairs={{0,24},{2,26},{4,28},{6,30},{8,16},{10,18},{12,20},{14,22},{16,8},... | collective-permute-start | bytes 147464 | tf_op jit(solution)/shard_map/ppermute | solution.py:440
  18.9 5.0 %collective-permute-start.2 = (bf16[32,768]{1,0:T(8,128)(2,1)S(1)}, bf16[32,768]{1,0:T(8,128)(2,1)S(1)}, u32[]{:S(2)}, u32[]{:S(2)}) collective-permute-start(bf16[32,768]{1,0:T(8,128)(2,1)S(1)} %get-tuple-element.26._.refs_1_), channel_id=1, source_target_pairs={{0,16},{2,18},{4,20},{6,22},{8,24},{10,26},{12,28},{14,30},{16,0},... | collective-permute-start | bytes 147464 | tf_op jit(solution)/shard_map/ppermute | solution.py:440
  19.0 5.0 %collective-permute-start.3 = (bf16[32,768]{1,0:T(8,128)(2,1)S(1)}, bf16[32,768]{1,0:T(8,128)(2,1)S(1)}, u32[]{:S(2)}, u32[]{:S(2)}) collective-permute-start(bf16[32,768]{1,0:T(8,128)(2,1)S(1)} %get-tuple-element.26._.refs_1_), channel_id=1, source_target_pairs={{0,8},{2,10},{4,12},{6,14},{8,0},{10,2},{12,4},{14,6},{16,24},{18,... | collective-permute-start | bytes 147464 | tf_op jit(solution)/shard_map/ppermute | solution.py:440
  19.6 6.0 %copy-start.4 = (s32[32]{0:T(128)S(1)}, s32[32]{0:T(128)}, u32[]{:S(2)}) copy-start(s32[32]{0:T(128)} %constant.62.clone) | copy-start | bytes 388
  19.6 6.0 %copy-start.1 = (bf16[16,32,1536]{2,1,0:T(8,128)(2,1)S(1)}, bf16[16,32,1536]{2,1,0:T(8,128)(2,1)}, u32[]{:S(2)}) copy-start(bf16[16,32,1536]{2,1,0:T(8,128)(2,1)} %param.11) | copy-start | bytes 4718596
  24.0 5.7 %collective-permute-start.4 = (bf16[4,32,768]{2,1,0:T(8,128)(2,1)S(1)}, bf16[4,32,768]{2,1,0:T(8,128)(2,1)S(1)}, u32[]{:S(2)}, u32[]{:S(2)}) collective-permute-start(bf16[4,32,768]{2,1,0:T(8,128)(2,1)S(1)} %shard_map.124._.refs_0_), channel_id=1, source_target_pairs={{0,4},{2,6},{4,0},{6,2},{8,12},{10,14},{12,8},{14,10},{16,20},{18,... | collective-permute-start | bytes 589832 | tf_op jit(solution)/shard_map/ppermute | solution.py:440
  25.6 4.2 %collective-permute-start.5 = (bf16[4,32,768]{2,1,0:T(8,128)(2,1)S(1)}, bf16[4,32,768]{2,1,0:T(8,128)(2,1)S(1)}, u32[]{:S(2)}, u32[]{:S(2)}) collective-permute-start(bf16[4,32,768]{2,1,0:T(8,128)(2,1)S(1)} %shard_map.124._.refs_0_), channel_id=1, source_target_pairs={{0,2},{2,0},{4,6},{6,4},{8,10},{10,8},{12,14},{14,12},{16,18},{18,... | collective-permute-start | bytes 589832 | tf_op jit(solution)/shard_map/ppermute | solution.py:440
  27.1 9.0 %copy-start.3 = (f32[512,768]{1,0:T(8,128)S(1)}, f32[512,768]{1,0:T(8,128)}, u32[]{:S(2)}) copy-start(f32[512,768]{1,0:T(8,128)} %get-tuple-element.35.slope_ref) | copy-start | bytes 4718596
  29.7 1.5 %collective-permute-start.6 = (bf16[4,32,768]{2,1,0:T(8,128)(2,1)S(1)}, bf16[4,32,768]{2,1,0:T(8,128)(2,1)S(1)}, u32[]{:S(2)}, u32[]{:S(2)}) collective-permute-start(bf16[4,32,768]{2,1,0:T(8,128)(2,1)S(1)} %bitcast.8), channel_id=1, source_target_pairs={{0,2},{2,0},{4,6},{6,4},{8,10},{10,8},{12,14},{14,12},{16,18},{18,... | collective-permute-start | bytes 589832 | tf_op jit(solution)/shard_map/ppermute | solution.py:440
  31.6 3.9 %collective-permute-start.7 = (f32[32,256]{1,0:T(8,128)S(1)}, f32[32,256]{1,0:T(8,128)S(1)}, u32[]{:S(2)}, u32[]{:S(2)}) collective-permute-start(f32[32,256]{1,0:T(8,128)S(1)} %get-tuple-element.29.own_ref), channel_id=1, source_target_pairs={{0,1},{1,0},{2,3},{3,2},{4,5},{5,4},{6,7},{7,6},{8,9},{9,8},{10,11... | collective-permute-start | bytes 98312 | tf_op jit(solution)/shard_map/ppermute | solution.py:443
  36.1 1.9 %copy-start.2 = (f32[1024,768]{1,0:T(8,128)S(1)}, f32[1024,768]{1,0:T(8,128)}, u32[]{:S(2)}) copy-start(f32[1024,768]{1,0:T(8,128)} %get-tuple-element.40.slope_ref) | copy-start | bytes 9437188
  37.6 3.6 %collective-permute-start.8 = (f32[392,768]{1,0:T(8,128)S(1)}, f32[392,768]{1,0:T(8,128)S(1)}, u32[]{:S(2)}, u32[]{:S(2)}) collective-permute-start(f32[392,768]{1,0:T(8,128)S(1)} %get-tuple-element.37._), channel_id=1, source_target_pairs={{0,2},{2,0},{4,6},{6,4},{8,10},{10,8},{12,14},{14,12},{16,18},{18,... | collective-permute-start | bytes 3612680 | tf_op jit(solution)/shard_map/ppermute | solution.py:440
  40.9 2.9 %collective-permute-start.11 = (f32[384,768]{1,0:T(8,128)S(1)}, f32[384,768]{1,0:T(8,128)S(1)}, u32[]{:S(2)}, u32[]{:S(2)}) collective-permute-start(f32[384,768]{1,0:T(8,128)S(1)} %get-tuple-element.43), channel_id=1, source_target_pairs={{0,2},{2,0},{4,6},{6,4},{8,10},{10,8},{12,14},{14,12},{16,18},{18,... | collective-permute-start | bytes 3538952 | tf_op jit(solution)/shard_map/ppermute | solution.py:440
  41.6 15.9 %collective-permute-start.9 = (f16[392,768]{1,0:T(8,128)(2,1)S(1)}, f16[392,768]{1,0:T(8,128)(2,1)S(1)}, u32[]{:S(2)}, u32[]{:S(2)}) collective-permute-start(f16[392,768]{1,0:T(8,128)(2,1)S(1)} %add_convert_fusion.1), channel_id=1, source_target_pairs={{0,4},{2,6},{4,0},{6,2},{8,12},{10,14},{12,8},{14,10},{16,20},{18,... | collective-permute-start | bytes 1806344 | tf_op jit(solution)/shard_map/ppermute | solution.py:440
  43.4 14.2 %collective-permute-start.10 = (f32[384,768]{1,0:T(8,128)S(1)}, f32[384,768]{1,0:T(8,128)S(1)}, u32[]{:S(2)}, u32[]{:S(2)}) collective-permute-start(f32[384,768]{1,0:T(8,128)S(1)} %get-tuple-element.124), channel_id=1, source_target_pairs={{0,2},{2,0},{4,6},{6,4},{8,10},{10,8},{12,14},{14,12},{16,18},{18,... | collective-permute-start | bytes 3538952 | tf_op jit(solution)/shard_map/ppermute | solution.py:440
  44.1 16.7 %collective-permute-start.14 = (f16[392,768]{1,0:T(8,128)(2,1)S(1)}, f16[392,768]{1,0:T(8,128)(2,1)S(1)}, u32[]{:S(2)}, u32[]{:S(2)}) collective-permute-start(f16[392,768]{1,0:T(8,128)(2,1)S(1)} %add_convert_fusion), channel_id=1, source_target_pairs={{0,8},{2,10},{4,12},{6,14},{8,0},{10,2},{12,4},{14,6},{16,24},{18,... | collective-permute-start | bytes 1806344 | tf_op jit(solution)/shard_map/ppermute | solution.py:440
  44.3 16.7 %collective-permute-start.13 = (f32[384,768]{1,0:T(8,128)S(1)}, f32[384,768]{1,0:T(8,128)S(1)}, u32[]{:S(2)}, u32[]{:S(2)}) collective-permute-start(f32[384,768]{1,0:T(8,128)S(1)} %get-tuple-element.123), channel_id=1, source_target_pairs={{0,2},{2,0},{4,6},{6,4},{8,10},{10,8},{12,14},{14,12},{16,18},{18,... | collective-permute-start | bytes 3538952 | tf_op jit(solution)/shard_map/ppermute | solution.py:440
  57.8 9.0 %collective-permute-start.12 = (f16[104,768]{1,0:T(8,128)(2,1)S(1)}, f16[104,768]{1,0:T(8,128)(2,1)S(1)}, u32[]{:S(2)}, u32[]{:S(2)}) collective-permute-start(f16[104,768]{1,0:T(8,128)(2,1)S(1)} %add_convert_fusion.5), channel_id=1, source_target_pairs={{0,8},{2,10},{4,12},{6,14},{8,0},{10,2},{12,4},{14,6},{16,24},{18,... | collective-permute-start | bytes 479240 | tf_op jit(solution)/shard_map/ppermute | solution.py:440
  58.2 7.8 %collective-permute-start.18 = (f16[104,768]{1,0:T(8,128)(2,1)S(1)}, f16[104,768]{1,0:T(8,128)(2,1)S(1)}, u32[]{:S(2)}, u32[]{:S(2)}) collective-permute-start(f16[104,768]{1,0:T(8,128)(2,1)S(1)} %add_convert_fusion.4), channel_id=1, source_target_pairs={{0,16},{2,18},{4,20},{6,22},{8,24},{10,26},{12,28},{14,30},{16,0},... | collective-permute-start | bytes 479240 | tf_op jit(solution)/shard_map/ppermute | solution.py:440
  61.3 8.2 %collective-permute-start.16 = (f16[200,768]{1,0:T(8,128)(2,1)S(1)}, f16[200,768]{1,0:T(8,128)(2,1)S(1)}, u32[]{:S(2)}, u32[]{:S(2)}) collective-permute-start(f16[200,768]{1,0:T(8,128)(2,1)S(1)} %add_convert_fusion.2), channel_id=1, source_target_pairs={{0,4},{2,6},{4,0},{6,2},{8,12},{10,14},{12,8},{14,10},{16,20},{18,... | collective-permute-start | bytes 921608 | tf_op jit(solution)/shard_map/ppermute | solution.py:440
  70.2 10.4 %collective-permute-start.15 = (f16[56,768]{1,0:T(8,128)(2,1)S(1)}, f16[56,768]{1,0:T(8,128)(2,1)S(1)}, u32[]{:S(2)}, u32[]{:S(2)}) collective-permute-start(f16[56,768]{1,0:T(8,128)(2,1)S(1)} %add_convert_fusion.7), channel_id=1, source_target_pairs={{0,16},{2,18},{4,20},{6,22},{8,24},{10,26},{12,28},{14,30},{16,0},... | collective-permute-start | bytes 258056 | tf_op jit(solution)/shard_map/ppermute | solution.py:440
  71.8 10.5 %collective-permute-start.17 = (f16[104,768]{1,0:T(8,128)(2,1)S(1)}, f16[104,768]{1,0:T(8,128)(2,1)S(1)}, u32[]{:S(2)}, u32[]{:S(2)}) collective-permute-start(f16[104,768]{1,0:T(8,128)(2,1)S(1)} %add_convert_fusion.3), channel_id=1, source_target_pairs={{0,16},{2,18},{4,20},{6,22},{8,24},{10,26},{12,28},{14,30},{16,0},... | collective-permute-start | bytes 479240 | tf_op jit(solution)/shard_map/ppermute | solution.py:440
  73.2 8.0 %collective-permute-start.19 = (f16[56,768]{1,0:T(8,128)(2,1)S(1)}, f16[56,768]{1,0:T(8,128)(2,1)S(1)}, u32[]{:S(2)}, u32[]{:S(2)}) collective-permute-start(f16[56,768]{1,0:T(8,128)(2,1)S(1)} %add_convert_fusion.6), channel_id=1, source_target_pairs={{0,8},{2,10},{4,12},{6,14},{8,0},{10,2},{12,4},{14,6},{16,24},{18,... | collective-permute-start | bytes 258056 | tf_op jit(solution)/shard_map/ppermute | solution.py:440

commit v12 on v10

--- a/solution.py
+++ b/solution.py
@@ -563,10 +563,10 @@
     text = [(keep[: late.shape[0]], None), (swap(late, 1), None)]
     text, text_stat = take(text, start_stat, 1, text_in)
     parts = [(terms, text_stat) for terms in halves(text)]
-    image, image_stat = take(image, start_stat, 0, image_in)
     for step in range(bits - 2):
-        image, image_leaves = halves(image)
         arrivals = [None, None]
+        if step > 0:
+            image, image_leaves = halves(image)
         if step < bits - 3:
             terms, leaves = halves(parts[0][0])
             made, arrival = leave(leaves, parts[0][1], 1, text_orders[0][step], coded)
@@ -574,6 +574,10 @@
             terms, leaves = halves(parts[1][0])
             made, arrival = leave(leaves, parts[1][1], 1, text_orders[1][step], made)
             arrivals[1] = (terms, parts[1][1], arrival)
+            if step == 0:
+                image_in = image_in.astype(F32) + 0.0 * made[:1].astype(F32)
+                image, image_stat = take(image, start_stat, 0, image_in)
+                image, image_leaves = halves(image)
             coded, image_in = leave(image_leaves, image_stat, 0, image_order[step + 1], made)
         else:
             coded, image_in = leave(image_leaves, image_stat, 0, image_order[step + 1], coded)

time: 87.4 us -> 84.6 us (0.968)
  waiting for transfers between devices: 36.8 us -> 34.2 us
    ppermute x18, waiting for transfers between devices: 35.3 us -> 32.6 us  [swap(): return lax.ppermute(array, 'dp', [(i, i ^ mask) for i in range(cycle)])]
  transfers between devices with their start and end apart: 20 -> 20, of which waited for: 12 -> 11; matrix products, arithmetic and copies ran while one was open for 5% -> 5% of each run, Pallas kernels for 8% -> 8%
where the time goes in v12:
time: 84.6 us; the launch traced here: 84.4 us
  waiting for transfers between devices  34.2 us (40%)
  starting transfers between devices  22.3 us (26%)
  Pallas kernels  18.7 us (22%)
  other arithmetic  5.26 us (6%)
  between operations  3.67 us (4%)
    ppermute x18, waiting for transfers between devices, swap(): return lax.ppermute(array, 'dp', [(i, i ^ mask) for i in range(cycle)])  32.6 us
    ppermute x18, starting transfers between devices, swap(): return lax.ppermute(array, 'dp', [(i, i ^ mask) for i in range(cycle)])  17.7 us
    pallas_call x1, Pallas kernels, forward(): pl.pallas_call(functools.partial(forward_kernel, (rows_i // samples, rows...  9.25 us
    ppermute x2, starting transfers between devices, swap_halves(): return lax.ppermute(array, 'mp', [(0, 1), (1, 0)])  4.52 us
    pallas_call x2, Pallas kernels, weight_terms(): pl.pallas_call(functools.partial(weight_kernel, base, carries), out_shape...  4.38 us
    pallas_call x2, Pallas kernels, turn(): pl.pallas_call(turn_kernel, out_shape=(jax.ShapeDtypeStruct((depth, rows)...  4.08 us
  transfers between devices with their start and end apart: 20, of which 11 were waited for; matrix products, arithmetic and copies ran while one was open for 5% of the time, Pallas kernels for 8%

profile of v12, /device:TPU:0, one launch (start us, length us, event | category | flops | bytes accessed | tf_op | source)
XLA Modules:
  0.0 84.4 jit_solution(10362603439135899660)
XLA Ops:
  0.7 9.2 %shard_map.121 = (f32[32,768]{1,0:T(8,128)S(1)}, f32[32,128]{1,0:T(8,128)S(1)}, f32[1024,768]{1,0:T(8,128)}, f32[512,768]{1,0:T(8,128)}) custom-call(s32[1]{0:T(128)} %bitcast.1.place_ref, bf16[1024,1536]{1,0:T(8,128)(2,1)} %bitcast.4, bf16[512,1536]{1,0:T(8,128)(2,1)} %bitcast.6, bf16[1536,768]{1,0:T(8,128)(2,1)} %image_w_hbm.1, bf16[1536,768]{1,0:T(8,128)(2,1)} %text_w_hbm.1), custom_call_target="tpu_custom_call" | custom-call | flops 3623878656 | bytes 14155776 | tf_op jit(solution)/shard_map/pallas_call | solution.py:141
  9.9 3.0 %collective-permute-start = (f32[32,128]{1,0:T(8,128)S(1)}, f32[32,128]{1,0:T(8,128)S(1)}, u32[]{:S(2)}, u32[]{:S(2)}) collective-permute-start(f32[32,128]{1,0:T(8,128)S(1)} %get-tuple-element.25.own_ref), channel_id=1, source_target_pairs={{0,1},{1,0},{2,3},{3,2},{4,5},{5,4},{6,7},{7,6},{8,9},{9,8},{10,11... | collective-permute-start | bytes 49160 | tf_op jit(solution)/shard_map/ppermute | solution.py:443
  13.6 1.1 %collective-permute-done.other_ref = f32[32,128]{1,0:T(8,128)S(1)} collective-permute-done((f32[32,128]{1,0:T(8,128)S(1)}, f32[32,128]{1,0:T(8,128)S(1)}, u32[]{:S(2)}, u32[]{:S(2)}) %collective-permute-start) | collective-permute-done | bytes 16416 | tf_op jit(solution)/shard_map/ppermute | solution.py:443
  14.7 4.2 %collective-permute-start.1 = (bf16[32,768]{1,0:T(8,128)(2,1)S(1)}, bf16[32,768]{1,0:T(8,128)(2,1)S(1)}, u32[]{:S(2)}, u32[]{:S(2)}) collective-permute-start(bf16[32,768]{1,0:T(8,128)(2,1)S(1)} %get-tuple-element.26._.refs_1_), channel_id=1, source_target_pairs={{0,24},{2,26},{4,28},{6,30},{8,16},{10,18},{12,20},{14,22},{16,8},... | collective-permute-start | bytes 147464 | tf_op jit(solution)/shard_map/ppermute | solution.py:440
  19.0 0.6 collective-permute-start.3
  19.6 2.6 %shard_map.123 = (bf16[1536,1024]{1,0:T(8,128)(2,1)S(1)}, f32[8,128]{1,0:T(8,128)S(1)}) custom-call(s32[16]{0:T(128)S(1)} %broadcast_xor_fusion.1.source_ref, bf16[1024,1536]{1,0:T(8,128)(2,1)S(1)} %bitcast.5, bf16[32,768]{1,0:T(8,128)(2,1)S(1)} %get-tuple-element.26._.refs_1_), custom_call_target="tpu_custom_call" | custom-call | bytes 6291456 | tf_op jit(solution)/shard_map/pallas_call | solution.py:236
  22.2 1.7 %collective-permute-done.2.refs_3_ = bf16[32,768]{1,0:T(8,128)(2,1)S(1)} collective-permute-done((bf16[32,768]{1,0:T(8,128)(2,1)S(1)}, bf16[32,768]{1,0:T(8,128)(2,1)S(1)}, u32[]{:S(2)}, u32[]{:S(2)}) %collective-permute-start.2) | collective-permute-done | bytes 49184 | tf_op jit(solution)/shard_map/ppermute | solution.py:440
  24.0 1.6 %collective-permute-start.4 = (bf16[4,32,768]{2,1,0:T(8,128)(2,1)S(1)}, bf16[4,32,768]{2,1,0:T(8,128)(2,1)S(1)}, u32[]{:S(2)}, u32[]{:S(2)}) collective-permute-start(bf16[4,32,768]{2,1,0:T(8,128)(2,1)S(1)} %shard_map.124._.refs_0_), channel_id=1, source_target_pairs={{0,4},{2,6},{4,0},{6,2},{8,12},{10,14},{12,8},{14,10},{16,20},{18,... | collective-permute-start | bytes 589832 | tf_op jit(solution)/shard_map/ppermute | solution.py:440
  25.6 1.5 %shard_map.125 = (bf16[1536,512]{1,0:T(8,128)(2,1)S(1)}, f32[8,128]{1,0:T(8,128)S(1)}) custom-call(s32[32]{0:T(128)S(1)} %broadcast_xor_fusion.source_ref, bf16[512,1536]{1,0:T(8,128)(2,1)S(1)} %bitcast.7, bf16[4,32,768]{2,1,0:T(8,128)(2,1)S(1)} %shard_map.124._.refs_0_), custom_call_target="tpu_custom_call" | custom-call | bytes 3145728 | tf_op jit(solution)/shard_map/pallas_call | solution.py:236
  27.1 2.6 %collective-permute-done.4.refs_1_ = bf16[4,32,768]{2,1,0:T(8,128)(2,1)S(1)} collective-permute-done((bf16[4,32,768]{2,1,0:T(8,128)(2,1)S(1)}, bf16[4,32,768]{2,1,0:T(8,128)(2,1)S(1)}, u32[]{:S(2)}, u32[]{:S(2)}) %collective-permute-start.4) | collective-permute-done | bytes 196640 | tf_op jit(solution)/shard_map/ppermute | solution.py:440
  29.8 1.4 %collective-permute-done.6.refs_3_ = bf16[4,32,768]{2,1,0:T(8,128)(2,1)S(1)} collective-permute-done((bf16[4,32,768]{2,1,0:T(8,128)(2,1)S(1)}, bf16[4,32,768]{2,1,0:T(8,128)(2,1)S(1)}, u32[]{:S(2)}, u32[]{:S(2)}) %collective-permute-start.6) | collective-permute-done | bytes 196640 | tf_op jit(solution)/shard_map/ppermute | solution.py:440
  31.2 0.4 shard_map.127
  31.6 1.5 %collective-permute-start.7 = (f32[32,256]{1,0:T(8,128)S(1)}, f32[32,256]{1,0:T(8,128)S(1)}, u32[]{:S(2)}, u32[]{:S(2)}) collective-permute-start(f32[32,256]{1,0:T(8,128)S(1)} %get-tuple-element.29.own_ref), channel_id=1, source_target_pairs={{0,1},{1,0},{2,3},{3,2},{4,5},{5,4},{6,7},{7,6},{8,9},{9,8},{10,11... | collective-permute-start | bytes 98312 | tf_op jit(solution)/shard_map/ppermute | solution.py:443
  35.0 0.5 collective-permute-done.7.other_ref
  35.5 0.5 shard_map.128
  36.1 1.5 %shard_map.129 = (f32[392,768]{1,0:T(8,128)S(1)}, f32[384,768]{1,0:T(8,128)S(1)}, f32[768,768]{1,0:T(8,128)S(1)}) custom-call(f32[32,768]{1,0:T(8,128)S(1)} %get-tuple-element.34.grad_ref, f32[512,768]{1,0:T(8,128)S(1)} %copy-done.3, bf16[1536,512]{1,0:T(8,128)(2,1)S(1)} %get-tuple-element.36.turned_ref, f32[8,768]{1,0:T(8,128)S(1)} %get-tuple-element.33.stat_ref._, ...), custom_call_target="tpu_custom_call" | custom-call | flops 1207959552 | bytes 7864320 | tf_op jit(solution)/shard_map/pallas_call | solution.py:399
  37.7 0.3 copy-done.2
  38.0 2.9 %shard_map.130 = (f32[384,768]{1,0:T(8,128)S(1)}, f32[384,768]{1,0:T(8,128)S(1)}, f32[768,768]{1,0:T(8,128)S(1)}) custom-call(f32[32,768]{1,0:T(8,128)S(1)} %get-tuple-element.34.grad_ref, f32[1024,768]{1,0:T(8,128)S(1)} %copy-done.2, bf16[1536,1024]{1,0:T(8,128)(2,1)S(1)} %get-tuple-element.41.turned_ref, f32[8,768]{1,0:T(8,128)S(1)} %get-tuple-element.33.stat_ref._, ...), custom_call_target="tpu_custom_call" | custom-call | flops 2415919104 | bytes 11010048 | tf_op jit(solution)/shard_map/pallas_call | solution.py:399
  40.9 0.3 collective-permute-start.11
  41.1 0.1 fusion.34
  41.3 0.1 fusion
  41.6 1.6 %collective-permute-start.9 = (f16[392,768]{1,0:T(8,128)(2,1)S(1)}, f16[392,768]{1,0:T(8,128)(2,1)S(1)}, u32[]{:S(2)}, u32[]{:S(2)}) collective-permute-start(f16[392,768]{1,0:T(8,128)(2,1)S(1)} %add_convert_fusion.1), channel_id=1, source_target_pairs={{0,4},{2,6},{4,0},{6,2},{8,12},{10,14},{12,8},{14,10},{16,20},{18,... | collective-permute-start | bytes 1806344 | tf_op jit(solution)/shard_map/ppermute | solution.py:440
  43.2 0.2 broadcast_add_fusion
  43.4 0.1 collective-permute-start.10
  43.5 0.3 collective-permute-done.11
  43.8 0.1 add_multiply_fusion
  44.1 0.2 collective-permute-start.14
  44.3 0.1 collective-permute-start.13
  44.4 13.0 %collective-permute-done.9 = f16[392,768]{1,0:T(8,128)(2,1)S(1)} collective-permute-done((f16[392,768]{1,0:T(8,128)(2,1)S(1)}, f16[392,768]{1,0:T(8,128)(2,1)S(1)}, u32[]{:S(2)}, u32[]{:S(2)}) %collective-permute-start.9) | collective-permute-done | bytes 602144 | tf_op jit(solution)/shard_map/ppermute | solution.py:440
  57.5 0.1 fusion.38
  57.8 0.2 collective-permute-start.12
  58.2 2.5 %collective-permute-start.18 = (f16[104,768]{1,0:T(8,128)(2,1)S(1)}, f16[104,768]{1,0:T(8,128)(2,1)S(1)}, u32[]{:S(2)}, u32[]{:S(2)}) collective-permute-start(f16[104,768]{1,0:T(8,128)(2,1)S(1)} %add_convert_fusion.4), channel_id=1, source_target_pairs={{0,16},{2,18},{4,20},{6,22},{8,24},{10,26},{12,28},{14,30},{16,0},... | collective-permute-start | bytes 479240 | tf_op jit(solution)/shard_map/ppermute | solution.py:440
  60.9 0.1 fusion.42
  61.0 0.1 fusion.2
  61.3 1.6 %collective-permute-start.15 = (f16[200,768]{1,0:T(8,128)(2,1)S(1)}, f16[200,768]{1,0:T(8,128)(2,1)S(1)}, u32[]{:S(2)}, u32[]{:S(2)}) collective-permute-start(f16[200,768]{1,0:T(8,128)(2,1)S(1)} %add_convert_fusion.2), channel_id=1, source_target_pairs={{0,4},{2,6},{4,0},{6,2},{8,12},{10,14},{12,8},{14,10},{16,20},{18,... | collective-permute-start | bytes 921608 | tf_op jit(solution)/shard_map/ppermute | solution.py:440
  62.9 3.1 %collective-permute-done.18 = f16[104,768]{1,0:T(8,128)(2,1)S(1)} collective-permute-done((f16[104,768]{1,0:T(8,128)(2,1)S(1)}, f16[104,768]{1,0:T(8,128)(2,1)S(1)}, u32[]{:S(2)}, u32[]{:S(2)}) %collective-permute-start.18) | collective-permute-done | bytes 159776 | tf_op jit(solution)/shard_map/ppermute | solution.py:440
  66.0 0.8 collective-permute-done.12
  66.8 0.1 ceil_reduce_fusion
  67.0 2.5 %collective-permute-done.15 = f16[200,768]{1,0:T(8,128)(2,1)S(1)} collective-permute-done((f16[200,768]{1,0:T(8,128)(2,1)S(1)}, f16[200,768]{1,0:T(8,128)(2,1)S(1)}, u32[]{:S(2)}, u32[]{:S(2)}) %collective-permute-start.15) | collective-permute-done | bytes 307232 | tf_op jit(solution)/shard_map/ppermute | solution.py:440
  69.6 0.1 fusion.8
  69.9 1.6 %collective-permute-start.17 = (f16[104,768]{1,0:T(8,128)(2,1)S(1)}, f16[104,768]{1,0:T(8,128)(2,1)S(1)}, u32[]{:S(2)}, u32[]{:S(2)}) collective-permute-start(f16[104,768]{1,0:T(8,128)(2,1)S(1)} %add_convert_fusion.3), channel_id=1, source_target_pairs={{0,16},{2,18},{4,20},{6,22},{8,24},{10,26},{12,28},{14,30},{16,0},... | collective-permute-start | bytes 479240 | tf_op jit(solution)/shard_map/ppermute | solution.py:440
  71.7 1.4 %collective-permute-start.16 = (f16[56,768]{1,0:T(8,128)(2,1)S(1)}, f16[56,768]{1,0:T(8,128)(2,1)S(1)}, u32[]{:S(2)}, u32[]{:S(2)}) collective-permute-start(f16[56,768]{1,0:T(8,128)(2,1)S(1)} %add_convert_fusion.7), channel_id=1, source_target_pairs={{0,16},{2,18},{4,20},{6,22},{8,24},{10,26},{12,28},{14,30},{16,0},... | collective-permute-start | bytes 258056 | tf_op jit(solution)/shard_map/ppermute | solution.py:440
  73.3 1.5 %collective-permute-start.19 = (f16[56,768]{1,0:T(8,128)(2,1)S(1)}, f16[56,768]{1,0:T(8,128)(2,1)S(1)}, u32[]{:S(2)}, u32[]{:S(2)}) collective-permute-start(f16[56,768]{1,0:T(8,128)(2,1)S(1)} %add_convert_fusion.6), channel_id=1, source_target_pairs={{0,8},{2,10},{4,12},{6,14},{8,0},{10,2},{12,4},{14,6},{16,24},{18,... | collective-permute-start | bytes 258056 | tf_op jit(solution)/shard_map/ppermute | solution.py:440
  74.8 7.2 %collective-permute-done.16 = f16[56,768]{1,0:T(8,128)(2,1)S(1)} collective-permute-done((f16[56,768]{1,0:T(8,128)(2,1)S(1)}, f16[56,768]{1,0:T(8,128)(2,1)S(1)}, u32[]{:S(2)}, u32[]{:S(2)}) %collective-permute-start.16) | collective-permute-done | bytes 86048 | tf_op jit(solution)/shard_map/ppermute | solution.py:440
  82.0 0.6 fusion.120
  82.7 0.1 fusion.23
  82.8 0.7 pad_maximum_fusion
  83.6 0.8 fusion.5
  (78 shorter events, 2.1 us)
Async XLA Ops:
  0.6 19.0 %copy-start.5 = (s32[16]{0:T(128)S(1)}, s32[16]{0:T(128)}, u32[]{:S(2)}) copy-start(s32[16]{0:T(128)} %constant.63.clone) | copy-start | bytes 196
  0.6 19.0 %copy-start = (bf16[16,64,1536]{2,1,0:T(8,128)(2,1)S(1)}, bf16[16,64,1536]{2,1,0:T(8,128)(2,1)}, u32[]{:S(2)}) copy-start(bf16[16,64,1536]{2,1,0:T(8,128)(2,1)} %param.10) | copy-start | bytes 9437188
  9.9 4.7 %collective-permute-start = (f32[32,128]{1,0:T(8,128)S(1)}, f32[32,128]{1,0:T(8,128)S(1)}, u32[]{:S(2)}, u32[]{:S(2)}) collective-permute-start(f32[32,128]{1,0:T(8,128)S(1)} %get-tuple-element.25.own_ref), channel_id=1, source_target_pairs={{0,1},{1,0},{2,3},{3,2},{4,5},{5,4},{6,7},{7,6},{8,9},{9,8},{10,11... | collective-permute-start | bytes 49160 | tf_op jit(solution)/shard_map/ppermute | solution.py:443
  14.7 7.5 %collective-permute-start.1 = (bf16[32,768]{1,0:T(8,128)(2,1)S(1)}, bf16[32,768]{1,0:T(8,128)(2,1)S(1)}, u32[]{:S(2)}, u32[]{:S(2)}) collective-permute-start(bf16[32,768]{1,0:T(8,128)(2,1)S(1)} %get-tuple-element.26._.refs_1_), channel_id=1, source_target_pairs={{0,24},{2,26},{4,28},{6,30},{8,16},{10,18},{12,20},{14,22},{16,8},... | collective-permute-start | bytes 147464 | tf_op jit(solution)/shard_map/ppermute | solution.py:440
  18.9 5.0 %collective-permute-start.2 = (bf16[32,768]{1,0:T(8,128)(2,1)S(1)}, bf16[32,768]{1,0:T(8,128)(2,1)S(1)}, u32[]{:S(2)}, u32[]{:S(2)}) collective-permute-start(bf16[32,768]{1,0:T(8,128)(2,1)S(1)} %get-tuple-element.26._.refs_1_), channel_id=1, source_target_pairs={{0,16},{2,18},{4,20},{6,22},{8,24},{10,26},{12,28},{14,30},{16,0},... | collective-permute-start | bytes 147464 | tf_op jit(solution)/shard_map/ppermute | solution.py:440
  19.0 5.0 %collective-permute-start.3 = (bf16[32,768]{1,0:T(8,128)(2,1)S(1)}, bf16[32,768]{1,0:T(8,128)(2,1)S(1)}, u32[]{:S(2)}, u32[]{:S(2)}) collective-permute-start(bf16[32,768]{1,0:T(8,128)(2,1)S(1)} %get-tuple-element.26._.refs_1_), channel_id=1, source_target_pairs={{0,8},{2,10},{4,12},{6,14},{8,0},{10,2},{12,4},{14,6},{16,24},{18,... | collective-permute-start | bytes 147464 | tf_op jit(solution)/shard_map/ppermute | solution.py:440
  19.6 6.0 %copy-start.4 = (s32[32]{0:T(128)S(1)}, s32[32]{0:T(128)}, u32[]{:S(2)}) copy-start(s32[32]{0:T(128)} %constant.62.clone) | copy-start | bytes 388
  19.6 6.0 %copy-start.1 = (bf16[16,32,1536]{2,1,0:T(8,128)(2,1)S(1)}, bf16[16,32,1536]{2,1,0:T(8,128)(2,1)}, u32[]{:S(2)}) copy-start(bf16[16,32,1536]{2,1,0:T(8,128)(2,1)} %param.11) | copy-start | bytes 4718596
  24.0 5.7 %collective-permute-start.4 = (bf16[4,32,768]{2,1,0:T(8,128)(2,1)S(1)}, bf16[4,32,768]{2,1,0:T(8,128)(2,1)S(1)}, u32[]{:S(2)}, u32[]{:S(2)}) collective-permute-start(bf16[4,32,768]{2,1,0:T(8,128)(2,1)S(1)} %shard_map.124._.refs_0_), channel_id=1, source_target_pairs={{0,4},{2,6},{4,0},{6,2},{8,12},{10,14},{12,8},{14,10},{16,20},{18,... | collective-permute-start | bytes 589832 | tf_op jit(solution)/shard_map/ppermute | solution.py:440
  25.6 4.2 %collective-permute-start.5 = (bf16[4,32,768]{2,1,0:T(8,128)(2,1)S(1)}, bf16[4,32,768]{2,1,0:T(8,128)(2,1)S(1)}, u32[]{:S(2)}, u32[]{:S(2)}) collective-permute-start(bf16[4,32,768]{2,1,0:T(8,128)(2,1)S(1)} %shard_map.124._.refs_0_), channel_id=1, source_target_pairs={{0,2},{2,0},{4,6},{6,4},{8,10},{10,8},{12,14},{14,12},{16,18},{18,... | collective-permute-start | bytes 589832 | tf_op jit(solution)/shard_map/ppermute | solution.py:440
  27.1 9.0 %copy-start.3 = (f32[512,768]{1,0:T(8,128)S(1)}, f32[512,768]{1,0:T(8,128)}, u32[]{:S(2)}) copy-start(f32[512,768]{1,0:T(8,128)} %get-tuple-element.35.slope_ref) | copy-start | bytes 4718596
  29.7 1.5 %collective-permute-start.6 = (bf16[4,32,768]{2,1,0:T(8,128)(2,1)S(1)}, bf16[4,32,768]{2,1,0:T(8,128)(2,1)S(1)}, u32[]{:S(2)}, u32[]{:S(2)}) collective-permute-start(bf16[4,32,768]{2,1,0:T(8,128)(2,1)S(1)} %bitcast.8), channel_id=1, source_target_pairs={{0,2},{2,0},{4,6},{6,4},{8,10},{10,8},{12,14},{14,12},{16,18},{18,... | collective-permute-start | bytes 589832 | tf_op jit(solution)/shard_map/ppermute | solution.py:440
  31.6 3.9 %collective-permute-start.7 = (f32[32,256]{1,0:T(8,128)S(1)}, f32[32,256]{1,0:T(8,128)S(1)}, u32[]{:S(2)}, u32[]{:S(2)}) collective-permute-start(f32[32,256]{1,0:T(8,128)S(1)} %get-tuple-element.29.own_ref), channel_id=1, source_target_pairs={{0,1},{1,0},{2,3},{3,2},{4,5},{5,4},{6,7},{7,6},{8,9},{9,8},{10,11... | collective-permute-start | bytes 98312 | tf_op jit(solution)/shard_map/ppermute | solution.py:443
  36.1 1.9 %copy-start.2 = (f32[1024,768]{1,0:T(8,128)S(1)}, f32[1024,768]{1,0:T(8,128)}, u32[]{:S(2)}) copy-start(f32[1024,768]{1,0:T(8,128)} %get-tuple-element.40.slope_ref) | copy-start | bytes 9437188
  37.6 3.6 %collective-permute-start.8 = (f32[392,768]{1,0:T(8,128)S(1)}, f32[392,768]{1,0:T(8,128)S(1)}, u32[]{:S(2)}, u32[]{:S(2)}) collective-permute-start(f32[392,768]{1,0:T(8,128)S(1)} %get-tuple-element.37._), channel_id=1, source_target_pairs={{0,2},{2,0},{4,6},{6,4},{8,10},{10,8},{12,14},{14,12},{16,18},{18,... | collective-permute-start | bytes 3612680 | tf_op jit(solution)/shard_map/ppermute | solution.py:440
  40.9 2.9 %collective-permute-start.11 = (f32[384,768]{1,0:T(8,128)S(1)}, f32[384,768]{1,0:T(8,128)S(1)}, u32[]{:S(2)}, u32[]{:S(2)}) collective-permute-start(f32[384,768]{1,0:T(8,128)S(1)} %get-tuple-element.43), channel_id=1, source_target_pairs={{0,2},{2,0},{4,6},{6,4},{8,10},{10,8},{12,14},{14,12},{16,18},{18,... | collective-permute-start | bytes 3538952 | tf_op jit(solution)/shard_map/ppermute | solution.py:440
  41.6 15.9 %collective-permute-start.9 = (f16[392,768]{1,0:T(8,128)(2,1)S(1)}, f16[392,768]{1,0:T(8,128)(2,1)S(1)}, u32[]{:S(2)}, u32[]{:S(2)}) collective-permute-start(f16[392,768]{1,0:T(8,128)(2,1)S(1)} %add_convert_fusion.1), channel_id=1, source_target_pairs={{0,4},{2,6},{4,0},{6,2},{8,12},{10,14},{12,8},{14,10},{16,20},{18,... | collective-permute-start | bytes 1806344 | tf_op jit(solution)/shard_map/ppermute | solution.py:440
  43.4 14.2 %collective-permute-start.10 = (f32[384,768]{1,0:T(8,128)S(1)}, f32[384,768]{1,0:T(8,128)S(1)}, u32[]{:S(2)}, u32[]{:S(2)}) collective-permute-start(f32[384,768]{1,0:T(8,128)S(1)} %get-tuple-element.122), channel_id=1, source_target_pairs={{0,2},{2,0},{4,6},{6,4},{8,10},{10,8},{12,14},{14,12},{16,18},{18,... | collective-permute-start | bytes 3538952 | tf_op jit(solution)/shard_map/ppermute | solution.py:440
  44.1 16.7 %collective-permute-start.14 = (f16[392,768]{1,0:T(8,128)(2,1)S(1)}, f16[392,768]{1,0:T(8,128)(2,1)S(1)}, u32[]{:S(2)}, u32[]{:S(2)}) collective-permute-start(f16[392,768]{1,0:T(8,128)(2,1)S(1)} %add_convert_fusion), channel_id=1, source_target_pairs={{0,8},{2,10},{4,12},{6,14},{8,0},{10,2},{12,4},{14,6},{16,24},{18,... | collective-permute-start | bytes 1806344 | tf_op jit(solution)/shard_map/ppermute | solution.py:440
  44.3 16.7 %collective-permute-start.13 = (f32[384,768]{1,0:T(8,128)S(1)}, f32[384,768]{1,0:T(8,128)S(1)}, u32[]{:S(2)}, u32[]{:S(2)}) collective-permute-start(f32[384,768]{1,0:T(8,128)S(1)} %get-tuple-element.121), channel_id=1, source_target_pairs={{0,2},{2,0},{4,6},{6,4},{8,10},{10,8},{12,14},{14,12},{16,18},{18,... | collective-permute-start | bytes 3538952 | tf_op jit(solution)/shard_map/ppermute | solution.py:440
  57.8 9.0 %collective-permute-start.12 = (f16[104,768]{1,0:T(8,128)(2,1)S(1)}, f16[104,768]{1,0:T(8,128)(2,1)S(1)}, u32[]{:S(2)}, u32[]{:S(2)}) collective-permute-start(f16[104,768]{1,0:T(8,128)(2,1)S(1)} %add_convert_fusion.5), channel_id=1, source_target_pairs={{0,8},{2,10},{4,12},{6,14},{8,0},{10,2},{12,4},{14,6},{16,24},{18,... | collective-permute-start | bytes 479240 | tf_op jit(solution)/shard_map/ppermute | solution.py:440
  58.2 7.8 %collective-permute-start.18 = (f16[104,768]{1,0:T(8,128)(2,1)S(1)}, f16[104,768]{1,0:T(8,128)(2,1)S(1)}, u32[]{:S(2)}, u32[]{:S(2)}) collective-permute-start(f16[104,768]{1,0:T(8,128)(2,1)S(1)} %add_convert_fusion.4), channel_id=1, source_target_pairs={{0,16},{2,18},{4,20},{6,22},{8,24},{10,26},{12,28},{14,30},{16,0},... | collective-permute-start | bytes 479240 | tf_op jit(solution)/shard_map/ppermute | solution.py:440
  61.3 8.2 %collective-permute-start.15 = (f16[200,768]{1,0:T(8,128)(2,1)S(1)}, f16[200,768]{1,0:T(8,128)(2,1)S(1)}, u32[]{:S(2)}, u32[]{:S(2)}) collective-permute-start(f16[200,768]{1,0:T(8,128)(2,1)S(1)} %add_convert_fusion.2), channel_id=1, source_target_pairs={{0,4},{2,6},{4,0},{6,2},{8,12},{10,14},{12,8},{14,10},{16,20},{18,... | collective-permute-start | bytes 921608 | tf_op jit(solution)/shard_map/ppermute | solution.py:440
  69.9 13.7 %collective-permute-start.17 = (f16[104,768]{1,0:T(8,128)(2,1)S(1)}, f16[104,768]{1,0:T(8,128)(2,1)S(1)}, u32[]{:S(2)}, u32[]{:S(2)}) collective-permute-start(f16[104,768]{1,0:T(8,128)(2,1)S(1)} %add_convert_fusion.3), channel_id=1, source_target_pairs={{0,16},{2,18},{4,20},{6,22},{8,24},{10,26},{12,28},{14,30},{16,0},... | collective-permute-start | bytes 479240 | tf_op jit(solution)/shard_map/ppermute | solution.py:440
  71.7 10.3 %collective-permute-start.16 = (f16[56,768]{1,0:T(8,128)(2,1)S(1)}, f16[56,768]{1,0:T(8,128)(2,1)S(1)}, u32[]{:S(2)}, u32[]{:S(2)}) collective-permute-start(f16[56,768]{1,0:T(8,128)(2,1)S(1)} %add_convert_fusion.7), channel_id=1, source_target_pairs={{0,16},{2,18},{4,20},{6,22},{8,24},{10,26},{12,28},{14,30},{16,0},... | collective-permute-start | bytes 258056 | tf_op jit(solution)/shard_map/ppermute | solution.py:440
  73.3 9.3 %collective-permute-start.19 = (f16[56,768]{1,0:T(8,128)(2,1)S(1)}, f16[56,768]{1,0:T(8,128)(2,1)S(1)}, u32[]{:S(2)}, u32[]{:S(2)}) collective-permute-start(f16[56,768]{1,0:T(8,128)(2,1)S(1)} %add_convert_fusion.6), channel_id=1, source_target_pairs={{0,8},{2,10},{4,12},{6,14},{8,0},{10,2},{12,4},{14,6},{16,24},{18,... | collective-permute-start | bytes 258056 | tf_op jit(solution)/shard_map/ppermute | solution.py:440
